TPU v7x, 32 devices: a whole 2x2x4 slice. The times are simulated.
32 devices in a mesh: ctx: 8 (over z, y), head: 4 (over x, core).
Axes of the slice: x: 2, y: 2, z: 4, core: 2. Of those that a mesh axis runs over, the one named last changes fastest.
Arguments:
- queries: bfloat16 [8192, 32, 128], P('ctx', 'head'), may hold values from -16 to 16
- keys: bfloat16 [8192, 32, 128], P('ctx', 'head'), may hold values from -16 to 16
- values: bfloat16 [8192, 32, 128], P('ctx', 'head'), may hold values from -6 to 6
- out_grad: bfloat16 [8192, 4096], P('ctx'), may hold values from -6 to 6
- wo: bfloat16 [4096, 4096], P('head', 'ctx'), may hold values from -0.125 to 0.125
Outputs:
- layer_out: bfloat16 [8192, 4096], P('ctx', 'head')
- queries_gradient: bfloat16 [8192, 32, 128], P('ctx', 'head')
- keys_gradient: bfloat16 [8192, 32, 128], P('ctx', 'head')
- values_gradient: bfloat16 [8192, 32, 128], P('ctx', 'head')
- proj_grad: bfloat16 [4096, 4096], P('head', 'ctx')
All inputs are finite; a program needn't handle non-finite values.
Results may differ from a plain program's by a relative error of at most 0.015.
Values may be sent and summed in bfloat16 or wider, within the bound.
No kernel may reach another device: no remote copies, remote signals or barrier semaphores. Data moves between devices by JAX's collectives and lax.ppermute only.
A program may use at most 128 MiB of HBM per device.

v0:
```python
import functools

import jax
import jax.numpy as jnp
from jax import lax
from jax.experimental import pallas as pl
from jax.experimental.pallas import tpu as pltpu
from jax.sharding import PartitionSpec as P

C = 512
LANE = 16
VMEM = pl.BlockSpec(memory_space=pltpu.VMEM)
BF16 = jnp.bfloat16
F32 = jnp.float32


def params(mib):
    return pltpu.CompilerParams(vmem_limit_bytes=mib * 1024 * 1024)


def dot(a, b, dims):
    return lax.dot_general(a, b, (dims, ((), ())), preferred_element_type=F32)


def softmax(scores):
    highest = jnp.max(scores, axis=-1, keepdims=True)
    lifted = jnp.exp(scores - highest)
    return lifted * (1.0 / jnp.sum(lifted, axis=-1, keepdims=True))


def split_kernel(n, rows, me, q_ref, k_ref, v_ref, *rest):
    chunks, row_refs, wide = rest[:n], rest[n : n + 3], rest[n + 3]
    step, row = pl.program_id(0), pl.program_id(1)
    width, heads, _ = q_ref.shape
    for array, ref in enumerate((q_ref, k_ref, v_ref)):
        wide[array] = ref[...].astype(F32).reshape(width * heads, ref.shape[2])
    for array in range(3):
        for head in range(heads // 2):
            even = wide[array, pl.ds(2 * head, width, stride=heads), :]
            row_refs[array][head] = even.astype(BF16)
    for d in range(n):

        @pl.when(step == d)
        def _():
            for array in range(3):
                for head in range(heads // 2):
                    odd = wide[array, pl.ds(2 * head + 1, width, stride=heads), :]
                    chunks[d][array, head, row] = odd.astype(BF16)


def split_inputs(me, queries, keys, values, n):
    tokens, heads, dim = queries.shape
    rows, width, half = tokens // C, C // n, heads // 2
    block = pl.BlockSpec((width, heads, dim), lambda d, r, me: (r * n + (me[0] ^ d), 0, 0))
    chunk = jax.ShapeDtypeStruct((3, half, rows, width, dim), BF16)
    by_head = jax.ShapeDtypeStruct((half, tokens, dim), BF16)
    out = pl.pallas_call(
        functools.partial(split_kernel, n, rows),
        grid_spec=pltpu.PrefetchScalarGridSpec(
            num_scalar_prefetch=1,
            grid=(n, rows),
            in_specs=[block] * 3,
            out_specs=[pl.BlockSpec(chunk.shape, lambda d, r, me: (0, 0, 0, 0, 0))] * n
            + [pl.BlockSpec((half, width, dim), lambda d, r, me: (0, r * n + (me[0] ^ d), 0))] * 3,
            scratch_shapes=[pltpu.VMEM((3, width * heads, dim), F32)],
        ),
        out_shape=[chunk] * n + [by_head] * 3,
        compiler_params=params(40),
        name="split_inputs",
    )(me, queries, keys, values)
    return out[:n], out[n:]


def join_kernel(n, rows, me, *refs):
    chunks, row_refs, outs, wide = refs[:n], refs[n : n + 3], refs[n + 3 : n + 6], refs[n + 6]
    step, row = pl.program_id(0), pl.program_id(1)
    width, heads, dim = outs[0].shape
    for d in range(n):

        @pl.when(step == d)
        def _():
            for array in range(3):
                for head in range(heads // 2):
                    wide[array, pl.ds(2 * head + 1, width, stride=heads), :] = chunks[d][array, head, row].astype(F32)

    for array in range(3):
        for head in range(heads // 2):
            wide[array, pl.ds(2 * head, width, stride=heads), :] = row_refs[array][head].astype(F32)
        outs[array][...] = wide[array].reshape(width, heads, dim).astype(BF16)


def join_gradients(me, chunks, by_head, n):
    _, half, rows, width, dim = chunks[0].shape
    tokens, heads = by_head[0].shape[1], 2 * half
    whole = jax.ShapeDtypeStruct((tokens, heads, dim), BF16)
    return pl.pallas_call(
        functools.partial(join_kernel, n, rows),
        grid_spec=pltpu.PrefetchScalarGridSpec(
            num_scalar_prefetch=1,
            grid=(n, rows),
            in_specs=[pl.BlockSpec(chunks[0].shape, lambda d, r, me: (0, 0, 0, 0, 0))] * n
            + [pl.BlockSpec((half, width, dim), lambda d, r, me: (0, r * n + (me[0] ^ d), 0))] * 3,
            out_specs=[pl.BlockSpec((width, heads, dim), lambda d, r, me: (r * n + (me[0] ^ d), 0, 0))] * 3,
            scratch_shapes=[pltpu.VMEM((3, width * heads, dim), F32)],
        ),
        out_shape=[whole] * 3,
        compiler_params=params(40),
        name="join_gradients",
    )(me, *chunks, *by_head)


def collect_kernel(n, me, row_ref, *refs):
    chunks, flat_ref, both_ref = refs[:n], refs[n], refs[n + 1]
    half, rows, width, dim = chunks[0].shape
    for head in range(half):
        both_ref[:, 2 * head * dim : (2 * head + 1) * dim] = row_ref[:, head * dim : (head + 1) * dim]
    for d in range(n):
        column = pl.multiple_of((me[0] ^ d) * width, width)
        for row in range(rows):
            for head in range(half):
                part = chunks[d][head, row]
                flat_ref[pl.ds(row * C + column, width), head * dim : (head + 1) * dim] = part
                both_ref[pl.ds(row * C + column, width), (2 * head + 1) * dim : (2 * head + 2) * dim] = part


def collect(me, row_out, chunks, n):
    half, rows, width, dim = chunks[0].shape
    return pl.pallas_call(
        functools.partial(collect_kernel, n),
        in_specs=[pl.BlockSpec(memory_space=pltpu.SMEM)] + [VMEM] * (n + 1),
        out_specs=[VMEM] * 2,
        out_shape=[
            jax.ShapeDtypeStruct((rows * C, half * dim), BF16),
            jax.ShapeDtypeStruct((rows * C, 2 * half * dim), BF16),
        ],
        compiler_params=params(24),
        name="collect",
    )(me, row_out, *chunks)


def attn_grad_kernel(n, dim, me, ids, grad_ref, *refs):
    blocks, row_ref, chunks = refs[:n], refs[n], refs[n + 1 : 2 * n + 1]
    weight, total, sem = refs[2 * n + 1 :]
    step = pl.program_id(0)
    half, rows, width, _ = chunks[0].shape
    tokens = grad_ref.shape[0]
    tile = tokens // 4

    @pl.when(step == 0)
    def _():
        for d in range(n):
            pltpu.make_async_copy(blocks[d], weight.at[ids[d]], sem.at[ids[d]]).start()
        total[...] = jnp.zeros_like(total)

    pltpu.make_async_copy(blocks[0], weight.at[step], sem.at[step]).wait()

    @pl.loop(0, tokens, step=tile)
    def _(at):
        at = pl.multiple_of(at, tile)
        total[pl.ds(at, tile)] += dot(grad_ref[pl.ds(at, tile)], weight[step], ((1,), (1,)))

    @pl.when(step == n - 1)
    def _():
        for head in range(half):
            row_ref[:, head * dim : (head + 1) * dim] = total[:, 2 * head * dim : (2 * head + 1) * dim].astype(BF16)
            for d in range(n):
                column = pl.multiple_of((me[0] ^ d) * width, width)
                for row in range(rows):
                    part = total[pl.ds(row * C + column, width), (2 * head + 1) * dim : (2 * head + 2) * dim]
                    chunks[d][head, row] = part.astype(BF16)


def attn_grad(me, ids, out_grad, blocks, dim):
    n, (span, depth) = len(blocks), blocks[0].shape
    tokens, half = out_grad.shape[0], span // dim // 2
    chunk = jax.ShapeDtypeStruct((half, tokens // C, C // n, dim), BF16)
    out = pl.pallas_call(
        functools.partial(attn_grad_kernel, n, dim),
        grid_spec=pltpu.PrefetchScalarGridSpec(
            num_scalar_prefetch=2,
            grid=(n,),
            in_specs=[pl.BlockSpec((tokens, depth), lambda b, me, ids: (0, b))] + [pl.BlockSpec(memory_space=pl.ANY)] * n,
            out_specs=[pl.BlockSpec((tokens, half * dim), lambda b, me, ids: (0, 0))]
            + [pl.BlockSpec(chunk.shape, lambda b, me, ids: (0, 0, 0, 0))] * n,
            scratch_shapes=[
                pltpu.VMEM((n, span, depth), BF16),
                pltpu.VMEM((tokens, span), F32),
                pltpu.SemaphoreType.DMA((n,)),
            ],
        ),
        out_shape=[jax.ShapeDtypeStruct((tokens, half * dim), BF16)] + [chunk] * n,
        compiler_params=params(40),
        cost_estimate=pl.CostEstimate(
            flops=2 * tokens * span * depth * n,
            bytes_accessed=2 * n * depth * (tokens + span) + 2 * tokens * span,
            transcendentals=0,
        ),
        name="attn_grad",
    )(me, ids, out_grad, *blocks)
    return out[0], out[1:]


def layer_kernel(n, count, adds, ids, wanted, flat_ref, *refs):
    blocks, extra, out_ref = refs[:n], refs[n : n + adds], refs[n + adds]
    weight, sem = refs[n + adds + 1 :]
    step = pl.program_id(0)
    tokens = flat_ref.shape[0]
    tile = tokens // 4

    @pl.when(step == 0)
    def _():
        for s in range(count):
            for d in range(n):

                @pl.when(ids[d] == wanted[s])
                def _():
                    pltpu.make_async_copy(blocks[d], weight.at[s], sem.at[s]).start()

    pltpu.make_async_copy(blocks[0], weight.at[step], sem.at[step]).wait()

    @pl.loop(0, tokens, step=tile)
    def _(at):
        at = pl.multiple_of(at, tile)
        value = dot(flat_ref[pl.ds(at, tile)], weight[step], ((1,), (0,)))
        for ref in extra:
            value = value + ref[pl.ds(at, tile)].astype(F32)
        out_ref[pl.ds(at, tile)] = value.astype(BF16)


def layer_part(ids, flat, blocks, wanted, extra, first):
    n, (span, depth) = len(blocks), blocks[0].shape
    tokens, count = flat.shape[0], wanted.shape[0]
    by_column = pl.BlockSpec((tokens, depth), lambda s, ids, wanted: (0, s))
    return pl.pallas_call(
        functools.partial(layer_kernel, n, count, len(extra)),
        grid_spec=pltpu.PrefetchScalarGridSpec(
            num_scalar_prefetch=2,
            grid=(count,),
            in_specs=[pl.BlockSpec((tokens, span), lambda s, ids, wanted: (0, 0))]
            + [pl.BlockSpec(memory_space=pl.ANY)] * n
            + [pl.BlockSpec((tokens, depth), functools.partial(lambda f, s, ids, wanted: (0, s + f), f)) for f in first],
            out_specs=by_column,
            scratch_shapes=[pltpu.VMEM((count, span, depth), BF16), pltpu.SemaphoreType.DMA((count,))],
        ),
        out_shape=jax.ShapeDtypeStruct((tokens, count * depth), BF16),
        compiler_params=params(32),
        cost_estimate=pl.CostEstimate(
            flops=2 * tokens * span * depth * count,
            bytes_accessed=2 * (count * depth * (tokens + span) + tokens * span),
            transcendentals=0,
        ),
        name="layer_part",
    )(ids, wanted, flat, *blocks, *extra)


def row_blocks(length):
    step = length // 2
    return [(start, step) for start in range(0, length, step)]


def row_probs(q, k, start, step, scale):
    scores = dot(q, k, ((1,), (1,))) * scale
    place = lax.broadcasted_iota(jnp.int32, scores.shape, 0) + start
    seen = lax.broadcasted_iota(jnp.int32, scores.shape, 1)
    return softmax(jnp.where(place >= seen, scores, -jnp.inf))


def row_forward_kernel(scale, q_ref, k_ref, v_ref, o_ref):
    for start, step in row_blocks(q_ref.shape[0]):
        stop = start + step
        probs = row_probs(q_ref[start:stop], k_ref[:stop], start, step, scale)
        o_ref[start:stop] = dot(probs.astype(BF16), v_ref[:stop], ((1,), (0,))).astype(BF16)


def row_forward(q, k, v):
    half, tokens, dim = q.shape
    by_head = pl.BlockSpec((pl.squeezed, C, dim), lambda r, h: (h, r, 0))
    return pl.pallas_call(
        functools.partial(row_forward_kernel, dim**-0.5),
        grid=(tokens // C, half),
        in_specs=[by_head] * 3,
        out_specs=pl.BlockSpec((C, dim), lambda r, h: (r, h)),
        out_shape=jax.ShapeDtypeStruct((tokens, half * dim), BF16),
        compiler_params=params(24),
        cost_estimate=pl.CostEstimate(
            flops=4 * tokens * C * half * dim, bytes_accessed=8 * tokens * half * dim, transcendentals=tokens * C * half
        ),
        name="row_forward",
    )(q, k, v)


def row_backward_kernel(scale, q_ref, k_ref, v_ref, g_ref, dq_ref, dk_ref, dv_ref, k_sum, v_sum):
    k_sum[...] = jnp.zeros_like(k_sum)
    v_sum[...] = jnp.zeros_like(v_sum)
    for start, step in row_blocks(q_ref.shape[0]):
        stop = start + step
        q, k, grad = q_ref[start:stop], k_ref[:stop], g_ref[start:stop]
        probs = row_probs(q, k, start, step, scale)
        prob_grad = dot(grad, v_ref[:stop], ((1,), (1,)))
        inner = jnp.sum(probs * prob_grad, axis=-1, keepdims=True)
        score_low = (probs * (prob_grad - inner)).astype(BF16)
        dq_ref[start:stop] = (dot(score_low, k, ((1,), (0,))) * scale).astype(BF16)
        k_sum[:stop] += dot(score_low, q, ((0,), (0,)))
        v_sum[:stop] += dot(probs.astype(BF16), grad, ((0,), (0,)))
    dk_ref[...] = (k_sum[...] * scale).astype(BF16)
    dv_ref[...] = v_sum[...].astype(BF16)


def row_backward(q, k, v, grad):
    half, tokens, dim = q.shape
    by_head = pl.BlockSpec((pl.squeezed, C, dim), lambda r, h: (h, r, 0))
    return pl.pallas_call(
        functools.partial(row_backward_kernel, dim**-0.5),
        grid=(tokens // C, half),
        in_specs=[by_head] * 3 + [pl.BlockSpec((C, dim), lambda r, h: (r, h))],
        out_specs=[by_head] * 3,
        out_shape=[jax.ShapeDtypeStruct(q.shape, BF16)] * 3,
        scratch_shapes=[pltpu.VMEM((C, dim), F32)] * 2,
        compiler_params=params(32),
        cost_estimate=pl.CostEstimate(
            flops=10 * tokens * C * half * dim, bytes_accessed=14 * tokens * half * dim, transcendentals=tokens * C * half
        ),
        name="row_backward",
    )(q, k, v, grad)


def column_mask(me, n, rows):
    size = n * rows * LANE

    def parts(axis):
        place = lax.broadcasted_iota(jnp.int32, (size, size), axis)
        line, column = place // LANE, place % LANE
        return ((line // rows) ^ me) * rows + line % rows, column

    row_q, column_q = parts(0)
    row_k, column_k = parts(1)
    return (column_q == column_k) & (row_q >= row_k)


def gathered(chunks, index, at):
    rows, dim = chunks[0].shape[-3], chunks[0].shape[-1]
    return jnp.concatenate(
        [chunk[(*index, row, pl.ds(at, LANE), slice(None))] for chunk in chunks for row in range(rows)], axis=0
    )


def scattered(chunks, index, at, value):
    rows = chunks[0].shape[-3]
    for d, chunk in enumerate(chunks):
        for row in range(rows):
            line = d * rows + row
            chunk[(*index, row, pl.ds(at, LANE), slice(None))] = value[line * LANE : (line + 1) * LANE]


def column_probs(bias, q, k, scale):
    return softmax(dot(q, k, ((1,), (1,))) * scale + bias[...])


def column_forward_kernel(n, scale, me, *refs):
    chunks, outs, bias = refs[:n], refs[n : 2 * n], refs[2 * n]
    _, half, rows, width, _ = chunks[0].shape
    bias[...] = jnp.where(column_mask(me[0], n, rows), 0.0, -jnp.inf)
    blocks = width // LANE

    @pl.loop(0, half * blocks)
    def _(step):
        head, at = step // blocks, pl.multiple_of(step % blocks * LANE, LANE)
        q, k, v = (gathered(chunks, (array, head), at) for array in range(3))
        probs = column_probs(bias, q, k, scale)
        scattered(outs, (head,), at, dot(probs.astype(BF16), v, ((1,), (0,))).astype(BF16))


def column_forward(me, chunks, n):
    _, half, rows, width, dim = chunks[0].shape
    size = n * rows * LANE
    return pl.pallas_call(
        functools.partial(column_forward_kernel, n, dim**-0.5),
        in_specs=[pl.BlockSpec(memory_space=pltpu.SMEM)] + [VMEM] * n,
        out_specs=[VMEM] * n,
        out_shape=[jax.ShapeDtypeStruct((half, rows, width, dim), BF16)] * n,
        scratch_shapes=[pltpu.VMEM((size, size), F32)],
        compiler_params=params(24),
        cost_estimate=pl.CostEstimate(
            flops=4 * size * size * dim * half * width // LANE,
            bytes_accessed=8 * n * half * rows * width * dim,
            transcendentals=size * size * half * width // LANE,
        ),
        name="column_forward",
    )(me, *chunks)


def column_backward_kernel(n, scale, me, *refs):
    chunks, grads, outs, bias = refs[:n], refs[n : 2 * n], refs[2 * n : 3 * n], refs[3 * n]
    _, half, rows, width, _ = chunks[0].shape
    bias[...] = jnp.where(column_mask(me[0], n, rows), 0.0, -jnp.inf)
    blocks = width // LANE

    @pl.loop(0, half * blocks)
    def _(step):
        head, at = step // blocks, pl.multiple_of(step % blocks * LANE, LANE)
        q, k, v = (gathered(chunks, (array, head), at) for array in range(3))
        grad = gathered(grads, (head,), at)
        probs = column_probs(bias, q, k, scale)
        prob_grad = dot(grad, v, ((1,), (1,)))
        inner = jnp.sum(probs * prob_grad, axis=-1, keepdims=True)
        score_low = (probs * (prob_grad - inner)).astype(BF16)
        scattered(outs, (0, head), at, (dot(score_low, k, ((1,), (0,))) * scale).astype(BF16))
        scattered(outs, (1, head), at, (dot(score_low, q, ((0,), (0,))) * scale).astype(BF16))
        scattered(outs, (2, head), at, dot(probs.astype(BF16), grad, ((0,), (0,))).astype(BF16))


def column_backward(me, chunks, grads, n):
    _, half, rows, width, dim = chunks[0].shape
    size = n * rows * LANE
    return pl.pallas_call(
        functools.partial(column_backward_kernel, n, dim**-0.5),
        in_specs=[pl.BlockSpec(memory_space=pltpu.SMEM)] + [VMEM] * (2 * n),
        out_specs=[VMEM] * n,
        out_shape=[jax.ShapeDtypeStruct(chunks[0].shape, BF16)] * n,
        scratch_shapes=[pltpu.VMEM((size, size), F32)],
        compiler_params=params(24),
        cost_estimate=pl.CostEstimate(
            flops=10 * size * size * dim * half * width // LANE,
            bytes_accessed=14 * n * half * rows * width * dim,
            transcendentals=size * size * half * width // LANE,
        ),
        name="column_backward",
    )(me, *chunks, *grads)


def swap(chunks, n):
    order = [d for pair in zip(range(n // 2, n), range(n // 2)) for d in pair if d]
    out = list(chunks)
    for d in order:
        out[d] = lax.ppermute(chunks[d], "ctx", [(place, place ^ d) for place in range(n)])
    return out


def gather_weight(me, wo, n):
    inner = n // 4
    line = me[0] // inner

    def along(pairs, block):
        return lax.ppermute(block, "ctx", [(a * inner + y, b * inner + y) for a, b in pairs for y in range(inner)])

    middle = (line == 1) | (line == 2)
    pair, cross, outward = [(0, 1), (1, 0), (2, 3), (3, 2)], [(1, 2), (2, 1)], [(1, 0), (2, 3)]
    near = along(pair, wo)
    cross_own = along(cross, wo)
    cross_near = along(cross, near)
    far_own = jnp.where(middle, cross_own, along(outward, cross_own))
    far_near = jnp.where(middle, cross_near, along(outward, cross_near))
    upper = line < 2
    lines = [line, line ^ 1, jnp.where(upper, 2, 1), jnp.where(upper, 3, 0)]
    blocks, ids = [], []
    for block, owner in zip((wo, near, far_own, far_near), lines):
        for e in range(inner):
            if e:
                blocks.append(lax.ppermute(block, "ctx", [(place, place ^ e) for place in range(n)]))
            else:
                blocks.append(block)
            ids.append(owner * inner + (me[0] % inner ^ e))
    return blocks, jnp.stack(ids).astype(jnp.int32)


def scatter_layer(ids, flat, blocks, heads_n):
    mine = lax.axis_index("head").astype(jnp.int32)
    per = len(blocks) // heads_n

    def wanted(offsets):
        return jnp.stack([(mine ^ g) * per + b for g in offsets for b in range(per)]).astype(jnp.int32)

    def move(part, g):
        return lax.ppermute(part, "head", [(place, place ^ g) for place in range(heads_n)])

    even = list(range(0, heads_n, 2))
    near = move(layer_part(ids, flat, blocks, wanted([g + 1 for g in even]), [], []), 1)
    far = [move(layer_part(ids, flat, blocks, wanted([g]), [near], [g // 2 * per]), g) for g in even[1:]]
    return layer_part(ids, flat, blocks, wanted([0]), [near] + far, [0] * (1 + len(far)))


def on_device(queries, keys, values, out_grad, wo, *, n, heads_n):
    tokens, heads, dim = queries.shape
    half = heads // 2
    me = lax.axis_index("ctx").astype(jnp.int32).reshape(1)
    chunks, by_head = split_inputs(me, queries, keys, values, n)
    chunks = swap(chunks, n)
    blocks, ids = gather_weight(me, wo, n)

    row_out = row_forward(*by_head)
    proj_row = dot(row_out, out_grad, ((0,), (0,))).astype(BF16)
    proj_row = lax.psum_scatter(proj_row, "ctx", scatter_dimension=1, tiled=True)

    grad_row, grads = attn_grad(me, ids, out_grad, blocks, dim)
    grads = swap(grads, n)
    column_out, flat = collect(me, row_out, swap(column_forward(me, chunks, n), n), n)
    column_out, proj_row = lax.optimization_barrier((column_out, proj_row))
    proj_column = dot(column_out, out_grad, ((0,), (0,))).astype(BF16)
    proj_column = lax.psum_scatter(proj_column, "ctx", scatter_dimension=1, tiled=True)

    layer_out = scatter_layer(ids, flat, blocks, heads_n)
    column_grads = swap(column_backward(me, chunks, grads, n), n)
    row_grads = row_backward(*by_head, grad_row)
    gradients = join_gradients(me, column_grads, row_grads, n)

    shape = (half, dim, proj_row.shape[1])
    proj_grad = jnp.stack([proj_row.reshape(shape), proj_column.reshape(shape)], axis=1)
    return (layer_out, *gradients, proj_grad.reshape(heads * dim, shape[2]))


def solution(mesh):
    in_specs = (
        P("ctx", "head", None),
        P("ctx", "head", None),
        P("ctx", "head", None),
        P("ctx", None),
        P("head", "ctx"),
    )
    out_specs = (
        P("ctx", "head"),
        P("ctx", "head", None),
        P("ctx", "head", None),
        P("ctx", "head", None),
        P("head", "ctx"),
    )
    return jax.shard_map(
        functools.partial(on_device, n=mesh.shape["ctx"], heads_n=mesh.shape["head"]),
        mesh=mesh,
        in_specs=in_specs,
        out_specs=out_specs,
        check_vma=False,
    )
```

profile of v0, /device:TPU:8, one launch (start us, length us, event | category | flops | bytes accessed | tf_op | source)
XLA Modules:
  0.0 541.6 jit_solution(16010586207132547687)
XLA Ops:
  12.0 4.1 split_inputs.1
  19.1 7.9 %row_forward.1.row_ref = bf16[1024,512]{1,0:T(8,128)(2,1)S(1)} custom-call(bf16[4,1024,128]{2,1,0:T(8,128)(2,1)S(1)} %get-tuple-element.51.q_ref, bf16[4,1024,128]{2,1,0:T(8,128)(2,1)S(1)} %get-tuple-element.52.k_ref, bf16[4,1024,128]{2,1,0:T(8,128)(2,1)S(1)} %get-tuple-element.53.v_ref), custom_call_target="tpu_custom_call" | custom-call | flops 1073741824 | bytes 4194304 | tf_op jit(solution)/shard_map/row_forward/pallas_call | solution.py:278
  27.1 6.1 %convolution_convert_fusion.1 = bf16[512,4096]{1,0:T(8,128)(2,1)} fusion(bf16[1024,512]{1,0:T(8,128)(2,1)S(1)} %row_forward.1.row_ref, bf16[1024,4096]{1,0:T(8,128)(2,1)S(1)} %copy-done.44), kind=kOutput, calls=%fused_computation.1 | convolution fusion | flops 4297064448 | bytes 13631488 | tf_op jit(solution)/shard_map/dot_general | solution.py:22
  34.5 5.0 collective-permute-start.17
  43.1 12.6 %collective-permute-done.refs_1_ = bf16[3,4,2,64,128]{4,3,2,1,0:T(8,128)(2,1)S(1)} collective-permute-done((bf16[3,4,2,64,128]{4,3,2,1,0:T(8,128)(2,1)}, bf16[3,4,2,64,128]{4,3,2,1,0:T(8,128)(2,1)S(1)}, u32[]{:S(2)}, u32[]{:S(2)}) %collective-permute-start) | collective-permute-done | bytes 393248 | tf_op jit(solution)/shard_map/ppermute | solution.py:435
  55.7 23.0 %collective-permute-done.15.refs_2_ = bf16[1024,512]{1,0:T(8,128)(2,1)} collective-permute-done((bf16[1024,512]{1,0:T(8,128)(2,1)S(1)}, bf16[1024,512]{1,0:T(8,128)(2,1)}, u32[]{:S(2)}, u32[]{:S(2)}) %collective-permute-start.15) | collective-permute-done | bytes 1048608 | tf_op jit(solution)/shard_map/ppermute | solution.py:444
  78.8 8.0 %collective-permute-start.20 = (bf16[1024,512]{1,0:T(8,128)(2,1)}, bf16[1024,512]{1,0:T(8,128)(2,1)}, u32[]{:S(2)}, u32[]{:S(2)}) collective-permute-start(bf16[1024,512]{1,0:T(8,128)(2,1)} %collective-permute-done.15.refs_2_), channel_id=1, source_target_pairs={{8,16},{12,20},{16,8},{20,12},{9,17},{13,21},{17,9},{21,13},{10,18... | collective-permute-start | bytes 3145736 | tf_op jit(solution)/shard_map/ppermute | solution.py:444
  89.2 19.4 %collective-permute-done.1.refs_2_ = bf16[3,4,2,64,128]{4,3,2,1,0:T(8,128)(2,1)S(1)} collective-permute-done((bf16[3,4,2,64,128]{4,3,2,1,0:T(8,128)(2,1)}, bf16[3,4,2,64,128]{4,3,2,1,0:T(8,128)(2,1)S(1)}, u32[]{:S(2)}, u32[]{:S(2)}) %collective-permute-start.1) | collective-permute-done | bytes 393248 | tf_op jit(solution)/shard_map/ppermute | solution.py:435
  108.7 6.0 %collective-permute-start.4 = (bf16[3,4,2,64,128]{4,3,2,1,0:T(8,128)(2,1)}, bf16[3,4,2,64,128]{4,3,2,1,0:T(8,128)(2,1)S(1)}, u32[]{:S(2)}, u32[]{:S(2)}) collective-permute-start(bf16[3,4,2,64,128]{4,3,2,1,0:T(8,128)(2,1)} %copy-done.37), channel_id=1, source_target_pairs={{0,20},{4,16},{8,28},{12,24},{16,4},{20,0},{24,12},{28,8},{1,21},{... | collective-permute-start | bytes 1179656 | tf_op jit(solution)/shard_map/ppermute | solution.py:435
  117.1 3.2 collective-permute-start.5
  122.0 64.8 %collective-permute-done.4.refs_5_ = bf16[3,4,2,64,128]{4,3,2,1,0:T(8,128)(2,1)S(1)} collective-permute-done((bf16[3,4,2,64,128]{4,3,2,1,0:T(8,128)(2,1)}, bf16[3,4,2,64,128]{4,3,2,1,0:T(8,128)(2,1)S(1)}, u32[]{:S(2)}, u32[]{:S(2)}) %collective-permute-start.4) | collective-permute-done | bytes 393248 | tf_op jit(solution)/shard_map/ppermute | solution.py:435
  186.8 8.7 %collective-permute-done.5.refs_6_ = bf16[3,4,2,64,128]{4,3,2,1,0:T(8,128)(2,1)S(1)} collective-permute-done((bf16[3,4,2,64,128]{4,3,2,1,0:T(8,128)(2,1)S(1)}, bf16[3,4,2,64,128]{4,3,2,1,0:T(8,128)(2,1)S(1)}, u32[]{:S(2)}, u32[]{:S(2)}) %collective-permute-start.5) | collective-permute-done | bytes 393248 | tf_op jit(solution)/shard_map/ppermute | solution.py:435
  195.6 8.2 %collective-permute-done.6.refs_7_ = bf16[3,4,2,64,128]{4,3,2,1,0:T(8,128)(2,1)S(1)} collective-permute-done((bf16[3,4,2,64,128]{4,3,2,1,0:T(8,128)(2,1)S(1)}, bf16[3,4,2,64,128]{4,3,2,1,0:T(8,128)(2,1)S(1)}, u32[]{:S(2)}, u32[]{:S(2)}) %collective-permute-start.6) | collective-permute-done | bytes 393248 | tf_op jit(solution)/shard_map/ppermute | solution.py:435
  203.8 8.7 %column_forward.1 = (bf16[4,2,64,128]{3,2,1,0:T(8,128)(2,1)S(1)}, bf16[4,2,64,128]{3,2,1,0:T(8,128)(2,1)S(1)}, bf16[4,2,64,128]{3,2,1,0:T(8,128)(2,1)S(1)}, bf16...) custom-call(s32[1]{0:T(128)} %bitcast.10.me, ...), custom_call_target="tpu_custom_call" | custom-call | flops 536870912 | bytes 4194304 | tf_op jit(solution)/shard_map/column_forward/pallas_call | solution.py:376
  213.1 3.0 collective-permute-start.9
  216.1 2.9 collective-permute-done.7.refs_1_
  219.0 3.1 collective-permute-start.11
  225.2 6.4 %collective-permute-done.10.refs_4_ = bf16[4,2,64,128]{3,2,1,0:T(8,128)(2,1)S(1)} collective-permute-done((bf16[4,2,64,128]{3,2,1,0:T(8,128)(2,1)S(1)}, bf16[4,2,64,128]{3,2,1,0:T(8,128)(2,1)S(1)}, u32[]{:S(2)}, u32[]{:S(2)}) %collective-permute-start.10) | collective-permute-done | bytes 131104 | tf_op jit(solution)/shard_map/ppermute | solution.py:435
  234.9 2.8 collective-permute-done.12.refs_6_
  237.7 3.6 collective-permute-done.13.refs_7_
  245.0 4.1 collective-permute-start.21
  251.9 10.3 %convolution_convert_fusion = bf16[512,4096]{1,0:T(8,128)(2,1)} fusion(bf16[1024,512]{1,0:T(8,128)(2,1)} %copy-done.36, bf16[1024,4096]{1,0:T(8,128)(2,1)} %grad_ref.1), kind=kOutput, calls=%fused_computation | convolution fusion | flops 4297064448 | bytes 13631488 | tf_op jit(solution)/shard_map/dot_general | solution.py:22
  262.2 2.6 collective-permute-done.21
  268.2 22.7 %collective-permute-done.16.refs_3_ = bf16[1024,512]{1,0:T(8,128)(2,1)} collective-permute-done((bf16[1024,512]{1,0:T(8,128)(2,1)}, bf16[1024,512]{1,0:T(8,128)(2,1)}, u32[]{:S(2)}, u32[]{:S(2)}) %collective-permute-start.16) | collective-permute-done | bytes 1048608 | tf_op jit(solution)/shard_map/ppermute | solution.py:459
  290.8 33.8 %collective-permute-done.19.refs_5_ = bf16[1024,512]{1,0:T(8,128)(2,1)} collective-permute-done((bf16[1024,512]{1,0:T(8,128)(2,1)S(1)}, bf16[1024,512]{1,0:T(8,128)(2,1)}, u32[]{:S(2)}, u32[]{:S(2)}) %collective-permute-start.19) | collective-permute-done | bytes 1048608 | tf_op jit(solution)/shard_map/ppermute | solution.py:459
  324.6 22.8 %collective-permute-done.22.refs_7_ = bf16[1024,512]{1,0:T(8,128)(2,1)} collective-permute-done((bf16[1024,512]{1,0:T(8,128)(2,1)S(1)}, bf16[1024,512]{1,0:T(8,128)(2,1)}, u32[]{:S(2)}, u32[]{:S(2)}) %collective-permute-start.22) | collective-permute-done | bytes 1048608 | tf_op jit(solution)/shard_map/ppermute | solution.py:459
  349.0 9.0 %layer_part.3 = bf16[1024,2048]{1,0:T(8,128)(2,1)} custom-call(s32[8]{0:T(128)S(1)} %stack.71.ids, s32[4]{0:T(128)S(1)} %pad_add_fusion.1.wanted, bf16[1024,1024]{1,0:T(8,128)(2,1)S(1)} %copy-done.1, bf16[1024,512]{1,0:T(8,128)(2,1)S(1)} %copy-done.4, bf16[1024,512]{1,0:T(8,128)(2,1)} %collective-permute-done.14.refs_1_, ...), custom_call_target="tpu_custom_call" | custom-call | flops 4294967296 | bytes 10485760 | tf_op jit(solution)/shard_map/layer_part/pallas_call | solution.py:234
  358.2 7.4 %collective-permute-done.23.refs_8_ = bf16[1024,2048]{1,0:T(8,128)(2,1)} collective-permute-done((bf16[1024,2048]{1,0:T(8,128)(2,1)}, bf16[1024,2048]{1,0:T(8,128)(2,1)}, u32[]{:S(2)}, u32[]{:S(2)}) %collective-permute-start.23) | collective-permute-done | bytes 4194336 | tf_op jit(solution)/shard_map/ppermute | solution.py:474
  367.2 6.5 %layer_part.4 = bf16[1024,1024]{1,0:T(8,128)(2,1)} custom-call(s32[8]{0:T(128)S(1)} %stack.71.ids, s32[2]{0:T(128)S(1)} %pad_add_fusion.2.wanted, bf16[1024,1024]{1,0:T(8,128)(2,1)S(1)} %copy-done.2, bf16[1024,512]{1,0:T(8,128)(2,1)S(1)} %copy-done.4, bf16[1024,512]{1,0:T(8,128)(2,1)} %collective-permute-done.14.refs_1_, ...), custom_call_target="tpu_custom_call" | custom-call | flops 2147483648 | bytes 6291456 | tf_op jit(solution)/shard_map/layer_part/pallas_call | solution.py:234
  373.8 2.7 collective-permute-start.24
  376.5 19.3 %attn_grad.1 = (bf16[1024,512]{1,0:T(8,128)(2,1)S(1)}, bf16[4,2,64,128]{3,2,1,0:T(8,128)(2,1)S(1)}, bf16[4,2,64,128]{3,2,1,0:T(8,128)(2,1)S(1)}, bf16[4,2,64,128...) custom-call(s32[1]{0:T(128)} %bitcast.10.me, ...), custom_call_target="tpu_custom_call" | custom-call | flops 8589934592 | bytes 18874368 | tf_op jit(solution)/shard_map/attn_grad/pallas_call | solution.py:177
  395.8 3.0 collective-permute-start.25
  398.8 4.0 collective-permute-start.26
  403.8 3.4 collective-permute-start.29
  412.3 9.3 %collective-permute-done.29.refs_13_ = bf16[4,2,64,128]{3,2,1,0:T(8,128)(2,1)S(1)} collective-permute-done((bf16[4,2,64,128]{3,2,1,0:T(8,128)(2,1)S(1)}, bf16[4,2,64,128]{3,2,1,0:T(8,128)(2,1)S(1)}, u32[]{:S(2)}, u32[]{:S(2)}) %collective-permute-start.29) | collective-permute-done | bytes 131104 | tf_op jit(solution)/shard_map/ppermute | solution.py:435
  421.6 4.6 collective-permute-done.30.refs_14_
  426.2 2.9 collective-permute-done.31.refs_15_
  429.2 12.9 %column_backward.1 = (bf16[3,4,2,64,128]{4,3,2,1,0:T(8,128)(2,1)S(1)}, bf16[3,4,2,64,128]{4,3,2,1,0:T(8,128)(2,1)S(1)}, bf16[3,4,2,64,128]{4,3,2,1,0:T(8,128)(2,...) custom-call(s32[1]{0:T(128)} %bitcast.10.me, ...), custom_call_target="tpu_custom_call" | custom-call | flops 1342177280 | bytes 7340032 | tf_op jit(solution)/shard_map/column_backward/pallas_call | solution.py:415
  442.8 2.9 collective-permute-start.34
  445.7 7.6 %collective-permute-done.32.refs_1_ = bf16[3,4,2,64,128]{4,3,2,1,0:T(8,128)(2,1)S(1)} collective-permute-done((bf16[3,4,2,64,128]{4,3,2,1,0:T(8,128)(2,1)S(1)}, bf16[3,4,2,64,128]{4,3,2,1,0:T(8,128)(2,1)S(1)}, u32[]{:S(2)}, u32[]{:S(2)}) %collective-permute-start.32) | collective-permute-done | bytes 393248 | tf_op jit(solution)/shard_map/ppermute | solution.py:435
  454.1 12.2 %collective-permute-done.33.refs_2_ = bf16[3,4,2,64,128]{4,3,2,1,0:T(8,128)(2,1)S(1)} collective-permute-done((bf16[3,4,2,64,128]{4,3,2,1,0:T(8,128)(2,1)S(1)}, bf16[3,4,2,64,128]{4,3,2,1,0:T(8,128)(2,1)S(1)}, u32[]{:S(2)}, u32[]{:S(2)}) %collective-permute-start.33) | collective-permute-done | bytes 393248 | tf_op jit(solution)/shard_map/ppermute | solution.py:435
  469.1 4.0 collective-permute-done.34.refs_3_
  481.4 11.9 %row_backward.1 = (bf16[4,1024,128]{2,1,0:T(8,128)(2,1)S(1)}, bf16[4,1024,128]{2,1,0:T(8,128)(2,1)S(1)}, bf16[4,1024,128]{2,1,0:T(8,128)(2,1)S(1)}) custom-call(bf16[4,1024,128]{2,1,0:T(8,128)(2,1)S(1)} %copy-done.9, bf16[4,1024,128]{2,1,0:T(8,128)(2,1)S(1)} %copy-done.11, bf16[4,1024,128]{2,1,0:T(8,128)(2,1)S(1)} %copy-done.13, bf16[1024,512]{1,0:T(8,128)(2,1)S(1)} %copy-done.43), custom_call_target="tpu_custom_call" | custom-call | flops 2684354560 | bytes 7340032 | tf_op jit(solution)/shard_map/row_backward/pallas_call | solution.py:312
  493.3 2.9 collective-permute-done.36.refs_5_
  496.1 11.9 %collective-permute-done.37.refs_6_ = bf16[3,4,2,64,128]{4,3,2,1,0:T(8,128)(2,1)} collective-permute-done((bf16[3,4,2,64,128]{4,3,2,1,0:T(8,128)(2,1)}, bf16[3,4,2,64,128]{4,3,2,1,0:T(8,128)(2,1)}, u32[]{:S(2)}, u32[]{:S(2)}) %collective-permute-start.37) | collective-permute-done | bytes 393248 | tf_op jit(solution)/shard_map/ppermute | solution.py:435
  508.0 6.3 %collective-permute-done.38.refs_7_ = bf16[3,4,2,64,128]{4,3,2,1,0:T(8,128)(2,1)} collective-permute-done((bf16[3,4,2,64,128]{4,3,2,1,0:T(8,128)(2,1)}, bf16[3,4,2,64,128]{4,3,2,1,0:T(8,128)(2,1)}, u32[]{:S(2)}, u32[]{:S(2)}) %collective-permute-start.38) | collective-permute-done | bytes 393248 | tf_op jit(solution)/shard_map/ppermute | solution.py:435
  514.3 9.9 %join_gradients.1 = (bf16[1024,8,128]{2,1,0:T(8,128)(2,1)}, bf16[1024,8,128]{2,1,0:T(8,128)(2,1)}, bf16[1024,8,128]{2,1,0:T(8,128)(2,1)}) custom-call(s32[1]{0:T(128)} %bitcast.10.me, bf16[3,4,2,64,128]{4,3,2,1,0:T(8,128)(2,1)S(1)} %get-tuple-element.79.refs_0_, bf16[3,4,2,64,128]{4,3,2,1,0:T(8,128)(2,1)S(1)} %copy-done.15, ...), custom_call_target="tpu_custom_call" | custom-call | tf_op jit(solution)/shard_map/join_gradients/pallas_call | solution.py:96
  524.2 8.1 %layer_part.5 = bf16[1024,1024]{1,0:T(8,128)(2,1)} custom-call(s32[8]{0:T(128)S(1)} %stack.71.ids, s32[2]{0:T(128)S(1)} %pad_add_fusion.wanted, bf16[1024,1024]{1,0:T(8,128)(2,1)S(1)} %copy-done.3, bf16[1024,512]{1,0:T(8,128)(2,1)S(1)} %copy-done.4, bf16[1024,512]{1,0:T(8,128)(2,1)} %collective-permute-done.14.refs_1_, ...), custom_call_target="tpu_custom_call" | custom-call | flops 2147483648 | bytes 6291456 | tf_op jit(solution)/shard_map/layer_part/pallas_call | solution.py:234
  (147 shorter events, 60.3 us)
Async XLA Ops:
  7.2 244.7 %reduce-scatter.3.cloned.1.call-start = ((), (), s32[]{:S(2)}) async-start(), calls=%async_computation.2 | async-start | bytes 4718592 | tf_op jit(solution)/shard_map/reduce_scatter | solution.py:492
  19.1 184.7 %copy-start.20 = (bf16[3,4,2,64,128]{4,3,2,1,0:T(8,128)(2,1)}, bf16[3,4,2,64,128]{4,3,2,1,0:T(8,128)(2,1)S(1)}, u32[]{:S(2)}) copy-start(bf16[3,4,2,64,128]{4,3,2,1,0:T(8,128)(2,1)S(1)} %get-tuple-element.54.refs_0_) | copy-start | bytes 1179652
  33.3 499.1 %reduce-scatter.5.cloned.1.call-start = ((), (), s32[]{:S(2)}) async-start(), calls=%async_computation.3 | async-start | bytes 4718592 | tf_op jit(solution)/shard_map/reduce_scatter | solution.py:499
  34.5 44.3 %collective-permute-start.15 = (bf16[1024,512]{1,0:T(8,128)(2,1)S(1)}, bf16[1024,512]{1,0:T(8,128)(2,1)}, u32[]{:S(2)}, u32[]{:S(2)}) collective-permute-start(bf16[1024,512]{1,0:T(8,128)(2,1)S(1)} %copy-done.4), channel_id=1, source_target_pairs={{0,8},{4,12},{8,0},{12,4},{16,24},{20,28},{24,16},{28,20},{1,9},{5... | collective-permute-start | bytes 3145736 | tf_op jit(solution)/shard_map/ppermute | solution.py:444
  34.5 52.4 %collective-permute-start.17 = (bf16[1024,512]{1,0:T(8,128)(2,1)S(1)}, bf16[1024,512]{1,0:T(8,128)(2,1)}, u32[]{:S(2)}, u32[]{:S(2)}) collective-permute-start(bf16[1024,512]{1,0:T(8,128)(2,1)S(1)} %copy-done.4), channel_id=1, source_target_pairs={{8,16},{12,20},{16,8},{20,12},{9,17},{13,21},{17,9},{21,13},{10,18... | collective-permute-start | bytes 3145736 | tf_op jit(solution)/shard_map/ppermute | solution.py:444
  39.5 16.2 %collective-permute-start = (bf16[3,4,2,64,128]{4,3,2,1,0:T(8,128)(2,1)}, bf16[3,4,2,64,128]{4,3,2,1,0:T(8,128)(2,1)S(1)}, u32[]{:S(2)}, u32[]{:S(2)}) collective-permute-start(bf16[3,4,2,64,128]{4,3,2,1,0:T(8,128)(2,1)} %copy-done.41), channel_id=1, source_target_pairs={{0,4},{4,0},{8,12},{12,8},{16,20},{20,16},{24,28},{28,24},{1,5},{5... | collective-permute-start | bytes 1179656 | tf_op jit(solution)/shard_map/ppermute | solution.py:435
  41.1 67.5 %collective-permute-start.1 = (bf16[3,4,2,64,128]{4,3,2,1,0:T(8,128)(2,1)}, bf16[3,4,2,64,128]{4,3,2,1,0:T(8,128)(2,1)S(1)}, u32[]{:S(2)}, u32[]{:S(2)}) collective-permute-start(bf16[3,4,2,64,128]{4,3,2,1,0:T(8,128)(2,1)} %copy-done.40), channel_id=1, source_target_pairs={{0,8},{4,12},{8,0},{12,4},{16,24},{20,28},{24,16},{28,20},{1,9},{5... | collective-permute-start | bytes 1179656 | tf_op jit(solution)/shard_map/ppermute | solution.py:435
  41.1 76.0 %collective-permute-start.2 = (bf16[3,4,2,64,128]{4,3,2,1,0:T(8,128)(2,1)}, bf16[3,4,2,64,128]{4,3,2,1,0:T(8,128)(2,1)S(1)}, u32[]{:S(2)}, u32[]{:S(2)}) collective-permute-start(bf16[3,4,2,64,128]{4,3,2,1,0:T(8,128)(2,1)} %copy-done.39), channel_id=1, source_target_pairs={{0,12},{4,8},{8,4},{12,0},{16,28},{20,24},{24,20},{28,16},{1,13},{... | collective-permute-start | bytes 1179656 | tf_op jit(solution)/shard_map/ppermute | solution.py:435
  55.7 156.8 %copy-start.22 = (bf16[3,4,2,64,128]{4,3,2,1,0:T(8,128)(2,1)}, bf16[3,4,2,64,128]{4,3,2,1,0:T(8,128)(2,1)S(1)}, u32[]{:S(2)}) copy-start(bf16[3,4,2,64,128]{4,3,2,1,0:T(8,128)(2,1)S(1)} %collective-permute-done.refs_1_) | copy-start | bytes 1179652
  55.7 64.9 %collective-permute-start.3 = (bf16[3,4,2,64,128]{4,3,2,1,0:T(8,128)(2,1)}, bf16[3,4,2,64,128]{4,3,2,1,0:T(8,128)(2,1)S(1)}, u32[]{:S(2)}, u32[]{:S(2)}) collective-permute-start(bf16[3,4,2,64,128]{4,3,2,1,0:T(8,128)(2,1)} %copy-done.38), channel_id=1, source_target_pairs={{0,16},{4,20},{8,24},{12,28},{16,0},{20,4},{24,8},{28,12},{1,17},{... | collective-permute-start | bytes 1179656 | tf_op jit(solution)/shard_map/ppermute | solution.py:435
  78.8 166.3 %collective-permute-start.20 = (bf16[1024,512]{1,0:T(8,128)(2,1)}, bf16[1024,512]{1,0:T(8,128)(2,1)}, u32[]{:S(2)}, u32[]{:S(2)}) collective-permute-start(bf16[1024,512]{1,0:T(8,128)(2,1)} %collective-permute-done.15.refs_2_), channel_id=1, source_target_pairs={{8,16},{12,20},{16,8},{20,12},{9,17},{13,21},{17,9},{21,13},{10,18... | collective-permute-start | bytes 3145736 | tf_op jit(solution)/shard_map/ppermute | solution.py:444
  86.9 162.3 %collective-permute-start.18 = (bf16[1024,512]{1,0:T(8,128)(2,1)}, bf16[1024,512]{1,0:T(8,128)(2,1)}, u32[]{:S(2)}, u32[]{:S(2)}) collective-permute-start(bf16[1024,512]{1,0:T(8,128)(2,1)} %collective-permute-done.17), channel_id=1, source_target_pairs={{8,0},{12,4},{16,24},{20,28},{9,1},{13,5},{17,25},{21,29},{10,2},{... | collective-permute-start | bytes 3145736 | tf_op jit(solution)/shard_map/ppermute | solution.py:444
  108.7 103.9 %copy-start.24 = (bf16[3,4,2,64,128]{4,3,2,1,0:T(8,128)(2,1)}, bf16[3,4,2,64,128]{4,3,2,1,0:T(8,128)(2,1)S(1)}, u32[]{:S(2)}) copy-start(bf16[3,4,2,64,128]{4,3,2,1,0:T(8,128)(2,1)S(1)} %collective-permute-done.1.refs_2_) | copy-start | bytes 1179652
  108.7 78.1 %collective-permute-start.4 = (bf16[3,4,2,64,128]{4,3,2,1,0:T(8,128)(2,1)}, bf16[3,4,2,64,128]{4,3,2,1,0:T(8,128)(2,1)S(1)}, u32[]{:S(2)}, u32[]{:S(2)}) collective-permute-start(bf16[3,4,2,64,128]{4,3,2,1,0:T(8,128)(2,1)} %copy-done.37), channel_id=1, source_target_pairs={{0,20},{4,16},{8,28},{12,24},{16,4},{20,0},{24,12},{28,8},{1,21},{... | collective-permute-start | bytes 1179656 | tf_op jit(solution)/shard_map/ppermute | solution.py:435
  117.1 96.0 %copy-start.26 = (bf16[3,4,2,64,128]{4,3,2,1,0:T(8,128)(2,1)}, bf16[3,4,2,64,128]{4,3,2,1,0:T(8,128)(2,1)S(1)}, u32[]{:S(2)}) copy-start(bf16[3,4,2,64,128]{4,3,2,1,0:T(8,128)(2,1)S(1)} %collective-permute-done.2.refs_3_) | copy-start | bytes 1179652
  117.1 78.4 %collective-permute-start.5 = (bf16[3,4,2,64,128]{4,3,2,1,0:T(8,128)(2,1)S(1)}, bf16[3,4,2,64,128]{4,3,2,1,0:T(8,128)(2,1)S(1)}, u32[]{:S(2)}, u32[]{:S(2)}) collective-permute-start(bf16[3,4,2,64,128]{4,3,2,1,0:T(8,128)(2,1)S(1)} %get-tuple-element.60), channel_id=1, source_target_pairs={{0,24},{4,28},{8,16},{12,20},{16,8},{20,12},{24,0},{28,4},{1,25},{... | collective-permute-start | bytes 1179656 | tf_op jit(solution)/shard_map/ppermute | solution.py:435
  120.6 92.5 %copy-start.28 = (bf16[3,4,2,64,128]{4,3,2,1,0:T(8,128)(2,1)}, bf16[3,4,2,64,128]{4,3,2,1,0:T(8,128)(2,1)S(1)}, u32[]{:S(2)}) copy-start(bf16[3,4,2,64,128]{4,3,2,1,0:T(8,128)(2,1)S(1)} %collective-permute-done.3.refs_4_) | copy-start | bytes 1179652
  120.6 83.2 %collective-permute-start.6 = (bf16[3,4,2,64,128]{4,3,2,1,0:T(8,128)(2,1)S(1)}, bf16[3,4,2,64,128]{4,3,2,1,0:T(8,128)(2,1)S(1)}, u32[]{:S(2)}, u32[]{:S(2)}) collective-permute-start(bf16[3,4,2,64,128]{4,3,2,1,0:T(8,128)(2,1)S(1)} %get-tuple-element.61), channel_id=1, source_target_pairs={{0,28},{4,24},{8,20},{12,16},{16,12},{20,8},{24,4},{28,0},{1,29},{... | collective-permute-start | bytes 1179656 | tf_op jit(solution)/shard_map/ppermute | solution.py:435
  212.5 6.4 %collective-permute-start.7 = (bf16[4,2,64,128]{3,2,1,0:T(8,128)(2,1)S(1)}, bf16[4,2,64,128]{3,2,1,0:T(8,128)(2,1)S(1)}, u32[]{:S(2)}, u32[]{:S(2)}) collective-permute-start(bf16[4,2,64,128]{3,2,1,0:T(8,128)(2,1)S(1)} %get-tuple-element.63), channel_id=1, source_target_pairs={{0,4},{4,0},{8,12},{12,8},{16,20},{20,16},{24,28},{28,24},{1,5},{5... | collective-permute-start | bytes 393224 | tf_op jit(solution)/shard_map/ppermute | solution.py:435
  213.1 5.9 %collective-permute-start.8 = (bf16[4,2,64,128]{3,2,1,0:T(8,128)(2,1)S(1)}, bf16[4,2,64,128]{3,2,1,0:T(8,128)(2,1)S(1)}, u32[]{:S(2)}, u32[]{:S(2)}) collective-permute-start(bf16[4,2,64,128]{3,2,1,0:T(8,128)(2,1)S(1)} %get-tuple-element.64), channel_id=1, source_target_pairs={{0,8},{4,12},{8,0},{12,4},{16,24},{20,28},{24,16},{28,20},{1,9},{5... | collective-permute-start | bytes 393224 | tf_op jit(solution)/shard_map/ppermute | solution.py:435
  213.1 10.1 %collective-permute-start.9 = (bf16[4,2,64,128]{3,2,1,0:T(8,128)(2,1)S(1)}, bf16[4,2,64,128]{3,2,1,0:T(8,128)(2,1)S(1)}, u32[]{:S(2)}, u32[]{:S(2)}) collective-permute-start(bf16[4,2,64,128]{3,2,1,0:T(8,128)(2,1)S(1)} %get-tuple-element.65), channel_id=1, source_target_pairs={{0,12},{4,8},{8,4},{12,0},{16,28},{20,24},{24,20},{28,16},{1,13},{... | collective-permute-start | bytes 393224 | tf_op jit(solution)/shard_map/ppermute | solution.py:435
  219.0 12.7 %collective-permute-start.10 = (bf16[4,2,64,128]{3,2,1,0:T(8,128)(2,1)S(1)}, bf16[4,2,64,128]{3,2,1,0:T(8,128)(2,1)S(1)}, u32[]{:S(2)}, u32[]{:S(2)}) collective-permute-start(bf16[4,2,64,128]{3,2,1,0:T(8,128)(2,1)S(1)} %get-tuple-element.66), channel_id=1, source_target_pairs={{0,16},{4,20},{8,24},{12,28},{16,0},{20,4},{24,8},{28,12},{1,17},{... | collective-permute-start | bytes 393224 | tf_op jit(solution)/shard_map/ppermute | solution.py:435
  219.0 15.5 %collective-permute-start.11 = (bf16[4,2,64,128]{3,2,1,0:T(8,128)(2,1)S(1)}, bf16[4,2,64,128]{3,2,1,0:T(8,128)(2,1)S(1)}, u32[]{:S(2)}, u32[]{:S(2)}) collective-permute-start(bf16[4,2,64,128]{3,2,1,0:T(8,128)(2,1)S(1)} %get-tuple-element.67), channel_id=1, source_target_pairs={{0,20},{4,16},{8,28},{12,24},{16,4},{20,0},{24,12},{28,8},{1,21},{... | collective-permute-start | bytes 393224 | tf_op jit(solution)/shard_map/ppermute | solution.py:435
  223.2 14.5 %collective-permute-start.12 = (bf16[4,2,64,128]{3,2,1,0:T(8,128)(2,1)S(1)}, bf16[4,2,64,128]{3,2,1,0:T(8,128)(2,1)S(1)}, u32[]{:S(2)}, u32[]{:S(2)}) collective-permute-start(bf16[4,2,64,128]{3,2,1,0:T(8,128)(2,1)S(1)} %get-tuple-element.68), channel_id=1, source_target_pairs={{0,24},{4,28},{8,16},{12,20},{16,8},{20,12},{24,0},{28,4},{1,25},{... | collective-permute-start | bytes 393224 | tf_op jit(solution)/shard_map/ppermute | solution.py:435
  231.7 9.6 %collective-permute-start.13 = (bf16[4,2,64,128]{3,2,1,0:T(8,128)(2,1)S(1)}, bf16[4,2,64,128]{3,2,1,0:T(8,128)(2,1)S(1)}, u32[]{:S(2)}, u32[]{:S(2)}) collective-permute-start(bf16[4,2,64,128]{3,2,1,0:T(8,128)(2,1)S(1)} %get-tuple-element.69), channel_id=1, source_target_pairs={{0,28},{4,24},{8,20},{12,16},{16,12},{20,8},{24,4},{28,0},{1,29},{... | collective-permute-start | bytes 393224 | tf_op jit(solution)/shard_map/ppermute | solution.py:435
  234.5 33.7 %collective-permute-start.14 = (bf16[1024,512]{1,0:T(8,128)(2,1)S(1)}, bf16[1024,512]{1,0:T(8,128)(2,1)}, u32[]{:S(2)}, u32[]{:S(2)}) collective-permute-start(bf16[1024,512]{1,0:T(8,128)(2,1)S(1)} %copy-done.4), channel_id=1, source_target_pairs={{0,4},{4,0},{8,12},{12,8},{16,20},{20,16},{24,28},{28,24},{1,5},{5... | collective-permute-start | bytes 3145736 | tf_op jit(solution)/shard_map/ppermute | solution.py:459
  244.2 46.6 %collective-permute-start.16 = (bf16[1024,512]{1,0:T(8,128)(2,1)}, bf16[1024,512]{1,0:T(8,128)(2,1)}, u32[]{:S(2)}, u32[]{:S(2)}) collective-permute-start(bf16[1024,512]{1,0:T(8,128)(2,1)} %collective-permute-done.15.refs_2_), channel_id=1, source_target_pairs={{0,4},{4,0},{8,12},{12,8},{16,20},{20,16},{24,28},{28,24},{1,5},{5... | collective-permute-start | bytes 3145736 | tf_op jit(solution)/shard_map/ppermute | solution.py:459
  245.0 19.8 %collective-permute-start.21 = (bf16[1024,512]{1,0:T(8,128)(2,1)}, bf16[1024,512]{1,0:T(8,128)(2,1)}, u32[]{:S(2)}, u32[]{:S(2)}) collective-permute-start(bf16[1024,512]{1,0:T(8,128)(2,1)} %collective-permute-done.20), channel_id=1, source_target_pairs={{8,0},{12,4},{16,24},{20,28},{9,1},{13,5},{17,25},{21,29},{10,2},{... | collective-permute-start | bytes 3145736 | tf_op jit(solution)/shard_map/ppermute | solution.py:444
  250.5 74.2 %collective-permute-start.19 = (bf16[1024,512]{1,0:T(8,128)(2,1)S(1)}, bf16[1024,512]{1,0:T(8,128)(2,1)}, u32[]{:S(2)}, u32[]{:S(2)}) collective-permute-start(bf16[1024,512]{1,0:T(8,128)(2,1)S(1)} %broadcast_select_fusion.1.refs_4_), channel_id=1, source_target_pairs={{0,4},{4,0},{8,12},{12,8},{16,20},{20,16},{24,28},{28,24},{1,5},{5... | collective-permute-start | bytes 3145736 | tf_op jit(solution)/shard_map/ppermute | solution.py:459
  266.2 81.2 %collective-permute-start.22 = (bf16[1024,512]{1,0:T(8,128)(2,1)S(1)}, bf16[1024,512]{1,0:T(8,128)(2,1)}, u32[]{:S(2)}, u32[]{:S(2)}) collective-permute-start(bf16[1024,512]{1,0:T(8,128)(2,1)S(1)} %broadcast_select_fusion.refs_6_), channel_id=1, source_target_pairs={{0,4},{4,0},{8,12},{12,8},{16,20},{20,16},{24,28},{28,24},{1,5},{5... | collective-permute-start | bytes 3145736 | tf_op jit(solution)/shard_map/ppermute | solution.py:459
  358.0 7.6 %collective-permute-start.23 = (bf16[1024,2048]{1,0:T(8,128)(2,1)}, bf16[1024,2048]{1,0:T(8,128)(2,1)}, u32[]{:S(2)}, u32[]{:S(2)}) collective-permute-start(bf16[1024,2048]{1,0:T(8,128)(2,1)} %layer_part.3), channel_id=1, source_target_pairs={{0,1},{1,0},{2,3},{3,2},{4,5},{5,4},{6,7},{7,6},{8,9},{9,8},{10,11... | collective-permute-start | bytes 12582920 | tf_op jit(solution)/shard_map/ppermute | solution.py:474
  373.7 55.5 %copy-start.21 = (bf16[3,4,2,64,128]{4,3,2,1,0:T(8,128)(2,1)S(1)}, bf16[3,4,2,64,128]{4,3,2,1,0:T(8,128)(2,1)}, u32[]{:S(2)}) copy-start(bf16[3,4,2,64,128]{4,3,2,1,0:T(8,128)(2,1)} %copy-done.20) | copy-start | bytes 1179652
  373.8 150.4 %collective-permute-start.24 = (bf16[1024,1024]{1,0:T(8,128)(2,1)}, bf16[1024,1024]{1,0:T(8,128)(2,1)}, u32[]{:S(2)}, u32[]{:S(2)}) collective-permute-start(bf16[1024,1024]{1,0:T(8,128)(2,1)} %layer_part.4), channel_id=1, source_target_pairs={{0,2},{1,3},{2,0},{3,1},{4,6},{5,7},{6,4},{7,5},{8,10},{9,11},{10,... | collective-permute-start | bytes 6291464 | tf_op jit(solution)/shard_map/ppermute | solution.py:474
  395.8 77.3 %copy-start.42 = (bf16[1024,512]{1,0:T(8,128)(2,1)}, bf16[1024,512]{1,0:T(8,128)(2,1)S(1)}, u32[]{:S(2)}) copy-start(bf16[1024,512]{1,0:T(8,128)(2,1)S(1)} %get-tuple-element.87.g_ref) | copy-start | bytes 3145732
  395.8 8.0 %collective-permute-start.25 = (bf16[4,2,64,128]{3,2,1,0:T(8,128)(2,1)S(1)}, bf16[4,2,64,128]{3,2,1,0:T(8,128)(2,1)S(1)}, u32[]{:S(2)}, u32[]{:S(2)}) collective-permute-start(bf16[4,2,64,128]{3,2,1,0:T(8,128)(2,1)S(1)} %get-tuple-element.72), channel_id=1, source_target_pairs={{0,4},{4,0},{8,12},{12,8},{16,20},{20,16},{24,28},{28,24},{1,5},{5... | collective-permute-start | bytes 393224 | tf_op jit(solution)/shard_map/ppermute | solution.py:435
  398.8 10.5 %collective-permute-start.26 = (bf16[4,2,64,128]{3,2,1,0:T(8,128)(2,1)S(1)}, bf16[4,2,64,128]{3,2,1,0:T(8,128)(2,1)S(1)}, u32[]{:S(2)}, u32[]{:S(2)}) collective-permute-start(bf16[4,2,64,128]{3,2,1,0:T(8,128)(2,1)S(1)} %get-tuple-element.73), channel_id=1, source_target_pairs={{0,8},{4,12},{8,0},{12,4},{16,24},{20,28},{24,16},{28,20},{1,9},{5... | collective-permute-start | bytes 393224 | tf_op jit(solution)/shard_map/ppermute | solution.py:435
  402.8 8.4 %collective-permute-start.27 = (bf16[4,2,64,128]{3,2,1,0:T(8,128)(2,1)S(1)}, bf16[4,2,64,128]{3,2,1,0:T(8,128)(2,1)S(1)}, u32[]{:S(2)}, u32[]{:S(2)}) collective-permute-start(bf16[4,2,64,128]{3,2,1,0:T(8,128)(2,1)S(1)} %get-tuple-element.74), channel_id=1, source_target_pairs={{0,12},{4,8},{8,4},{12,0},{16,28},{20,24},{24,20},{28,16},{1,13},{... | collective-permute-start | bytes 393224 | tf_op jit(solution)/shard_map/ppermute | solution.py:435
  402.8 9.6 %collective-permute-start.28 = (bf16[4,2,64,128]{3,2,1,0:T(8,128)(2,1)S(1)}, bf16[4,2,64,128]{3,2,1,0:T(8,128)(2,1)S(1)}, u32[]{:S(2)}, u32[]{:S(2)}) collective-permute-start(bf16[4,2,64,128]{3,2,1,0:T(8,128)(2,1)S(1)} %get-tuple-element.75), channel_id=1, source_target_pairs={{0,16},{4,20},{8,24},{12,28},{16,0},{20,4},{24,8},{28,12},{1,17},{... | collective-permute-start | bytes 393224 | tf_op jit(solution)/shard_map/ppermute | solution.py:435
  403.8 17.8 %collective-permute-start.29 = (bf16[4,2,64,128]{3,2,1,0:T(8,128)(2,1)S(1)}, bf16[4,2,64,128]{3,2,1,0:T(8,128)(2,1)S(1)}, u32[]{:S(2)}, u32[]{:S(2)}) collective-permute-start(bf16[4,2,64,128]{3,2,1,0:T(8,128)(2,1)S(1)} %get-tuple-element.76), channel_id=1, source_target_pairs={{0,20},{4,16},{8,28},{12,24},{16,4},{20,0},{24,12},{28,8},{1,21},{... | collective-permute-start | bytes 393224 | tf_op jit(solution)/shard_map/ppermute | solution.py:435
  409.3 17.0 %collective-permute-start.30 = (bf16[4,2,64,128]{3,2,1,0:T(8,128)(2,1)S(1)}, bf16[4,2,64,128]{3,2,1,0:T(8,128)(2,1)S(1)}, u32[]{:S(2)}, u32[]{:S(2)}) collective-permute-start(bf16[4,2,64,128]{3,2,1,0:T(8,128)(2,1)S(1)} %get-tuple-element.77), channel_id=1, source_target_pairs={{0,24},{4,28},{8,16},{12,20},{16,8},{20,12},{24,0},{28,4},{1,25},{... | collective-permute-start | bytes 393224 | tf_op jit(solution)/shard_map/ppermute | solution.py:435
  411.2 18.0 %collective-permute-start.31 = (bf16[4,2,64,128]{3,2,1,0:T(8,128)(2,1)S(1)}, bf16[4,2,64,128]{3,2,1,0:T(8,128)(2,1)S(1)}, u32[]{:S(2)}, u32[]{:S(2)}) collective-permute-start(bf16[4,2,64,128]{3,2,1,0:T(8,128)(2,1)S(1)} %get-tuple-element.78), channel_id=1, source_target_pairs={{0,28},{4,24},{8,20},{12,16},{16,12},{20,8},{24,4},{28,0},{1,29},{... | collective-permute-start | bytes 393224 | tf_op jit(solution)/shard_map/ppermute | solution.py:435
  442.2 11.1 %collective-permute-start.32 = (bf16[3,4,2,64,128]{4,3,2,1,0:T(8,128)(2,1)S(1)}, bf16[3,4,2,64,128]{4,3,2,1,0:T(8,128)(2,1)S(1)}, u32[]{:S(2)}, u32[]{:S(2)}) collective-permute-start(bf16[3,4,2,64,128]{4,3,2,1,0:T(8,128)(2,1)S(1)} %get-tuple-element.80), channel_id=1, source_target_pairs={{0,4},{4,0},{8,12},{12,8},{16,20},{20,16},{24,28},{28,24},{1,5},{5... | collective-permute-start | bytes 1179656 | tf_op jit(solution)/shard_map/ppermute | solution.py:435
  442.8 23.5 %collective-permute-start.33 = (bf16[3,4,2,64,128]{4,3,2,1,0:T(8,128)(2,1)S(1)}, bf16[3,4,2,64,128]{4,3,2,1,0:T(8,128)(2,1)S(1)}, u32[]{:S(2)}, u32[]{:S(2)}) collective-permute-start(bf16[3,4,2,64,128]{4,3,2,1,0:T(8,128)(2,1)S(1)} %get-tuple-element.81), channel_id=1, source_target_pairs={{0,8},{4,12},{8,0},{12,4},{16,24},{20,28},{24,16},{28,20},{1,9},{5... | collective-permute-start | bytes 1179656 | tf_op jit(solution)/shard_map/ppermute | solution.py:435
  442.8 30.3 %collective-permute-start.34 = (bf16[3,4,2,64,128]{4,3,2,1,0:T(8,128)(2,1)S(1)}, bf16[3,4,2,64,128]{4,3,2,1,0:T(8,128)(2,1)S(1)}, u32[]{:S(2)}, u32[]{:S(2)}) collective-permute-start(bf16[3,4,2,64,128]{4,3,2,1,0:T(8,128)(2,1)S(1)} %get-tuple-element.82), channel_id=1, source_target_pairs={{0,12},{4,8},{8,4},{12,0},{16,28},{20,24},{24,20},{28,16},{1,13},{... | collective-permute-start | bytes 1179656 | tf_op jit(solution)/shard_map/ppermute | solution.py:435
  445.6 47.6 %collective-permute-start.35 = (bf16[3,4,2,64,128]{4,3,2,1,0:T(8,128)(2,1)}, bf16[3,4,2,64,128]{4,3,2,1,0:T(8,128)(2,1)}, u32[]{:S(2)}, u32[]{:S(2)}) collective-permute-start(bf16[3,4,2,64,128]{4,3,2,1,0:T(8,128)(2,1)} %get-tuple-element.83), channel_id=1, source_target_pairs={{0,16},{4,20},{8,24},{12,28},{16,0},{20,4},{24,8},{28,12},{1,17},{... | collective-permute-start | bytes 1179656 | tf_op jit(solution)/shard_map/ppermute | solution.py:435
  454.1 42.1 %collective-permute-start.36 = (bf16[3,4,2,64,128]{4,3,2,1,0:T(8,128)(2,1)}, bf16[3,4,2,64,128]{4,3,2,1,0:T(8,128)(2,1)}, u32[]{:S(2)}, u32[]{:S(2)}) collective-permute-start(bf16[3,4,2,64,128]{4,3,2,1,0:T(8,128)(2,1)} %get-tuple-element.84), channel_id=1, source_target_pairs={{0,20},{4,16},{8,28},{12,24},{16,4},{20,0},{24,12},{28,8},{1,21},{... | collective-permute-start | bytes 1179656 | tf_op jit(solution)/shard_map/ppermute | solution.py:435
  467.1 41.0 %collective-permute-start.37 = (bf16[3,4,2,64,128]{4,3,2,1,0:T(8,128)(2,1)}, bf16[3,4,2,64,128]{4,3,2,1,0:T(8,128)(2,1)}, u32[]{:S(2)}, u32[]{:S(2)}) collective-permute-start(bf16[3,4,2,64,128]{4,3,2,1,0:T(8,128)(2,1)} %get-tuple-element.85), channel_id=1, source_target_pairs={{0,24},{4,28},{8,16},{12,20},{16,8},{20,12},{24,0},{28,4},{1,25},{... | collective-permute-start | bytes 1179656 | tf_op jit(solution)/shard_map/ppermute | solution.py:435
  473.8 40.5 %collective-permute-start.38 = (bf16[3,4,2,64,128]{4,3,2,1,0:T(8,128)(2,1)}, bf16[3,4,2,64,128]{4,3,2,1,0:T(8,128)(2,1)}, u32[]{:S(2)}, u32[]{:S(2)}) collective-permute-start(bf16[3,4,2,64,128]{4,3,2,1,0:T(8,128)(2,1)} %get-tuple-element.86), channel_id=1, source_target_pairs={{0,28},{4,24},{8,20},{12,16},{16,12},{20,8},{24,4},{28,0},{1,29},{... | collective-permute-start | bytes 1179656 | tf_op jit(solution)/shard_map/ppermute | solution.py:435
  (38 other events, 642.9 us)
Sparse Core Ops, SparseCore 0:
  33.4 136.3 reduce-scatter.2
  262.3 105.3 reduce-scatter.4
where the time goes:
time: 542 us
  waiting for transfers between devices  313 us (58%)
  Pallas kernels  98.9 us (18%)
  starting transfers between devices  72.2 us (13%)
  local copies, waits for them, and re-layouts  22.8 us (4%)
  matrix products  16.4 us (3%)
  between operations  14.5 us (3%)
    ppermute x28, waiting for transfers between devices, swap(): lax.ppermute(chunks[d], 'ctx', [(place, place ^ d) for place in range(n)])  200 us
    ppermute x4, waiting for transfers between devices, gather_weight(): lax.ppermute(block, 'ctx', [(place, place ^ e) for place in range(n)])  79.2 us
    ppermute x28, starting transfers between devices, swap(): lax.ppermute(chunks[d], 'ctx', [(place, place ^ d) for place in range(n)])  45.4 us
    ppermute x5, waiting for transfers between devices, along(): lax.ppermute(block, 'ctx', [(a * inner + y, b * inner + y) for a, b in pa...  25.8 us
    pallas_call x3, Pallas kernels, layer_part(): pl.pallas_call(functools.partial(layer_kernel, n, count, len(extra)), gri...  23.6 us
    unnamed x90, local copies, waits for them, and re-layouts  21.7 us
    ppermute x5, starting transfers between devices, along(): lax.ppermute(block, 'ctx', [(a * inner + y, b * inner + y) for a, b in pa...  19.5 us
    pallas_call x1, Pallas kernels, attn_grad(): pl.pallas_call(functools.partial(attn_grad_kernel, n, dim), grid_spec=plt...  19.3 us
  transfers between devices with their start and end apart: 41, of which 31 were waited for; matrix products, arithmetic and copies ran while one was open for 2% of the time, Pallas kernels for 16%

commit v1 on v0

--- a/solution.py
+++ b/solution.py
@@ -253,6 +253,62 @@
     )(ids, wanted, flat, *blocks, *extra)
 
 
+def proj_kernel(lead, adds, dim, order, flat_ref, grad_ref, *refs):
+    extra, outs, turned = refs[:adds], refs[adds:-1], refs[-1]
+    step = pl.program_id(0)
+    span = flat_ref.shape[1]
+
+    @pl.when(step == 0)
+    def _():
+        for at in range(0, span, dim):
+            turned[at : at + dim] = flat_ref[:, at : at + dim].T
+
+    def value(at):
+        out = dot(turned[at : at + dim], grad_ref[...], ((1,), (0,)))
+        for ref in extra:
+            out = out + ref[at : at + dim].astype(F32)
+        return out.astype(BF16)
+
+    @pl.when(step < lead)
+    def _():
+        for at in range(0, span, dim):
+            outs[0][at : at + dim] = value(at)
+
+    @pl.when(step >= lead)
+    def _():
+        for at in range(0, span, dim):
+            outs[-1][at : at + dim] = value(at)
+
+
+def proj_part(order, flat, out_grad, extra, depth, dim, lead):
+    tokens, span = flat.shape
+    count = order.shape[0]
+    sizes = [size for size in (lead, count - lead) if size]
+    places = [lambda s, order: (jnp.minimum(s, lead - 1), 0, 0), lambda s, order: (jnp.maximum(s - lead, 0), 0, 0)]
+    return pl.pallas_call(
+        functools.partial(proj_kernel, lead, len(extra), dim),
+        grid_spec=pltpu.PrefetchScalarGridSpec(
+            num_scalar_prefetch=1,
+            grid=(count,),
+            in_specs=[
+                pl.BlockSpec((tokens, span), lambda s, order: (0, 0)),
+                pl.BlockSpec((tokens, depth), lambda s, order: (0, order[s])),
+            ]
+            + [pl.BlockSpec((pl.squeezed, span, depth), lambda s, order: (s, 0, 0))] * len(extra),
+            out_specs=[pl.BlockSpec((pl.squeezed, span, depth), place) for place in places[-len(sizes) :]],
+            scratch_shapes=[pltpu.VMEM((span, tokens), BF16)],
+        ),
+        out_shape=[jax.ShapeDtypeStruct((size, span, depth), BF16) for size in sizes],
+        compiler_params=params(24),
+        cost_estimate=pl.CostEstimate(
+            flops=2 * tokens * span * depth * count,
+            bytes_accessed=2 * (count * depth * (tokens + span * (1 + len(extra))) + tokens * span),
+            transcendentals=0,
+        ),
+        name="proj_part",
+    )(order, flat, out_grad, *extra)
+
+
 def row_blocks(length):
     step = length // 2
     return [(start, step) for start in range(0, length, step)]
@@ -428,39 +484,38 @@
     )(me, *chunks, *grads)
 
 
-def swap(chunks, n):
-    order = [d for pair in zip(range(n // 2, n), range(n // 2)) for d in pair if d]
-    out = list(chunks)
-    for d in order:
-        out[d] = lax.ppermute(chunks[d], "ctx", [(place, place ^ d) for place in range(n)])
-    return out
-
-
-def gather_weight(me, wo, n):
-    inner = n // 4
-    line = me[0] // inner
-
-    def along(pairs, block):
-        return lax.ppermute(block, "ctx", [(a * inner + y, b * inner + y) for a, b in pairs for y in range(inner)])
-
-    middle = (line == 1) | (line == 2)
-    pair, cross, outward = [(0, 1), (1, 0), (2, 3), (3, 2)], [(1, 2), (2, 1)], [(1, 0), (2, 3)]
-    near = along(pair, wo)
-    cross_own = along(cross, wo)
-    cross_near = along(cross, near)
-    far_own = jnp.where(middle, cross_own, along(outward, cross_own))
-    far_near = jnp.where(middle, cross_near, along(outward, cross_near))
-    upper = line < 2
-    lines = [line, line ^ 1, jnp.where(upper, 2, 1), jnp.where(upper, 3, 0)]
-    blocks, ids = [], []
-    for block, owner in zip((wo, near, far_own, far_near), lines):
-        for e in range(inner):
-            if e:
-                blocks.append(lax.ppermute(block, "ctx", [(place, place ^ e) for place in range(n)]))
-            else:
-                blocks.append(block)
-            ids.append(owner * inner + (me[0] % inner ^ e))
-    return blocks, jnp.stack(ids).astype(jnp.int32)
+PAIRS = [(0, 1), (1, 0), (2, 3), (3, 2)]
+INWARD = [(0, 1), (3, 2)]
+CROSS = [(1, 2), (2, 1)]
+OUTWARD = [(1, 0), (2, 3)]
+
+
+def after(value, *done):
+    return lax.optimization_barrier((value, *done))[0]
+
+
+class Links:
+    def __init__(self, n, window):
+        self.n, self.inner, self.window, self.sent = n, n // 4, window, []
+
+    def send(self, value, pairs):
+        if len(self.sent) >= self.window:
+            value = after(value, self.sent[-self.window])
+        out = lax.ppermute(value, "ctx", pairs)
+        self.sent.append(out)
+        return out
+
+    def along(self, value, pairs):
+        return self.send(value, [(a * self.inner + y, b * self.inner + y) for a, b in pairs for y in range(self.inner)])
+
+    def flip(self, value, d):
+        return self.send(value, [(place, place ^ d) for place in range(self.n)])
+
+    def swap(self, chunks, order):
+        out = list(chunks)
+        for d in order:
+            out[d] = self.flip(chunks[d], d)
+        return out
 
 
 def scatter_layer(ids, flat, blocks, heads_n):
@@ -481,31 +536,80 @@
 
 def on_device(queries, keys, values, out_grad, wo, *, n, heads_n):
     tokens, heads, dim = queries.shape
-    half = heads // 2
+    half, depth, inner = heads // 2, wo.shape[1], n // 4
     me = lax.axis_index("ctx").astype(jnp.int32).reshape(1)
+    line, spot = me[0] // inner, me[0] % inner
+    middle, upper = (line == 1) | (line == 2), line < 2
+    far = [jnp.where(upper, 2, 1), jnp.where(upper, 3, 0)]
+    links = Links(n, 5)
+    wide = [d for d in range(n) if d >= 2 * inner]
+    close = [d for d in range(1, n) if d < 2 * inner]
+    order = [d for d in wide if d % inner == 0] + [d for d in close if d % inner == 0]
+    order += [d for d in wide if d % inner] + [d for d in close if d % inner]
+
+    def around(block):
+        return [block if e == 0 else links.flip(block, e) for e in range(inner)]
+
+    near = links.along(wo, PAIRS)
+    cross_own = links.along(wo, CROSS)
+    own_blocks = around(wo)
     chunks, by_head = split_inputs(me, queries, keys, values, n)
-    chunks = swap(chunks, n)
-    blocks, ids = gather_weight(me, wo, n)
-
-    row_out = row_forward(*by_head)
-    proj_row = dot(row_out, out_grad, ((0,), (0,))).astype(BF16)
-    proj_row = lax.psum_scatter(proj_row, "ctx", scatter_dimension=1, tiled=True)
+    sent = list(chunks)
+    sent[order[0]] = links.flip(chunks[order[0]], order[0])
+    cross_near = links.along(near, CROSS)
+    near_blocks = around(near)
+    far_own = jnp.where(middle, cross_own, links.along(cross_own, OUTWARD))
+    far_near = jnp.where(middle, cross_near, links.along(cross_near, OUTWARD))
+    far_own_blocks = around(far_own)
+    far_near_blocks = around(far_near)
+    for d in order[1:]:
+        sent[d] = links.flip(chunks[d], d)
+    chunks = sent
+    blocks = own_blocks + near_blocks + far_own_blocks + far_near_blocks
+    ids = [owner * inner + (spot ^ e) for owner in (line, line ^ 1, *far) for e in range(inner)]
+    ids = jnp.stack(ids).astype(jnp.int32)
+
+    def targets(e):
+        return jnp.stack([owner * inner + (spot ^ e) for owner in (line ^ 1, *far, line)]).astype(jnp.int32)
+
+    def within(flat):
+        theirs = [links.flip(proj_part(targets(e), flat, out_grad, [], depth, dim, 0)[0], e) for e in range(1, inner)]
+        return proj_part(targets(0), flat, out_grad, theirs, depth, dim, 3)
+
+    def add(*terms):
+        return sum(term.astype(F32) for term in terms).astype(BF16)
+
+    row_out = row_forward(*(after(tensor, near) for tensor in by_head))
+    row_lead, row_own = within(row_out)
 
     grad_row, grads = attn_grad(me, ids, out_grad, blocks, dim)
-    grads = swap(grads, n)
-    column_out, flat = collect(me, row_out, swap(column_forward(me, chunks, n), n), n)
-    column_out, proj_row = lax.optimization_barrier((column_out, proj_row))
-    proj_column = dot(column_out, out_grad, ((0,), (0,))).astype(BF16)
-    proj_column = lax.psum_scatter(proj_column, "ctx", scatter_dimension=1, tiled=True)
+    grads = links.swap(grads, order)
+    column_part = links.swap(column_forward(me, chunks, n), order)
+    column_out, flat = collect(me, row_out, column_part, n)
+
+    row_in = links.along(row_lead, INWARD)
+    row_cross = links.along(add(row_lead[1:], row_in[1:]), CROSS)
+    column_lead, column_own = within(column_out)
+    gradients = column_backward(me, chunks, grads, n)
+    column_in = links.along(column_lead, INWARD)
+    column_grads = list(gradients)
+    for d in order[: n // 2]:
+        column_grads[d] = links.flip(gradients[d], d)
+    column_cross = links.along(add(column_lead[1:], column_in[1:]), CROSS)
+    row_back = links.along(add(row_lead[0], row_cross[1]), OUTWARD)
+    for d in order[n // 2 :]:
+        column_grads[d] = links.flip(gradients[d], d)
+    column_back = links.along(add(column_lead[0], column_cross[1]), OUTWARD)
 
     layer_out = scatter_layer(ids, flat, blocks, heads_n)
-    column_grads = swap(column_backward(me, chunks, grads, n), n)
     row_grads = row_backward(*by_head, grad_row)
     gradients = join_gradients(me, column_grads, row_grads, n)
 
-    shape = (half, dim, proj_row.shape[1])
+    proj_row = add(row_own[0], row_in[0], row_cross[0], row_back)
+    proj_column = add(column_own[0], column_in[0], column_cross[0], column_back)
+    shape = (half, dim, depth)
     proj_grad = jnp.stack([proj_row.reshape(shape), proj_column.reshape(shape)], axis=1)
-    return (layer_out, *gradients, proj_grad.reshape(heads * dim, shape[2]))
+    return (layer_out, *gradients, proj_grad.reshape(heads * dim, depth))
 
 
 def solution(mesh):

time: 542 us -> 532 us (0.982)
  waiting for transfers between devices: 313 us -> 256 us
  local copies, waits for them, and re-layouts: 22.8 us -> 49.1 us
  Pallas kernels: 98.9 us -> 124 us
  matrix products: 16.4 us -> 0 us
  starting transfers between devices: 72.2 us -> 85.9 us
  between operations: 14.5 us -> 1.45 us
  other arithmetic: 4.2 us -> 14.2 us
    ppermute x37 -> x45, waiting for transfers between devices: 305 us -> 256 us  [send(): out = lax.ppermute(value, 'ctx', pairs)]
    unnamed x90 -> x162, local copies, waits for them, and re-layouts: 21.7 us -> 47.9 us
    pallas_call x0 -> x4, Pallas kernels: none -> 20.6 us  [proj_part(): pl.pallas_call(functools.partial(proj_kernel, lead, len(extra), dim), gri...]
    dot_general x2 -> x0, matrix products: 16.4 us -> none  [dot(): return lax.dot_general(a, b, (dims, ((), ())), preferred_element_type=F32)]
    ppermute x37 -> x45, starting transfers between devices: 69.4 us -> 81.4 us  [send(): out = lax.ppermute(value, 'ctx', pairs)]
    convert_element_type x0 -> x6, other arithmetic: none -> 11 us  [add(): return sum((term.astype(F32) for term in terms)).astype(BF16)]
    ppermute x2, waiting for transfers between devices: 7.41 us -> 0.01 us  [move(): lax.ppermute(part, 'head', [(place, place ^ g) for place in range(heads_n)])]
  transfers between devices with their start and end apart: 41 -> 47, of which waited for: 31 -> 16; matrix products, arithmetic and copies ran while one was open for 2% -> 3% of each run, Pallas kernels for 16% -> 20%
where the time goes in v1:
time: 532 us; the launch traced here: 530 us
  waiting for transfers between devices  256 us (48%)
  Pallas kernels  124 us (23%)
  starting transfers between devices  85.9 us (16%)
  local copies, waits for them, and re-layouts  49.1 us (9%)
  other arithmetic  14.2 us (3%)
    ppermute x45, waiting for transfers between devices, send(): out = lax.ppermute(value, 'ctx', pairs)  256 us
    ppermute x45, starting transfers between devices, send(): out = lax.ppermute(value, 'ctx', pairs)  81.4 us
    unnamed x162, local copies, waits for them, and re-layouts  47.9 us
    pallas_call x3, Pallas kernels, layer_part(): pl.pallas_call(functools.partial(layer_kernel, n, count, len(extra)), gri...  23.7 us
    pallas_call x4, Pallas kernels, proj_part(): pl.pallas_call(functools.partial(proj_kernel, lead, len(extra), dim), gri...  20.6 us
    pallas_call x1, Pallas kernels, attn_grad(): pl.pallas_call(functools.partial(attn_grad_kernel, n, dim), grid_spec=plt...  19 us
    pallas_call x1, Pallas kernels, column_backward(): pl.pallas_call(functools.partial(column_backward_kernel, n, dim ** (-0.5)...  13.8 us
    pallas_call x1, Pallas kernels, row_backward(): pl.pallas_call(functools.partial(row_backward_kernel, dim ** (-0.5)), gri...  11.9 us
  transfers between devices with their start and end apart: 47, of which 16 were waited for; matrix products, arithmetic and copies ran while one was open for 3% of the time, Pallas kernels for 20%

profile of v1, /device:TPU:8, one launch (start us, length us, event | category | flops | bytes accessed | tf_op | source)
XLA Modules:
  0.0 530.1 jit_solution(12649429944952382254)
XLA Ops:
  0.7 5.0 collective-permute-start.6
  7.3 18.6 %collective-permute-done.refs_2_ = bf16[1024,512]{1,0:T(8,128)(2,1)} collective-permute-done((bf16[1024,512]{1,0:T(8,128)(2,1)}, bf16[1024,512]{1,0:T(8,128)(2,1)}, u32[]{:S(2)}, u32[]{:S(2)}) %collective-permute-start) | collective-permute-done | bytes 1048608 | tf_op jit(solution)/shard_map/ppermute | solution.py:504
  25.9 3.5 collective-permute-start.1
  29.4 2.3 collective-permute-start.7
  32.7 19.4 %collective-permute-done.1 = bf16[1024,512]{1,0:T(8,128)(2,1)} collective-permute-done((bf16[1024,512]{1,0:T(8,128)(2,1)}, bf16[1024,512]{1,0:T(8,128)(2,1)}, u32[]{:S(2)}, u32[]{:S(2)}) %collective-permute-start.1) | collective-permute-done | bytes 1048608 | tf_op jit(solution)/shard_map/ppermute | solution.py:504
  52.1 2.3 collective-permute-start.3
  59.2 5.0 split_inputs.1
  71.8 7.9 %row_forward.1.flat_ref.row_ref = bf16[1024,512]{1,0:T(8,128)(2,1)S(1)} custom-call(bf16[4,1024,128]{2,1,0:T(8,128)(2,1)S(1)} %get-tuple-element.97.q_ref, bf16[4,1024,128]{2,1,0:T(8,128)(2,1)S(1)} %get-tuple-element.99.k_ref, bf16[4,1024,128]{2,1,0:T(8,128)(2,1)S(1)} %copy-done.25), custom_call_target="tpu_custom_call" | custom-call | flops 1073741824 | bytes 4194304 | tf_op jit(solution)/shard_map/row_forward/pallas_call | solution.py:334
  79.8 3.0 collective-permute-start.8
  82.8 3.4 copy-done
  86.2 5.0 proj_part.4
  98.9 18.7 %collective-permute-done.10.refs_6_ = bf16[3,4,2,64,128]{4,3,2,1,0:T(8,128)(2,1)} collective-permute-done((bf16[3,4,2,64,128]{4,3,2,1,0:T(8,128)(2,1)}, bf16[3,4,2,64,128]{4,3,2,1,0:T(8,128)(2,1)}, u32[]{:S(2)}, u32[]{:S(2)}) %collective-permute-start.10) | collective-permute-done | bytes 393248 | tf_op jit(solution)/shard_map/ppermute | solution.py:504
  117.6 2.8 collective-permute-start.13
  120.4 2.5 collective-permute-start.15
  122.9 84.7 %collective-permute-done.4.refs_7_ = bf16[1024,512]{1,0:T(8,128)(2,1)} collective-permute-done((bf16[1024,512]{1,0:T(8,128)(2,1)S(1)}, bf16[1024,512]{1,0:T(8,128)(2,1)}, u32[]{:S(2)}, u32[]{:S(2)}) %collective-permute-start.4) | collective-permute-done | bytes 1048608 | tf_op jit(solution)/shard_map/ppermute | solution.py:504
  212.8 19.0 %attn_grad.1 = (bf16[1024,512]{1,0:T(8,128)(2,1)S(1)}, bf16[4,2,64,128]{3,2,1,0:T(8,128)(2,1)S(1)}, bf16[4,2,64,128]{3,2,1,0:T(8,128)(2,1)S(1)}, bf16[4,2,64,128...) custom-call(s32[1]{0:T(128)} %bitcast.10.me, ...), custom_call_target="tpu_custom_call" | custom-call | flops 8589934592 | bytes 18874368 | tf_op jit(solution)/shard_map/attn_grad/pallas_call | solution.py:177
  232.8 3.7 collective-permute-start.25
  237.1 2.5 collective-permute-start.16
  239.5 3.5 collective-permute-done.28.refs_14_
  243.0 3.1 collective-permute-done.25.refs_12_
  246.1 2.5 collective-permute-start.26
  248.6 10.6 %column_forward.1 = (bf16[4,2,64,128]{3,2,1,0:T(8,128)(2,1)S(1)}, bf16[4,2,64,128]{3,2,1,0:T(8,128)(2,1)}, bf16[4,2,64,128]{3,2,1,0:T(8,128)(2,1)}, bf16[4,2,64,...) custom-call(s32[1]{0:T(128)} %bitcast.10.me, ...), custom_call_target="tpu_custom_call" | custom-call | flops 536870912 | bytes 4194304 | tf_op jit(solution)/shard_map/column_forward/pallas_call | solution.py:432
  262.7 5.2 collective-permute-start.17
  275.6 2.8 collective-permute-done.17.refs_4_
  280.5 2.6 collective-permute-done.30.refs_7_
  289.6 9.1 %layer_part.3 = bf16[1024,2048]{1,0:T(8,128)(2,1)} custom-call(s32[8]{0:T(128)S(1)} %stack.95.ids, s32[4]{0:T(128)S(1)} %pad_add_fusion.2.wanted, bf16[1024,1024]{1,0:T(8,128)(2,1)S(1)} %get-tuple-element.151.flat_ref, bf16[1024,512]{1,0:T(8,128)(2,1)S(1)} %copy-done.5, bf16[1024,512]{1,0:T(8,128)(2,1)S(1)} %copy-done.9, ...), custom_call_target="tpu_custom_call" | custom-call | flops 4294967296 | bytes 10485760 | tf_op jit(solution)/shard_map/layer_part/pallas_call | solution.py:234
  299.1 4.2 proj_part.6
  304.2 6.4 %proj_part.5 = (bf16[3,512,512]{2,1,0:T(8,128)(2,1)}, bf16[1,512,512]{2,1,0:T(8,128)(2,1)S(1)}) custom-call(s32[4]{0:T(128)S(1)} %pad_add_fusion.4.order, bf16[1024,512]{1,0:T(8,128)(2,1)S(1)} %row_forward.1.flat_ref.row_ref, bf16[1024,4096]{1,0:T(8,128)(2,1)S(1)} %bitcast.33, bf16[4,512,512]{2,1,0:T(8,128)(2,1)} %collective-permute-done.19.refs_0_), custom_call_target="tpu_custom_call" | custom-call | flops 2147483648 | bytes 9437184 | tf_op jit(solution)/shard_map/proj_part/pallas_call | solution.py:288
  312.9 38.1 %collective-permute-done.37.refs_0_ = bf16[4,512,512]{2,1,0:T(8,128)(2,1)S(1)} collective-permute-done((bf16[4,512,512]{2,1,0:T(8,128)(2,1)S(1)}, bf16[4,512,512]{2,1,0:T(8,128)(2,1)S(1)}, u32[]{:S(2)}, u32[]{:S(2)}) %collective-permute-start.37) | collective-permute-done | bytes 2097184 | tf_op jit(solution)/shard_map/ppermute | solution.py:504
  351.1 5.0 proj_part.7
  360.1 3.7 collective-permute-start.34
  373.4 13.8 %column_backward.1 = (bf16[3,4,2,64,128]{4,3,2,1,0:T(8,128)(2,1)S(1)}, bf16[3,4,2,64,128]{4,3,2,1,0:T(8,128)(2,1)S(1)}, bf16[3,4,2,64,128]{4,3,2,1,0:T(8,128)(2,...) custom-call(s32[1]{0:T(128)} %bitcast.10.me, ...), custom_call_target="tpu_custom_call" | custom-call | flops 1342177280 | bytes 7340032 | tf_op jit(solution)/shard_map/column_backward/pallas_call | solution.py:471
  389.5 2.1 collective-permute-start.40
  391.6 6.3 %collective-permute-done.44 = bf16[3,512,512]{2,1,0:T(8,128)(2,1)} collective-permute-done((bf16[3,512,512]{2,1,0:T(8,128)(2,1)}, bf16[3,512,512]{2,1,0:T(8,128)(2,1)}, u32[]{:S(2)}, u32[]{:S(2)}) %collective-permute-start.44) | collective-permute-done | bytes 1572896 | tf_op jit(solution)/shard_map/ppermute | solution.py:504
  397.9 2.8 add_convert_fusion
  400.7 2.4 collective-permute-start.45
  403.1 6.5 %layer_part.4 = bf16[1024,1024]{1,0:T(8,128)(2,1)} custom-call(s32[8]{0:T(128)S(1)} %stack.95.ids, s32[2]{0:T(128)S(1)} %pad_add_fusion.3.wanted, bf16[1024,1024]{1,0:T(8,128)(2,1)S(1)} %copy-done.2, bf16[1024,512]{1,0:T(8,128)(2,1)S(1)} %copy-done.6, bf16[1024,512]{1,0:T(8,128)(2,1)S(1)} %copy-done.10, bf16[1024,512]{1,0:T(8,128)(2,1)} %collective-permute-done.refs_2_, ...), custom_call_target="tpu_custom_call" | custom-call | flops 2147483648 | bytes 6291456 | tf_op jit(solution)/shard_map/layer_part/pallas_call | solution.py:234
  409.7 4.1 collective-permute-start.32
  414.7 2.1 collective-permute-start.35
  418.9 40.5 %collective-permute-done.41.refs_6_ = bf16[3,4,2,64,128]{4,3,2,1,0:T(8,128)(2,1)S(1)} collective-permute-done((bf16[3,4,2,64,128]{4,3,2,1,0:T(8,128)(2,1)S(1)}, bf16[3,4,2,64,128]{4,3,2,1,0:T(8,128)(2,1)S(1)}, u32[]{:S(2)}, u32[]{:S(2)}) %collective-permute-start.41) | collective-permute-done | bytes 393248 | tf_op jit(solution)/shard_map/ppermute | solution.py:504
  460.1 2.1 collective-permute-start.43
  462.3 2.5 collective-permute-done.38.refs_5_
  466.1 5.5 %collective-permute-start.39 = (bf16[3,4,2,64,128]{4,3,2,1,0:T(8,128)(2,1)}, bf16[3,4,2,64,128]{4,3,2,1,0:T(8,128)(2,1)S(1)}, u32[]{:S(2)}, u32[]{:S(2)}) collective-permute-start(bf16[3,4,2,64,128]{4,3,2,1,0:T(8,128)(2,1)} %copy-done.55), channel_id=1, source_target_pairs={{0,12},{4,8},{8,4},{12,0},{16,28},{20,24},{24,20},{28,16},{1,13},{... | collective-permute-start | bytes 1179656 | tf_op jit(solution)/shard_map/ppermute | solution.py:504
  473.4 11.9 %collective-permute-done.43 = bf16[512,512]{1,0:T(8,128)(2,1)} collective-permute-done((bf16[512,512]{1,0:T(8,128)(2,1)}, bf16[512,512]{1,0:T(8,128)(2,1)}, u32[]{:S(2)}, u32[]{:S(2)}) %collective-permute-start.43) | collective-permute-done | bytes 524320 | tf_op jit(solution)/shard_map/ppermute | solution.py:504
  485.3 4.4 collective-permute-start.46
  494.6 11.9 %row_backward.1 = (bf16[4,1024,128]{2,1,0:T(8,128)(2,1)S(1)}, bf16[4,1024,128]{2,1,0:T(8,128)(2,1)S(1)}, bf16[4,1024,128]{2,1,0:T(8,128)(2,1)S(1)}) custom-call(bf16[4,1024,128]{2,1,0:T(8,128)(2,1)S(1)} %copy-done.21, bf16[4,1024,128]{2,1,0:T(8,128)(2,1)S(1)} %copy-done.23, bf16[4,1024,128]{2,1,0:T(8,128)(2,1)S(1)} %copy-done.26, ...), custom_call_target="tpu_custom_call" | custom-call | flops 2684354560 | bytes 7340032 | tf_op jit(solution)/shard_map/row_backward/pallas_call | solution.py:368
  508.1 9.7 %join_gradients.1 = (bf16[1024,8,128]{2,1,0:T(8,128)(2,1)}, bf16[1024,8,128]{2,1,0:T(8,128)(2,1)}, bf16[1024,8,128]{2,1,0:T(8,128)(2,1)}) custom-call(s32[1]{0:T(128)} %bitcast.10.me, bf16[3,4,2,64,128]{4,3,2,1,0:T(8,128)(2,1)S(1)} %get-tuple-element.153.refs_0_, bf16[3,4,2,64,128]{4,3,2,1,0:T(8,128)(2,1)S(1)} %collective-permute-done.36.refs_1_, ...), custom_call_target="tpu_custom_call" | custom-call | tf_op jit(solution)/shard_map/join_gradients/pallas_call | solution.py:96
  521.8 8.1 %layer_part.5 = bf16[1024,1024]{1,0:T(8,128)(2,1)} custom-call(s32[8]{0:T(128)S(1)} %stack.95.ids, s32[2]{0:T(128)S(1)} %pad_add_fusion.wanted, bf16[1024,1024]{1,0:T(8,128)(2,1)S(1)} %copy-done.3, bf16[1024,512]{1,0:T(8,128)(2,1)S(1)} %copy-done.6, bf16[1024,512]{1,0:T(8,128)(2,1)S(1)} %copy-done.11, bf16[1024,512]{1,0:T(8,128)(2,1)} %collective-permute-done.refs_2_, ...), custom_call_target="tpu_custom_call" | custom-call | flops 2147483648 | bytes 6291456 | tf_op jit(solution)/shard_map/layer_part/pallas_call | solution.py:234
  (240 shorter events, 85.9 us)
Async XLA Ops:
  0.6 25.3 %collective-permute-start = (bf16[1024,512]{1,0:T(8,128)(2,1)}, bf16[1024,512]{1,0:T(8,128)(2,1)}, u32[]{:S(2)}, u32[]{:S(2)}) collective-permute-start(bf16[1024,512]{1,0:T(8,128)(2,1)} %refs_0_.7), channel_id=1, source_target_pairs={{0,8},{4,12},{8,0},{12,4},{16,24},{20,28},{24,16},{28,20},{1,9},{5... | collective-permute-start | bytes 3145736 | tf_op jit(solution)/shard_map/ppermute | solution.py:504
  0.7 28.7 %collective-permute-start.6 = (bf16[1024,512]{1,0:T(8,128)(2,1)}, bf16[1024,512]{1,0:T(8,128)(2,1)}, u32[]{:S(2)}, u32[]{:S(2)}) collective-permute-start(bf16[1024,512]{1,0:T(8,128)(2,1)} %refs_0_.7), channel_id=1, source_target_pairs={{8,16},{12,20},{16,8},{20,12},{9,17},{13,21},{17,9},{21,13},{10,18... | collective-permute-start | bytes 3145736 | tf_op jit(solution)/shard_map/ppermute | solution.py:504
  5.8 26.0 %collective-permute-start.2 = (bf16[1024,512]{1,0:T(8,128)(2,1)}, bf16[1024,512]{1,0:T(8,128)(2,1)S(1)}, u32[]{:S(2)}, u32[]{:S(2)}) collective-permute-start(bf16[1024,512]{1,0:T(8,128)(2,1)} %refs_0_.7), channel_id=1, source_target_pairs={{0,4},{4,0},{8,12},{12,8},{16,20},{20,16},{24,28},{28,24},{1,5},{5... | collective-permute-start | bytes 3145736 | tf_op jit(solution)/shard_map/ppermute | solution.py:504
  25.9 26.2 %collective-permute-start.1 = (bf16[1024,512]{1,0:T(8,128)(2,1)}, bf16[1024,512]{1,0:T(8,128)(2,1)}, u32[]{:S(2)}, u32[]{:S(2)}) collective-permute-start(bf16[1024,512]{1,0:T(8,128)(2,1)} %collective-permute-done.refs_2_), channel_id=1, source_target_pairs={{8,16},{12,20},{16,8},{20,12},{9,17},{13,21},{17,9},{21,13},{10,18... | collective-permute-start | bytes 3145736 | tf_op jit(solution)/shard_map/ppermute | solution.py:504
  29.4 50.3 %collective-permute-start.7 = (bf16[1024,512]{1,0:T(8,128)(2,1)}, bf16[1024,512]{1,0:T(8,128)(2,1)}, u32[]{:S(2)}, u32[]{:S(2)}) collective-permute-start(bf16[1024,512]{1,0:T(8,128)(2,1)} %collective-permute-done.6), channel_id=1, source_target_pairs={{8,0},{12,4},{16,24},{20,28},{9,1},{13,5},{17,25},{21,29},{10,2},{... | collective-permute-start | bytes 3145736 | tf_op jit(solution)/shard_map/ppermute | solution.py:504
  52.1 43.3 %collective-permute-start.3 = (bf16[1024,512]{1,0:T(8,128)(2,1)}, bf16[1024,512]{1,0:T(8,128)(2,1)}, u32[]{:S(2)}, u32[]{:S(2)}) collective-permute-start(bf16[1024,512]{1,0:T(8,128)(2,1)} %collective-permute-done.1), channel_id=1, source_target_pairs={{8,0},{12,4},{16,24},{20,28},{9,1},{13,5},{17,25},{21,29},{10,2},{... | collective-permute-start | bytes 3145736 | tf_op jit(solution)/shard_map/ppermute | solution.py:504
  68.9 179.7 %copy-start.35 = (bf16[3,4,2,64,128]{4,3,2,1,0:T(8,128)(2,1)}, bf16[3,4,2,64,128]{4,3,2,1,0:T(8,128)(2,1)S(1)}, u32[]{:S(2)}) copy-start(bf16[3,4,2,64,128]{4,3,2,1,0:T(8,128)(2,1)S(1)} %get-tuple-element.102.refs_0_) | copy-start | bytes 1179652
  68.9 23.6 %collective-permute-start.12 = (bf16[3,4,2,64,128]{4,3,2,1,0:T(8,128)(2,1)}, bf16[3,4,2,64,128]{4,3,2,1,0:T(8,128)(2,1)}, u32[]{:S(2)}, u32[]{:S(2)}) collective-permute-start(bf16[3,4,2,64,128]{4,3,2,1,0:T(8,128)(2,1)} %get-tuple-element.115), channel_id=1, source_target_pairs={{0,16},{4,20},{8,24},{12,28},{16,0},{20,4},{24,8},{28,12},{1,17},{... | collective-permute-start | bytes 1179656 | tf_op jit(solution)/shard_map/ppermute | solution.py:504
  69.1 28.3 %collective-permute-start.9 = (bf16[1024,512]{1,0:T(8,128)(2,1)}, bf16[1024,512]{1,0:T(8,128)(2,1)S(1)}, u32[]{:S(2)}, u32[]{:S(2)}) collective-permute-start(bf16[1024,512]{1,0:T(8,128)(2,1)} %collective-permute-done.refs_2_), channel_id=1, source_target_pairs={{0,4},{4,0},{8,12},{12,8},{16,20},{20,16},{24,28},{28,24},{1,5},{5... | collective-permute-start | bytes 3145736 | tf_op jit(solution)/shard_map/ppermute | solution.py:504
  79.8 14.2 %collective-permute-start.8 = (bf16[3,4,2,64,128]{4,3,2,1,0:T(8,128)(2,1)S(1)}, bf16[3,4,2,64,128]{4,3,2,1,0:T(8,128)(2,1)S(1)}, u32[]{:S(2)}, u32[]{:S(2)}) collective-permute-start(bf16[3,4,2,64,128]{4,3,2,1,0:T(8,128)(2,1)S(1)} %copy-done.58), channel_id=1, source_target_pairs={{0,8},{4,12},{8,0},{12,4},{16,24},{20,28},{24,16},{28,20},{1,9},{5... | collective-permute-start | bytes 1179656 | tf_op jit(solution)/shard_map/ppermute | solution.py:504
  92.5 27.9 %collective-permute-start.14 = (bf16[1024,512]{1,0:T(8,128)(2,1)S(1)}, bf16[1024,512]{1,0:T(8,128)(2,1)}, u32[]{:S(2)}, u32[]{:S(2)}) collective-permute-start(bf16[1024,512]{1,0:T(8,128)(2,1)S(1)} %broadcast_select_fusion.refs_4_), channel_id=1, source_target_pairs={{0,4},{4,0},{8,12},{12,8},{16,20},{20,16},{24,28},{28,24},{1,5},{5... | collective-permute-start | bytes 3145736 | tf_op jit(solution)/shard_map/ppermute | solution.py:504
  93.9 154.7 %collective-permute-start.19 = (bf16[4,512,512]{2,1,0:T(8,128)(2,1)}, bf16[4,512,512]{2,1,0:T(8,128)(2,1)}, u32[]{:S(2)}, u32[]{:S(2)}) collective-permute-start(bf16[4,512,512]{2,1,0:T(8,128)(2,1)} %proj_part.4), channel_id=1, source_target_pairs={{0,4},{4,0},{8,12},{12,8},{16,20},{20,16},{24,28},{28,24},{1,5},{5... | collective-permute-start | bytes 6291464 | tf_op jit(solution)/shard_map/ppermute | solution.py:504
  96.8 110.9 %collective-permute-start.4 = (bf16[1024,512]{1,0:T(8,128)(2,1)S(1)}, bf16[1024,512]{1,0:T(8,128)(2,1)}, u32[]{:S(2)}, u32[]{:S(2)}) collective-permute-start(bf16[1024,512]{1,0:T(8,128)(2,1)S(1)} %broadcast_select_fusion.1.refs_6_), channel_id=1, source_target_pairs={{0,4},{4,0},{8,12},{12,8},{16,20},{20,16},{24,28},{28,24},{1,5},{5... | collective-permute-start | bytes 3145736 | tf_op jit(solution)/shard_map/ppermute | solution.py:504
  98.4 19.2 %collective-permute-start.10 = (bf16[3,4,2,64,128]{4,3,2,1,0:T(8,128)(2,1)}, bf16[3,4,2,64,128]{4,3,2,1,0:T(8,128)(2,1)}, u32[]{:S(2)}, u32[]{:S(2)}) collective-permute-start(bf16[3,4,2,64,128]{4,3,2,1,0:T(8,128)(2,1)} %get-tuple-element.113), channel_id=1, source_target_pairs={{0,24},{4,28},{8,16},{12,20},{16,8},{20,12},{24,0},{28,4},{1,25},{... | collective-permute-start | bytes 1179656 | tf_op jit(solution)/shard_map/ppermute | solution.py:504
  117.6 118.9 %collective-permute-start.11 = (bf16[3,4,2,64,128]{4,3,2,1,0:T(8,128)(2,1)}, bf16[3,4,2,64,128]{4,3,2,1,0:T(8,128)(2,1)S(1)}, u32[]{:S(2)}, u32[]{:S(2)}) collective-permute-start(bf16[3,4,2,64,128]{4,3,2,1,0:T(8,128)(2,1)} %copy-done.51), channel_id=1, source_target_pairs={{0,12},{4,8},{8,4},{12,0},{16,28},{20,24},{24,20},{28,16},{1,13},{... | collective-permute-start | bytes 1179656 | tf_op jit(solution)/shard_map/ppermute | solution.py:504
  117.6 115.2 %collective-permute-start.13 = (bf16[3,4,2,64,128]{4,3,2,1,0:T(8,128)(2,1)}, bf16[3,4,2,64,128]{4,3,2,1,0:T(8,128)(2,1)S(1)}, u32[]{:S(2)}, u32[]{:S(2)}) collective-permute-start(bf16[3,4,2,64,128]{4,3,2,1,0:T(8,128)(2,1)} %copy-done.52), channel_id=1, source_target_pairs={{0,20},{4,16},{8,28},{12,24},{16,4},{20,0},{24,12},{28,8},{1,21},{... | collective-permute-start | bytes 1179656 | tf_op jit(solution)/shard_map/ppermute | solution.py:504
  120.4 111.5 %collective-permute-start.15 = (bf16[3,4,2,64,128]{4,3,2,1,0:T(8,128)(2,1)}, bf16[3,4,2,64,128]{4,3,2,1,0:T(8,128)(2,1)S(1)}, u32[]{:S(2)}, u32[]{:S(2)}) collective-permute-start(bf16[3,4,2,64,128]{4,3,2,1,0:T(8,128)(2,1)} %copy-done.53), channel_id=1, source_target_pairs={{0,28},{4,24},{8,20},{12,16},{16,12},{20,8},{24,4},{28,0},{1,29},{... | collective-permute-start | bytes 1179656 | tf_op jit(solution)/shard_map/ppermute | solution.py:504
  207.7 29.4 %collective-permute-start.5 = (bf16[3,4,2,64,128]{4,3,2,1,0:T(8,128)(2,1)}, bf16[3,4,2,64,128]{4,3,2,1,0:T(8,128)(2,1)S(1)}, u32[]{:S(2)}, u32[]{:S(2)}) collective-permute-start(bf16[3,4,2,64,128]{4,3,2,1,0:T(8,128)(2,1)} %copy-done.50), channel_id=1, source_target_pairs={{0,4},{4,0},{8,12},{12,8},{16,20},{20,16},{24,28},{28,24},{1,5},{5... | collective-permute-start | bytes 1179656 | tf_op jit(solution)/shard_map/ppermute | solution.py:504
  231.9 11.1 %collective-permute-start.28 = (bf16[4,2,64,128]{3,2,1,0:T(8,128)(2,1)S(1)}, bf16[4,2,64,128]{3,2,1,0:T(8,128)(2,1)S(1)}, u32[]{:S(2)}, u32[]{:S(2)}) collective-permute-start(bf16[4,2,64,128]{3,2,1,0:T(8,128)(2,1)S(1)} %get-tuple-element.148), channel_id=1, source_target_pairs={{0,24},{4,28},{8,16},{12,20},{16,8},{20,12},{24,0},{28,4},{1,25},{... | collective-permute-start | bytes 393224 | tf_op jit(solution)/shard_map/ppermute | solution.py:504
  232.8 13.3 %collective-permute-start.25 = (bf16[4,2,64,128]{3,2,1,0:T(8,128)(2,1)S(1)}, bf16[4,2,64,128]{3,2,1,0:T(8,128)(2,1)S(1)}, u32[]{:S(2)}, u32[]{:S(2)}) collective-permute-start(bf16[4,2,64,128]{3,2,1,0:T(8,128)(2,1)S(1)} %get-tuple-element.142), channel_id=1, source_target_pairs={{0,16},{4,20},{8,24},{12,28},{16,0},{20,4},{24,8},{28,12},{1,17},{... | collective-permute-start | bytes 393224 | tf_op jit(solution)/shard_map/ppermute | solution.py:504
  236.5 23.4 %collective-permute-start.22 = (bf16[4,2,64,128]{3,2,1,0:T(8,128)(2,1)S(1)}, bf16[4,2,64,128]{3,2,1,0:T(8,128)(2,1)S(1)}, u32[]{:S(2)}, u32[]{:S(2)}) collective-permute-start(bf16[4,2,64,128]{3,2,1,0:T(8,128)(2,1)S(1)} %get-tuple-element.136), channel_id=1, source_target_pairs={{0,20},{4,16},{8,28},{12,24},{16,4},{20,0},{24,12},{28,8},{1,21},{... | collective-permute-start | bytes 393224 | tf_op jit(solution)/shard_map/ppermute | solution.py:504
  237.1 24.9 %collective-permute-start.16 = (bf16[4,2,64,128]{3,2,1,0:T(8,128)(2,1)S(1)}, bf16[4,2,64,128]{3,2,1,0:T(8,128)(2,1)S(1)}, u32[]{:S(2)}, u32[]{:S(2)}) collective-permute-start(bf16[4,2,64,128]{3,2,1,0:T(8,128)(2,1)S(1)} %get-tuple-element.125), channel_id=1, source_target_pairs={{0,8},{4,12},{8,0},{12,4},{16,24},{20,28},{24,16},{28,20},{1,9},{5... | collective-permute-start | bytes 393224 | tf_op jit(solution)/shard_map/ppermute | solution.py:504
  243.0 24.9 %collective-permute-start.29 = (bf16[4,2,64,128]{3,2,1,0:T(8,128)(2,1)S(1)}, bf16[4,2,64,128]{3,2,1,0:T(8,128)(2,1)S(1)}, u32[]{:S(2)}, u32[]{:S(2)}) collective-permute-start(bf16[4,2,64,128]{3,2,1,0:T(8,128)(2,1)S(1)} %get-tuple-element.149), channel_id=1, source_target_pairs={{0,12},{4,8},{8,4},{12,0},{16,28},{20,24},{24,20},{28,16},{1,13},{... | collective-permute-start | bytes 393224 | tf_op jit(solution)/shard_map/ppermute | solution.py:504
  246.1 23.7 %collective-permute-start.26 = (bf16[4,2,64,128]{3,2,1,0:T(8,128)(2,1)S(1)}, bf16[4,2,64,128]{3,2,1,0:T(8,128)(2,1)S(1)}, u32[]{:S(2)}, u32[]{:S(2)}) collective-permute-start(bf16[4,2,64,128]{3,2,1,0:T(8,128)(2,1)S(1)} %get-tuple-element.143), channel_id=1, source_target_pairs={{0,4},{4,0},{8,12},{12,8},{16,20},{20,16},{24,28},{28,24},{1,5},{5... | collective-permute-start | bytes 393224 | tf_op jit(solution)/shard_map/ppermute | solution.py:504
  248.6 22.9 %collective-permute-start.20 = (bf16[4,2,64,128]{3,2,1,0:T(8,128)(2,1)S(1)}, bf16[4,2,64,128]{3,2,1,0:T(8,128)(2,1)S(1)}, u32[]{:S(2)}, u32[]{:S(2)}) collective-permute-start(bf16[4,2,64,128]{3,2,1,0:T(8,128)(2,1)S(1)} %get-tuple-element.131), channel_id=1, source_target_pairs={{0,28},{4,24},{8,20},{12,16},{16,12},{20,8},{24,4},{28,0},{1,29},{... | collective-permute-start | bytes 393224 | tf_op jit(solution)/shard_map/ppermute | solution.py:504
  260.5 14.0 %collective-permute-start.23 = (bf16[4,2,64,128]{3,2,1,0:T(8,128)(2,1)S(1)}, bf16[4,2,64,128]{3,2,1,0:T(8,128)(2,1)S(1)}, u32[]{:S(2)}, u32[]{:S(2)}) collective-permute-start(bf16[4,2,64,128]{3,2,1,0:T(8,128)(2,1)S(1)} %get-tuple-element.137), channel_id=1, source_target_pairs={{0,24},{4,28},{8,16},{12,20},{16,8},{20,12},{24,0},{28,4},{1,25},{... | collective-permute-start | bytes 393224 | tf_op jit(solution)/shard_map/ppermute | solution.py:504
  262.7 15.8 %collective-permute-start.17 = (bf16[4,2,64,128]{3,2,1,0:T(8,128)(2,1)S(1)}, bf16[4,2,64,128]{3,2,1,0:T(8,128)(2,1)S(1)}, u32[]{:S(2)}, u32[]{:S(2)}) collective-permute-start(bf16[4,2,64,128]{3,2,1,0:T(8,128)(2,1)S(1)} %get-tuple-element.126), channel_id=1, source_target_pairs={{0,16},{4,20},{8,24},{12,28},{16,0},{20,4},{24,8},{28,12},{1,17},{... | collective-permute-start | bytes 393224 | tf_op jit(solution)/shard_map/ppermute | solution.py:504
  268.5 14.6 %collective-permute-start.30 = (bf16[4,2,64,128]{3,2,1,0:T(8,128)(2,1)}, bf16[4,2,64,128]{3,2,1,0:T(8,128)(2,1)S(1)}, u32[]{:S(2)}, u32[]{:S(2)}) collective-permute-start(bf16[4,2,64,128]{3,2,1,0:T(8,128)(2,1)} %get-tuple-element.150), channel_id=1, source_target_pairs={{0,28},{4,24},{8,20},{12,16},{16,12},{20,8},{24,4},{28,0},{1,29},{... | collective-permute-start | bytes 393224 | tf_op jit(solution)/shard_map/ppermute | solution.py:504
  270.5 12.6 %collective-permute-start.27 = (bf16[4,2,64,128]{3,2,1,0:T(8,128)(2,1)}, bf16[4,2,64,128]{3,2,1,0:T(8,128)(2,1)}, u32[]{:S(2)}, u32[]{:S(2)}) collective-permute-start(bf16[4,2,64,128]{3,2,1,0:T(8,128)(2,1)} %get-tuple-element.144), channel_id=1, source_target_pairs={{0,20},{4,16},{8,28},{12,24},{16,4},{20,0},{24,12},{28,8},{1,21},{... | collective-permute-start | bytes 393224 | tf_op jit(solution)/shard_map/ppermute | solution.py:504
  272.1 11.0 %collective-permute-start.21 = (bf16[4,2,64,128]{3,2,1,0:T(8,128)(2,1)}, bf16[4,2,64,128]{3,2,1,0:T(8,128)(2,1)}, u32[]{:S(2)}, u32[]{:S(2)}) collective-permute-start(bf16[4,2,64,128]{3,2,1,0:T(8,128)(2,1)} %get-tuple-element.132), channel_id=1, source_target_pairs={{0,8},{4,12},{8,0},{12,4},{16,24},{20,28},{24,16},{28,20},{1,9},{5... | collective-permute-start | bytes 393224 | tf_op jit(solution)/shard_map/ppermute | solution.py:504
  274.5 8.6 %collective-permute-start.24 = (bf16[4,2,64,128]{3,2,1,0:T(8,128)(2,1)}, bf16[4,2,64,128]{3,2,1,0:T(8,128)(2,1)}, u32[]{:S(2)}, u32[]{:S(2)}) collective-permute-start(bf16[4,2,64,128]{3,2,1,0:T(8,128)(2,1)} %get-tuple-element.138), channel_id=1, source_target_pairs={{0,12},{4,8},{8,4},{12,0},{16,28},{20,24},{24,20},{28,16},{1,13},{... | collective-permute-start | bytes 393224 | tf_op jit(solution)/shard_map/ppermute | solution.py:504
  278.4 6.4 %collective-permute-start.18 = (bf16[4,2,64,128]{3,2,1,0:T(8,128)(2,1)}, bf16[4,2,64,128]{3,2,1,0:T(8,128)(2,1)}, u32[]{:S(2)}, u32[]{:S(2)}) collective-permute-start(bf16[4,2,64,128]{3,2,1,0:T(8,128)(2,1)} %get-tuple-element.127), channel_id=1, source_target_pairs={{0,4},{4,0},{8,12},{12,8},{16,20},{20,16},{24,28},{28,24},{1,5},{5... | collective-permute-start | bytes 393224 | tf_op jit(solution)/shard_map/ppermute | solution.py:504
  298.7 104.4 %collective-permute-start.31 = (bf16[1024,2048]{1,0:T(8,128)(2,1)}, bf16[1024,2048]{1,0:T(8,128)(2,1)}, u32[]{:S(2)}, u32[]{:S(2)}) collective-permute-start(bf16[1024,2048]{1,0:T(8,128)(2,1)} %layer_part.3), channel_id=1, source_target_pairs={{0,1},{1,0},{2,3},{3,2},{4,5},{5,4},{6,7},{7,6},{8,9},{9,8},{10,11... | collective-permute-start | bytes 12582920 | tf_op jit(solution)/shard_map/ppermute | solution.py:529
  303.3 47.7 %collective-permute-start.37 = (bf16[4,512,512]{2,1,0:T(8,128)(2,1)S(1)}, bf16[4,512,512]{2,1,0:T(8,128)(2,1)S(1)}, u32[]{:S(2)}, u32[]{:S(2)}) collective-permute-start(bf16[4,512,512]{2,1,0:T(8,128)(2,1)S(1)} %proj_part.6), channel_id=1, source_target_pairs={{0,4},{4,0},{8,12},{12,8},{16,20},{20,16},{24,28},{28,24},{1,5},{5... | collective-permute-start | bytes 6291464 | tf_op jit(solution)/shard_map/ppermute | solution.py:504
  311.5 46.9 %collective-permute-start.33 = (bf16[3,512,512]{2,1,0:T(8,128)(2,1)}, bf16[3,512,512]{2,1,0:T(8,128)(2,1)}, u32[]{:S(2)}, u32[]{:S(2)}) collective-permute-start(bf16[3,512,512]{2,1,0:T(8,128)(2,1)} %get-tuple-element.157), channel_id=1, source_target_pairs={{0,8},{4,12},{24,16},{28,20},{1,9},{5,13},{25,17},{29,21},{2,10},{... | collective-permute-start | bytes 4718600 | tf_op jit(solution)/shard_map/ppermute | solution.py:504
  356.9 41.0 %collective-permute-start.44 = (bf16[3,512,512]{2,1,0:T(8,128)(2,1)}, bf16[3,512,512]{2,1,0:T(8,128)(2,1)}, u32[]{:S(2)}, u32[]{:S(2)}) collective-permute-start(bf16[3,512,512]{2,1,0:T(8,128)(2,1)} %get-tuple-element.184), channel_id=1, source_target_pairs={{0,8},{4,12},{24,16},{28,20},{1,9},{5,13},{25,17},{29,21},{2,10},{... | collective-permute-start | bytes 4718600 | tf_op jit(solution)/shard_map/ppermute | solution.py:504
  360.1 53.6 %collective-permute-start.34 = (bf16[2,512,512]{2,1,0:T(8,128)(2,1)S(1)}, bf16[2,512,512]{2,1,0:T(8,128)(2,1)S(1)}, u32[]{:S(2)}, u32[]{:S(2)}) collective-permute-start(bf16[2,512,512]{2,1,0:T(8,128)(2,1)S(1)} %add_convert_fusion.1), channel_id=1, source_target_pairs={{8,16},{12,20},{16,8},{20,12},{9,17},{13,21},{17,9},{21,13},{10,18... | collective-permute-start | bytes 3145736 | tf_op jit(solution)/shard_map/ppermute | solution.py:504
  389.5 24.3 %collective-permute-start.40 = (bf16[3,4,2,64,128]{4,3,2,1,0:T(8,128)(2,1)S(1)}, bf16[3,4,2,64,128]{4,3,2,1,0:T(8,128)(2,1)S(1)}, u32[]{:S(2)}, u32[]{:S(2)}) collective-permute-start(bf16[3,4,2,64,128]{4,3,2,1,0:T(8,128)(2,1)S(1)} %get-tuple-element.168), channel_id=1, source_target_pairs={{0,16},{4,20},{8,24},{12,28},{16,0},{20,4},{24,8},{28,12},{1,17},{... | collective-permute-start | bytes 1179656 | tf_op jit(solution)/shard_map/ppermute | solution.py:504
  400.7 70.9 %collective-permute-start.45 = (bf16[2,512,512]{2,1,0:T(8,128)(2,1)}, bf16[2,512,512]{2,1,0:T(8,128)(2,1)}, u32[]{:S(2)}, u32[]{:S(2)}) collective-permute-start(bf16[2,512,512]{2,1,0:T(8,128)(2,1)} %add_convert_fusion), channel_id=1, source_target_pairs={{8,16},{12,20},{16,8},{20,12},{9,17},{13,21},{17,9},{21,13},{10,18... | collective-permute-start | bytes 3145736 | tf_op jit(solution)/shard_map/ppermute | solution.py:504
  409.7 110.8 %collective-permute-start.32 = (bf16[1024,1024]{1,0:T(8,128)(2,1)}, bf16[1024,1024]{1,0:T(8,128)(2,1)}, u32[]{:S(2)}, u32[]{:S(2)}) collective-permute-start(bf16[1024,1024]{1,0:T(8,128)(2,1)} %layer_part.4), channel_id=1, source_target_pairs={{0,2},{1,3},{2,0},{3,1},{4,6},{5,7},{6,4},{7,5},{8,10},{9,11},{10,... | collective-permute-start | bytes 6291464 | tf_op jit(solution)/shard_map/ppermute | solution.py:529
  413.7 45.6 %collective-permute-start.41 = (bf16[3,4,2,64,128]{4,3,2,1,0:T(8,128)(2,1)S(1)}, bf16[3,4,2,64,128]{4,3,2,1,0:T(8,128)(2,1)S(1)}, u32[]{:S(2)}, u32[]{:S(2)}) collective-permute-start(bf16[3,4,2,64,128]{4,3,2,1,0:T(8,128)(2,1)S(1)} %get-tuple-element.170), channel_id=1, source_target_pairs={{0,24},{4,28},{8,16},{12,20},{16,8},{20,12},{24,0},{28,4},{1,25},{... | collective-permute-start | bytes 1179656 | tf_op jit(solution)/shard_map/ppermute | solution.py:504
  413.7 51.0 %collective-permute-start.38 = (bf16[3,4,2,64,128]{4,3,2,1,0:T(8,128)(2,1)}, bf16[3,4,2,64,128]{4,3,2,1,0:T(8,128)(2,1)}, u32[]{:S(2)}, u32[]{:S(2)}) collective-permute-start(bf16[3,4,2,64,128]{4,3,2,1,0:T(8,128)(2,1)} %get-tuple-element.165), channel_id=1, source_target_pairs={{0,20},{4,16},{8,28},{12,24},{16,4},{20,0},{24,12},{28,8},{1,21},{... | collective-permute-start | bytes 1179656 | tf_op jit(solution)/shard_map/ppermute | solution.py:504
  414.7 51.4 %collective-permute-start.35 = (bf16[3,4,2,64,128]{4,3,2,1,0:T(8,128)(2,1)}, bf16[3,4,2,64,128]{4,3,2,1,0:T(8,128)(2,1)}, u32[]{:S(2)}, u32[]{:S(2)}) collective-permute-start(bf16[3,4,2,64,128]{4,3,2,1,0:T(8,128)(2,1)} %get-tuple-element.159), channel_id=1, source_target_pairs={{0,8},{4,12},{8,0},{12,4},{16,24},{20,28},{24,16},{28,20},{1,9},{5... | collective-permute-start | bytes 1179656 | tf_op jit(solution)/shard_map/ppermute | solution.py:504
  460.1 25.2 %collective-permute-start.43 = (bf16[512,512]{1,0:T(8,128)(2,1)}, bf16[512,512]{1,0:T(8,128)(2,1)}, u32[]{:S(2)}, u32[]{:S(2)}) collective-permute-start(bf16[512,512]{1,0:T(8,128)(2,1)} %fusion.2), channel_id=1, source_target_pairs={{8,0},{12,4},{16,24},{20,28},{9,1},{13,5},{17,25},{21,29},{10,2},{... | collective-permute-start | bytes 1572872 | tf_op jit(solution)/shard_map/ppermute | solution.py:504
  464.8 43.3 %collective-permute-start.42 = (bf16[3,4,2,64,128]{4,3,2,1,0:T(8,128)(2,1)}, bf16[3,4,2,64,128]{4,3,2,1,0:T(8,128)(2,1)S(1)}, u32[]{:S(2)}, u32[]{:S(2)}) collective-permute-start(bf16[3,4,2,64,128]{4,3,2,1,0:T(8,128)(2,1)} %copy-done.56), channel_id=1, source_target_pairs={{0,28},{4,24},{8,20},{12,16},{16,12},{20,8},{24,4},{28,0},{1,29},{... | collective-permute-start | bytes 1179656 | tf_op jit(solution)/shard_map/ppermute | solution.py:504
  466.1 42.0 %collective-permute-start.39 = (bf16[3,4,2,64,128]{4,3,2,1,0:T(8,128)(2,1)}, bf16[3,4,2,64,128]{4,3,2,1,0:T(8,128)(2,1)S(1)}, u32[]{:S(2)}, u32[]{:S(2)}) collective-permute-start(bf16[3,4,2,64,128]{4,3,2,1,0:T(8,128)(2,1)} %copy-done.55), channel_id=1, source_target_pairs={{0,12},{4,8},{8,4},{12,0},{16,28},{20,24},{24,20},{28,16},{1,13},{... | collective-permute-start | bytes 1179656 | tf_op jit(solution)/shard_map/ppermute | solution.py:504
  471.6 36.5 %collective-permute-start.36 = (bf16[3,4,2,64,128]{4,3,2,1,0:T(8,128)(2,1)}, bf16[3,4,2,64,128]{4,3,2,1,0:T(8,128)(2,1)S(1)}, u32[]{:S(2)}, u32[]{:S(2)}) collective-permute-start(bf16[3,4,2,64,128]{4,3,2,1,0:T(8,128)(2,1)} %copy-done.54), channel_id=1, source_target_pairs={{0,4},{4,0},{8,12},{12,8},{16,20},{20,16},{24,28},{28,24},{1,5},{5... | collective-permute-start | bytes 1179656 | tf_op jit(solution)/shard_map/ppermute | solution.py:504
  485.3 32.5 %collective-permute-start.46 = (bf16[512,512]{1,0:T(8,128)(2,1)S(1)}, bf16[512,512]{1,0:T(8,128)(2,1)S(1)}, u32[]{:S(2)}, u32[]{:S(2)}) collective-permute-start(bf16[512,512]{1,0:T(8,128)(2,1)S(1)} %fusion.3), channel_id=1, source_target_pairs={{8,0},{12,4},{16,24},{20,28},{9,1},{13,5},{17,25},{21,29},{10,2},{... | collective-permute-start | bytes 1572872 | tf_op jit(solution)/shard_map/ppermute | solution.py:504
  (80 other events, 630.2 us)

commit v2 on v1

--- a/solution.py
+++ b/solution.py
@@ -65,7 +65,7 @@
             scratch_shapes=[pltpu.VMEM((3, width * heads, dim), F32)],
         ),
         out_shape=[chunk] * n + [by_head] * 3,
-        compiler_params=params(40),
+        compiler_params=params(60),
         name="split_inputs",
     )(me, queries, keys, values)
     return out[:n], out[n:]
@@ -104,7 +104,7 @@
             scratch_shapes=[pltpu.VMEM((3, width * heads, dim), F32)],
         ),
         out_shape=[whole] * 3,
-        compiler_params=params(40),
+        compiler_params=params(60),
         name="join_gradients",
     )(me, *chunks, *by_head)
 
@@ -133,7 +133,7 @@
             jax.ShapeDtypeStruct((rows * C, half * dim), BF16),
             jax.ShapeDtypeStruct((rows * C, 2 * half * dim), BF16),
         ],
-        compiler_params=params(24),
+        compiler_params=params(60),
         name="collect",
     )(me, row_out, *chunks)
 
@@ -189,7 +189,7 @@
             ],
         ),
         out_shape=[jax.ShapeDtypeStruct((tokens, half * dim), BF16)] + [chunk] * n,
-        compiler_params=params(40),
+        compiler_params=params(60),
         cost_estimate=pl.CostEstimate(
             flops=2 * tokens * span * depth * n,
             bytes_accessed=2 * n * depth * (tokens + span) + 2 * tokens * span,
@@ -243,7 +243,7 @@
             scratch_shapes=[pltpu.VMEM((count, span, depth), BF16), pltpu.SemaphoreType.DMA((count,))],
         ),
         out_shape=jax.ShapeDtypeStruct((tokens, count * depth), BF16),
-        compiler_params=params(32),
+        compiler_params=params(60),
         cost_estimate=pl.CostEstimate(
             flops=2 * tokens * span * depth * count,
             bytes_accessed=2 * (count * depth * (tokens + span) + tokens * span),
@@ -299,7 +299,7 @@
             scratch_shapes=[pltpu.VMEM((span, tokens), BF16)],
         ),
         out_shape=[jax.ShapeDtypeStruct((size, span, depth), BF16) for size in sizes],
-        compiler_params=params(24),
+        compiler_params=params(60),
         cost_estimate=pl.CostEstimate(
             flops=2 * tokens * span * depth * count,
             bytes_accessed=2 * (count * depth * (tokens + span * (1 + len(extra))) + tokens * span),
@@ -337,7 +337,7 @@
         in_specs=[by_head] * 3,
         out_specs=pl.BlockSpec((C, dim), lambda r, h: (r, h)),
         out_shape=jax.ShapeDtypeStruct((tokens, half * dim), BF16),
-        compiler_params=params(24),
+        compiler_params=params(60),
         cost_estimate=pl.CostEstimate(
             flops=4 * tokens * C * half * dim, bytes_accessed=8 * tokens * half * dim, transcendentals=tokens * C * half
         ),
@@ -372,7 +372,7 @@
         out_specs=[by_head] * 3,
         out_shape=[jax.ShapeDtypeStruct(q.shape, BF16)] * 3,
         scratch_shapes=[pltpu.VMEM((C, dim), F32)] * 2,
-        compiler_params=params(32),
+        compiler_params=params(60),
         cost_estimate=pl.CostEstimate(
             flops=10 * tokens * C * half * dim, bytes_accessed=14 * tokens * half * dim, transcendentals=tokens * C * half
         ),
@@ -435,7 +435,7 @@
         out_specs=[VMEM] * n,
         out_shape=[jax.ShapeDtypeStruct((half, rows, width, dim), BF16)] * n,
         scratch_shapes=[pltpu.VMEM((size, size), F32)],
-        compiler_params=params(24),
+        compiler_params=params(60),
         cost_estimate=pl.CostEstimate(
             flops=4 * size * size * dim * half * width // LANE,
             bytes_accessed=8 * n * half * rows * width * dim,
@@ -474,7 +474,7 @@
         out_specs=[VMEM] * n,
         out_shape=[jax.ShapeDtypeStruct(chunks[0].shape, BF16)] * n,
         scratch_shapes=[pltpu.VMEM((size, size), F32)],
-        compiler_params=params(24),
+        compiler_params=params(60),
         cost_estimate=pl.CostEstimate(
             flops=10 * size * size * dim * half * width // LANE,
             bytes_accessed=14 * n * half * rows * width * dim,
@@ -499,8 +499,9 @@
         self.n, self.inner, self.window, self.sent = n, n // 4, window, []
 
     def send(self, value, pairs):
-        if len(self.sent) >= self.window:
-            value = after(value, self.sent[-self.window])
+        over = len(self.sent) - self.window + 1
+        if over > 0:
+            value = after(value, *self.sent[max(0, over - self.window) : over])
         out = lax.ppermute(value, "ctx", pairs)
         self.sent.append(out)
         return out
@@ -555,58 +556,81 @@
     own_blocks = around(wo)
     chunks, by_head = split_inputs(me, queries, keys, values, n)
     sent = list(chunks)
-    sent[order[0]] = links.flip(chunks[order[0]], order[0])
+
+    def deal(*which):
+        for d in which:
+            sent[d] = links.flip(chunks[d], d)
+
+    deal(order[0])
+    near_blocks = around(after(near, chunks[0]))
+    deal(*order[1 : n // 4])
     cross_near = links.along(near, CROSS)
-    near_blocks = around(near)
     far_own = jnp.where(middle, cross_own, links.along(cross_own, OUTWARD))
+    deal(*order[n // 4 : n // 2])
+    far_own_blocks = around(far_own)
     far_near = jnp.where(middle, cross_near, links.along(cross_near, OUTWARD))
-    far_own_blocks = around(far_own)
+    deal(*order[n // 2 :])
     far_near_blocks = around(far_near)
-    for d in order[1:]:
-        sent[d] = links.flip(chunks[d], d)
     chunks = sent
     blocks = own_blocks + near_blocks + far_own_blocks + far_near_blocks
     ids = [owner * inner + (spot ^ e) for owner in (line, line ^ 1, *far) for e in range(inner)]
     ids = jnp.stack(ids).astype(jnp.int32)
 
-    def targets(e):
-        return jnp.stack([owner * inner + (spot ^ e) for owner in (line ^ 1, *far, line)]).astype(jnp.int32)
-
-    def within(flat):
-        theirs = [links.flip(proj_part(targets(e), flat, out_grad, [], depth, dim, 0)[0], e) for e in range(1, inner)]
-        return proj_part(targets(0), flat, out_grad, theirs, depth, dim, 3)
+    def targets(owners, e):
+        return jnp.stack([owner * inner + (spot ^ e) for owner in owners]).astype(jnp.int32)
+
+    def exchanged(flat, owners):
+        return [
+            links.flip(proj_part(targets(owners, e), flat, out_grad, [], depth, dim, 0)[0], e) for e in range(1, inner)
+        ]
+
+    def summed(flat, owners, theirs, lead):
+        return proj_part(targets(owners, 0), flat, out_grad, theirs, depth, dim, lead)
 
     def add(*terms):
         return sum(term.astype(F32) for term in terms).astype(BF16)
 
+    close = [line ^ 1, line]
     row_out = row_forward(*(after(tensor, near) for tensor in by_head))
-    row_lead, row_own = within(row_out)
-
-    grad_row, grads = attn_grad(me, ids, out_grad, blocks, dim)
+    row_far = exchanged(row_out, far)
+    outs = column_forward(me, chunks, n)
+    column_part = links.swap(outs, order)
+    grad_row, grads = attn_grad(me, ids, after(out_grad, outs[0]), blocks, dim)
     grads = links.swap(grads, order)
-    column_part = links.swap(column_forward(me, chunks, n), order)
     column_out, flat = collect(me, row_out, column_part, n)
-
-    row_in = links.along(row_lead, INWARD)
-    row_cross = links.along(add(row_lead[1:], row_in[1:]), CROSS)
-    column_lead, column_own = within(column_out)
+    column_far = exchanged(column_out, far)
+    (row_far,) = summed(row_out, far, row_far, 0)
+    row_far_in = links.along(row_far, INWARD)
     gradients = column_backward(me, chunks, grads, n)
-    column_in = links.along(column_lead, INWARD)
     column_grads = list(gradients)
-    for d in order[: n // 2]:
-        column_grads[d] = links.flip(gradients[d], d)
-    column_cross = links.along(add(column_lead[1:], column_in[1:]), CROSS)
-    row_back = links.along(add(row_lead[0], row_cross[1]), OUTWARD)
-    for d in order[n // 2 :]:
-        column_grads[d] = links.flip(gradients[d], d)
-    column_back = links.along(add(column_lead[0], column_cross[1]), OUTWARD)
-
-    layer_out = scatter_layer(ids, flat, blocks, heads_n)
-    row_grads = row_backward(*by_head, grad_row)
+
+    def give_back(*which):
+        for d in which:
+            column_grads[d] = links.flip(gradients[d], d)
+
+    give_back(*order[: n // 4])
+    (column_far,) = summed(column_out, far, column_far, 0)
+    column_far_in = links.along(column_far, INWARD)
+    column_close = exchanged(column_out, close)
+    row_cross = links.along(add(row_far, row_far_in), CROSS)
+    give_back(*order[n // 4 : n // 4 + 1])
+    column_cross = links.along(add(column_far, column_far_in), CROSS)
+    row_close = exchanged(row_out, close)
+    column_near, column_own = summed(column_out, close, column_close, 1)
+    column_near_in = links.along(column_near[0], INWARD)
+    give_back(*order[n // 4 + 1 : n // 2 + 1])
+    column_back = links.along(add(column_near[0], column_cross[1]), OUTWARD)
+    row_near, row_own = summed(row_out, close, row_close, 1)
+    row_near_in = links.along(row_near[0], INWARD)
+    row_back = links.along(add(row_near[0], row_cross[1]), OUTWARD)
+    give_back(*order[n // 2 + 1 :])
+
+    layer_out = scatter_layer(ids, after(flat, gradients[0]), blocks, heads_n)
+    row_grads = row_backward(*by_head, after(grad_row, gradients[0]))
     gradients = join_gradients(me, column_grads, row_grads, n)
 
-    proj_row = add(row_own[0], row_in[0], row_cross[0], row_back)
-    proj_column = add(column_own[0], column_in[0], column_cross[0], column_back)
+    proj_row = add(row_own[0], row_near_in, row_cross[0], row_back)
+    proj_column = add(column_own[0], column_near_in, column_cross[0], column_back)
     shape = (half, dim, depth)
     proj_grad = jnp.stack([proj_row.reshape(shape), proj_column.reshape(shape)], axis=1)
     return (layer_out, *gradients, proj_grad.reshape(heads * dim, depth))

time: 532 us -> 539 us (1.013)
  Pallas kernels: 124 us -> 170 us
  local copies, waits for them, and re-layouts: 49.1 us -> 5.52 us
    unnamed x162 -> x68, local copies, waits for them, and re-layouts: 47.9 us -> 3.77 us
    pallas_call x4 -> x8, Pallas kernels: 20.6 us -> 40.1 us  [proj_part(): pl.pallas_call(functools.partial(proj_kernel, lead, len(extra), dim), gri...]
    pallas_call x1, Pallas kernels: 5.02 us -> 13.1 us  [split_inputs(): pl.pallas_call(functools.partial(split_kernel, n, rows), grid_spec=pltpu....]
    ppermute x45 -> x49, starting transfers between devices: 81.4 us -> 87.3 us  [send(): out = lax.ppermute(value, 'ctx', pairs)]
    pallas_call x3, Pallas kernels: 23.7 us -> 29.3 us  [layer_part(): pl.pallas_call(functools.partial(layer_kernel, n, count, len(extra)), gri...]
    ppermute x45 -> x49, waiting for transfers between devices: 256 us -> 254 us  [send(): out = lax.ppermute(value, 'ctx', pairs)]
  transfers between devices with their start and end apart: 47 -> 51, of which waited for: 16 -> 18; matrix products, arithmetic and copies ran while one was open for 3% -> 3% of each run, Pallas kernels for 20% -> 25%
where the time goes in v2:
time: 539 us; the launch traced here: 537 us
  waiting for transfers between devices  254 us (47%)
  Pallas kernels  170 us (32%)
  starting transfers between devices  88.9 us (16%)
  other arithmetic  17 us (3%)
  local copies, waits for them, and re-layouts  5.52 us (1%)
    ppermute x49, waiting for transfers between devices, send(): out = lax.ppermute(value, 'ctx', pairs)  254 us
    ppermute x49, starting transfers between devices, send(): out = lax.ppermute(value, 'ctx', pairs)  87.3 us
    pallas_call x8, Pallas kernels, proj_part(): pl.pallas_call(functools.partial(proj_kernel, lead, len(extra), dim), gri...  40.1 us
    pallas_call x3, Pallas kernels, layer_part(): pl.pallas_call(functools.partial(layer_kernel, n, count, len(extra)), gri...  29.3 us
    pallas_call x1, Pallas kernels, attn_grad(): pl.pallas_call(functools.partial(attn_grad_kernel, n, dim), grid_spec=plt...  21.1 us
    pallas_call x1, Pallas kernels, column_backward(): pl.pallas_call(functools.partial(column_backward_kernel, n, dim ** (-0.5)...  15.5 us
    pallas_call x1, Pallas kernels, row_backward(): pl.pallas_call(functools.partial(row_backward_kernel, dim ** (-0.5)), gri...  13.6 us
    pallas_call x1, Pallas kernels, split_inputs(): pl.pallas_call(functools.partial(split_kernel, n, rows), grid_spec=pltpu....  13.1 us
  transfers between devices with their start and end apart: 51, of which 18 were waited for; matrix products, arithmetic and copies ran while one was open for 3% of the time, Pallas kernels for 25%

profile of v2, /device:TPU:8, one launch (start us, length us, event | category | flops | bytes accessed | tf_op | source)
XLA Modules:
  0.0 537.3 jit_solution(8582774105108523937)
XLA Ops:
  0.7 5.0 collective-permute-start.3
  7.3 13.1 %split_inputs.1 = (bf16[3,4,2,64,128]{4,3,2,1,0:T(8,128)(2,1)}, bf16[3,4,2,64,128]{4,3,2,1,0:T(8,128)(2,1)}, bf16[3,4,2,64,128]{4,3,2,1,0:T(8,128)(2,1)}, bf16[3...) custom-call(s32[1]{0:T(128)} %bitcast.10.me, ...), custom_call_target="tpu_custom_call" | custom-call | tf_op jit(solution)/shard_map/split_inputs/pallas_call | solution.py:57
  20.5 5.3 collective-permute-done.refs_2_
  28.9 3.6 collective-permute-start.4
  35.2 46.4 %collective-permute-done.7.refs_4_ = bf16[3,4,2,64,128]{4,3,2,1,0:T(8,128)(2,1)S(1)} collective-permute-done((bf16[3,4,2,64,128]{4,3,2,1,0:T(8,128)(2,1)}, bf16[3,4,2,64,128]{4,3,2,1,0:T(8,128)(2,1)S(1)}, u32[]{:S(2)}, u32[]{:S(2)}) %collective-permute-start.7) | collective-permute-done | bytes 393248 | tf_op jit(solution)/shard_map/ppermute | solution.py:505
  81.6 7.1 %collective-permute-done.2.refs_6_ = bf16[3,4,2,64,128]{4,3,2,1,0:T(8,128)(2,1)} collective-permute-done((bf16[3,4,2,64,128]{4,3,2,1,0:T(8,128)(2,1)}, bf16[3,4,2,64,128]{4,3,2,1,0:T(8,128)(2,1)}, u32[]{:S(2)}, u32[]{:S(2)}) %collective-permute-start.2) | collective-permute-done | bytes 393248 | tf_op jit(solution)/shard_map/ppermute | solution.py:505
  94.5 9.9 %row_forward.1.flat_ref.row_ref = bf16[1024,512]{1,0:T(8,128)(2,1)} custom-call(bf16[4,1024,128]{2,1,0:T(8,128)(2,1)} %get-tuple-element.105.q_ref, bf16[4,1024,128]{2,1,0:T(8,128)(2,1)} %get-tuple-element.107.k_ref, bf16[4,1024,128]{2,1,0:T(8,128)(2,1)} %get-tuple-element.109.v_ref), custom_call_target="tpu_custom_call" | custom-call | flops 1073741824 | bytes 4194304 | tf_op jit(solution)/shard_map/row_forward/pallas_call | solution.py:334
  104.3 2.9 collective-permute-start.10
  107.2 4.8 proj_part.8
  112.1 10.1 %collective-permute-done.13 = bf16[1024,512]{1,0:T(8,128)(2,1)} collective-permute-done((bf16[1024,512]{1,0:T(8,128)(2,1)}, bf16[1024,512]{1,0:T(8,128)(2,1)}, u32[]{:S(2)}, u32[]{:S(2)}) %collective-permute-start.13) | collective-permute-done | bytes 1048608 | tf_op jit(solution)/shard_map/ppermute | solution.py:505
  123.5 4.5 collective-permute-done.8.refs_2_
  132.7 4.2 collective-permute-start.11
  136.9 61.5 %collective-permute-done.9.refs_1_ = bf16[3,4,2,64,128]{4,3,2,1,0:T(8,128)(2,1)} collective-permute-done((bf16[3,4,2,64,128]{4,3,2,1,0:T(8,128)(2,1)S(1)}, bf16[3,4,2,64,128]{4,3,2,1,0:T(8,128)(2,1)}, u32[]{:S(2)}, u32[]{:S(2)}) %collective-permute-start.9) | collective-permute-done | bytes 393248 | tf_op jit(solution)/shard_map/ppermute | solution.py:505
  198.4 11.4 %column_forward.1 = (bf16[4,2,64,128]{3,2,1,0:T(8,128)(2,1)}, bf16[4,2,64,128]{3,2,1,0:T(8,128)(2,1)}, bf16[4,2,64,128]{3,2,1,0:T(8,128)(2,1)}, bf16[4,2,64,128]...) custom-call(s32[1]{0:T(128)} %bitcast.10.me, ...), custom_call_target="tpu_custom_call" | custom-call | flops 536870912 | bytes 4194304 | tf_op jit(solution)/shard_map/column_forward/pallas_call | solution.py:432
  210.7 4.0 collective-permute-start.17
  217.1 3.5 collective-permute-start.22
  220.7 2.5 collective-permute-done.20.refs_6_
  223.2 3.7 collective-permute-done.17.refs_4_
  226.9 4.3 collective-permute-start.21
  231.9 21.1 %attn_grad.1 = (bf16[1024,512]{1,0:T(8,128)(2,1)}, bf16[4,2,64,128]{3,2,1,0:T(8,128)(2,1)}, bf16[4,2,64,128]{3,2,1,0:T(8,128)(2,1)}, bf16[4,2,64,128]{3,2,1,0:T(...) custom-call(s32[1]{0:T(128)} %bitcast.10.me, ...), custom_call_target="tpu_custom_call" | custom-call | flops 8589934592 | bytes 18874368 | tf_op jit(solution)/shard_map/attn_grad/pallas_call | solution.py:177
  257.2 3.6 collective-permute-start.29
  263.0 5.9 %collective-permute-done.27.refs_14_ = bf16[4,2,64,128]{3,2,1,0:T(8,128)(2,1)S(1)} collective-permute-done((bf16[4,2,64,128]{3,2,1,0:T(8,128)(2,1)}, bf16[4,2,64,128]{3,2,1,0:T(8,128)(2,1)S(1)}, u32[]{:S(2)}, u32[]{:S(2)}) %collective-permute-start.27) | collective-permute-done | bytes 131104 | tf_op jit(solution)/shard_map/ppermute | solution.py:505
  269.5 3.9 collect.1
  275.6 15.5 %column_backward.1 = (bf16[3,4,2,64,128]{4,3,2,1,0:T(8,128)(2,1)}, bf16[3,4,2,64,128]{4,3,2,1,0:T(8,128)(2,1)}, bf16[3,4,2,64,128]{4,3,2,1,0:T(8,128)(2,1)}, bf1...) custom-call(s32[1]{0:T(128)} %bitcast.10.me, ...), custom_call_target="tpu_custom_call" | custom-call | flops 1342177280 | bytes 7340032 | tf_op jit(solution)/shard_map/column_backward/pallas_call | solution.py:471
  291.1 11.7 %layer_part.3 = bf16[1024,2048]{1,0:T(8,128)(2,1)} custom-call(s32[8]{0:T(128)} %stack.103.ids, s32[4]{0:T(128)} %pad_add_fusion.2.wanted, bf16[1024,1024]{1,0:T(8,128)(2,1)} %get-tuple-element.164.flat_ref, bf16[1024,512]{1,0:T(8,128)(2,1)} %refs_0_.7, bf16[1024,512]{1,0:T(8,128)(2,1)} %copy-done.3, bf16[1024,512]{1,0:T(8,128)(2,1)} %copy-done.2, ...), custom_call_target="tpu_custom_call" | custom-call | flops 4294967296 | bytes 10485760 | tf_op jit(solution)/shard_map/layer_part/pallas_call | solution.py:234
  302.8 4.9 proj_part.9
  309.4 5.0 proj_part.10
  315.9 17.6 %collective-permute-done.33.refs_0_ = bf16[2,512,512]{2,1,0:T(8,128)(2,1)S(1)} collective-permute-done((bf16[2,512,512]{2,1,0:T(8,128)(2,1)}, bf16[2,512,512]{2,1,0:T(8,128)(2,1)S(1)}, u32[]{:S(2)}, u32[]{:S(2)}) %collective-permute-start.33) | collective-permute-done | bytes 1048608 | tf_op jit(solution)/shard_map/ppermute | solution.py:505
  334.5 5.0 proj_part.11
  341.3 4.6 collective-permute-start.35
  345.9 4.8 proj_part.13
  351.1 2.4 collective-permute-start.43
  354.6 21.2 %collective-permute-done.35.refs_4_ = bf16[3,4,2,64,128]{4,3,2,1,0:T(8,128)(2,1)S(1)} collective-permute-done((bf16[3,4,2,64,128]{4,3,2,1,0:T(8,128)(2,1)}, bf16[3,4,2,64,128]{4,3,2,1,0:T(8,128)(2,1)S(1)}, u32[]{:S(2)}, u32[]{:S(2)}) %collective-permute-start.35) | collective-permute-done | bytes 393248 | tf_op jit(solution)/shard_map/ppermute | solution.py:505
  376.4 26.6 %collective-permute-done.38.refs_6_ = bf16[3,4,2,64,128]{4,3,2,1,0:T(8,128)(2,1)} collective-permute-done((bf16[3,4,2,64,128]{4,3,2,1,0:T(8,128)(2,1)S(1)}, bf16[3,4,2,64,128]{4,3,2,1,0:T(8,128)(2,1)}, u32[]{:S(2)}, u32[]{:S(2)}) %collective-permute-start.38) | collective-permute-done | bytes 393248 | tf_op jit(solution)/shard_map/ppermute | solution.py:505
  402.9 4.9 proj_part.12
  408.9 2.5 add_convert_fusion.1
  412.9 3.6 collective-permute-start.39
  419.1 5.3 proj_part.14
  425.7 8.5 %layer_part.4 = bf16[1024,1024]{1,0:T(8,128)(2,1)} custom-call(s32[8]{0:T(128)} %stack.103.ids, s32[2]{0:T(128)} %pad_add_fusion.3.wanted, bf16[1024,1024]{1,0:T(8,128)(2,1)} %get-tuple-element.164.flat_ref, bf16[1024,512]{1,0:T(8,128)(2,1)} %refs_0_.7, bf16[1024,512]{1,0:T(8,128)(2,1)} %copy-done.3, bf16[1024,512]{1,0:T(8,128)(2,1)} %copy-done.2, ...), custom_call_target="tpu_custom_call" | custom-call | flops 2147483648 | bytes 6291456 | tf_op jit(solution)/shard_map/layer_part/pallas_call | solution.py:234
  435.8 20.7 %collective-permute-done.46.refs_7_ = bf16[3,4,2,64,128]{4,3,2,1,0:T(8,128)(2,1)S(1)} collective-permute-done((bf16[3,4,2,64,128]{4,3,2,1,0:T(8,128)(2,1)}, bf16[3,4,2,64,128]{4,3,2,1,0:T(8,128)(2,1)S(1)}, u32[]{:S(2)}, u32[]{:S(2)}) %collective-permute-start.46) | collective-permute-done | bytes 393248 | tf_op jit(solution)/shard_map/ppermute | solution.py:505
  457.1 14.7 %collective-permute-done.44.refs_5_ = bf16[3,4,2,64,128]{4,3,2,1,0:T(8,128)(2,1)} collective-permute-done((bf16[3,4,2,64,128]{4,3,2,1,0:T(8,128)(2,1)}, bf16[3,4,2,64,128]{4,3,2,1,0:T(8,128)(2,1)}, u32[]{:S(2)}, u32[]{:S(2)}) %collective-permute-start.44) | collective-permute-done | bytes 393248 | tf_op jit(solution)/shard_map/ppermute | solution.py:505
  471.8 2.9 collective-permute-start.47
  476.8 2.9 collective-permute-start.50
  479.7 5.3 proj_part.15
  489.2 6.1 %collective-permute-start.49 = (bf16[512,512]{1,0:T(8,128)(2,1)}, bf16[512,512]{1,0:T(8,128)(2,1)}, u32[]{:S(2)}, u32[]{:S(2)}) collective-permute-start(bf16[512,512]{1,0:T(8,128)(2,1)} %fusion.3), channel_id=1, source_target_pairs={{8,0},{12,4},{16,24},{20,28},{9,1},{13,5},{17,25},{21,29},{10,2},{... | collective-permute-start | bytes 1572872 | tf_op jit(solution)/shard_map/ppermute | solution.py:505
  495.3 13.6 %row_backward.1 = (bf16[4,1024,128]{2,1,0:T(8,128)(2,1)}, bf16[4,1024,128]{2,1,0:T(8,128)(2,1)}, bf16[4,1024,128]{2,1,0:T(8,128)(2,1)}) custom-call(bf16[4,1024,128]{2,1,0:T(8,128)(2,1)} %get-tuple-element.105.q_ref, bf16[4,1024,128]{2,1,0:T(8,128)(2,1)} %get-tuple-element.107.k_ref, bf16[4,1024,128]{2,1,0:T(8,128)(2,1)} %get-tuple-element.109.v_ref, ...), custom_call_target="tpu_custom_call" | custom-call | flops 2684354560 | bytes 7340032 | tf_op jit(solution)/shard_map/row_backward/pallas_call | solution.py:368
  509.6 12.6 %join_gradients.1 = (bf16[1024,8,128]{2,1,0:T(8,128)(2,1)}, bf16[1024,8,128]{2,1,0:T(8,128)(2,1)}, bf16[1024,8,128]{2,1,0:T(8,128)(2,1)}) custom-call(s32[1]{0:T(128)} %bitcast.10.me, bf16[3,4,2,64,128]{4,3,2,1,0:T(8,128)(2,1)} %get-tuple-element.163.refs_0_, bf16[3,4,2,64,128]{4,3,2,1,0:T(8,128)(2,1)} %copy-done.16, ...), custom_call_target="tpu_custom_call" | custom-call | tf_op jit(solution)/shard_map/join_gradients/pallas_call | solution.py:96
  527.9 9.2 %layer_part.5 = bf16[1024,1024]{1,0:T(8,128)(2,1)} custom-call(s32[8]{0:T(128)} %stack.103.ids, s32[2]{0:T(128)} %pad_add_fusion.wanted, bf16[1024,1024]{1,0:T(8,128)(2,1)} %get-tuple-element.164.flat_ref, bf16[1024,512]{1,0:T(8,128)(2,1)} %refs_0_.7, bf16[1024,512]{1,0:T(8,128)(2,1)} %copy-done.3, bf16[1024,512]{1,0:T(8,128)(2,1)} %copy-done.2, ...), custom_call_target="tpu_custom_call" | custom-call | flops 2147483648 | bytes 6291456 | tf_op jit(solution)/shard_map/layer_part/pallas_call | solution.py:234
  (159 shorter events, 61.6 us)
Async XLA Ops:
  0.6 25.2 %collective-permute-start = (bf16[1024,512]{1,0:T(8,128)(2,1)}, bf16[1024,512]{1,0:T(8,128)(2,1)S(1)}, u32[]{:S(2)}, u32[]{:S(2)}) collective-permute-start(bf16[1024,512]{1,0:T(8,128)(2,1)} %refs_0_.7), channel_id=1, source_target_pairs={{0,8},{4,12},{8,0},{12,4},{16,24},{20,28},{24,16},{28,20},{1,9},{5... | collective-permute-start | bytes 3145736 | tf_op jit(solution)/shard_map/ppermute | solution.py:505
  0.7 28.2 %collective-permute-start.3 = (bf16[1024,512]{1,0:T(8,128)(2,1)}, bf16[1024,512]{1,0:T(8,128)(2,1)}, u32[]{:S(2)}, u32[]{:S(2)}) collective-permute-start(bf16[1024,512]{1,0:T(8,128)(2,1)} %refs_0_.7), channel_id=1, source_target_pairs={{8,16},{12,20},{16,8},{20,12},{9,17},{13,21},{17,9},{21,13},{10,18... | collective-permute-start | bytes 3145736 | tf_op jit(solution)/shard_map/ppermute | solution.py:505
  5.8 26.8 %collective-permute-start.5 = (bf16[1024,512]{1,0:T(8,128)(2,1)}, bf16[1024,512]{1,0:T(8,128)(2,1)S(1)}, u32[]{:S(2)}, u32[]{:S(2)}) collective-permute-start(bf16[1024,512]{1,0:T(8,128)(2,1)} %refs_0_.7), channel_id=1, source_target_pairs={{0,4},{4,0},{8,12},{12,8},{16,20},{20,16},{24,28},{28,24},{1,5},{5... | collective-permute-start | bytes 3145736 | tf_op jit(solution)/shard_map/ppermute | solution.py:505
  25.8 62.9 %collective-permute-start.1 = (bf16[1024,512]{1,0:T(8,128)(2,1)S(1)}, bf16[1024,512]{1,0:T(8,128)(2,1)S(1)}, u32[]{:S(2)}, u32[]{:S(2)}) collective-permute-start(bf16[1024,512]{1,0:T(8,128)(2,1)S(1)} %collective-permute-done.refs_2_), channel_id=1, source_target_pairs={{0,4},{4,0},{8,12},{12,8},{16,20},{20,16},{24,28},{28,24},{1,5},{5... | collective-permute-start | bytes 3145736 | tf_op jit(solution)/shard_map/ppermute | solution.py:505
  28.9 59.7 %collective-permute-start.4 = (bf16[1024,512]{1,0:T(8,128)(2,1)S(1)}, bf16[1024,512]{1,0:T(8,128)(2,1)}, u32[]{:S(2)}, u32[]{:S(2)}) collective-permute-start(bf16[1024,512]{1,0:T(8,128)(2,1)S(1)} %collective-permute-done.refs_2_), channel_id=1, source_target_pairs={{8,16},{12,20},{16,8},{20,12},{9,17},{13,21},{17,9},{21,13},{10,18... | collective-permute-start | bytes 3145736 | tf_op jit(solution)/shard_map/ppermute | solution.py:505
  32.6 58.3 %collective-permute-start.6 = (bf16[1024,512]{1,0:T(8,128)(2,1)}, bf16[1024,512]{1,0:T(8,128)(2,1)}, u32[]{:S(2)}, u32[]{:S(2)}) collective-permute-start(bf16[1024,512]{1,0:T(8,128)(2,1)} %collective-permute-done.3), channel_id=1, source_target_pairs={{8,0},{12,4},{16,24},{20,28},{9,1},{13,5},{17,25},{21,29},{10,2},{... | collective-permute-start | bytes 3145736 | tf_op jit(solution)/shard_map/ppermute | solution.py:505
  34.9 46.6 %collective-permute-start.7 = (bf16[3,4,2,64,128]{4,3,2,1,0:T(8,128)(2,1)}, bf16[3,4,2,64,128]{4,3,2,1,0:T(8,128)(2,1)S(1)}, u32[]{:S(2)}, u32[]{:S(2)}) collective-permute-start(bf16[3,4,2,64,128]{4,3,2,1,0:T(8,128)(2,1)} %get-tuple-element.118), channel_id=1, source_target_pairs={{0,16},{4,20},{8,24},{12,28},{16,0},{20,4},{24,8},{28,12},{1,17},{... | collective-permute-start | bytes 1179656 | tf_op jit(solution)/shard_map/ppermute | solution.py:505
  34.9 53.8 %collective-permute-start.2 = (bf16[3,4,2,64,128]{4,3,2,1,0:T(8,128)(2,1)}, bf16[3,4,2,64,128]{4,3,2,1,0:T(8,128)(2,1)}, u32[]{:S(2)}, u32[]{:S(2)}) collective-permute-start(bf16[3,4,2,64,128]{4,3,2,1,0:T(8,128)(2,1)} %get-tuple-element.114), channel_id=1, source_target_pairs={{0,24},{4,28},{8,16},{12,20},{16,8},{20,12},{24,0},{28,4},{1,25},{... | collective-permute-start | bytes 1179656 | tf_op jit(solution)/shard_map/ppermute | solution.py:505
  88.7 33.5 %collective-permute-start.13 = (bf16[1024,512]{1,0:T(8,128)(2,1)}, bf16[1024,512]{1,0:T(8,128)(2,1)}, u32[]{:S(2)}, u32[]{:S(2)}) collective-permute-start(bf16[1024,512]{1,0:T(8,128)(2,1)} %collective-permute-done.4), channel_id=1, source_target_pairs={{8,0},{12,4},{16,24},{20,28},{9,1},{13,5},{17,25},{21,29},{10,2},{... | collective-permute-start | bytes 3145736 | tf_op jit(solution)/shard_map/ppermute | solution.py:505
  92.3 35.7 %collective-permute-start.14 = (bf16[1024,512]{1,0:T(8,128)(2,1)S(1)}, bf16[1024,512]{1,0:T(8,128)(2,1)}, u32[]{:S(2)}, u32[]{:S(2)}) collective-permute-start(bf16[1024,512]{1,0:T(8,128)(2,1)S(1)} %broadcast_select_fusion.refs_4_), channel_id=1, source_target_pairs={{0,4},{4,0},{8,12},{12,8},{16,20},{20,16},{24,28},{28,24},{1,5},{5... | collective-permute-start | bytes 3145736 | tf_op jit(solution)/shard_map/ppermute | solution.py:505
  94.4 33.6 %collective-permute-start.8 = (bf16[3,4,2,64,128]{4,3,2,1,0:T(8,128)(2,1)}, bf16[3,4,2,64,128]{4,3,2,1,0:T(8,128)(2,1)S(1)}, u32[]{:S(2)}, u32[]{:S(2)}) collective-permute-start(bf16[3,4,2,64,128]{4,3,2,1,0:T(8,128)(2,1)} %get-tuple-element.119), channel_id=1, source_target_pairs={{0,8},{4,12},{8,0},{12,4},{16,24},{20,28},{24,16},{28,20},{1,9},{5... | collective-permute-start | bytes 1179656 | tf_op jit(solution)/shard_map/ppermute | solution.py:505
  104.3 23.7 %collective-permute-start.10 = (bf16[3,4,2,64,128]{4,3,2,1,0:T(8,128)(2,1)}, bf16[3,4,2,64,128]{4,3,2,1,0:T(8,128)(2,1)S(1)}, u32[]{:S(2)}, u32[]{:S(2)}) collective-permute-start(bf16[3,4,2,64,128]{4,3,2,1,0:T(8,128)(2,1)} %get-tuple-element.123), channel_id=1, source_target_pairs={{0,20},{4,16},{8,28},{12,24},{16,4},{20,0},{24,12},{28,8},{1,21},{... | collective-permute-start | bytes 1179656 | tf_op jit(solution)/shard_map/ppermute | solution.py:505
  128.0 87.3 %collective-permute-start.15 = (bf16[1024,512]{1,0:T(8,128)(2,1)S(1)}, bf16[1024,512]{1,0:T(8,128)(2,1)S(1)}, u32[]{:S(2)}, u32[]{:S(2)}) collective-permute-start(bf16[1024,512]{1,0:T(8,128)(2,1)S(1)} %broadcast_select_fusion.1.refs_6_), channel_id=1, source_target_pairs={{0,4},{4,0},{8,12},{12,8},{16,20},{20,16},{24,28},{28,24},{1,5},{5... | collective-permute-start | bytes 3145736 | tf_op jit(solution)/shard_map/ppermute | solution.py:505
  129.6 85.7 %collective-permute-start.16 = (bf16[2,512,512]{2,1,0:T(8,128)(2,1)}, bf16[2,512,512]{2,1,0:T(8,128)(2,1)S(1)}, u32[]{:S(2)}, u32[]{:S(2)}) collective-permute-start(bf16[2,512,512]{2,1,0:T(8,128)(2,1)} %proj_part.8), channel_id=1, source_target_pairs={{0,4},{4,0},{8,12},{12,8},{16,20},{20,16},{24,28},{28,24},{1,5},{5... | collective-permute-start | bytes 3145736 | tf_op jit(solution)/shard_map/ppermute | solution.py:505
  130.1 68.3 %collective-permute-start.9 = (bf16[3,4,2,64,128]{4,3,2,1,0:T(8,128)(2,1)S(1)}, bf16[3,4,2,64,128]{4,3,2,1,0:T(8,128)(2,1)}, u32[]{:S(2)}, u32[]{:S(2)}) collective-permute-start(bf16[3,4,2,64,128]{4,3,2,1,0:T(8,128)(2,1)S(1)} %copy-done.25), channel_id=1, source_target_pairs={{0,4},{4,0},{8,12},{12,8},{16,20},{20,16},{24,28},{28,24},{1,5},{5... | collective-permute-start | bytes 1179656 | tf_op jit(solution)/shard_map/ppermute | solution.py:505
  131.7 66.8 %collective-permute-start.12 = (bf16[3,4,2,64,128]{4,3,2,1,0:T(8,128)(2,1)S(1)}, bf16[3,4,2,64,128]{4,3,2,1,0:T(8,128)(2,1)}, u32[]{:S(2)}, u32[]{:S(2)}) collective-permute-start(bf16[3,4,2,64,128]{4,3,2,1,0:T(8,128)(2,1)S(1)} %copy-done.24), channel_id=1, source_target_pairs={{0,28},{4,24},{8,20},{12,16},{16,12},{20,8},{24,4},{28,0},{1,29},{... | collective-permute-start | bytes 1179656 | tf_op jit(solution)/shard_map/ppermute | solution.py:505
  132.7 65.7 %collective-permute-start.11 = (bf16[3,4,2,64,128]{4,3,2,1,0:T(8,128)(2,1)S(1)}, bf16[3,4,2,64,128]{4,3,2,1,0:T(8,128)(2,1)}, u32[]{:S(2)}, u32[]{:S(2)}) collective-permute-start(bf16[3,4,2,64,128]{4,3,2,1,0:T(8,128)(2,1)S(1)} %copy-done.23), channel_id=1, source_target_pairs={{0,12},{4,8},{8,4},{12,0},{16,28},{20,24},{24,20},{28,16},{1,13},{... | collective-permute-start | bytes 1179656 | tf_op jit(solution)/shard_map/ppermute | solution.py:505
  209.9 13.3 %collective-permute-start.20 = (bf16[4,2,64,128]{3,2,1,0:T(8,128)(2,1)}, bf16[4,2,64,128]{3,2,1,0:T(8,128)(2,1)S(1)}, u32[]{:S(2)}, u32[]{:S(2)}) collective-permute-start(bf16[4,2,64,128]{3,2,1,0:T(8,128)(2,1)} %get-tuple-element.140), channel_id=1, source_target_pairs={{0,24},{4,28},{8,16},{12,20},{16,8},{20,12},{24,0},{28,4},{1,25},{... | collective-permute-start | bytes 393224 | tf_op jit(solution)/shard_map/ppermute | solution.py:505
  210.7 16.2 %collective-permute-start.17 = (bf16[4,2,64,128]{3,2,1,0:T(8,128)(2,1)}, bf16[4,2,64,128]{3,2,1,0:T(8,128)(2,1)S(1)}, u32[]{:S(2)}, u32[]{:S(2)}) collective-permute-start(bf16[4,2,64,128]{3,2,1,0:T(8,128)(2,1)} %get-tuple-element.134), channel_id=1, source_target_pairs={{0,16},{4,20},{8,24},{12,28},{16,0},{20,4},{24,8},{28,12},{1,17},{... | collective-permute-start | bytes 393224 | tf_op jit(solution)/shard_map/ppermute | solution.py:505
  215.3 37.7 %collective-permute-start.19 = (bf16[4,2,64,128]{3,2,1,0:T(8,128)(2,1)}, bf16[4,2,64,128]{3,2,1,0:T(8,128)(2,1)S(1)}, u32[]{:S(2)}, u32[]{:S(2)}) collective-permute-start(bf16[4,2,64,128]{3,2,1,0:T(8,128)(2,1)} %get-tuple-element.137), channel_id=1, source_target_pairs={{0,8},{4,12},{8,0},{12,4},{16,24},{20,28},{24,16},{28,20},{1,9},{5... | collective-permute-start | bytes 393224 | tf_op jit(solution)/shard_map/ppermute | solution.py:505
  215.3 39.5 %collective-permute-start.23 = (bf16[4,2,64,128]{3,2,1,0:T(8,128)(2,1)}, bf16[4,2,64,128]{3,2,1,0:T(8,128)(2,1)}, u32[]{:S(2)}, u32[]{:S(2)}) collective-permute-start(bf16[4,2,64,128]{3,2,1,0:T(8,128)(2,1)} %get-tuple-element.145), channel_id=1, source_target_pairs={{0,28},{4,24},{8,20},{12,16},{16,12},{20,8},{24,4},{28,0},{1,29},{... | collective-permute-start | bytes 393224 | tf_op jit(solution)/shard_map/ppermute | solution.py:505
  217.1 37.0 %collective-permute-start.22 = (bf16[4,2,64,128]{3,2,1,0:T(8,128)(2,1)}, bf16[4,2,64,128]{3,2,1,0:T(8,128)(2,1)}, u32[]{:S(2)}, u32[]{:S(2)}) collective-permute-start(bf16[4,2,64,128]{3,2,1,0:T(8,128)(2,1)} %get-tuple-element.143), channel_id=1, source_target_pairs={{0,20},{4,16},{8,28},{12,24},{16,4},{20,0},{24,12},{28,8},{1,21},{... | collective-permute-start | bytes 393224 | tf_op jit(solution)/shard_map/ppermute | solution.py:505
  226.9 28.0 %collective-permute-start.21 = (bf16[4,2,64,128]{3,2,1,0:T(8,128)(2,1)}, bf16[4,2,64,128]{3,2,1,0:T(8,128)(2,1)}, u32[]{:S(2)}, u32[]{:S(2)}) collective-permute-start(bf16[4,2,64,128]{3,2,1,0:T(8,128)(2,1)} %get-tuple-element.141), channel_id=1, source_target_pairs={{0,12},{4,8},{8,4},{12,0},{16,28},{20,24},{24,20},{28,16},{1,13},{... | collective-permute-start | bytes 393224 | tf_op jit(solution)/shard_map/ppermute | solution.py:505
  231.3 23.6 %collective-permute-start.18 = (bf16[4,2,64,128]{3,2,1,0:T(8,128)(2,1)}, bf16[4,2,64,128]{3,2,1,0:T(8,128)(2,1)}, u32[]{:S(2)}, u32[]{:S(2)}) collective-permute-start(bf16[4,2,64,128]{3,2,1,0:T(8,128)(2,1)} %get-tuple-element.135), channel_id=1, source_target_pairs={{0,4},{4,0},{8,12},{12,8},{16,20},{20,16},{24,28},{28,24},{1,5},{5... | collective-permute-start | bytes 393224 | tf_op jit(solution)/shard_map/ppermute | solution.py:505
  254.2 14.7 %collective-permute-start.27 = (bf16[4,2,64,128]{3,2,1,0:T(8,128)(2,1)}, bf16[4,2,64,128]{3,2,1,0:T(8,128)(2,1)S(1)}, u32[]{:S(2)}, u32[]{:S(2)}) collective-permute-start(bf16[4,2,64,128]{3,2,1,0:T(8,128)(2,1)} %get-tuple-element.157), channel_id=1, source_target_pairs={{0,24},{4,28},{8,16},{12,20},{16,8},{20,12},{24,0},{28,4},{1,25},{... | collective-permute-start | bytes 393224 | tf_op jit(solution)/shard_map/ppermute | solution.py:505
  254.9 18.5 %collective-permute-start.30 = (bf16[4,2,64,128]{3,2,1,0:T(8,128)(2,1)}, bf16[4,2,64,128]{3,2,1,0:T(8,128)(2,1)S(1)}, u32[]{:S(2)}, u32[]{:S(2)}) collective-permute-start(bf16[4,2,64,128]{3,2,1,0:T(8,128)(2,1)} %get-tuple-element.162), channel_id=1, source_target_pairs={{0,28},{4,24},{8,20},{12,16},{16,12},{20,8},{24,4},{28,0},{1,29},{... | collective-permute-start | bytes 393224 | tf_op jit(solution)/shard_map/ppermute | solution.py:505
  257.2 16.2 %collective-permute-start.29 = (bf16[4,2,64,128]{3,2,1,0:T(8,128)(2,1)}, bf16[4,2,64,128]{3,2,1,0:T(8,128)(2,1)S(1)}, u32[]{:S(2)}, u32[]{:S(2)}) collective-permute-start(bf16[4,2,64,128]{3,2,1,0:T(8,128)(2,1)} %get-tuple-element.160), channel_id=1, source_target_pairs={{0,20},{4,16},{8,28},{12,24},{16,4},{20,0},{24,12},{28,8},{1,21},{... | collective-permute-start | bytes 393224 | tf_op jit(solution)/shard_map/ppermute | solution.py:505
  260.8 12.6 %collective-permute-start.26 = (bf16[4,2,64,128]{3,2,1,0:T(8,128)(2,1)}, bf16[4,2,64,128]{3,2,1,0:T(8,128)(2,1)S(1)}, u32[]{:S(2)}, u32[]{:S(2)}) collective-permute-start(bf16[4,2,64,128]{3,2,1,0:T(8,128)(2,1)} %get-tuple-element.154), channel_id=1, source_target_pairs={{0,8},{4,12},{8,0},{12,4},{16,24},{20,28},{24,16},{28,20},{1,9},{5... | collective-permute-start | bytes 393224 | tf_op jit(solution)/shard_map/ppermute | solution.py:505
  263.0 10.4 %collective-permute-start.25 = (bf16[4,2,64,128]{3,2,1,0:T(8,128)(2,1)}, bf16[4,2,64,128]{3,2,1,0:T(8,128)(2,1)S(1)}, u32[]{:S(2)}, u32[]{:S(2)}) collective-permute-start(bf16[4,2,64,128]{3,2,1,0:T(8,128)(2,1)} %get-tuple-element.152), channel_id=1, source_target_pairs={{0,4},{4,0},{8,12},{12,8},{16,20},{20,16},{24,28},{28,24},{1,5},{5... | collective-permute-start | bytes 393224 | tf_op jit(solution)/shard_map/ppermute | solution.py:505
  302.8 123.0 %collective-permute-start.31 = (bf16[1024,2048]{1,0:T(8,128)(2,1)}, bf16[1024,2048]{1,0:T(8,128)(2,1)}, u32[]{:S(2)}, u32[]{:S(2)}) collective-permute-start(bf16[1024,2048]{1,0:T(8,128)(2,1)} %layer_part.3), channel_id=1, source_target_pairs={{0,1},{1,0},{2,3},{3,2},{4,5},{5,4},{6,7},{7,6},{8,9},{9,8},{10,11... | collective-permute-start | bytes 12582920 | tf_op jit(solution)/shard_map/ppermute | solution.py:530
  307.7 25.8 %collective-permute-start.33 = (bf16[2,512,512]{2,1,0:T(8,128)(2,1)}, bf16[2,512,512]{2,1,0:T(8,128)(2,1)S(1)}, u32[]{:S(2)}, u32[]{:S(2)}) collective-permute-start(bf16[2,512,512]{2,1,0:T(8,128)(2,1)} %proj_part.9), channel_id=1, source_target_pairs={{0,4},{4,0},{8,12},{12,8},{16,20},{20,16},{24,28},{28,24},{1,5},{5... | collective-permute-start | bytes 3145736 | tf_op jit(solution)/shard_map/ppermute | solution.py:505
  314.4 36.3 %collective-permute-start.34 = (bf16[2,512,512]{2,1,0:T(8,128)(2,1)}, bf16[2,512,512]{2,1,0:T(8,128)(2,1)S(1)}, u32[]{:S(2)}, u32[]{:S(2)}) collective-permute-start(bf16[2,512,512]{2,1,0:T(8,128)(2,1)} %proj_part.10), channel_id=1, source_target_pairs={{0,8},{4,12},{24,16},{28,20},{1,9},{5,13},{25,17},{29,21},{2,10},{... | collective-permute-start | bytes 3145736 | tf_op jit(solution)/shard_map/ppermute | solution.py:505
  339.5 68.3 %collective-permute-start.37 = (bf16[2,512,512]{2,1,0:T(8,128)(2,1)}, bf16[2,512,512]{2,1,0:T(8,128)(2,1)}, u32[]{:S(2)}, u32[]{:S(2)}) collective-permute-start(bf16[2,512,512]{2,1,0:T(8,128)(2,1)} %proj_part.11), channel_id=1, source_target_pairs={{0,8},{4,12},{24,16},{28,20},{1,9},{5,13},{25,17},{29,21},{2,10},{... | collective-permute-start | bytes 3145736 | tf_op jit(solution)/shard_map/ppermute | solution.py:505
  341.3 34.5 %collective-permute-start.35 = (bf16[3,4,2,64,128]{4,3,2,1,0:T(8,128)(2,1)}, bf16[3,4,2,64,128]{4,3,2,1,0:T(8,128)(2,1)S(1)}, u32[]{:S(2)}, u32[]{:S(2)}) collective-permute-start(bf16[3,4,2,64,128]{4,3,2,1,0:T(8,128)(2,1)} %get-tuple-element.171), channel_id=1, source_target_pairs={{0,16},{4,20},{8,24},{12,28},{16,0},{20,4},{24,8},{28,12},{1,17},{... | collective-permute-start | bytes 1179656 | tf_op jit(solution)/shard_map/ppermute | solution.py:505
  351.1 66.6 %collective-permute-start.43 = (bf16[2,512,512]{2,1,0:T(8,128)(2,1)S(1)}, bf16[2,512,512]{2,1,0:T(8,128)(2,1)S(1)}, u32[]{:S(2)}, u32[]{:S(2)}) collective-permute-start(bf16[2,512,512]{2,1,0:T(8,128)(2,1)S(1)} %add_convert_fusion), channel_id=1, source_target_pairs={{8,16},{12,20},{16,8},{20,12},{9,17},{13,21},{17,9},{21,13},{10,18... | collective-permute-start | bytes 3145736 | tf_op jit(solution)/shard_map/ppermute | solution.py:505
  353.5 64.2 %collective-permute-start.41 = (bf16[2,512,512]{2,1,0:T(8,128)(2,1)}, bf16[2,512,512]{2,1,0:T(8,128)(2,1)}, u32[]{:S(2)}, u32[]{:S(2)}) collective-permute-start(bf16[2,512,512]{2,1,0:T(8,128)(2,1)} %proj_part.13), channel_id=1, source_target_pairs={{0,4},{4,0},{8,12},{12,8},{16,20},{20,16},{24,28},{28,24},{1,5},{5... | collective-permute-start | bytes 3145736 | tf_op jit(solution)/shard_map/ppermute | solution.py:505
  375.9 27.1 %collective-permute-start.38 = (bf16[3,4,2,64,128]{4,3,2,1,0:T(8,128)(2,1)S(1)}, bf16[3,4,2,64,128]{4,3,2,1,0:T(8,128)(2,1)}, u32[]{:S(2)}, u32[]{:S(2)}) collective-permute-start(bf16[3,4,2,64,128]{4,3,2,1,0:T(8,128)(2,1)S(1)} %copy-done.26), channel_id=1, source_target_pairs={{0,24},{4,28},{8,16},{12,20},{16,8},{20,12},{24,0},{28,4},{1,25},{... | collective-permute-start | bytes 1179656 | tf_op jit(solution)/shard_map/ppermute | solution.py:505
  407.8 64.0 %collective-permute-start.40 = (bf16[2,512,512]{2,1,0:T(8,128)(2,1)}, bf16[2,512,512]{2,1,0:T(8,128)(2,1)}, u32[]{:S(2)}, u32[]{:S(2)}) collective-permute-start(bf16[2,512,512]{2,1,0:T(8,128)(2,1)} %proj_part.12), channel_id=1, source_target_pairs={{0,4},{4,0},{8,12},{12,8},{16,20},{20,16},{24,28},{28,24},{1,5},{5... | collective-permute-start | bytes 3145736 | tf_op jit(solution)/shard_map/ppermute | solution.py:505
  412.9 58.9 %collective-permute-start.39 = (bf16[2,512,512]{2,1,0:T(8,128)(2,1)}, bf16[2,512,512]{2,1,0:T(8,128)(2,1)}, u32[]{:S(2)}, u32[]{:S(2)}) collective-permute-start(bf16[2,512,512]{2,1,0:T(8,128)(2,1)} %add_convert_fusion.1), channel_id=1, source_target_pairs={{8,16},{12,20},{16,8},{20,12},{9,17},{13,21},{17,9},{21,13},{10,18... | collective-permute-start | bytes 3145736 | tf_op jit(solution)/shard_map/ppermute | solution.py:505
  417.7 38.8 %collective-permute-start.46 = (bf16[3,4,2,64,128]{4,3,2,1,0:T(8,128)(2,1)}, bf16[3,4,2,64,128]{4,3,2,1,0:T(8,128)(2,1)S(1)}, u32[]{:S(2)}, u32[]{:S(2)}) collective-permute-start(bf16[3,4,2,64,128]{4,3,2,1,0:T(8,128)(2,1)} %get-tuple-element.187), channel_id=1, source_target_pairs={{0,28},{4,24},{8,20},{12,16},{16,12},{20,8},{24,4},{28,0},{1,29},{... | collective-permute-start | bytes 1179656 | tf_op jit(solution)/shard_map/ppermute | solution.py:505
  424.4 47.3 %collective-permute-start.42 = (bf16[512,512]{1,0:T(8,128)(2,1)}, bf16[512,512]{1,0:T(8,128)(2,1)}, u32[]{:S(2)}, u32[]{:S(2)}) collective-permute-start(bf16[512,512]{1,0:T(8,128)(2,1)} %bitcast.54), channel_id=1, source_target_pairs={{0,8},{4,12},{24,16},{28,20},{1,9},{5,13},{25,17},{29,21},{2,10},{... | collective-permute-start | bytes 1572872 | tf_op jit(solution)/shard_map/ppermute | solution.py:505
  434.2 92.4 %collective-permute-start.32 = (bf16[1024,1024]{1,0:T(8,128)(2,1)}, bf16[1024,1024]{1,0:T(8,128)(2,1)S(1)}, u32[]{:S(2)}, u32[]{:S(2)}) collective-permute-start(bf16[1024,1024]{1,0:T(8,128)(2,1)} %layer_part.4), channel_id=1, source_target_pairs={{0,2},{1,3},{2,0},{3,1},{4,6},{5,7},{6,4},{7,5},{8,10},{9,11},{10,... | collective-permute-start | bytes 6291464 | tf_op jit(solution)/shard_map/ppermute | solution.py:530
  456.5 15.3 %collective-permute-start.44 = (bf16[3,4,2,64,128]{4,3,2,1,0:T(8,128)(2,1)}, bf16[3,4,2,64,128]{4,3,2,1,0:T(8,128)(2,1)}, u32[]{:S(2)}, u32[]{:S(2)}) collective-permute-start(bf16[3,4,2,64,128]{4,3,2,1,0:T(8,128)(2,1)} %get-tuple-element.183), channel_id=1, source_target_pairs={{0,20},{4,16},{8,28},{12,24},{16,4},{20,0},{24,12},{28,8},{1,21},{... | collective-permute-start | bytes 1179656 | tf_op jit(solution)/shard_map/ppermute | solution.py:505
  471.8 17.4 %collective-permute-start.47 = (bf16[3,4,2,64,128]{4,3,2,1,0:T(8,128)(2,1)}, bf16[3,4,2,64,128]{4,3,2,1,0:T(8,128)(2,1)S(1)}, u32[]{:S(2)}, u32[]{:S(2)}) collective-permute-start(bf16[3,4,2,64,128]{4,3,2,1,0:T(8,128)(2,1)} %get-tuple-element.188), channel_id=1, source_target_pairs={{0,12},{4,8},{8,4},{12,0},{16,28},{20,24},{24,20},{28,16},{1,13},{... | collective-permute-start | bytes 1179656 | tf_op jit(solution)/shard_map/ppermute | solution.py:505
  476.8 45.4 %collective-permute-start.50 = (bf16[512,512]{1,0:T(8,128)(2,1)}, bf16[512,512]{1,0:T(8,128)(2,1)}, u32[]{:S(2)}, u32[]{:S(2)}) collective-permute-start(bf16[512,512]{1,0:T(8,128)(2,1)} %fusion), channel_id=1, source_target_pairs={{8,0},{12,4},{16,24},{20,28},{9,1},{13,5},{17,25},{21,29},{10,2},{... | collective-permute-start | bytes 1572872 | tf_op jit(solution)/shard_map/ppermute | solution.py:505
  485.0 38.9 %collective-permute-start.48 = (bf16[512,512]{1,0:T(8,128)(2,1)}, bf16[512,512]{1,0:T(8,128)(2,1)}, u32[]{:S(2)}, u32[]{:S(2)}) collective-permute-start(bf16[512,512]{1,0:T(8,128)(2,1)} %bitcast.53), channel_id=1, source_target_pairs={{0,8},{4,12},{24,16},{28,20},{1,9},{5,13},{25,17},{29,21},{2,10},{... | collective-permute-start | bytes 1572872 | tf_op jit(solution)/shard_map/ppermute | solution.py:505
  486.3 22.6 %collective-permute-start.45 = (bf16[3,4,2,64,128]{4,3,2,1,0:T(8,128)(2,1)}, bf16[3,4,2,64,128]{4,3,2,1,0:T(8,128)(2,1)S(1)}, u32[]{:S(2)}, u32[]{:S(2)}) collective-permute-start(bf16[3,4,2,64,128]{4,3,2,1,0:T(8,128)(2,1)} %get-tuple-element.184), channel_id=1, source_target_pairs={{0,4},{4,0},{8,12},{12,8},{16,20},{20,16},{24,28},{28,24},{1,5},{5... | collective-permute-start | bytes 1179656 | tf_op jit(solution)/shard_map/ppermute | solution.py:505
  489.2 34.7 %collective-permute-start.49 = (bf16[512,512]{1,0:T(8,128)(2,1)}, bf16[512,512]{1,0:T(8,128)(2,1)}, u32[]{:S(2)}, u32[]{:S(2)}) collective-permute-start(bf16[512,512]{1,0:T(8,128)(2,1)} %fusion.3), channel_id=1, source_target_pairs={{8,0},{12,4},{16,24},{20,28},{9,1},{13,5},{17,25},{21,29},{10,2},{... | collective-permute-start | bytes 1572872 | tf_op jit(solution)/shard_map/ppermute | solution.py:505
  (37 other events, 837.1 us)

commit v3 on v2

--- a/solution.py
+++ b/solution.py
@@ -28,121 +28,97 @@
     return lifted * (1.0 / jnp.sum(lifted, axis=-1, keepdims=True))
 
 
-def split_kernel(n, rows, me, q_ref, k_ref, v_ref, *rest):
-    chunks, row_refs, wide = rest[:n], rest[n : n + 3], rest[n + 3]
-    step, row = pl.program_id(0), pl.program_id(1)
-    width, heads, _ = q_ref.shape
+def split_kernel(q_ref, k_ref, v_ref, chunk_ref, *rest):
+    row_refs, wide = rest[:3], rest[3]
+    n, width = chunk_ref.shape[0], chunk_ref.shape[3]
+    span, heads, dim = q_ref.shape
     for array, ref in enumerate((q_ref, k_ref, v_ref)):
-        wide[array] = ref[...].astype(F32).reshape(width * heads, ref.shape[2])
+        wide[...] = ref[...].astype(F32).reshape(span * heads, dim)
+        for head in range(heads // 2):
+            row_refs[array][head] = wide[pl.ds(2 * head, span, stride=heads), :].astype(BF16)
+            for d in range(n):
+                odd = wide[pl.ds(d * width * heads + 2 * head + 1, width, stride=heads), :]
+                chunk_ref[d, array, head] = odd.astype(BF16)
+
+
+def split_inputs(queries, keys, values, n):
+    tokens, heads, dim = queries.shape
+    rows, width, half = tokens // C, C // n, heads // 2
+    by_head = jax.ShapeDtypeStruct((half, tokens, dim), BF16)
+    out = pl.pallas_call(
+        split_kernel,
+        grid=(rows,),
+        in_specs=[pl.BlockSpec((C, heads, dim), lambda r: (r, 0, 0))] * 3,
+        out_specs=[pl.BlockSpec((n, 3, half, pl.squeezed, width, dim), lambda r: (0, 0, 0, r, 0, 0))]
+        + [pl.BlockSpec((half, C, dim), lambda r: (0, r, 0))] * 3,
+        scratch_shapes=[pltpu.VMEM((C * heads, dim), F32)],
+        out_shape=[jax.ShapeDtypeStruct((n, 3, half, rows, width, dim), BF16)] + [by_head] * 3,
+        compiler_params=params(60),
+        name="split_inputs",
+    )(queries, keys, values)
+    return out[0], out[1:]
+
+
+def join_kernel(chunk_ref, *refs):
+    row_refs, outs, wide = refs[:3], refs[3:6], refs[6]
+    n, width = chunk_ref.shape[0], chunk_ref.shape[3]
+    span, heads, dim = outs[0].shape
     for array in range(3):
         for head in range(heads // 2):
-            even = wide[array, pl.ds(2 * head, width, stride=heads), :]
-            row_refs[array][head] = even.astype(BF16)
-    for d in range(n):
-
-        @pl.when(step == d)
-        def _():
-            for array in range(3):
-                for head in range(heads // 2):
-                    odd = wide[array, pl.ds(2 * head + 1, width, stride=heads), :]
-                    chunks[d][array, head, row] = odd.astype(BF16)
-
-
-def split_inputs(me, queries, keys, values, n):
-    tokens, heads, dim = queries.shape
-    rows, width, half = tokens // C, C // n, heads // 2
-    block = pl.BlockSpec((width, heads, dim), lambda d, r, me: (r * n + (me[0] ^ d), 0, 0))
-    chunk = jax.ShapeDtypeStruct((3, half, rows, width, dim), BF16)
-    by_head = jax.ShapeDtypeStruct((half, tokens, dim), BF16)
-    out = pl.pallas_call(
-        functools.partial(split_kernel, n, rows),
-        grid_spec=pltpu.PrefetchScalarGridSpec(
-            num_scalar_prefetch=1,
-            grid=(n, rows),
-            in_specs=[block] * 3,
-            out_specs=[pl.BlockSpec(chunk.shape, lambda d, r, me: (0, 0, 0, 0, 0))] * n
-            + [pl.BlockSpec((half, width, dim), lambda d, r, me: (0, r * n + (me[0] ^ d), 0))] * 3,
-            scratch_shapes=[pltpu.VMEM((3, width * heads, dim), F32)],
-        ),
-        out_shape=[chunk] * n + [by_head] * 3,
-        compiler_params=params(60),
-        name="split_inputs",
-    )(me, queries, keys, values)
-    return out[:n], out[n:]
-
-
-def join_kernel(n, rows, me, *refs):
-    chunks, row_refs, outs, wide = refs[:n], refs[n : n + 3], refs[n + 3 : n + 6], refs[n + 6]
-    step, row = pl.program_id(0), pl.program_id(1)
-    width, heads, dim = outs[0].shape
-    for d in range(n):
-
-        @pl.when(step == d)
-        def _():
-            for array in range(3):
-                for head in range(heads // 2):
-                    wide[array, pl.ds(2 * head + 1, width, stride=heads), :] = chunks[d][array, head, row].astype(F32)
-
-    for array in range(3):
-        for head in range(heads // 2):
-            wide[array, pl.ds(2 * head, width, stride=heads), :] = row_refs[array][head].astype(F32)
-        outs[array][...] = wide[array].reshape(width, heads, dim).astype(BF16)
-
-
-def join_gradients(me, chunks, by_head, n):
-    _, half, rows, width, dim = chunks[0].shape
+            wide[pl.ds(2 * head, span, stride=heads), :] = row_refs[array][head].astype(F32)
+            for d in range(n):
+                part = chunk_ref[d, array, head].astype(F32)
+                wide[pl.ds(d * width * heads + 2 * head + 1, width, stride=heads), :] = part
+        outs[array][...] = wide[...].reshape(span, heads, dim).astype(BF16)
+
+
+def join_gradients(chunks, by_head):
+    n, _, half, rows, width, dim = chunks.shape
     tokens, heads = by_head[0].shape[1], 2 * half
-    whole = jax.ShapeDtypeStruct((tokens, heads, dim), BF16)
-    return pl.pallas_call(
-        functools.partial(join_kernel, n, rows),
-        grid_spec=pltpu.PrefetchScalarGridSpec(
-            num_scalar_prefetch=1,
-            grid=(n, rows),
-            in_specs=[pl.BlockSpec(chunks[0].shape, lambda d, r, me: (0, 0, 0, 0, 0))] * n
-            + [pl.BlockSpec((half, width, dim), lambda d, r, me: (0, r * n + (me[0] ^ d), 0))] * 3,
-            out_specs=[pl.BlockSpec((width, heads, dim), lambda d, r, me: (r * n + (me[0] ^ d), 0, 0))] * 3,
-            scratch_shapes=[pltpu.VMEM((3, width * heads, dim), F32)],
-        ),
-        out_shape=[whole] * 3,
+    return pl.pallas_call(
+        join_kernel,
+        grid=(rows,),
+        in_specs=[pl.BlockSpec((n, 3, half, pl.squeezed, width, dim), lambda r: (0, 0, 0, r, 0, 0))]
+        + [pl.BlockSpec((half, C, dim), lambda r: (0, r, 0))] * 3,
+        out_specs=[pl.BlockSpec((C, heads, dim), lambda r: (r, 0, 0))] * 3,
+        scratch_shapes=[pltpu.VMEM((C * heads, dim), F32)],
+        out_shape=[jax.ShapeDtypeStruct((tokens, heads, dim), BF16)] * 3,
         compiler_params=params(60),
         name="join_gradients",
-    )(me, *chunks, *by_head)
-
-
-def collect_kernel(n, me, row_ref, *refs):
-    chunks, flat_ref, both_ref = refs[:n], refs[n], refs[n + 1]
-    half, rows, width, dim = chunks[0].shape
+    )(chunks, *by_head)
+
+
+def collect_kernel(row_ref, chunk_ref, flat_ref, both_ref):
+    n, half, rows, width, dim = chunk_ref.shape
     for head in range(half):
         both_ref[:, 2 * head * dim : (2 * head + 1) * dim] = row_ref[:, head * dim : (head + 1) * dim]
-    for d in range(n):
-        column = pl.multiple_of((me[0] ^ d) * width, width)
-        for row in range(rows):
-            for head in range(half):
-                part = chunks[d][head, row]
-                flat_ref[pl.ds(row * C + column, width), head * dim : (head + 1) * dim] = part
-                both_ref[pl.ds(row * C + column, width), (2 * head + 1) * dim : (2 * head + 2) * dim] = part
-
-
-def collect(me, row_out, chunks, n):
-    half, rows, width, dim = chunks[0].shape
-    return pl.pallas_call(
-        functools.partial(collect_kernel, n),
-        in_specs=[pl.BlockSpec(memory_space=pltpu.SMEM)] + [VMEM] * (n + 1),
+        for d in range(n):
+            for row in range(rows):
+                part = chunk_ref[d, head, row]
+                at = row * C + d * width
+                flat_ref[at : at + width, head * dim : (head + 1) * dim] = part
+                both_ref[at : at + width, (2 * head + 1) * dim : (2 * head + 2) * dim] = part
+
+
+def collect(row_out, chunks):
+    n, half, rows, width, dim = chunks.shape
+    return pl.pallas_call(
+        collect_kernel,
+        in_specs=[VMEM] * 2,
         out_specs=[VMEM] * 2,
         out_shape=[
             jax.ShapeDtypeStruct((rows * C, half * dim), BF16),
             jax.ShapeDtypeStruct((rows * C, 2 * half * dim), BF16),
         ],
-        compiler_params=params(60),
+        compiler_params=params(24),
         name="collect",
-    )(me, row_out, *chunks)
-
-
-def attn_grad_kernel(n, dim, me, ids, grad_ref, *refs):
-    blocks, row_ref, chunks = refs[:n], refs[n], refs[n + 1 : 2 * n + 1]
-    weight, total, sem = refs[2 * n + 1 :]
+    )(row_out, chunks)
+
+
+def attn_grad_kernel(n, dim, ids, grad_ref, *refs):
+    blocks, (row_ref, chunk_ref, weight, total, sem) = refs[:n], refs[n:]
     step = pl.program_id(0)
-    half, rows, width, _ = chunks[0].shape
+    _, half, rows, width, _ = chunk_ref.shape
     tokens = grad_ref.shape[0]
     tile = tokens // 4
 
@@ -164,31 +140,33 @@
         for head in range(half):
             row_ref[:, head * dim : (head + 1) * dim] = total[:, 2 * head * dim : (2 * head + 1) * dim].astype(BF16)
             for d in range(n):
-                column = pl.multiple_of((me[0] ^ d) * width, width)
                 for row in range(rows):
-                    part = total[pl.ds(row * C + column, width), (2 * head + 1) * dim : (2 * head + 2) * dim]
-                    chunks[d][head, row] = part.astype(BF16)
-
-
-def attn_grad(me, ids, out_grad, blocks, dim):
+                    at = row * C + d * width
+                    part = total[at : at + width, (2 * head + 1) * dim : (2 * head + 2) * dim]
+                    chunk_ref[d, head, row] = part.astype(BF16)
+
+
+def attn_grad(ids, out_grad, blocks, dim):
     n, (span, depth) = len(blocks), blocks[0].shape
     tokens, half = out_grad.shape[0], span // dim // 2
-    chunk = jax.ShapeDtypeStruct((half, tokens // C, C // n, dim), BF16)
-    out = pl.pallas_call(
+    chunk = jax.ShapeDtypeStruct((n, half, tokens // C, C // n, dim), BF16)
+    return pl.pallas_call(
         functools.partial(attn_grad_kernel, n, dim),
         grid_spec=pltpu.PrefetchScalarGridSpec(
-            num_scalar_prefetch=2,
+            num_scalar_prefetch=1,
             grid=(n,),
-            in_specs=[pl.BlockSpec((tokens, depth), lambda b, me, ids: (0, b))] + [pl.BlockSpec(memory_space=pl.ANY)] * n,
-            out_specs=[pl.BlockSpec((tokens, half * dim), lambda b, me, ids: (0, 0))]
-            + [pl.BlockSpec(chunk.shape, lambda b, me, ids: (0, 0, 0, 0))] * n,
+            in_specs=[pl.BlockSpec((tokens, depth), lambda b, ids: (0, b))] + [pl.BlockSpec(memory_space=pl.ANY)] * n,
+            out_specs=[
+                pl.BlockSpec((tokens, half * dim), lambda b, ids: (0, 0)),
+                pl.BlockSpec(chunk.shape, lambda b, ids: (0, 0, 0, 0, 0)),
+            ],
             scratch_shapes=[
                 pltpu.VMEM((n, span, depth), BF16),
                 pltpu.VMEM((tokens, span), F32),
                 pltpu.SemaphoreType.DMA((n,)),
             ],
         ),
-        out_shape=[jax.ShapeDtypeStruct((tokens, half * dim), BF16)] + [chunk] * n,
+        out_shape=[jax.ShapeDtypeStruct((tokens, half * dim), BF16), chunk],
         compiler_params=params(60),
         cost_estimate=pl.CostEstimate(
             flops=2 * tokens * span * depth * n,
@@ -196,8 +174,7 @@
             transcendentals=0,
         ),
         name="attn_grad",
-    )(me, ids, out_grad, *blocks)
-    return out[0], out[1:]
+    )(ids, out_grad, *blocks)
 
 
 def layer_kernel(n, count, adds, ids, wanted, flat_ref, *refs):
@@ -380,108 +357,101 @@
     )(q, k, v, grad)
 
 
-def column_mask(me, n, rows):
-    size = n * rows * LANE
-
+def column_mask(size):
     def parts(axis):
         place = lax.broadcasted_iota(jnp.int32, (size, size), axis)
-        line, column = place // LANE, place % LANE
-        return ((line // rows) ^ me) * rows + line % rows, column
+        return place // LANE, place % LANE
 
     row_q, column_q = parts(0)
     row_k, column_k = parts(1)
     return (column_q == column_k) & (row_q >= row_k)
 
 
-def gathered(chunks, index, at):
-    rows, dim = chunks[0].shape[-3], chunks[0].shape[-1]
-    return jnp.concatenate(
-        [chunk[(*index, row, pl.ds(at, LANE), slice(None))] for chunk in chunks for row in range(rows)], axis=0
-    )
-
-
-def scattered(chunks, index, at, value):
-    rows = chunks[0].shape[-3]
-    for d, chunk in enumerate(chunks):
+def gathered(ref, index, at):
+    n, rows = ref.shape[0], ref.shape[-3]
+    return jnp.concatenate([ref[(d, *index, row, pl.ds(at, LANE))] for d in range(n) for row in range(rows)], axis=0)
+
+
+def scattered(ref, index, at, value):
+    n, rows = ref.shape[0], ref.shape[-3]
+    for d in range(n):
         for row in range(rows):
             line = d * rows + row
-            chunk[(*index, row, pl.ds(at, LANE), slice(None))] = value[line * LANE : (line + 1) * LANE]
+            ref[(d, *index, row, pl.ds(at, LANE))] = value[line * LANE : (line + 1) * LANE]
 
 
 def column_probs(bias, q, k, scale):
     return softmax(dot(q, k, ((1,), (1,))) * scale + bias[...])
 
 
-def column_forward_kernel(n, scale, me, *refs):
-    chunks, outs, bias = refs[:n], refs[n : 2 * n], refs[2 * n]
-    _, half, rows, width, _ = chunks[0].shape
-    bias[...] = jnp.where(column_mask(me[0], n, rows), 0.0, -jnp.inf)
+def column_forward_kernel(scale, chunk_ref, out_ref, bias):
+    half, width = chunk_ref.shape[2], chunk_ref.shape[4]
+    bias[...] = jnp.where(column_mask(bias.shape[0]), 0.0, -jnp.inf)
     blocks = width // LANE
 
     @pl.loop(0, half * blocks)
     def _(step):
         head, at = step // blocks, pl.multiple_of(step % blocks * LANE, LANE)
-        q, k, v = (gathered(chunks, (array, head), at) for array in range(3))
+        q, k, v = (gathered(chunk_ref, (array, head), at) for array in range(3))
         probs = column_probs(bias, q, k, scale)
-        scattered(outs, (head,), at, dot(probs.astype(BF16), v, ((1,), (0,))).astype(BF16))
-
-
-def column_forward(me, chunks, n):
-    _, half, rows, width, dim = chunks[0].shape
+        scattered(out_ref, (head,), at, dot(probs.astype(BF16), v, ((1,), (0,))).astype(BF16))
+
+
+def column_forward(chunks):
+    n, _, half, rows, width, dim = chunks.shape
     size = n * rows * LANE
     return pl.pallas_call(
-        functools.partial(column_forward_kernel, n, dim**-0.5),
-        in_specs=[pl.BlockSpec(memory_space=pltpu.SMEM)] + [VMEM] * n,
-        out_specs=[VMEM] * n,
-        out_shape=[jax.ShapeDtypeStruct((half, rows, width, dim), BF16)] * n,
+        functools.partial(column_forward_kernel, dim**-0.5),
+        in_specs=[VMEM],
+        out_specs=VMEM,
+        out_shape=jax.ShapeDtypeStruct((n, half, rows, width, dim), BF16),
         scratch_shapes=[pltpu.VMEM((size, size), F32)],
-        compiler_params=params(60),
+        compiler_params=params(24),
         cost_estimate=pl.CostEstimate(
             flops=4 * size * size * dim * half * width // LANE,
             bytes_accessed=8 * n * half * rows * width * dim,
             transcendentals=size * size * half * width // LANE,
         ),
         name="column_forward",
-    )(me, *chunks)
-
-
-def column_backward_kernel(n, scale, me, *refs):
-    chunks, grads, outs, bias = refs[:n], refs[n : 2 * n], refs[2 * n : 3 * n], refs[3 * n]
-    _, half, rows, width, _ = chunks[0].shape
-    bias[...] = jnp.where(column_mask(me[0], n, rows), 0.0, -jnp.inf)
+    )(chunks)
+
+
+def column_backward_kernel(scale, chunk_ref, grad_ref, out_ref, bias):
+    half, width = chunk_ref.shape[2], chunk_ref.shape[4]
+    bias[...] = jnp.where(column_mask(bias.shape[0]), 0.0, -jnp.inf)
     blocks = width // LANE
 
     @pl.loop(0, half * blocks)
     def _(step):
         head, at = step // blocks, pl.multiple_of(step % blocks * LANE, LANE)
-        q, k, v = (gathered(chunks, (array, head), at) for array in range(3))
-        grad = gathered(grads, (head,), at)
+        q, k, v = (gathered(chunk_ref, (array, head), at) for array in range(3))
+        grad = gathered(grad_ref, (head,), at)
         probs = column_probs(bias, q, k, scale)
         prob_grad = dot(grad, v, ((1,), (1,)))
         inner = jnp.sum(probs * prob_grad, axis=-1, keepdims=True)
         score_low = (probs * (prob_grad - inner)).astype(BF16)
-        scattered(outs, (0, head), at, (dot(score_low, k, ((1,), (0,))) * scale).astype(BF16))
-        scattered(outs, (1, head), at, (dot(score_low, q, ((0,), (0,))) * scale).astype(BF16))
-        scattered(outs, (2, head), at, dot(probs.astype(BF16), grad, ((0,), (0,))).astype(BF16))
-
-
-def column_backward(me, chunks, grads, n):
-    _, half, rows, width, dim = chunks[0].shape
+        scattered(out_ref, (0, head), at, (dot(score_low, k, ((1,), (0,))) * scale).astype(BF16))
+        scattered(out_ref, (1, head), at, (dot(score_low, q, ((0,), (0,))) * scale).astype(BF16))
+        scattered(out_ref, (2, head), at, dot(probs.astype(BF16), grad, ((0,), (0,))).astype(BF16))
+
+
+def column_backward(chunks, grads):
+    n, _, half, rows, width, dim = chunks.shape
     size = n * rows * LANE
     return pl.pallas_call(
-        functools.partial(column_backward_kernel, n, dim**-0.5),
-        in_specs=[pl.BlockSpec(memory_space=pltpu.SMEM)] + [VMEM] * (2 * n),
-        out_specs=[VMEM] * n,
-        out_shape=[jax.ShapeDtypeStruct(chunks[0].shape, BF16)] * n,
+        functools.partial(column_backward_kernel, dim**-0.5),
+        in_specs=[VMEM] * 2,
+        out_specs=VMEM,
+        out_shape=jax.ShapeDtypeStruct(chunks.shape, BF16),
         scratch_shapes=[pltpu.VMEM((size, size), F32)],
-        compiler_params=params(60),
+        compiler_params=params(24),
         cost_estimate=pl.CostEstimate(
             flops=10 * size * size * dim * half * width // LANE,
             bytes_accessed=14 * n * half * rows * width * dim,
             transcendentals=size * size * half * width // LANE,
         ),
         name="column_backward",
-    )(me, *chunks, *grads)
+    )(chunks, grads)
 
 
 PAIRS = [(0, 1), (1, 0), (2, 3), (3, 2)]
@@ -512,11 +482,9 @@
     def flip(self, value, d):
         return self.send(value, [(place, place ^ d) for place in range(self.n)])
 
-    def swap(self, chunks, order):
-        out = list(chunks)
-        for d in order:
-            out[d] = self.flip(chunks[d], d)
-        return out
+
+def swap(chunks):
+    return lax.all_to_all(chunks, "ctx", split_axis=0, concat_axis=0, tiled=True)
 
 
 def scatter_layer(ids, flat, blocks, heads_n):
@@ -538,15 +506,11 @@
 def on_device(queries, keys, values, out_grad, wo, *, n, heads_n):
     tokens, heads, dim = queries.shape
     half, depth, inner = heads // 2, wo.shape[1], n // 4
-    me = lax.axis_index("ctx").astype(jnp.int32).reshape(1)
-    line, spot = me[0] // inner, me[0] % inner
+    me = lax.axis_index("ctx").astype(jnp.int32)
+    line, spot = me // inner, me % inner
     middle, upper = (line == 1) | (line == 2), line < 2
-    far = [jnp.where(upper, 2, 1), jnp.where(upper, 3, 0)]
+    far, close = [jnp.where(upper, 2, 1), jnp.where(upper, 3, 0)], [line ^ 1, line]
     links = Links(n, 5)
-    wide = [d for d in range(n) if d >= 2 * inner]
-    close = [d for d in range(1, n) if d < 2 * inner]
-    order = [d for d in wide if d % inner == 0] + [d for d in close if d % inner == 0]
-    order += [d for d in wide if d % inner] + [d for d in close if d % inner]
 
     def around(block):
         return [block if e == 0 else links.flip(block, e) for e in range(inner)]
@@ -554,24 +518,14 @@
     near = links.along(wo, PAIRS)
     cross_own = links.along(wo, CROSS)
     own_blocks = around(wo)
-    chunks, by_head = split_inputs(me, queries, keys, values, n)
-    sent = list(chunks)
-
-    def deal(*which):
-        for d in which:
-            sent[d] = links.flip(chunks[d], d)
-
-    deal(order[0])
-    near_blocks = around(after(near, chunks[0]))
-    deal(*order[1 : n // 4])
+    chunks, by_head = split_inputs(queries, keys, values, n)
+    chunks, near = swap(chunks), after(near, chunks)
+    near_blocks = around(near)
     cross_near = links.along(near, CROSS)
     far_own = jnp.where(middle, cross_own, links.along(cross_own, OUTWARD))
-    deal(*order[n // 4 : n // 2])
     far_own_blocks = around(far_own)
     far_near = jnp.where(middle, cross_near, links.along(cross_near, OUTWARD))
-    deal(*order[n // 2 :])
     far_near_blocks = around(far_near)
-    chunks = sent
     blocks = own_blocks + near_blocks + far_own_blocks + far_near_blocks
     ids = [owner * inner + (spot ^ e) for owner in (line, line ^ 1, *far) for e in range(inner)]
     ids = jnp.stack(ids).astype(jnp.int32)
@@ -590,44 +544,36 @@
     def add(*terms):
         return sum(term.astype(F32) for term in terms).astype(BF16)
 
-    close = [line ^ 1, line]
     row_out = row_forward(*(after(tensor, near) for tensor in by_head))
     row_far = exchanged(row_out, far)
-    outs = column_forward(me, chunks, n)
-    column_part = links.swap(outs, order)
-    grad_row, grads = attn_grad(me, ids, after(out_grad, outs[0]), blocks, dim)
-    grads = links.swap(grads, order)
-    column_out, flat = collect(me, row_out, column_part, n)
+    row_close = exchanged(row_out, close)
+
+    outs = column_forward(chunks)
+    column_part = swap(outs)
+    grad_row, grads = attn_grad(ids, after(out_grad, outs), blocks, dim)
+    grads = swap(after(grads, column_part))
+    column_out, flat = collect(row_out, column_part)
     column_far = exchanged(column_out, far)
-    (row_far,) = summed(row_out, far, row_far, 0)
+    column_close = exchanged(column_out, close)
+    gradients = column_backward(chunks, grads)
+    column_grads = swap(gradients)
+
+    (row_far,) = summed(after(row_out, column_out), far, row_far, 0)
     row_far_in = links.along(row_far, INWARD)
-    gradients = column_backward(me, chunks, grads, n)
-    column_grads = list(gradients)
-
-    def give_back(*which):
-        for d in which:
-            column_grads[d] = links.flip(gradients[d], d)
-
-    give_back(*order[: n // 4])
-    (column_far,) = summed(column_out, far, column_far, 0)
+    row_near, row_own = summed(after(row_out, column_out), close, row_close, 1)
+    row_near_in = links.along(row_near[0], INWARD)
+    (column_far,) = summed(after(column_out, gradients), far, column_far, 0)
     column_far_in = links.along(column_far, INWARD)
-    column_close = exchanged(column_out, close)
     row_cross = links.along(add(row_far, row_far_in), CROSS)
-    give_back(*order[n // 4 : n // 4 + 1])
+    column_near, column_own = summed(after(column_out, gradients), close, column_close, 1)
+    column_near_in = links.along(column_near[0], INWARD)
     column_cross = links.along(add(column_far, column_far_in), CROSS)
-    row_close = exchanged(row_out, close)
-    column_near, column_own = summed(column_out, close, column_close, 1)
-    column_near_in = links.along(column_near[0], INWARD)
-    give_back(*order[n // 4 + 1 : n // 2 + 1])
+    row_back = links.along(add(row_near[0], row_cross[1]), OUTWARD)
     column_back = links.along(add(column_near[0], column_cross[1]), OUTWARD)
-    row_near, row_own = summed(row_out, close, row_close, 1)
-    row_near_in = links.along(row_near[0], INWARD)
-    row_back = links.along(add(row_near[0], row_cross[1]), OUTWARD)
-    give_back(*order[n // 2 + 1 :])
-
-    layer_out = scatter_layer(ids, after(flat, gradients[0]), blocks, heads_n)
-    row_grads = row_backward(*by_head, after(grad_row, gradients[0]))
-    gradients = join_gradients(me, column_grads, row_grads, n)
+
+    layer_out = scatter_layer(ids, after(flat, gradients), blocks, heads_n)
+    row_grads = row_backward(*by_head, after(grad_row, gradients))
+    gradients = join_gradients(column_grads, row_grads)
 
     proj_row = add(row_own[0], row_near_in, row_cross[0], row_back)
     proj_column = add(column_own[0], column_near_in, column_cross[0], column_back)

time: 539 us -> 516 us (0.957)
  starting transfers between devices: 88.9 us -> 67.5 us
  Pallas kernels: 170 us -> 153 us
  waiting for transfers between devices: 254 us -> 263 us
    ppermute x49 -> x21, starting transfers between devices: 87.3 us -> 43 us  [send(): out = lax.ppermute(value, 'ctx', pairs)]
    all_to_all x0 -> x4, starting transfers between devices: none -> 22.8 us  [swap(): lax.all_to_all(chunks, 'ctx', split_axis=0, concat_axis=0, tiled=True)]
    pallas_call x5, Pallas kernels: 56.5 us -> 39.5 us  [the longest x1 14.6 us: column_backward(): pl.pallas_call(functools.partial(column_backward_kernel, dim ** (-0.5)),...]
    all_to_all x0 -> x4, waiting for transfers between devices: none -> 6.3 us  [swap(): lax.all_to_all(chunks, 'ctx', split_axis=0, concat_axis=0, tiled=True)]
    ppermute x49 -> x21, waiting for transfers between devices: 254 us -> 257 us  [send(): out = lax.ppermute(value, 'ctx', pairs)]
  transfers between devices with their start and end apart: 51 -> 27, of which waited for: 18 -> 14; matrix products, arithmetic and copies ran while one was open for 3% -> 5% of each run, Pallas kernels for 25% -> 22%
where the time goes in v3:
time: 516 us; the launch traced here: 515 us
  waiting for transfers between devices  263 us (51%)
  Pallas kernels  153 us (30%)
  starting transfers between devices  67.5 us (13%)
  other arithmetic  22.1 us (4%)
  local copies, waits for them, and re-layouts  7.87 us (2%)
    ppermute x21, waiting for transfers between devices, send(): out = lax.ppermute(value, 'ctx', pairs)  257 us
    ppermute x21, starting transfers between devices, send(): out = lax.ppermute(value, 'ctx', pairs)  43 us
    pallas_call x8, Pallas kernels, proj_part(): pl.pallas_call(functools.partial(proj_kernel, lead, len(extra), dim), gri...  40 us
    pallas_call x3, Pallas kernels, layer_part(): pl.pallas_call(functools.partial(layer_kernel, n, count, len(extra)), gri...  29.3 us
    all_to_all x4, starting transfers between devices, swap(): lax.all_to_all(chunks, 'ctx', split_axis=0, concat_axis=0, tiled=True)  22.8 us
    pallas_call x1, Pallas kernels, attn_grad(): pl.pallas_call(functools.partial(attn_grad_kernel, n, dim), grid_spec=plt...  21 us
    pallas_call x1, Pallas kernels, column_backward(): pl.pallas_call(functools.partial(column_backward_kernel, dim ** (-0.5)),...  14.6 us
    pallas_call x1, Pallas kernels, row_backward(): pl.pallas_call(functools.partial(row_backward_kernel, dim ** (-0.5)), gri...  13.6 us
  transfers between devices with their start and end apart: 27, of which 14 were waited for; matrix products, arithmetic and copies ran while one was open for 5% of the time, Pallas kernels for 22%

profile of v3, /device:TPU:8, one launch (start us, length us, event | category | flops | bytes accessed | tf_op | source)
XLA Modules:
  0.0 515.0 jit_solution(18142595913730241903)
XLA Ops:
  0.6 7.1 %split_inputs.1 = (bf16[8,3,4,2,64,128]{5,4,3,2,1,0:T(8,128)(2,1)}, bf16[4,1024,128]{2,1,0:T(8,128)(2,1)}, bf16[4,1024,128]{2,1,0:T(8,128)(2,1)}, bf16[4,1024,128]{2,1,0:T(8,128)(2,1)}) custom-call(bf16[1024,8,128]{2,1,0:T(8,128)(2,1)} %q_ref.1, bf16[1024,8,128]{2,1,0:T(8,128)(2,1)} %k_ref.1, bf16[1024,8,128]{2,1,0:T(8,128)(2,1)} %v_ref.1), custom_call_target="tpu_custom_call" | custom-call | tf_op jit(solution)/shard_map/split_inputs/pallas_call | solution.py:48
  7.7 6.3 %all-to-all-start = ((bf16[8,3,4,2,64,128]{5,4,3,2,1,0:T(8,128)(2,1)}), bf16[8,3,4,2,64,128]{5,4,3,2,1,0:T(8,128)(2,1)S(1)}, u32[]{:S(2)}, u32[]{:S(2)}) async-start(bf16[8,3,4,2,64,128]{5,4,3,2,1,0:T(8,128)(2,1)} %get-tuple-element.50), calls=%async_computation | async-start | bytes 6291456 | tf_op jit(solution)/shard_map/all_to_all | solution.py:487
  14.0 4.8 collective-permute-start.3
  20.4 68.5 %collective-permute-done.refs_2_ = bf16[1024,512]{1,0:T(8,128)(2,1)} collective-permute-done((bf16[1024,512]{1,0:T(8,128)(2,1)}, bf16[1024,512]{1,0:T(8,128)(2,1)}, u32[]{:S(2)}, u32[]{:S(2)}) %collective-permute-start) | collective-permute-done | bytes 1048608 | tf_op jit(solution)/shard_map/ppermute | solution.py:475
  88.9 3.6 collective-permute-start.6
  92.5 14.8 %collective-permute-done.3 = bf16[1024,512]{1,0:T(8,128)(2,1)} collective-permute-done((bf16[1024,512]{1,0:T(8,128)(2,1)}, bf16[1024,512]{1,0:T(8,128)(2,1)}, u32[]{:S(2)}, u32[]{:S(2)}) %collective-permute-start.3) | collective-permute-done | bytes 1048608 | tf_op jit(solution)/shard_map/ppermute | solution.py:475
  107.3 2.3 collective-permute-start.4
  109.6 18.8 %collective-permute-done.6 = bf16[1024,512]{1,0:T(8,128)(2,1)} collective-permute-done((bf16[1024,512]{1,0:T(8,128)(2,1)}, bf16[1024,512]{1,0:T(8,128)(2,1)}, u32[]{:S(2)}, u32[]{:S(2)}) %collective-permute-start.6) | collective-permute-done | bytes 1048608 | tf_op jit(solution)/shard_map/ppermute | solution.py:475
  128.4 2.3 collective-permute-start.7
  132.1 2.3 broadcast_select_fusion.1.refs_4_
  135.0 16.8 %collective-permute-done.7 = bf16[1024,512]{1,0:T(8,128)(2,1)} collective-permute-done((bf16[1024,512]{1,0:T(8,128)(2,1)}, bf16[1024,512]{1,0:T(8,128)(2,1)}, u32[]{:S(2)}, u32[]{:S(2)}) %collective-permute-start.7) | collective-permute-done | bytes 1048608 | tf_op jit(solution)/shard_map/ppermute | solution.py:475
  151.7 2.3 broadcast_select_fusion.refs_6_
  154.0 3.0 collective-permute-done.2.refs_3_
  158.5 8.7 %column_forward.1 = bf16[8,4,2,64,128]{4,3,2,1,0:T(8,128)(2,1)S(1)} custom-call(bf16[8,3,4,2,64,128]{5,4,3,2,1,0:T(8,128)(2,1)S(1)} %all-to-all-done.chunk_ref), custom_call_target="tpu_custom_call" | custom-call | flops 536870912 | bytes 4194304 | tf_op jit(solution)/shard_map/column_forward/pallas_call | solution.py:403
  168.1 4.2 all-to-all-start.1
  173.0 11.7 %collective-permute-done.5.refs_5_ = bf16[1024,512]{1,0:T(8,128)(2,1)} collective-permute-done((bf16[1024,512]{1,0:T(8,128)(2,1)}, bf16[1024,512]{1,0:T(8,128)(2,1)}, u32[]{:S(2)}, u32[]{:S(2)}) %collective-permute-start.5) | collective-permute-done | bytes 1048608 | tf_op jit(solution)/shard_map/ppermute | solution.py:475
  184.7 25.0 %collective-permute-done.8.refs_7_ = bf16[1024,512]{1,0:T(8,128)(2,1)} collective-permute-done((bf16[1024,512]{1,0:T(8,128)(2,1)}, bf16[1024,512]{1,0:T(8,128)(2,1)}, u32[]{:S(2)}, u32[]{:S(2)}) %collective-permute-start.8) | collective-permute-done | bytes 1048608 | tf_op jit(solution)/shard_map/ppermute | solution.py:475
  209.7 21.0 %attn_grad.1 = (bf16[1024,512]{1,0:T(8,128)(2,1)}, bf16[8,4,2,64,128]{4,3,2,1,0:T(8,128)(2,1)}) custom-call(s32[8]{0:T(128)} %stack.103.ids, bf16[1024,4096]{1,0:T(8,128)(2,1)} %grad_ref.16, bf16[1024,512]{1,0:T(8,128)(2,1)} %refs_0_.7, bf16[1024,512]{1,0:T(8,128)(2,1)} %collective-permute-done.1.refs_1_, bf16[1024,512]{1,0:T(8,128)(2,1)} %collective-permute-done.refs_2_, ...), custom_call_target="tpu_custom_call" | custom-call | flops 8589934592 | bytes 18874368 | tf_op jit(solution)/shard_map/attn_grad/pallas_call | solution.py:153
  230.7 6.4 %all-to-all-start.2 = ((bf16[8,4,2,64,128]{4,3,2,1,0:T(8,128)(2,1)}), bf16[8,4,2,64,128]{4,3,2,1,0:T(8,128)(2,1)}, u32[]{:S(2)}, u32[]{:S(2)}) async-start(bf16[8,4,2,64,128]{4,3,2,1,0:T(8,128)(2,1)} %get-tuple-element.64), calls=%async_computation.2 | async-start | bytes 2097152 | tf_op jit(solution)/shard_map/all_to_all | solution.py:487
  237.8 9.9 %row_forward.1.row_ref.flat_ref = bf16[1024,512]{1,0:T(8,128)(2,1)} custom-call(bf16[4,1024,128]{2,1,0:T(8,128)(2,1)} %get-tuple-element.52.q_ref, bf16[4,1024,128]{2,1,0:T(8,128)(2,1)} %get-tuple-element.54.k_ref, bf16[4,1024,128]{2,1,0:T(8,128)(2,1)} %get-tuple-element.56.v_ref), custom_call_target="tpu_custom_call" | custom-call | flops 1073741824 | bytes 4194304 | tf_op jit(solution)/shard_map/row_forward/pallas_call | solution.py:311
  253.1 6.3 %all-to-all-done.2.grad_ref = bf16[8,4,2,64,128]{4,3,2,1,0:T(8,128)(2,1)} async-done(((bf16[8,4,2,64,128]{4,3,2,1,0:T(8,128)(2,1)}), bf16[8,4,2,64,128]{4,3,2,1,0:T(8,128)(2,1)}, u32[]{:S(2)}, u32[]{:S(2)}) %all-to-all-start.2) | async-done | bytes 1048608 | tf_op jit(solution)/shard_map/all_to_all | solution.py:487
  259.4 14.6 %column_backward.1 = bf16[8,3,4,2,64,128]{5,4,3,2,1,0:T(8,128)(2,1)} custom-call(bf16[8,3,4,2,64,128]{5,4,3,2,1,0:T(8,128)(2,1)S(1)} %all-to-all-done.chunk_ref, bf16[8,4,2,64,128]{4,3,2,1,0:T(8,128)(2,1)} %all-to-all-done.2.grad_ref), custom_call_target="tpu_custom_call" | custom-call | flops 1342177280 | bytes 7340032 | tf_op jit(solution)/shard_map/column_backward/pallas_call | solution.py:441
  273.9 11.6 %layer_part.3 = bf16[1024,2048]{1,0:T(8,128)(2,1)} custom-call(s32[8]{0:T(128)} %stack.103.ids, s32[4]{0:T(128)} %pad_add_fusion.1.wanted, bf16[1024,1024]{1,0:T(8,128)(2,1)} %copy-done.2, bf16[1024,512]{1,0:T(8,128)(2,1)} %refs_0_.7, bf16[1024,512]{1,0:T(8,128)(2,1)} %collective-permute-done.1.refs_1_, bf16[1024,512]{1,0:T(8,128)(2,1)} %collective-permute-done.refs_2_, ...), custom_call_target="tpu_custom_call" | custom-call | flops 4294967296 | bytes 10485760 | tf_op jit(solution)/shard_map/layer_part/pallas_call | solution.py:211
  285.7 5.9 %all-to-all-start.3 = ((bf16[8,3,4,2,64,128]{5,4,3,2,1,0:T(8,128)(2,1)}), bf16[8,3,4,2,64,128]{5,4,3,2,1,0:T(8,128)(2,1)S(1)}, u32[]{:S(2)}, u32[]{:S(2)}) async-start(bf16[8,3,4,2,64,128]{5,4,3,2,1,0:T(8,128)(2,1)} %column_backward.1), calls=%async_computation.3 | async-start | bytes 6291456 | tf_op jit(solution)/shard_map/all_to_all | solution.py:487
  292.2 4.9 proj_part.10
  299.2 4.8 proj_part.12
  304.6 4.9 proj_part.8
  311.6 37.5 %collective-permute-done.12.refs_0_ = bf16[2,512,512]{2,1,0:T(8,128)(2,1)} collective-permute-done((bf16[2,512,512]{2,1,0:T(8,128)(2,1)}, bf16[2,512,512]{2,1,0:T(8,128)(2,1)}, u32[]{:S(2)}, u32[]{:S(2)}) %collective-permute-start.12) | collective-permute-done | bytes 1048608 | tf_op jit(solution)/shard_map/ppermute | solution.py:475
  349.1 5.0 proj_part.11
  355.4 18.1 %collective-permute-done.15.refs_0_ = bf16[2,512,512]{2,1,0:T(8,128)(2,1)} collective-permute-done((bf16[2,512,512]{2,1,0:T(8,128)(2,1)}, bf16[2,512,512]{2,1,0:T(8,128)(2,1)}, u32[]{:S(2)}, u32[]{:S(2)}) %collective-permute-start.15) | collective-permute-done | bytes 1048608 | tf_op jit(solution)/shard_map/ppermute | solution.py:475
  373.5 5.0 proj_part.15
  378.5 17.0 %collective-permute-done.11.refs_0_ = bf16[2,512,512]{2,1,0:T(8,128)(2,1)} collective-permute-done((bf16[2,512,512]{2,1,0:T(8,128)(2,1)}, bf16[2,512,512]{2,1,0:T(8,128)(2,1)}, u32[]{:S(2)}, u32[]{:S(2)}) %collective-permute-start.11) | collective-permute-done | bytes 1048608 | tf_op jit(solution)/shard_map/ppermute | solution.py:475
  396.8 4.8 proj_part.13
  402.3 2.9 add_convert_fusion.1
  405.2 3.4 collective-permute-start.16
  409.2 13.3 %collective-permute-done.20 = bf16[2,512,512]{2,1,0:T(8,128)(2,1)} collective-permute-done((bf16[2,512,512]{2,1,0:T(8,128)(2,1)}, bf16[2,512,512]{2,1,0:T(8,128)(2,1)}, u32[]{:S(2)}, u32[]{:S(2)}) %collective-permute-start.20) | collective-permute-done | bytes 1048608 | tf_op jit(solution)/shard_map/ppermute | solution.py:475
  422.5 2.6 add_convert_fusion
  426.8 3.9 collective-permute-start.21
  430.7 8.5 %layer_part.4 = bf16[1024,1024]{1,0:T(8,128)(2,1)} custom-call(s32[8]{0:T(128)} %stack.103.ids, s32[2]{0:T(128)} %pad_add_fusion.2.wanted, bf16[1024,1024]{1,0:T(8,128)(2,1)} %copy-done.2, bf16[1024,512]{1,0:T(8,128)(2,1)} %refs_0_.7, bf16[1024,512]{1,0:T(8,128)(2,1)} %collective-permute-done.1.refs_1_, bf16[1024,512]{1,0:T(8,128)(2,1)} %collective-permute-done.refs_2_, ...), custom_call_target="tpu_custom_call" | custom-call | flops 2147483648 | bytes 6291456 | tf_op jit(solution)/shard_map/layer_part/pallas_call | solution.py:211
  441.3 5.3 %proj_part.9 = (bf16[1,512,512]{2,1,0:T(8,128)(2,1)}, bf16[1,512,512]{2,1,0:T(8,128)(2,1)}) custom-call(s32[2]{0:T(128)} %pad_add_fusion.3.order, bf16[1024,512]{1,0:T(8,128)(2,1)} %row_forward.1.row_ref.flat_ref, bf16[1024,4096]{1,0:T(8,128)(2,1)} %grad_ref.16, bf16[2,512,512]{2,1,0:T(8,128)(2,1)} %collective-permute-done.11.refs_0_), custom_call_target="tpu_custom_call" | custom-call | flops 1073741824 | bytes 5242880 | tf_op jit(solution)/shard_map/proj_part/pallas_call | solution.py:265
  450.6 10.7 %collective-permute-done.13 = bf16[512,512]{1,0:T(8,128)(2,1)} collective-permute-done((bf16[512,512]{1,0:T(8,128)(2,1)}, bf16[512,512]{1,0:T(8,128)(2,1)}, u32[]{:S(2)}, u32[]{:S(2)}) %collective-permute-start.13) | collective-permute-done | bytes 524320 | tf_op jit(solution)/shard_map/ppermute | solution.py:475
  461.3 2.3 collective-permute-start.18
  463.6 5.2 %proj_part.14 = (bf16[1,512,512]{2,1,0:T(8,128)(2,1)}, bf16[1,512,512]{2,1,0:T(8,128)(2,1)}) custom-call(s32[2]{0:T(128)} %pad_add_fusion.3.order, bf16[1024,512]{1,0:T(8,128)(2,1)} %copy-done.1, bf16[1024,4096]{1,0:T(8,128)(2,1)} %grad_ref.16, bf16[2,512,512]{2,1,0:T(8,128)(2,1)} %collective-permute-done.17.refs_0_), custom_call_target="tpu_custom_call" | custom-call | flops 1073741824 | bytes 5242880 | tf_op jit(solution)/shard_map/proj_part/pallas_call | solution.py:265
  470.1 2.2 fusion
  472.3 6.3 %collective-permute-start.22 = (bf16[512,512]{1,0:T(8,128)(2,1)}, bf16[512,512]{1,0:T(8,128)(2,1)}, u32[]{:S(2)}, u32[]{:S(2)}) collective-permute-start(bf16[512,512]{1,0:T(8,128)(2,1)} %fusion), channel_id=1, source_target_pairs={{8,0},{12,4},{16,24},{20,28},{9,1},{13,5},{17,25},{21,29},{10,2},{... | collective-permute-start | bytes 1572872 | tf_op jit(solution)/shard_map/ppermute | solution.py:475
  478.5 13.6 %row_backward.1 = (bf16[4,1024,128]{2,1,0:T(8,128)(2,1)}, bf16[4,1024,128]{2,1,0:T(8,128)(2,1)}, bf16[4,1024,128]{2,1,0:T(8,128)(2,1)}) custom-call(bf16[4,1024,128]{2,1,0:T(8,128)(2,1)} %get-tuple-element.52.q_ref, bf16[4,1024,128]{2,1,0:T(8,128)(2,1)} %get-tuple-element.54.k_ref, bf16[4,1024,128]{2,1,0:T(8,128)(2,1)} %get-tuple-element.56.v_ref, ...), custom_call_target="tpu_custom_call" | custom-call | flops 2684354560 | bytes 7340032 | tf_op jit(solution)/shard_map/row_backward/pallas_call | solution.py:345
  498.3 7.3 %join_gradients.1 = (bf16[1024,8,128]{2,1,0:T(8,128)(2,1)}, bf16[1024,8,128]{2,1,0:T(8,128)(2,1)}, bf16[1024,8,128]{2,1,0:T(8,128)(2,1)}) custom-call(bf16[8,3,4,2,64,128]{5,4,3,2,1,0:T(8,128)(2,1)} %copy-done.4, bf16[4,1024,128]{2,1,0:T(8,128)(2,1)} %get-tuple-element.68.refs_0_, bf16[4,1024,128]{2,1,0:T(8,128)(2,1)} %get-tuple-element.69.refs_1_, ...), custom_call_target="tpu_custom_call" | custom-call | tf_op jit(solution)/shard_map/join_gradients/pallas_call | solution.py:78
  505.6 9.2 %layer_part.5 = bf16[1024,1024]{1,0:T(8,128)(2,1)} custom-call(s32[8]{0:T(128)} %stack.103.ids, s32[2]{0:T(128)} %pad_add_fusion.wanted, bf16[1024,1024]{1,0:T(8,128)(2,1)} %copy-done.2, bf16[1024,512]{1,0:T(8,128)(2,1)} %refs_0_.7, bf16[1024,512]{1,0:T(8,128)(2,1)} %collective-permute-done.1.refs_1_, bf16[1024,512]{1,0:T(8,128)(2,1)} %collective-permute-done.refs_2_, ...), custom_call_target="tpu_custom_call" | custom-call | flops 2147483648 | bytes 6291456 | tf_op jit(solution)/shard_map/layer_part/pallas_call | solution.py:211
  (59 shorter events, 37.2 us)
Async XLA Ops:
  7.7 150.8 %all-to-all-start = ((bf16[8,3,4,2,64,128]{5,4,3,2,1,0:T(8,128)(2,1)}), bf16[8,3,4,2,64,128]{5,4,3,2,1,0:T(8,128)(2,1)S(1)}, u32[]{:S(2)}, u32[]{:S(2)}) async-start(bf16[8,3,4,2,64,128]{5,4,3,2,1,0:T(8,128)(2,1)} %get-tuple-element.50), calls=%async_computation | async-start | bytes 6291456 | tf_op jit(solution)/shard_map/all_to_all | solution.py:487
  14.0 74.9 %collective-permute-start = (bf16[1024,512]{1,0:T(8,128)(2,1)}, bf16[1024,512]{1,0:T(8,128)(2,1)}, u32[]{:S(2)}, u32[]{:S(2)}) collective-permute-start(bf16[1024,512]{1,0:T(8,128)(2,1)} %refs_0_.7), channel_id=1, source_target_pairs={{0,8},{4,12},{8,0},{12,4},{16,24},{20,28},{24,16},{28,20},{1,9},{5... | collective-permute-start | bytes 3145736 | tf_op jit(solution)/shard_map/ppermute | solution.py:475
  14.0 93.3 %collective-permute-start.3 = (bf16[1024,512]{1,0:T(8,128)(2,1)}, bf16[1024,512]{1,0:T(8,128)(2,1)}, u32[]{:S(2)}, u32[]{:S(2)}) collective-permute-start(bf16[1024,512]{1,0:T(8,128)(2,1)} %refs_0_.7), channel_id=1, source_target_pairs={{8,16},{12,20},{16,8},{20,12},{9,17},{13,21},{17,9},{21,13},{10,18... | collective-permute-start | bytes 3145736 | tf_op jit(solution)/shard_map/ppermute | solution.py:475
  18.8 90.7 %collective-permute-start.1 = (bf16[1024,512]{1,0:T(8,128)(2,1)}, bf16[1024,512]{1,0:T(8,128)(2,1)}, u32[]{:S(2)}, u32[]{:S(2)}) collective-permute-start(bf16[1024,512]{1,0:T(8,128)(2,1)} %refs_0_.7), channel_id=1, source_target_pairs={{0,4},{4,0},{8,12},{12,8},{16,20},{20,16},{24,28},{28,24},{1,5},{5... | collective-permute-start | bytes 3145736 | tf_op jit(solution)/shard_map/ppermute | solution.py:475
  88.9 39.5 %collective-permute-start.6 = (bf16[1024,512]{1,0:T(8,128)(2,1)}, bf16[1024,512]{1,0:T(8,128)(2,1)}, u32[]{:S(2)}, u32[]{:S(2)}) collective-permute-start(bf16[1024,512]{1,0:T(8,128)(2,1)} %collective-permute-done.refs_2_), channel_id=1, source_target_pairs={{8,16},{12,20},{16,8},{20,12},{9,17},{13,21},{17,9},{21,13},{10,18... | collective-permute-start | bytes 3145736 | tf_op jit(solution)/shard_map/ppermute | solution.py:475
  107.3 24.8 %collective-permute-start.4 = (bf16[1024,512]{1,0:T(8,128)(2,1)}, bf16[1024,512]{1,0:T(8,128)(2,1)}, u32[]{:S(2)}, u32[]{:S(2)}) collective-permute-start(bf16[1024,512]{1,0:T(8,128)(2,1)} %collective-permute-done.3), channel_id=1, source_target_pairs={{8,0},{12,4},{16,24},{20,28},{9,1},{13,5},{17,25},{21,29},{10,2},{... | collective-permute-start | bytes 3145736 | tf_op jit(solution)/shard_map/ppermute | solution.py:475
  128.4 23.4 %collective-permute-start.7 = (bf16[1024,512]{1,0:T(8,128)(2,1)}, bf16[1024,512]{1,0:T(8,128)(2,1)}, u32[]{:S(2)}, u32[]{:S(2)}) collective-permute-start(bf16[1024,512]{1,0:T(8,128)(2,1)} %collective-permute-done.6), channel_id=1, source_target_pairs={{8,0},{12,4},{16,24},{20,28},{9,1},{13,5},{17,25},{21,29},{10,2},{... | collective-permute-start | bytes 3145736 | tf_op jit(solution)/shard_map/ppermute | solution.py:475
  130.6 26.4 %collective-permute-start.2 = (bf16[1024,512]{1,0:T(8,128)(2,1)}, bf16[1024,512]{1,0:T(8,128)(2,1)}, u32[]{:S(2)}, u32[]{:S(2)}) collective-permute-start(bf16[1024,512]{1,0:T(8,128)(2,1)} %collective-permute-done.refs_2_), channel_id=1, source_target_pairs={{0,4},{4,0},{8,12},{12,8},{16,20},{20,16},{24,28},{28,24},{1,5},{5... | collective-permute-start | bytes 3145736 | tf_op jit(solution)/shard_map/ppermute | solution.py:475
  134.4 50.3 %collective-permute-start.5 = (bf16[1024,512]{1,0:T(8,128)(2,1)}, bf16[1024,512]{1,0:T(8,128)(2,1)}, u32[]{:S(2)}, u32[]{:S(2)}) collective-permute-start(bf16[1024,512]{1,0:T(8,128)(2,1)} %broadcast_select_fusion.1.refs_4_), channel_id=1, source_target_pairs={{0,4},{4,0},{8,12},{12,8},{16,20},{20,16},{24,28},{28,24},{1,5},{5... | collective-permute-start | bytes 3145736 | tf_op jit(solution)/shard_map/ppermute | solution.py:475
  157.0 52.6 %collective-permute-start.8 = (bf16[1024,512]{1,0:T(8,128)(2,1)}, bf16[1024,512]{1,0:T(8,128)(2,1)}, u32[]{:S(2)}, u32[]{:S(2)}) collective-permute-start(bf16[1024,512]{1,0:T(8,128)(2,1)} %broadcast_select_fusion.refs_6_), channel_id=1, source_target_pairs={{0,4},{4,0},{8,12},{12,8},{16,20},{20,16},{24,28},{28,24},{1,5},{5... | collective-permute-start | bytes 3145736 | tf_op jit(solution)/shard_map/ppermute | solution.py:475
  167.2 1.0 copy-start.3
  168.1 62.6 %all-to-all-start.1 = ((bf16[8,4,2,64,128]{4,3,2,1,0:T(8,128)(2,1)}), bf16[8,4,2,64,128]{4,3,2,1,0:T(8,128)(2,1)}, u32[]{:S(2)}, u32[]{:S(2)}) async-start(bf16[8,4,2,64,128]{4,3,2,1,0:T(8,128)(2,1)} %copy-done.3), calls=%async_computation.1 | async-start | bytes 2097152 | tf_op jit(solution)/shard_map/all_to_all | solution.py:487
  230.7 28.7 %all-to-all-start.2 = ((bf16[8,4,2,64,128]{4,3,2,1,0:T(8,128)(2,1)}), bf16[8,4,2,64,128]{4,3,2,1,0:T(8,128)(2,1)}, u32[]{:S(2)}, u32[]{:S(2)}) async-start(bf16[8,4,2,64,128]{4,3,2,1,0:T(8,128)(2,1)} %get-tuple-element.64), calls=%async_computation.2 | async-start | bytes 2097152 | tf_op jit(solution)/shard_map/all_to_all | solution.py:487
  247.6 1.2 copy-start
  250.7 1.0 copy-start.1
  251.7 1.4 copy-start.2
  285.6 145.1 %collective-permute-start.9 = (bf16[1024,2048]{1,0:T(8,128)(2,1)}, bf16[1024,2048]{1,0:T(8,128)(2,1)}, u32[]{:S(2)}, u32[]{:S(2)}) collective-permute-start(bf16[1024,2048]{1,0:T(8,128)(2,1)} %layer_part.3), channel_id=1, source_target_pairs={{0,1},{1,0},{2,3},{3,2},{4,5},{5,4},{6,7},{7,6},{8,9},{9,8},{10,11... | collective-permute-start | bytes 12582920 | tf_op jit(solution)/shard_map/ppermute | solution.py:498
  285.7 211.0 %all-to-all-start.3 = ((bf16[8,3,4,2,64,128]{5,4,3,2,1,0:T(8,128)(2,1)}), bf16[8,3,4,2,64,128]{5,4,3,2,1,0:T(8,128)(2,1)S(1)}, u32[]{:S(2)}, u32[]{:S(2)}) async-start(bf16[8,3,4,2,64,128]{5,4,3,2,1,0:T(8,128)(2,1)} %column_backward.1), calls=%async_computation.3 | async-start | bytes 6291456 | tf_op jit(solution)/shard_map/all_to_all | solution.py:487
  297.1 52.0 %collective-permute-start.12 = (bf16[2,512,512]{2,1,0:T(8,128)(2,1)}, bf16[2,512,512]{2,1,0:T(8,128)(2,1)}, u32[]{:S(2)}, u32[]{:S(2)}) collective-permute-start(bf16[2,512,512]{2,1,0:T(8,128)(2,1)} %proj_part.10), channel_id=1, source_target_pairs={{0,4},{4,0},{8,12},{12,8},{16,20},{20,16},{24,28},{28,24},{1,5},{5... | collective-permute-start | bytes 3145736 | tf_op jit(solution)/shard_map/ppermute | solution.py:475
  304.1 69.4 %collective-permute-start.15 = (bf16[2,512,512]{2,1,0:T(8,128)(2,1)}, bf16[2,512,512]{2,1,0:T(8,128)(2,1)}, u32[]{:S(2)}, u32[]{:S(2)}) collective-permute-start(bf16[2,512,512]{2,1,0:T(8,128)(2,1)} %proj_part.12), channel_id=1, source_target_pairs={{0,4},{4,0},{8,12},{12,8},{16,20},{20,16},{24,28},{28,24},{1,5},{5... | collective-permute-start | bytes 3145736 | tf_op jit(solution)/shard_map/ppermute | solution.py:475
  309.5 86.0 %collective-permute-start.11 = (bf16[2,512,512]{2,1,0:T(8,128)(2,1)}, bf16[2,512,512]{2,1,0:T(8,128)(2,1)}, u32[]{:S(2)}, u32[]{:S(2)}) collective-permute-start(bf16[2,512,512]{2,1,0:T(8,128)(2,1)} %proj_part.8), channel_id=1, source_target_pairs={{0,4},{4,0},{8,12},{12,8},{16,20},{20,16},{24,28},{28,24},{1,5},{5... | collective-permute-start | bytes 3145736 | tf_op jit(solution)/shard_map/ppermute | solution.py:475
  354.1 48.1 %collective-permute-start.14 = (bf16[2,512,512]{2,1,0:T(8,128)(2,1)}, bf16[2,512,512]{2,1,0:T(8,128)(2,1)}, u32[]{:S(2)}, u32[]{:S(2)}) collective-permute-start(bf16[2,512,512]{2,1,0:T(8,128)(2,1)} %proj_part.11), channel_id=1, source_target_pairs={{0,8},{4,12},{24,16},{28,20},{1,9},{5,13},{25,17},{29,21},{2,10},{... | collective-permute-start | bytes 3145736 | tf_op jit(solution)/shard_map/ppermute | solution.py:475
  395.5 27.0 %collective-permute-start.20 = (bf16[2,512,512]{2,1,0:T(8,128)(2,1)}, bf16[2,512,512]{2,1,0:T(8,128)(2,1)}, u32[]{:S(2)}, u32[]{:S(2)}) collective-permute-start(bf16[2,512,512]{2,1,0:T(8,128)(2,1)} %proj_part.15), channel_id=1, source_target_pairs={{0,8},{4,12},{24,16},{28,20},{1,9},{5,13},{25,17},{29,21},{2,10},{... | collective-permute-start | bytes 3145736 | tf_op jit(solution)/shard_map/ppermute | solution.py:475
  401.7 25.1 %collective-permute-start.17 = (bf16[2,512,512]{2,1,0:T(8,128)(2,1)}, bf16[2,512,512]{2,1,0:T(8,128)(2,1)}, u32[]{:S(2)}, u32[]{:S(2)}) collective-permute-start(bf16[2,512,512]{2,1,0:T(8,128)(2,1)} %proj_part.13), channel_id=1, source_target_pairs={{0,4},{4,0},{8,12},{12,8},{16,20},{20,16},{24,28},{28,24},{1,5},{5... | collective-permute-start | bytes 3145736 | tf_op jit(solution)/shard_map/ppermute | solution.py:475
  402.2 20.3 %copy-start.5 = (bf16[2,512,512]{2,1,0:T(8,128)(2,1)S(1)}, bf16[2,512,512]{2,1,0:T(8,128)(2,1)}, u32[]{:S(2)}) copy-start(bf16[2,512,512]{2,1,0:T(8,128)(2,1)} %proj_part.15) | copy-start | bytes 3145732
  405.2 43.3 %collective-permute-start.16 = (bf16[2,512,512]{2,1,0:T(8,128)(2,1)}, bf16[2,512,512]{2,1,0:T(8,128)(2,1)}, u32[]{:S(2)}, u32[]{:S(2)}) collective-permute-start(bf16[2,512,512]{2,1,0:T(8,128)(2,1)} %add_convert_fusion.1), channel_id=1, source_target_pairs={{8,16},{12,20},{16,8},{20,12},{9,17},{13,21},{17,9},{21,13},{10,18... | collective-permute-start | bytes 3145736 | tf_op jit(solution)/shard_map/ppermute | solution.py:475
  426.8 43.3 %collective-permute-start.21 = (bf16[2,512,512]{2,1,0:T(8,128)(2,1)}, bf16[2,512,512]{2,1,0:T(8,128)(2,1)}, u32[]{:S(2)}, u32[]{:S(2)}) collective-permute-start(bf16[2,512,512]{2,1,0:T(8,128)(2,1)} %add_convert_fusion), channel_id=1, source_target_pairs={{8,16},{12,20},{16,8},{20,12},{9,17},{13,21},{17,9},{21,13},{10,18... | collective-permute-start | bytes 3145736 | tf_op jit(solution)/shard_map/ppermute | solution.py:475
  439.2 66.5 %collective-permute-start.10 = (bf16[1024,1024]{1,0:T(8,128)(2,1)}, bf16[1024,1024]{1,0:T(8,128)(2,1)}, u32[]{:S(2)}, u32[]{:S(2)}) collective-permute-start(bf16[1024,1024]{1,0:T(8,128)(2,1)} %layer_part.4), channel_id=1, source_target_pairs={{0,2},{1,3},{2,0},{3,1},{4,6},{5,7},{6,4},{7,5},{8,10},{9,11},{10,... | collective-permute-start | bytes 6291464 | tf_op jit(solution)/shard_map/ppermute | solution.py:498
  446.6 14.7 %collective-permute-start.13 = (bf16[512,512]{1,0:T(8,128)(2,1)}, bf16[512,512]{1,0:T(8,128)(2,1)}, u32[]{:S(2)}, u32[]{:S(2)}) collective-permute-start(bf16[512,512]{1,0:T(8,128)(2,1)} %bitcast.53), channel_id=1, source_target_pairs={{0,8},{4,12},{24,16},{28,20},{1,9},{5,13},{25,17},{29,21},{2,10},{... | collective-permute-start | bytes 1572872 | tf_op jit(solution)/shard_map/ppermute | solution.py:475
  461.3 30.8 %collective-permute-start.18 = (bf16[512,512]{1,0:T(8,128)(2,1)}, bf16[512,512]{1,0:T(8,128)(2,1)}, u32[]{:S(2)}, u32[]{:S(2)}) collective-permute-start(bf16[512,512]{1,0:T(8,128)(2,1)} %fusion.3), channel_id=1, source_target_pairs={{8,0},{12,4},{16,24},{20,28},{9,1},{13,5},{17,25},{21,29},{10,2},{... | collective-permute-start | bytes 1572872 | tf_op jit(solution)/shard_map/ppermute | solution.py:475
  468.8 25.0 %collective-permute-start.19 = (bf16[512,512]{1,0:T(8,128)(2,1)}, bf16[512,512]{1,0:T(8,128)(2,1)}, u32[]{:S(2)}, u32[]{:S(2)}) collective-permute-start(bf16[512,512]{1,0:T(8,128)(2,1)} %bitcast.52), channel_id=1, source_target_pairs={{0,8},{4,12},{24,16},{28,20},{1,9},{5,13},{25,17},{29,21},{2,10},{... | collective-permute-start | bytes 1572872 | tf_op jit(solution)/shard_map/ppermute | solution.py:475
  472.3 19.9 %copy-start.6 = (bf16[1,512,512]{2,1,0:T(8,128)(2,1)S(1)}, bf16[1,512,512]{2,1,0:T(8,128)(2,1)}, u32[]{:S(2)}) copy-start(bf16[1,512,512]{2,1,0:T(8,128)(2,1)} %get-tuple-element.77) | copy-start | bytes 1572868
  472.3 21.6 %collective-permute-start.22 = (bf16[512,512]{1,0:T(8,128)(2,1)}, bf16[512,512]{1,0:T(8,128)(2,1)}, u32[]{:S(2)}, u32[]{:S(2)}) collective-permute-start(bf16[512,512]{1,0:T(8,128)(2,1)} %fusion), channel_id=1, source_target_pairs={{8,0},{12,4},{16,24},{20,28},{9,1},{13,5},{17,25},{21,29},{10,2},{... | collective-permute-start | bytes 1572872 | tf_op jit(solution)/shard_map/ppermute | solution.py:475
  492.1 1.7 copy-start.7
  496.7 1.6 copy-start.4

commit v4 on v3

--- a/solution.py
+++ b/solution.py
@@ -519,7 +519,7 @@
     cross_own = links.along(wo, CROSS)
     own_blocks = around(wo)
     chunks, by_head = split_inputs(queries, keys, values, n)
-    chunks, near = swap(chunks), after(near, chunks)
+    chunks = swap(after(chunks, near, cross_own, *own_blocks[1:]))
     near_blocks = around(near)
     cross_near = links.along(near, CROSS)
     far_own = jnp.where(middle, cross_own, links.along(cross_own, OUTWARD))
@@ -533,10 +533,11 @@
     def targets(owners, e):
         return jnp.stack([owner * inner + (spot ^ e) for owner in owners]).astype(jnp.int32)
 
-    def exchanged(flat, owners):
-        return [
-            links.flip(proj_part(targets(owners, e), flat, out_grad, [], depth, dim, 0)[0], e) for e in range(1, inner)
-        ]
+    def leaving(flat, owners):
+        return [proj_part(targets(owners, e), flat, out_grad, [], depth, dim, 0)[0] for e in range(1, inner)]
+
+    def exchanged(parts):
+        return [links.flip(part, e + 1) for e, part in enumerate(parts)]
 
     def summed(flat, owners, theirs, lead):
         return proj_part(targets(owners, 0), flat, out_grad, theirs, depth, dim, lead)
@@ -544,34 +545,36 @@
     def add(*terms):
         return sum(term.astype(F32) for term in terms).astype(BF16)
 
-    row_out = row_forward(*(after(tensor, near) for tensor in by_head))
-    row_far = exchanged(row_out, far)
-    row_close = exchanged(row_out, close)
-
-    outs = column_forward(chunks)
+    row_out = row_forward(*(after(tensor, near, cross_own) for tensor in by_head))
+    row_far, row_close = leaving(row_out, far), leaving(row_out, close)
+    outs = column_forward(after(chunks, *row_far, *row_close))
+    row_far, row_close = exchanged(row_far), exchanged(row_close)
+
     column_part = swap(outs)
     grad_row, grads = attn_grad(ids, after(out_grad, outs), blocks, dim)
     grads = swap(after(grads, column_part))
     column_out, flat = collect(row_out, column_part)
-    column_far = exchanged(column_out, far)
-    column_close = exchanged(column_out, close)
-    gradients = column_backward(chunks, grads)
+    column_far, column_close = leaving(column_out, far), leaving(column_out, close)
+    gradients = column_backward(chunks, after(grads, *column_far, *column_close, *row_far))
+    column_far, column_close = exchanged(column_far), exchanged(column_close)
     column_grads = swap(gradients)
 
-    (row_far,) = summed(after(row_out, column_out), far, row_far, 0)
+    later = after(row_out, gradients, *row_close)
+    (row_far,) = summed(later, far, row_far, 0)
     row_far_in = links.along(row_far, INWARD)
-    row_near, row_own = summed(after(row_out, column_out), close, row_close, 1)
+    row_near, row_own = summed(later, close, row_close, 1)
     row_near_in = links.along(row_near[0], INWARD)
-    (column_far,) = summed(after(column_out, gradients), far, column_far, 0)
+    (column_far,) = summed(column_out, far, column_far, 0)
     column_far_in = links.along(column_far, INWARD)
     row_cross = links.along(add(row_far, row_far_in), CROSS)
-    column_near, column_own = summed(after(column_out, gradients), close, column_close, 1)
+    flat = after(flat, column_far)
+    column_near, column_own = summed(column_out, close, column_close, 1)
     column_near_in = links.along(column_near[0], INWARD)
     column_cross = links.along(add(column_far, column_far_in), CROSS)
     row_back = links.along(add(row_near[0], row_cross[1]), OUTWARD)
     column_back = links.along(add(column_near[0], column_cross[1]), OUTWARD)
 
-    layer_out = scatter_layer(ids, after(flat, gradients), blocks, heads_n)
+    layer_out = scatter_layer(ids, flat, blocks, heads_n)
     row_grads = row_backward(*by_head, after(grad_row, gradients))
     gradients = join_gradients(column_grads, row_grads)
 

time: 516 us -> 516 us (level)
    all_to_all x4, waiting for transfers between devices: 6.3 us -> 16.8 us  [swap(): lax.all_to_all(chunks, 'ctx', split_axis=0, concat_axis=0, tiled=True)]
    ppermute x21, waiting for transfers between devices: 257 us -> 250 us  [send(): out = lax.ppermute(value, 'ctx', pairs)]
  transfers between devices with their start and end apart: 27 -> 27, of which waited for: 14 -> 12; matrix products, arithmetic and copies ran while one was open for 5% -> 4% of each run, Pallas kernels for 22% -> 28%
where the time goes in v4:
time: 516 us; the launch traced here: 514 us
  waiting for transfers between devices  267 us (52%)
  Pallas kernels  151 us (29%)
  starting transfers between devices  65.8 us (13%)
  other arithmetic  20.8 us (4%)
  local copies, waits for them, and re-layouts  9.27 us (2%)
    ppermute x21, waiting for transfers between devices, send(): out = lax.ppermute(value, 'ctx', pairs)  250 us
    ppermute x21, starting transfers between devices, send(): out = lax.ppermute(value, 'ctx', pairs)  44.1 us
    pallas_call x8, Pallas kernels, proj_part(): pl.pallas_call(functools.partial(proj_kernel, lead, len(extra), dim), gri...  40.3 us
    pallas_call x3, Pallas kernels, layer_part(): pl.pallas_call(functools.partial(layer_kernel, n, count, len(extra)), gri...  29.3 us
    pallas_call x1, Pallas kernels, attn_grad(): pl.pallas_call(functools.partial(attn_grad_kernel, n, dim), grid_spec=plt...  21 us
    all_to_all x4, starting transfers between devices, swap(): lax.all_to_all(chunks, 'ctx', split_axis=0, concat_axis=0, tiled=True)  20.1 us
    all_to_all x4, waiting for transfers between devices, swap(): lax.all_to_all(chunks, 'ctx', split_axis=0, concat_axis=0, tiled=True)  16.8 us
    pallas_call x1, Pallas kernels, row_backward(): pl.pallas_call(functools.partial(row_backward_kernel, dim ** (-0.5)), gri...  13.6 us
  transfers between devices with their start and end apart: 27, of which 12 were waited for; matrix products, arithmetic and copies ran while one was open for 4% of the time, Pallas kernels for 28%

profile of v4, /device:TPU:8, one launch (start us, length us, event | category | flops | bytes accessed | tf_op | source)
XLA Modules:
  0.0 514.2 jit_solution(13553082702290547219)
XLA Ops:
  2.2 3.5 collective-permute-start.1
  5.8 7.1 %split_inputs.1 = (bf16[8,3,4,2,64,128]{5,4,3,2,1,0:T(8,128)(2,1)}, bf16[4,1024,128]{2,1,0:T(8,128)(2,1)}, bf16[4,1024,128]{2,1,0:T(8,128)(2,1)}, bf16[4,1024,128]{2,1,0:T(8,128)(2,1)}) custom-call(bf16[1024,8,128]{2,1,0:T(8,128)(2,1)} %q_ref.1, bf16[1024,8,128]{2,1,0:T(8,128)(2,1)} %k_ref.1, bf16[1024,8,128]{2,1,0:T(8,128)(2,1)} %v_ref.1), custom_call_target="tpu_custom_call" | custom-call | tf_op jit(solution)/shard_map/split_inputs/pallas_call | solution.py:48
  12.9 13.0 %collective-permute-done.2.refs_1_ = bf16[1024,512]{1,0:T(8,128)(2,1)} collective-permute-done((bf16[1024,512]{1,0:T(8,128)(2,1)}, bf16[1024,512]{1,0:T(8,128)(2,1)}, u32[]{:S(2)}, u32[]{:S(2)}) %collective-permute-start.2) | collective-permute-done | bytes 1048608 | tf_op jit(solution)/shard_map/ppermute | solution.py:475
  25.9 3.1 collective-permute-done.1
  30.4 3.8 all-to-all-start
  34.3 3.4 collective-permute-start.4
  37.6 2.3 collective-permute-start.5
  40.6 84.6 %collective-permute-done.4 = bf16[1024,512]{1,0:T(8,128)(2,1)} collective-permute-done((bf16[1024,512]{1,0:T(8,128)(2,1)}, bf16[1024,512]{1,0:T(8,128)(2,1)}, u32[]{:S(2)}, u32[]{:S(2)}) %collective-permute-start.4) | collective-permute-done | bytes 1048608 | tf_op jit(solution)/shard_map/ppermute | solution.py:475
  125.2 2.3 collective-permute-start.8
  129.6 9.9 %row_forward.1.flat_ref.row_ref = bf16[1024,512]{1,0:T(8,128)(2,1)} custom-call(bf16[4,1024,128]{2,1,0:T(8,128)(2,1)} %get-tuple-element.51.q_ref, bf16[4,1024,128]{2,1,0:T(8,128)(2,1)} %get-tuple-element.53.k_ref, bf16[4,1024,128]{2,1,0:T(8,128)(2,1)} %get-tuple-element.55.v_ref), custom_call_target="tpu_custom_call" | custom-call | flops 1073741824 | bytes 4194304 | tf_op jit(solution)/shard_map/row_forward/pallas_call | solution.py:311
  139.5 4.8 proj_part.9
  144.3 4.9 proj_part.8
  149.2 8.7 %column_forward.1 = bf16[8,4,2,64,128]{4,3,2,1,0:T(8,128)(2,1)S(1)} custom-call(bf16[8,3,4,2,64,128]{5,4,3,2,1,0:T(8,128)(2,1)S(1)} %all-to-all-done.chunk_ref), custom_call_target="tpu_custom_call" | custom-call | flops 536870912 | bytes 4194304 | tf_op jit(solution)/shard_map/column_forward/pallas_call | solution.py:403
  158.8 4.1 all-to-all-start.1
  165.9 2.3 broadcast_select_fusion.refs_6_
  169.5 16.8 %all-to-all-done.1.chunk_ref = bf16[8,4,2,64,128]{4,3,2,1,0:T(8,128)(2,1)S(1)} async-done(((bf16[8,4,2,64,128]{4,3,2,1,0:T(8,128)(2,1)}), bf16[8,4,2,64,128]{4,3,2,1,0:T(8,128)(2,1)S(1)}, u32[]{:S(2)}, u32[]{:S(2)}) %all-to-all-start.1) | async-done | bytes 1048608 | tf_op jit(solution)/shard_map/all_to_all | solution.py:487
  189.3 4.9 proj_part.10
  194.1 5.8 %collective-permute-done.6.refs_5_ = bf16[1024,512]{1,0:T(8,128)(2,1)} collective-permute-done((bf16[1024,512]{1,0:T(8,128)(2,1)S(1)}, bf16[1024,512]{1,0:T(8,128)(2,1)}, u32[]{:S(2)}, u32[]{:S(2)}) %collective-permute-start.6) | collective-permute-done | bytes 1048608 | tf_op jit(solution)/shard_map/ppermute | solution.py:475
  200.1 22.3 %collective-permute-done.9.refs_7_ = bf16[1024,512]{1,0:T(8,128)(2,1)} collective-permute-done((bf16[1024,512]{1,0:T(8,128)(2,1)}, bf16[1024,512]{1,0:T(8,128)(2,1)}, u32[]{:S(2)}, u32[]{:S(2)}) %collective-permute-start.9) | collective-permute-done | bytes 1048608 | tf_op jit(solution)/shard_map/ppermute | solution.py:475
  222.4 21.0 %attn_grad.1 = (bf16[1024,512]{1,0:T(8,128)(2,1)}, bf16[8,4,2,64,128]{4,3,2,1,0:T(8,128)(2,1)}) custom-call(s32[8]{0:T(128)} %stack.103.ids, bf16[1024,4096]{1,0:T(8,128)(2,1)} %grad_ref.16, bf16[1024,512]{1,0:T(8,128)(2,1)} %refs_0_.7, bf16[1024,512]{1,0:T(8,128)(2,1)} %collective-permute-done.2.refs_1_, bf16[1024,512]{1,0:T(8,128)(2,1)} %collective-permute-done.refs_2_, ...), custom_call_target="tpu_custom_call" | custom-call | flops 8589934592 | bytes 18874368 | tf_op jit(solution)/shard_map/attn_grad/pallas_call | solution.py:153
  243.5 6.2 %all-to-all-start.2 = ((bf16[8,4,2,64,128]{4,3,2,1,0:T(8,128)(2,1)}), bf16[8,4,2,64,128]{4,3,2,1,0:T(8,128)(2,1)}, u32[]{:S(2)}, u32[]{:S(2)}) async-start(bf16[8,4,2,64,128]{4,3,2,1,0:T(8,128)(2,1)} %get-tuple-element.69), calls=%async_computation.2 | async-start | bytes 2097152 | tf_op jit(solution)/shard_map/all_to_all | solution.py:487
  251.9 5.0 proj_part.11
  256.9 11.7 %layer_part.3 = bf16[1024,2048]{1,0:T(8,128)(2,1)} custom-call(s32[8]{0:T(128)} %stack.103.ids, s32[4]{0:T(128)} %pad_add_fusion.4.wanted, bf16[1024,1024]{1,0:T(8,128)(2,1)} %copy-done.5, bf16[1024,512]{1,0:T(8,128)(2,1)} %refs_0_.7, bf16[1024,512]{1,0:T(8,128)(2,1)} %collective-permute-done.2.refs_1_, bf16[1024,512]{1,0:T(8,128)(2,1)} %collective-permute-done.refs_2_, ...), custom_call_target="tpu_custom_call" | custom-call | flops 4294967296 | bytes 10485760 | tf_op jit(solution)/shard_map/layer_part/pallas_call | solution.py:211
  270.2 5.1 proj_part.12
  275.3 19.3 %collective-permute-done.12.refs_0_ = bf16[2,512,512]{2,1,0:T(8,128)(2,1)} collective-permute-done((bf16[2,512,512]{2,1,0:T(8,128)(2,1)}, bf16[2,512,512]{2,1,0:T(8,128)(2,1)}, u32[]{:S(2)}, u32[]{:S(2)}) %collective-permute-start.12) | collective-permute-done | bytes 1048608 | tf_op jit(solution)/shard_map/ppermute | solution.py:475
  294.6 12.9 %column_backward.1 = bf16[8,3,4,2,64,128]{5,4,3,2,1,0:T(8,128)(2,1)S(1)} custom-call(bf16[8,3,4,2,64,128]{5,4,3,2,1,0:T(8,128)(2,1)S(1)} %copy-done.2, bf16[8,4,2,64,128]{4,3,2,1,0:T(8,128)(2,1)} %all-to-all-done.2.grad_ref), custom_call_target="tpu_custom_call" | custom-call | flops 1342177280 | bytes 7340032 | tf_op jit(solution)/shard_map/column_backward/pallas_call | solution.py:441
  309.2 5.9 %all-to-all-start.3 = ((bf16[8,3,4,2,64,128]{5,4,3,2,1,0:T(8,128)(2,1)}), bf16[8,3,4,2,64,128]{5,4,3,2,1,0:T(8,128)(2,1)S(1)}, u32[]{:S(2)}, u32[]{:S(2)}) async-start(bf16[8,3,4,2,64,128]{5,4,3,2,1,0:T(8,128)(2,1)} %copy-done.4), calls=%async_computation.3 | async-start | bytes 6291456 | tf_op jit(solution)/shard_map/all_to_all | solution.py:487
  316.6 54.5 %collective-permute-done.13.refs_0_ = bf16[2,512,512]{2,1,0:T(8,128)(2,1)} collective-permute-done((bf16[2,512,512]{2,1,0:T(8,128)(2,1)}, bf16[2,512,512]{2,1,0:T(8,128)(2,1)}, u32[]{:S(2)}, u32[]{:S(2)}) %collective-permute-start.13) | collective-permute-done | bytes 1048608 | tf_op jit(solution)/shard_map/ppermute | solution.py:475
  371.1 5.0 proj_part.14
  378.7 2.6 collective-permute-start.17
  381.2 23.2 %collective-permute-done.15 = bf16[2,512,512]{2,1,0:T(8,128)(2,1)} collective-permute-done((bf16[2,512,512]{2,1,0:T(8,128)(2,1)}, bf16[2,512,512]{2,1,0:T(8,128)(2,1)}, u32[]{:S(2)}, u32[]{:S(2)}) %collective-permute-start.15) | collective-permute-done | bytes 1048608 | tf_op jit(solution)/shard_map/ppermute | solution.py:475
  404.4 2.8 add_convert_fusion.1
  407.2 4.1 collective-permute-start.16
  411.9 13.0 %collective-permute-done.20 = bf16[2,512,512]{2,1,0:T(8,128)(2,1)} collective-permute-done((bf16[2,512,512]{2,1,0:T(8,128)(2,1)}, bf16[2,512,512]{2,1,0:T(8,128)(2,1)}, u32[]{:S(2)}, u32[]{:S(2)}) %collective-permute-start.20) | collective-permute-done | bytes 1048608 | tf_op jit(solution)/shard_map/ppermute | solution.py:475
  424.9 2.5 add_convert_fusion
  427.4 3.9 collective-permute-start.21
  431.3 8.5 %layer_part.4 = bf16[1024,1024]{1,0:T(8,128)(2,1)} custom-call(s32[8]{0:T(128)} %stack.103.ids, s32[2]{0:T(128)} %pad_add_fusion.5.wanted, bf16[1024,1024]{1,0:T(8,128)(2,1)} %copy-done.5, bf16[1024,512]{1,0:T(8,128)(2,1)} %refs_0_.7, bf16[1024,512]{1,0:T(8,128)(2,1)} %collective-permute-done.2.refs_1_, bf16[1024,512]{1,0:T(8,128)(2,1)} %collective-permute-done.refs_2_, ...), custom_call_target="tpu_custom_call" | custom-call | flops 2147483648 | bytes 6291456 | tf_op jit(solution)/shard_map/layer_part/pallas_call | solution.py:211
  441.9 5.3 %proj_part.13 = (bf16[1,512,512]{2,1,0:T(8,128)(2,1)}, bf16[1,512,512]{2,1,0:T(8,128)(2,1)}) custom-call(s32[2]{0:T(128)} %pad_add_fusion.6.order, bf16[1024,512]{1,0:T(8,128)(2,1)} %row_forward.1.flat_ref.row_ref, bf16[1024,4096]{1,0:T(8,128)(2,1)} %grad_ref.16, bf16[2,512,512]{2,1,0:T(8,128)(2,1)} %collective-permute-done.13.refs_0_), custom_call_target="tpu_custom_call" | custom-call | flops 1073741824 | bytes 5242880 | tf_op jit(solution)/shard_map/proj_part/pallas_call | solution.py:265
  449.0 2.1 fusion.3
  451.2 9.4 %collective-permute-done.14 = bf16[512,512]{1,0:T(8,128)(2,1)} collective-permute-done((bf16[512,512]{1,0:T(8,128)(2,1)}, bf16[512,512]{1,0:T(8,128)(2,1)}, u32[]{:S(2)}, u32[]{:S(2)}) %collective-permute-start.14) | collective-permute-done | bytes 524320 | tf_op jit(solution)/shard_map/ppermute | solution.py:475
  460.6 2.2 collective-permute-start.18
  462.8 5.2 %proj_part.15 = (bf16[1,512,512]{2,1,0:T(8,128)(2,1)}, bf16[1,512,512]{2,1,0:T(8,128)(2,1)}) custom-call(s32[2]{0:T(128)} %pad_add_fusion.6.order, bf16[1024,512]{1,0:T(8,128)(2,1)} %copy-done.3, bf16[1024,4096]{1,0:T(8,128)(2,1)} %grad_ref.16, bf16[2,512,512]{2,1,0:T(8,128)(2,1)} %collective-permute-done.17.refs_0_), custom_call_target="tpu_custom_call" | custom-call | flops 1073741824 | bytes 5242880 | tf_op jit(solution)/shard_map/proj_part/pallas_call | solution.py:265
  469.3 2.1 fusion
  471.5 6.3 %collective-permute-start.22 = (bf16[512,512]{1,0:T(8,128)(2,1)}, bf16[512,512]{1,0:T(8,128)(2,1)}, u32[]{:S(2)}, u32[]{:S(2)}) collective-permute-start(bf16[512,512]{1,0:T(8,128)(2,1)} %fusion), channel_id=1, source_target_pairs={{8,0},{12,4},{16,24},{20,28},{9,1},{13,5},{17,25},{21,29},{10,2},{... | collective-permute-start | bytes 1572872 | tf_op jit(solution)/shard_map/ppermute | solution.py:475
  477.8 13.6 %row_backward.1 = (bf16[4,1024,128]{2,1,0:T(8,128)(2,1)}, bf16[4,1024,128]{2,1,0:T(8,128)(2,1)}, bf16[4,1024,128]{2,1,0:T(8,128)(2,1)}) custom-call(bf16[4,1024,128]{2,1,0:T(8,128)(2,1)} %get-tuple-element.51.q_ref, bf16[4,1024,128]{2,1,0:T(8,128)(2,1)} %get-tuple-element.53.k_ref, bf16[4,1024,128]{2,1,0:T(8,128)(2,1)} %get-tuple-element.55.v_ref, ...), custom_call_target="tpu_custom_call" | custom-call | flops 2684354560 | bytes 7340032 | tf_op jit(solution)/shard_map/row_backward/pallas_call | solution.py:345
  491.5 1.7 fusion.5
  496.0 9.2 %layer_part.5 = bf16[1024,1024]{1,0:T(8,128)(2,1)} custom-call(s32[8]{0:T(128)} %stack.103.ids, s32[2]{0:T(128)} %pad_add_fusion.wanted, bf16[1024,1024]{1,0:T(8,128)(2,1)} %copy-done.5, bf16[1024,512]{1,0:T(8,128)(2,1)} %refs_0_.7, bf16[1024,512]{1,0:T(8,128)(2,1)} %collective-permute-done.2.refs_1_, bf16[1024,512]{1,0:T(8,128)(2,1)} %collective-permute-done.refs_2_, ...), custom_call_target="tpu_custom_call" | custom-call | flops 2147483648 | bytes 6291456 | tf_op jit(solution)/shard_map/layer_part/pallas_call | solution.py:211
  506.8 7.3 %join_gradients.1 = (bf16[1024,8,128]{2,1,0:T(8,128)(2,1)}, bf16[1024,8,128]{2,1,0:T(8,128)(2,1)}, bf16[1024,8,128]{2,1,0:T(8,128)(2,1)}) custom-call(bf16[8,3,4,2,64,128]{5,4,3,2,1,0:T(8,128)(2,1)} %copy-done.7, bf16[4,1024,128]{2,1,0:T(8,128)(2,1)} %get-tuple-element.74.refs_0_, bf16[4,1024,128]{2,1,0:T(8,128)(2,1)} %get-tuple-element.75.refs_1_, ...), custom_call_target="tpu_custom_call" | custom-call | tf_op jit(solution)/shard_map/join_gradients/pallas_call | solution.py:78
  (69 shorter events, 33.7 us)
Async XLA Ops:
  0.6 25.3 %collective-permute-start.2 = (bf16[1024,512]{1,0:T(8,128)(2,1)}, bf16[1024,512]{1,0:T(8,128)(2,1)}, u32[]{:S(2)}, u32[]{:S(2)}) collective-permute-start(bf16[1024,512]{1,0:T(8,128)(2,1)} %refs_0_.7), channel_id=1, source_target_pairs={{0,4},{4,0},{8,12},{12,8},{16,20},{20,16},{24,28},{28,24},{1,5},{5... | collective-permute-start | bytes 3145736 | tf_op jit(solution)/shard_map/ppermute | solution.py:475
  2.2 26.8 %collective-permute-start.1 = (bf16[1024,512]{1,0:T(8,128)(2,1)}, bf16[1024,512]{1,0:T(8,128)(2,1)}, u32[]{:S(2)}, u32[]{:S(2)}) collective-permute-start(bf16[1024,512]{1,0:T(8,128)(2,1)} %refs_0_.7), channel_id=1, source_target_pairs={{8,16},{12,20},{16,8},{20,12},{9,17},{13,21},{17,9},{21,13},{10,18... | collective-permute-start | bytes 3145736 | tf_op jit(solution)/shard_map/ppermute | solution.py:475
  5.7 24.7 %collective-permute-start = (bf16[1024,512]{1,0:T(8,128)(2,1)}, bf16[1024,512]{1,0:T(8,128)(2,1)}, u32[]{:S(2)}, u32[]{:S(2)}) collective-permute-start(bf16[1024,512]{1,0:T(8,128)(2,1)} %refs_0_.7), channel_id=1, source_target_pairs={{0,8},{4,12},{8,0},{12,4},{16,24},{20,28},{24,16},{28,20},{1,9},{5... | collective-permute-start | bytes 3145736 | tf_op jit(solution)/shard_map/ppermute | solution.py:475
  30.4 118.8 %all-to-all-start = ((bf16[8,3,4,2,64,128]{5,4,3,2,1,0:T(8,128)(2,1)}), bf16[8,3,4,2,64,128]{5,4,3,2,1,0:T(8,128)(2,1)S(1)}, u32[]{:S(2)}, u32[]{:S(2)}) async-start(bf16[8,3,4,2,64,128]{5,4,3,2,1,0:T(8,128)(2,1)} %get-tuple-element.57), calls=%async_computation | async-start | bytes 6291456 | tf_op jit(solution)/shard_map/all_to_all | solution.py:487
  34.3 91.0 %collective-permute-start.4 = (bf16[1024,512]{1,0:T(8,128)(2,1)}, bf16[1024,512]{1,0:T(8,128)(2,1)}, u32[]{:S(2)}, u32[]{:S(2)}) collective-permute-start(bf16[1024,512]{1,0:T(8,128)(2,1)} %collective-permute-done.refs_2_), channel_id=1, source_target_pairs={{8,16},{12,20},{16,8},{20,12},{9,17},{13,21},{17,9},{21,13},{10,18... | collective-permute-start | bytes 3145736 | tf_op jit(solution)/shard_map/ppermute | solution.py:475
  37.6 125.3 %collective-permute-start.5 = (bf16[1024,512]{1,0:T(8,128)(2,1)}, bf16[1024,512]{1,0:T(8,128)(2,1)}, u32[]{:S(2)}, u32[]{:S(2)}) collective-permute-start(bf16[1024,512]{1,0:T(8,128)(2,1)} %collective-permute-done.1), channel_id=1, source_target_pairs={{8,0},{12,4},{16,24},{20,28},{9,1},{13,5},{17,25},{21,29},{10,2},{... | collective-permute-start | bytes 3145736 | tf_op jit(solution)/shard_map/ppermute | solution.py:475
  125.2 40.6 %collective-permute-start.8 = (bf16[1024,512]{1,0:T(8,128)(2,1)}, bf16[1024,512]{1,0:T(8,128)(2,1)}, u32[]{:S(2)}, u32[]{:S(2)}) collective-permute-start(bf16[1024,512]{1,0:T(8,128)(2,1)} %collective-permute-done.4), channel_id=1, source_target_pairs={{8,0},{12,4},{16,24},{20,28},{9,1},{13,5},{17,25},{21,29},{10,2},{... | collective-permute-start | bytes 3145736 | tf_op jit(solution)/shard_map/ppermute | solution.py:475
  128.1 40.1 %collective-permute-start.3 = (bf16[1024,512]{1,0:T(8,128)(2,1)}, bf16[1024,512]{1,0:T(8,128)(2,1)}, u32[]{:S(2)}, u32[]{:S(2)}) collective-permute-start(bf16[1024,512]{1,0:T(8,128)(2,1)} %collective-permute-done.refs_2_), channel_id=1, source_target_pairs={{0,4},{4,0},{8,12},{12,8},{16,20},{20,16},{24,28},{28,24},{1,5},{5... | collective-permute-start | bytes 3145736 | tf_op jit(solution)/shard_map/ppermute | solution.py:475
  149.2 8.7 %copy-start.1 = (bf16[8,3,4,2,64,128]{5,4,3,2,1,0:T(8,128)(2,1)}, bf16[8,3,4,2,64,128]{5,4,3,2,1,0:T(8,128)(2,1)S(1)}, u32[]{:S(2)}) copy-start(bf16[8,3,4,2,64,128]{5,4,3,2,1,0:T(8,128)(2,1)S(1)} %all-to-all-done.chunk_ref) | copy-start | bytes 9437188
  157.9 1.0 copy-start.6
  158.8 27.4 %all-to-all-start.1 = ((bf16[8,4,2,64,128]{4,3,2,1,0:T(8,128)(2,1)}), bf16[8,4,2,64,128]{4,3,2,1,0:T(8,128)(2,1)S(1)}, u32[]{:S(2)}, u32[]{:S(2)}) async-start(bf16[8,4,2,64,128]{4,3,2,1,0:T(8,128)(2,1)} %copy-done.6), calls=%async_computation.1 | async-start | bytes 2097152 | tf_op jit(solution)/shard_map/all_to_all | solution.py:487
  164.3 22.6 %copy-start.8 = (bf16[1024,512]{1,0:T(8,128)(2,1)}, bf16[1024,512]{1,0:T(8,128)(2,1)S(1)}, u32[]{:S(2)}) copy-start(bf16[1024,512]{1,0:T(8,128)(2,1)S(1)} %broadcast_select_fusion.1.refs_4_) | copy-start | bytes 3145732
  164.3 22.0 %copy-start = (bf16[1024,512]{1,0:T(8,128)(2,1)S(1)}, bf16[1024,512]{1,0:T(8,128)(2,1)}, u32[]{:S(2)}) copy-start(bf16[1024,512]{1,0:T(8,128)(2,1)} %row_forward.1.flat_ref.row_ref) | copy-start | bytes 3145732
  164.3 35.6 %collective-permute-start.6 = (bf16[1024,512]{1,0:T(8,128)(2,1)S(1)}, bf16[1024,512]{1,0:T(8,128)(2,1)}, u32[]{:S(2)}, u32[]{:S(2)}) collective-permute-start(bf16[1024,512]{1,0:T(8,128)(2,1)S(1)} %broadcast_select_fusion.1.refs_4_), channel_id=1, source_target_pairs={{0,4},{4,0},{8,12},{12,8},{16,20},{20,16},{24,28},{28,24},{1,5},{5... | collective-permute-start | bytes 3145736 | tf_op jit(solution)/shard_map/ppermute | solution.py:475
  168.2 54.3 %collective-permute-start.9 = (bf16[1024,512]{1,0:T(8,128)(2,1)}, bf16[1024,512]{1,0:T(8,128)(2,1)}, u32[]{:S(2)}, u32[]{:S(2)}) collective-permute-start(bf16[1024,512]{1,0:T(8,128)(2,1)} %broadcast_select_fusion.refs_6_), channel_id=1, source_target_pairs={{0,4},{4,0},{8,12},{12,8},{16,20},{20,16},{24,28},{28,24},{1,5},{5... | collective-permute-start | bytes 3145736 | tf_op jit(solution)/shard_map/ppermute | solution.py:475
  186.9 1.0 copy-start.3
  187.9 1.3 copy-start.5
  200.0 50.9 %collective-permute-start.7 = (bf16[2,512,512]{2,1,0:T(8,128)(2,1)}, bf16[2,512,512]{2,1,0:T(8,128)(2,1)S(1)}, u32[]{:S(2)}, u32[]{:S(2)}) collective-permute-start(bf16[2,512,512]{2,1,0:T(8,128)(2,1)} %proj_part.10), channel_id=1, source_target_pairs={{0,4},{4,0},{8,12},{12,8},{16,20},{20,16},{24,28},{28,24},{1,5},{5... | collective-permute-start | bytes 3145736 | tf_op jit(solution)/shard_map/ppermute | solution.py:475
  243.5 51.2 %all-to-all-start.2 = ((bf16[8,4,2,64,128]{4,3,2,1,0:T(8,128)(2,1)}), bf16[8,4,2,64,128]{4,3,2,1,0:T(8,128)(2,1)}, u32[]{:S(2)}, u32[]{:S(2)}) async-start(bf16[8,4,2,64,128]{4,3,2,1,0:T(8,128)(2,1)} %get-tuple-element.69), calls=%async_computation.2 | async-start | bytes 2097152 | tf_op jit(solution)/shard_map/all_to_all | solution.py:487
  250.9 1.0 copy-start.10
  268.6 162.7 %collective-permute-start.10 = (bf16[1024,2048]{1,0:T(8,128)(2,1)}, bf16[1024,2048]{1,0:T(8,128)(2,1)}, u32[]{:S(2)}, u32[]{:S(2)}) collective-permute-start(bf16[1024,2048]{1,0:T(8,128)(2,1)} %layer_part.3), channel_id=1, source_target_pairs={{0,1},{1,0},{2,3},{3,2},{4,5},{5,4},{6,7},{7,6},{8,9},{9,8},{10,11... | collective-permute-start | bytes 12582920 | tf_op jit(solution)/shard_map/ppermute | solution.py:498
  268.7 26.0 %collective-permute-start.12 = (bf16[2,512,512]{2,1,0:T(8,128)(2,1)}, bf16[2,512,512]{2,1,0:T(8,128)(2,1)}, u32[]{:S(2)}, u32[]{:S(2)}) collective-permute-start(bf16[2,512,512]{2,1,0:T(8,128)(2,1)} %proj_part.8), channel_id=1, source_target_pairs={{0,4},{4,0},{8,12},{12,8},{16,20},{20,16},{24,28},{28,24},{1,5},{5... | collective-permute-start | bytes 3145736 | tf_op jit(solution)/shard_map/ppermute | solution.py:475
  270.2 24.4 %copy-start.2 = (bf16[8,3,4,2,64,128]{5,4,3,2,1,0:T(8,128)(2,1)S(1)}, bf16[8,3,4,2,64,128]{5,4,3,2,1,0:T(8,128)(2,1)}, u32[]{:S(2)}) copy-start(bf16[8,3,4,2,64,128]{5,4,3,2,1,0:T(8,128)(2,1)} %copy-done.1) | copy-start | bytes 9437188
  307.6 1.6 copy-start.4
  309.2 196.0 %all-to-all-start.3 = ((bf16[8,3,4,2,64,128]{5,4,3,2,1,0:T(8,128)(2,1)}), bf16[8,3,4,2,64,128]{5,4,3,2,1,0:T(8,128)(2,1)S(1)}, u32[]{:S(2)}, u32[]{:S(2)}) async-start(bf16[8,3,4,2,64,128]{5,4,3,2,1,0:T(8,128)(2,1)} %copy-done.4), calls=%async_computation.3 | async-start | bytes 6291456 | tf_op jit(solution)/shard_map/all_to_all | solution.py:487
  315.1 56.0 %collective-permute-start.13 = (bf16[2,512,512]{2,1,0:T(8,128)(2,1)}, bf16[2,512,512]{2,1,0:T(8,128)(2,1)}, u32[]{:S(2)}, u32[]{:S(2)}) collective-permute-start(bf16[2,512,512]{2,1,0:T(8,128)(2,1)} %proj_part.9), channel_id=1, source_target_pairs={{0,4},{4,0},{8,12},{12,8},{16,20},{20,16},{24,28},{28,24},{1,5},{5... | collective-permute-start | bytes 3145736 | tf_op jit(solution)/shard_map/ppermute | solution.py:475
  376.1 28.3 %collective-permute-start.15 = (bf16[2,512,512]{2,1,0:T(8,128)(2,1)}, bf16[2,512,512]{2,1,0:T(8,128)(2,1)}, u32[]{:S(2)}, u32[]{:S(2)}) collective-permute-start(bf16[2,512,512]{2,1,0:T(8,128)(2,1)} %proj_part.14), channel_id=1, source_target_pairs={{0,8},{4,12},{24,16},{28,20},{1,9},{5,13},{25,17},{29,21},{2,10},{... | collective-permute-start | bytes 3145736 | tf_op jit(solution)/shard_map/ppermute | solution.py:475
  377.4 47.5 %collective-permute-start.20 = (bf16[2,512,512]{2,1,0:T(8,128)(2,1)}, bf16[2,512,512]{2,1,0:T(8,128)(2,1)}, u32[]{:S(2)}, u32[]{:S(2)}) collective-permute-start(bf16[2,512,512]{2,1,0:T(8,128)(2,1)} %proj_part.11), channel_id=1, source_target_pairs={{0,8},{4,12},{24,16},{28,20},{1,9},{5,13},{25,17},{29,21},{2,10},{... | collective-permute-start | bytes 3145736 | tf_op jit(solution)/shard_map/ppermute | solution.py:475
  378.7 48.7 %collective-permute-start.17 = (bf16[2,512,512]{2,1,0:T(8,128)(2,1)}, bf16[2,512,512]{2,1,0:T(8,128)(2,1)}, u32[]{:S(2)}, u32[]{:S(2)}) collective-permute-start(bf16[2,512,512]{2,1,0:T(8,128)(2,1)} %proj_part.12), channel_id=1, source_target_pairs={{0,4},{4,0},{8,12},{12,8},{16,20},{20,16},{24,28},{28,24},{1,5},{5... | collective-permute-start | bytes 3145736 | tf_op jit(solution)/shard_map/ppermute | solution.py:475
  381.2 43.6 %copy-start.9 = (bf16[2,512,512]{2,1,0:T(8,128)(2,1)S(1)}, bf16[2,512,512]{2,1,0:T(8,128)(2,1)}, u32[]{:S(2)}) copy-start(bf16[2,512,512]{2,1,0:T(8,128)(2,1)} %proj_part.11) | copy-start | bytes 3145732
  407.2 41.8 %collective-permute-start.16 = (bf16[2,512,512]{2,1,0:T(8,128)(2,1)}, bf16[2,512,512]{2,1,0:T(8,128)(2,1)}, u32[]{:S(2)}, u32[]{:S(2)}) collective-permute-start(bf16[2,512,512]{2,1,0:T(8,128)(2,1)} %add_convert_fusion.1), channel_id=1, source_target_pairs={{8,16},{12,20},{16,8},{20,12},{9,17},{13,21},{17,9},{21,13},{10,18... | collective-permute-start | bytes 3145736 | tf_op jit(solution)/shard_map/ppermute | solution.py:475
  427.4 42.0 %collective-permute-start.21 = (bf16[2,512,512]{2,1,0:T(8,128)(2,1)}, bf16[2,512,512]{2,1,0:T(8,128)(2,1)}, u32[]{:S(2)}, u32[]{:S(2)}) collective-permute-start(bf16[2,512,512]{2,1,0:T(8,128)(2,1)} %add_convert_fusion), channel_id=1, source_target_pairs={{8,16},{12,20},{16,8},{20,12},{9,17},{13,21},{17,9},{21,13},{10,18... | collective-permute-start | bytes 3145736 | tf_op jit(solution)/shard_map/ppermute | solution.py:475
  439.8 56.2 %collective-permute-start.11 = (bf16[1024,1024]{1,0:T(8,128)(2,1)}, bf16[1024,1024]{1,0:T(8,128)(2,1)}, u32[]{:S(2)}, u32[]{:S(2)}) collective-permute-start(bf16[1024,1024]{1,0:T(8,128)(2,1)} %layer_part.4), channel_id=1, source_target_pairs={{0,2},{1,3},{2,0},{3,1},{4,6},{5,7},{6,4},{7,5},{8,10},{9,11},{10,... | collective-permute-start | bytes 6291464 | tf_op jit(solution)/shard_map/ppermute | solution.py:498
  447.2 13.4 %collective-permute-start.14 = (bf16[512,512]{1,0:T(8,128)(2,1)}, bf16[512,512]{1,0:T(8,128)(2,1)}, u32[]{:S(2)}, u32[]{:S(2)}) collective-permute-start(bf16[512,512]{1,0:T(8,128)(2,1)} %bitcast.53), channel_id=1, source_target_pairs={{0,8},{4,12},{24,16},{28,20},{1,9},{5,13},{25,17},{29,21},{2,10},{... | collective-permute-start | bytes 1572872 | tf_op jit(solution)/shard_map/ppermute | solution.py:475
  460.6 30.9 %collective-permute-start.18 = (bf16[512,512]{1,0:T(8,128)(2,1)}, bf16[512,512]{1,0:T(8,128)(2,1)}, u32[]{:S(2)}, u32[]{:S(2)}) collective-permute-start(bf16[512,512]{1,0:T(8,128)(2,1)} %fusion.3), channel_id=1, source_target_pairs={{8,0},{12,4},{16,24},{20,28},{9,1},{13,5},{17,25},{21,29},{10,2},{... | collective-permute-start | bytes 1572872 | tf_op jit(solution)/shard_map/ppermute | solution.py:475
  468.0 25.1 %collective-permute-start.19 = (bf16[512,512]{1,0:T(8,128)(2,1)}, bf16[512,512]{1,0:T(8,128)(2,1)}, u32[]{:S(2)}, u32[]{:S(2)}) collective-permute-start(bf16[512,512]{1,0:T(8,128)(2,1)} %bitcast.52), channel_id=1, source_target_pairs={{0,8},{4,12},{24,16},{28,20},{1,9},{5,13},{25,17},{29,21},{2,10},{... | collective-permute-start | bytes 1572872 | tf_op jit(solution)/shard_map/ppermute | solution.py:475
  471.5 20.0 %copy-start.11 = (bf16[1,512,512]{2,1,0:T(8,128)(2,1)S(1)}, bf16[1,512,512]{2,1,0:T(8,128)(2,1)}, u32[]{:S(2)}) copy-start(bf16[1,512,512]{2,1,0:T(8,128)(2,1)} %get-tuple-element.82) | copy-start | bytes 1572868
  471.5 21.7 %collective-permute-start.22 = (bf16[512,512]{1,0:T(8,128)(2,1)}, bf16[512,512]{1,0:T(8,128)(2,1)}, u32[]{:S(2)}, u32[]{:S(2)}) collective-permute-start(bf16[512,512]{1,0:T(8,128)(2,1)} %fusion), channel_id=1, source_target_pairs={{8,0},{12,4},{16,24},{20,28},{9,1},{13,5},{17,25},{21,29},{10,2},{... | collective-permute-start | bytes 1572872 | tf_op jit(solution)/shard_map/ppermute | solution.py:475
  491.4 1.7 copy-start.12
  505.2 1.6 copy-start.7

commit v5 on v3

--- a/solution.py
+++ b/solution.py
@@ -487,20 +487,31 @@
     return lax.all_to_all(chunks, "ctx", split_axis=0, concat_axis=0, tiled=True)
 
 
-def scatter_layer(ids, flat, blocks, heads_n):
-    mine = lax.axis_index("head").astype(jnp.int32)
-    per = len(blocks) // heads_n
-
-    def wanted(offsets):
-        return jnp.stack([(mine ^ g) * per + b for g in offsets for b in range(per)]).astype(jnp.int32)
-
-    def move(part, g):
-        return lax.ppermute(part, "head", [(place, place ^ g) for place in range(heads_n)])
-
-    even = list(range(0, heads_n, 2))
-    near = move(layer_part(ids, flat, blocks, wanted([g + 1 for g in even]), [], []), 1)
-    far = [move(layer_part(ids, flat, blocks, wanted([g]), [near], [g // 2 * per]), g) for g in even[1:]]
-    return layer_part(ids, flat, blocks, wanted([0]), [near] + far, [0] * (1 + len(far)))
+class LayerSum:
+    def __init__(self, ids, flat, blocks, heads_n):
+        self.ids, self.flat, self.blocks, self.heads_n = ids, flat, blocks, heads_n
+        self.mine = lax.axis_index("head").astype(jnp.int32)
+        self.per = len(blocks) // heads_n
+        self.even = list(range(0, heads_n, 2))
+
+    def part(self, offsets, extra, first):
+        wanted = [(self.mine ^ g) * self.per + b for g in offsets for b in range(self.per)]
+        wanted = jnp.stack(wanted).astype(jnp.int32)
+        return layer_part(self.ids, self.flat, self.blocks, wanted, extra, first)
+
+    def move(self, part, g):
+        return lax.ppermute(part, "head", [(place, place ^ g) for place in range(self.heads_n)])
+
+    def start(self):
+        self.first = self.part([g + 1 for g in self.even], [], [])
+        self.near = self.move(self.first, 1)
+
+    def turn(self, done):
+        self.flat = after(self.flat, done)
+        self.far = [self.move(self.part([g], [self.near], [g // 2 * self.per]), g) for g in self.even[1:]]
+
+    def finish(self):
+        return self.part([0], [self.near] + self.far, [0] * (1 + len(self.far)))
 
 
 def on_device(queries, keys, values, out_grad, wo, *, n, heads_n):
@@ -515,14 +526,34 @@
     def around(block):
         return [block if e == 0 else links.flip(block, e) for e in range(inner)]
 
+    def targets(owners, e):
+        return jnp.stack([owner * inner + (spot ^ e) for owner in owners]).astype(jnp.int32)
+
+    def leaving(flat, owners):
+        return [proj_part(targets(owners, e), flat, out_grad, [], depth, dim, 0)[0] for e in range(1, inner)]
+
+    def exchanged(parts):
+        return [links.flip(part, e + 1) for e, part in enumerate(parts)]
+
+    def summed(flat, owners, theirs, lead):
+        return proj_part(targets(owners, 0), flat, out_grad, theirs, depth, dim, lead)
+
+    def add(*terms):
+        return sum(term.astype(F32) for term in terms).astype(BF16)
+
+    everyone = [line ^ 1, *far, line]
     near = links.along(wo, PAIRS)
     cross_own = links.along(wo, CROSS)
     own_blocks = around(wo)
     chunks, by_head = split_inputs(queries, keys, values, n)
-    chunks, near = swap(chunks), after(near, chunks)
+    row_out = row_forward(*by_head)
+    row_theirs = leaving(row_out, everyone)
+    near = after(near, chunks)
     near_blocks = around(near)
     cross_near = links.along(near, CROSS)
-    far_own = jnp.where(middle, cross_own, links.along(cross_own, OUTWARD))
+    out_own = links.along(cross_own, OUTWARD)
+    chunks = swap(after(chunks, *near_blocks, cross_near, out_own, *row_theirs))
+    far_own = jnp.where(middle, cross_own, out_own)
     far_own_blocks = around(far_own)
     far_near = jnp.where(middle, cross_near, links.along(cross_near, OUTWARD))
     far_near_blocks = around(far_near)
@@ -530,56 +561,38 @@
     ids = [owner * inner + (spot ^ e) for owner in (line, line ^ 1, *far) for e in range(inner)]
     ids = jnp.stack(ids).astype(jnp.int32)
 
-    def targets(owners, e):
-        return jnp.stack([owner * inner + (spot ^ e) for owner in owners]).astype(jnp.int32)
-
-    def exchanged(flat, owners):
-        return [
-            links.flip(proj_part(targets(owners, e), flat, out_grad, [], depth, dim, 0)[0], e) for e in range(1, inner)
-        ]
-
-    def summed(flat, owners, theirs, lead):
-        return proj_part(targets(owners, 0), flat, out_grad, theirs, depth, dim, lead)
-
-    def add(*terms):
-        return sum(term.astype(F32) for term in terms).astype(BF16)
-
-    row_out = row_forward(*(after(tensor, near) for tensor in by_head))
-    row_far = exchanged(row_out, far)
-    row_close = exchanged(row_out, close)
-
-    outs = column_forward(chunks)
+    row_theirs = exchanged(row_theirs)
+    outs = column_forward(after(chunks, *far_own_blocks))
     column_part = swap(outs)
     grad_row, grads = attn_grad(ids, after(out_grad, outs), blocks, dim)
-    grads = swap(after(grads, column_part))
+    grads = swap(after(grads, column_part, *row_theirs))
     column_out, flat = collect(row_out, column_part)
-    column_far = exchanged(column_out, far)
-    column_close = exchanged(column_out, close)
-    gradients = column_backward(chunks, grads)
+    column_far, column_close = leaving(column_out, far), leaving(column_out, close)
+    layer = LayerSum(ids, flat, blocks, heads_n)
+    layer.start()
+    gradients = column_backward(chunks, after(grads, *column_far, *column_close, layer.first))
+    column_far, column_close = exchanged(column_far), exchanged(column_close)
     column_grads = swap(gradients)
 
-    (row_far,) = summed(after(row_out, column_out), far, row_far, 0)
-    row_far_in = links.along(row_far, INWARD)
-    row_near, row_own = summed(after(row_out, column_out), close, row_close, 1)
-    row_near_in = links.along(row_near[0], INWARD)
+    row_lead, row_own = summed(after(row_out, gradients), everyone, row_theirs, 3)
+    row_in = links.along(row_lead, INWARD)
+    layer.turn(gradients)
     (column_far,) = summed(after(column_out, gradients), far, column_far, 0)
     column_far_in = links.along(column_far, INWARD)
-    row_cross = links.along(add(row_far, row_far_in), CROSS)
+    row_grads = row_backward(*by_head, after(grad_row, column_far))
     column_near, column_own = summed(after(column_out, gradients), close, column_close, 1)
+    row_cross = links.along(add(row_lead[1:], row_in[1:]), CROSS)
+    column_cross = links.along(add(column_far, after(column_far_in, row_grads[0])), CROSS)
     column_near_in = links.along(column_near[0], INWARD)
-    column_cross = links.along(add(column_far, column_far_in), CROSS)
-    row_back = links.along(add(row_near[0], row_cross[1]), OUTWARD)
+    row_back = links.along(add(row_lead[0], row_cross[1]), OUTWARD)
     column_back = links.along(add(column_near[0], column_cross[1]), OUTWARD)
 
-    layer_out = scatter_layer(ids, after(flat, gradients), blocks, heads_n)
-    row_grads = row_backward(*by_head, after(grad_row, gradients))
     gradients = join_gradients(column_grads, row_grads)
-
-    proj_row = add(row_own[0], row_near_in, row_cross[0], row_back)
+    proj_row = add(row_own[0], row_in[0], row_cross[0], row_back)
     proj_column = add(column_own[0], column_near_in, column_cross[0], column_back)
     shape = (half, dim, depth)
     proj_grad = jnp.stack([proj_row.reshape(shape), proj_column.reshape(shape)], axis=1)
-    return (layer_out, *gradients, proj_grad.reshape(heads * dim, depth))
+    return (layer.finish(), *gradients, proj_grad.reshape(heads * dim, depth))
 
 
 def solution(mesh):

time: 516 us -> 499 us (0.967)
  waiting for transfers between devices: 263 us -> 247 us
  Pallas kernels: 153 us -> 146 us
    ppermute x21 -> x19, waiting for transfers between devices: 257 us -> 247 us  [send(): out = lax.ppermute(value, 'ctx', pairs)]
    all_to_all x4, waiting for transfers between devices: 6.3 us -> 0.01 us  [swap(): lax.all_to_all(chunks, 'ctx', split_axis=0, concat_axis=0, tiled=True)]
    pallas_call x8 -> x6, Pallas kernels: 40 us -> 34.7 us  [proj_part(): pl.pallas_call(functools.partial(proj_kernel, lead, len(extra), dim), gri...]
    ppermute x21 -> x19, starting transfers between devices: 43 us -> 40.5 us  [send(): out = lax.ppermute(value, 'ctx', pairs)]
  transfers between devices with their start and end apart: 27 -> 25, of which waited for: 14 -> 11; matrix products, arithmetic and copies ran while one was open for 5% -> 5% of each run, Pallas kernels for 22% -> 28%
where the time goes in v5:
time: 499 us; the launch traced here: 494 us
  waiting for transfers between devices  247 us (49%)
  Pallas kernels  146 us (29%)
  starting transfers between devices  68.3 us (14%)
  other arithmetic  22.3 us (4%)
  local copies, waits for them, and re-layouts  9.6 us (2%)
    ppermute x19, waiting for transfers between devices, send(): out = lax.ppermute(value, 'ctx', pairs)  247 us
    ppermute x19, starting transfers between devices, send(): out = lax.ppermute(value, 'ctx', pairs)  40.5 us
    pallas_call x6, Pallas kernels, proj_part(): pl.pallas_call(functools.partial(proj_kernel, lead, len(extra), dim), gri...  34.7 us
    pallas_call x3, Pallas kernels, layer_part(): pl.pallas_call(functools.partial(layer_kernel, n, count, len(extra)), gri...  29.3 us
    all_to_all x4, starting transfers between devices, swap(): lax.all_to_all(chunks, 'ctx', split_axis=0, concat_axis=0, tiled=True)  26.1 us
    pallas_call x1, Pallas kernels, attn_grad(): pl.pallas_call(functools.partial(attn_grad_kernel, n, dim), grid_spec=plt...  21.1 us
    pallas_call x1, Pallas kernels, row_backward(): pl.pallas_call(functools.partial(row_backward_kernel, dim ** (-0.5)), gri...  13.6 us
    convert_element_type x6, other arithmetic, add(): return sum((term.astype(F32) for term in terms)).astype(BF16)  13 us
  transfers between devices with their start and end apart: 25, of which 11 were waited for; matrix products, arithmetic and copies ran while one was open for 5% of the time, Pallas kernels for 28%

profile of v5, /device:TPU:8, one launch (start us, length us, event | category | flops | bytes accessed | tf_op | source)
XLA Modules:
  0.0 494.2 jit_solution(13791295694203585066)
XLA Ops:
  0.7 5.0 %collective-permute-start.3 = (bf16[1024,512]{1,0:T(8,128)(2,1)}, bf16[1024,512]{1,0:T(8,128)(2,1)S(1)}, u32[]{:S(2)}, u32[]{:S(2)}) collective-permute-start(bf16[1024,512]{1,0:T(8,128)(2,1)} %refs_0_.7), channel_id=1, source_target_pairs={{8,16},{12,20},{16,8},{20,12},{9,17},{13,21},{17,9},{21,13},{10,18... | collective-permute-start | bytes 3145736 | tf_op jit(solution)/shard_map/ppermute | solution.py:475
  5.8 7.1 %split_inputs.1 = (bf16[8,3,4,2,64,128]{5,4,3,2,1,0:T(8,128)(2,1)}, bf16[4,1024,128]{2,1,0:T(8,128)(2,1)}, bf16[4,1024,128]{2,1,0:T(8,128)(2,1)}, bf16[4,1024,128]{2,1,0:T(8,128)(2,1)}) custom-call(bf16[1024,8,128]{2,1,0:T(8,128)(2,1)} %q_ref.1, bf16[1024,8,128]{2,1,0:T(8,128)(2,1)} %k_ref.1, bf16[1024,8,128]{2,1,0:T(8,128)(2,1)} %v_ref.1), custom_call_target="tpu_custom_call" | custom-call | tf_op jit(solution)/shard_map/split_inputs/pallas_call | solution.py:48
  12.9 12.9 %collective-permute-done.refs_2_ = bf16[1024,512]{1,0:T(8,128)(2,1)S(1)} collective-permute-done((bf16[1024,512]{1,0:T(8,128)(2,1)}, bf16[1024,512]{1,0:T(8,128)(2,1)S(1)}, u32[]{:S(2)}, u32[]{:S(2)}) %collective-permute-start) | collective-permute-done | bytes 1048608 | tf_op jit(solution)/shard_map/ppermute | solution.py:475
  27.3 3.5 collective-permute-start.2
  30.8 2.3 collective-permute-start.4
  33.1 9.9 %row_forward.1.flat_ref.row_ref = bf16[1024,512]{1,0:T(8,128)(2,1)} custom-call(bf16[4,1024,128]{2,1,0:T(8,128)(2,1)} %get-tuple-element.48.q_ref, bf16[4,1024,128]{2,1,0:T(8,128)(2,1)} %get-tuple-element.49.k_ref, bf16[4,1024,128]{2,1,0:T(8,128)(2,1)} %get-tuple-element.50.v_ref), custom_call_target="tpu_custom_call" | custom-call | flops 1073741824 | bytes 4194304 | tf_op jit(solution)/shard_map/row_forward/pallas_call | solution.py:311
  43.6 7.1 %proj_part.6 = bf16[4,512,512]{2,1,0:T(8,128)(2,1)} custom-call(s32[4]{0:T(128)} %pad_add_fusion.1.order, bf16[1024,512]{1,0:T(8,128)(2,1)} %row_forward.1.flat_ref.row_ref, bf16[1024,4096]{1,0:T(8,128)(2,1)} %grad_ref.12), custom_call_target="tpu_custom_call" | custom-call | flops 2147483648 | bytes 7340032 | tf_op jit(solution)/shard_map/proj_part/pallas_call | solution.py:265
  50.7 2.4 collective-permute-done.2
  53.4 6.6 %all-to-all-start = ((bf16[8,3,4,2,64,128]{5,4,3,2,1,0:T(8,128)(2,1)}), bf16[8,3,4,2,64,128]{5,4,3,2,1,0:T(8,128)(2,1)S(1)}, u32[]{:S(2)}, u32[]{:S(2)}) async-start(bf16[8,3,4,2,64,128]{5,4,3,2,1,0:T(8,128)(2,1)} %get-tuple-element.54), calls=%async_computation | async-start | bytes 6291456 | tf_op jit(solution)/shard_map/all_to_all | solution.py:487
  61.5 52.6 %collective-permute-done.6.refs_1_ = bf16[1024,512]{1,0:T(8,128)(2,1)} collective-permute-done((bf16[1024,512]{1,0:T(8,128)(2,1)}, bf16[1024,512]{1,0:T(8,128)(2,1)}, u32[]{:S(2)}, u32[]{:S(2)}) %collective-permute-start.6) | collective-permute-done | bytes 1048608 | tf_op jit(solution)/shard_map/ppermute | solution.py:475
  114.1 5.3 %collective-permute-start.7 = (bf16[1024,512]{1,0:T(8,128)(2,1)}, bf16[1024,512]{1,0:T(8,128)(2,1)}, u32[]{:S(2)}, u32[]{:S(2)}) collective-permute-start(bf16[1024,512]{1,0:T(8,128)(2,1)} %collective-permute-done.2), channel_id=1, source_target_pairs={{8,0},{12,4},{16,24},{20,28},{9,1},{13,5},{17,25},{21,29},{10,2},{... | collective-permute-start | bytes 3145736 | tf_op jit(solution)/shard_map/ppermute | solution.py:475
  120.9 2.0 collective-permute-start.9
  122.9 25.9 %collective-permute-done.7 = bf16[1024,512]{1,0:T(8,128)(2,1)} collective-permute-done((bf16[1024,512]{1,0:T(8,128)(2,1)}, bf16[1024,512]{1,0:T(8,128)(2,1)}, u32[]{:S(2)}, u32[]{:S(2)}) %collective-permute-start.7) | collective-permute-done | bytes 1048608 | tf_op jit(solution)/shard_map/ppermute | solution.py:475
  148.8 2.3 broadcast_select_fusion.refs_6_
  151.1 8.7 %column_forward.1 = bf16[8,4,2,64,128]{4,3,2,1,0:T(8,128)(2,1)S(1)} custom-call(bf16[8,3,4,2,64,128]{5,4,3,2,1,0:T(8,128)(2,1)S(1)} %all-to-all-done.chunk_ref), custom_call_target="tpu_custom_call" | custom-call | flops 536870912 | bytes 4194304 | tf_op jit(solution)/shard_map/column_forward/pallas_call | solution.py:403
  160.7 7.0 %all-to-all-start.1 = ((bf16[8,4,2,64,128]{4,3,2,1,0:T(8,128)(2,1)}), bf16[8,4,2,64,128]{4,3,2,1,0:T(8,128)(2,1)}, u32[]{:S(2)}, u32[]{:S(2)}) async-start(bf16[8,4,2,64,128]{4,3,2,1,0:T(8,128)(2,1)} %copy-done.4), calls=%async_computation.1 | async-start | bytes 2097152 | tf_op jit(solution)/shard_map/all_to_all | solution.py:487
  168.4 52.1 %collective-permute-done.8.refs_7_ = bf16[1024,512]{1,0:T(8,128)(2,1)} collective-permute-done((bf16[1024,512]{1,0:T(8,128)(2,1)}, bf16[1024,512]{1,0:T(8,128)(2,1)}, u32[]{:S(2)}, u32[]{:S(2)}) %collective-permute-start.8) | collective-permute-done | bytes 1048608 | tf_op jit(solution)/shard_map/ppermute | solution.py:475
  220.6 21.1 %attn_grad.1 = (bf16[1024,512]{1,0:T(8,128)(2,1)}, bf16[8,4,2,64,128]{4,3,2,1,0:T(8,128)(2,1)}) custom-call(s32[8]{0:T(128)} %stack.105.ids, bf16[1024,4096]{1,0:T(8,128)(2,1)} %grad_ref.12, bf16[1024,512]{1,0:T(8,128)(2,1)} %refs_0_.7, bf16[1024,512]{1,0:T(8,128)(2,1)} %collective-permute-done.6.refs_1_, bf16[1024,512]{1,0:T(8,128)(2,1)} %copy-done.7, ...), custom_call_target="tpu_custom_call" | custom-call | flops 8589934592 | bytes 18874368 | tf_op jit(solution)/shard_map/attn_grad/pallas_call | solution.py:153
  241.6 6.4 %all-to-all-start.2 = ((bf16[8,4,2,64,128]{4,3,2,1,0:T(8,128)(2,1)}), bf16[8,4,2,64,128]{4,3,2,1,0:T(8,128)(2,1)}, u32[]{:S(2)}, u32[]{:S(2)}) async-start(bf16[8,4,2,64,128]{4,3,2,1,0:T(8,128)(2,1)} %get-tuple-element.63), calls=%async_computation.2 | async-start | bytes 2097152 | tf_op jit(solution)/shard_map/all_to_all | solution.py:487
  249.9 1.9 collect.1
  254.1 11.7 %layer_part.3 = bf16[1024,2048]{1,0:T(8,128)(2,1)} custom-call(s32[8]{0:T(128)} %stack.105.ids, s32[4]{0:T(128)} %pad_add_fusion.4.wanted, bf16[1024,1024]{1,0:T(8,128)(2,1)} %copy-done.3, bf16[1024,512]{1,0:T(8,128)(2,1)} %refs_0_.7, bf16[1024,512]{1,0:T(8,128)(2,1)} %collective-permute-done.6.refs_1_, bf16[1024,512]{1,0:T(8,128)(2,1)} %copy-done.7, ...), custom_call_target="tpu_custom_call" | custom-call | flops 4294967296 | bytes 10485760 | tf_op jit(solution)/shard_map/layer_part/pallas_call | solution.py:211
  267.1 4.8 proj_part.7
  271.9 4.8 proj_part.8
  276.8 12.9 %column_backward.1 = bf16[8,3,4,2,64,128]{5,4,3,2,1,0:T(8,128)(2,1)S(1)} custom-call(bf16[8,3,4,2,64,128]{5,4,3,2,1,0:T(8,128)(2,1)S(1)} %all-to-all-done.chunk_ref, bf16[8,4,2,64,128]{4,3,2,1,0:T(8,128)(2,1)} %all-to-all-done.2.grad_ref), custom_call_target="tpu_custom_call" | custom-call | flops 1342177280 | bytes 7340032 | tf_op jit(solution)/shard_map/column_backward/pallas_call | solution.py:441
  289.7 1.7 copy-done.2
  291.4 6.0 %all-to-all-start.3 = ((bf16[8,3,4,2,64,128]{5,4,3,2,1,0:T(8,128)(2,1)}), bf16[8,3,4,2,64,128]{5,4,3,2,1,0:T(8,128)(2,1)S(1)}, u32[]{:S(2)}, u32[]{:S(2)}) async-start(bf16[8,3,4,2,64,128]{5,4,3,2,1,0:T(8,128)(2,1)} %copy-done.2), calls=%async_computation.3 | async-start | bytes 6291456 | tf_op jit(solution)/shard_map/all_to_all | solution.py:487
  299.5 7.7 %proj_part.10 = (bf16[3,512,512]{2,1,0:T(8,128)(2,1)}, bf16[1,512,512]{2,1,0:T(8,128)(2,1)}) custom-call(s32[4]{0:T(128)} %pad_add_fusion.7.order, bf16[1024,512]{1,0:T(8,128)(2,1)} %row_forward.1.flat_ref.row_ref, bf16[1024,4096]{1,0:T(8,128)(2,1)} %grad_ref.12, bf16[4,512,512]{2,1,0:T(8,128)(2,1)} %collective-permute-done.9.refs_0_), custom_call_target="tpu_custom_call" | custom-call | flops 2147483648 | bytes 9437184 | tf_op jit(solution)/shard_map/proj_part/pallas_call | solution.py:265
  309.0 45.2 %collective-permute-done.12.refs_0_ = bf16[2,512,512]{2,1,0:T(8,128)(2,1)} collective-permute-done((bf16[2,512,512]{2,1,0:T(8,128)(2,1)}, bf16[2,512,512]{2,1,0:T(8,128)(2,1)}, u32[]{:S(2)}, u32[]{:S(2)}) %collective-permute-start.12) | collective-permute-done | bytes 1048608 | tf_op jit(solution)/shard_map/ppermute | solution.py:475
  354.2 5.0 %proj_part.9 = bf16[2,512,512]{2,1,0:T(8,128)(2,1)} custom-call(s32[2]{0:T(128)} %pad_add_fusion.6.order, bf16[1024,512]{1,0:T(8,128)(2,1)} %copy-done.1, bf16[1024,4096]{1,0:T(8,128)(2,1)} %grad_ref.12, bf16[2,512,512]{2,1,0:T(8,128)(2,1)} %collective-permute-done.12.refs_0_), custom_call_target="tpu_custom_call" | custom-call | flops 1073741824 | bytes 5242880 | tf_op jit(solution)/shard_map/proj_part/pallas_call | solution.py:265
  361.1 2.5 collective-permute-start.15
  363.6 13.6 %row_backward.1 = (bf16[4,1024,128]{2,1,0:T(8,128)(2,1)}, bf16[4,1024,128]{2,1,0:T(8,128)(2,1)}, bf16[4,1024,128]{2,1,0:T(8,128)(2,1)}) custom-call(bf16[4,1024,128]{2,1,0:T(8,128)(2,1)} %get-tuple-element.48.q_ref, bf16[4,1024,128]{2,1,0:T(8,128)(2,1)} %get-tuple-element.49.k_ref, bf16[4,1024,128]{2,1,0:T(8,128)(2,1)} %get-tuple-element.50.v_ref, ...), custom_call_target="tpu_custom_call" | custom-call | flops 2684354560 | bytes 7340032 | tf_op jit(solution)/shard_map/row_backward/pallas_call | solution.py:345
  377.2 29.6 %collective-permute-done.18 = bf16[2,512,512]{2,1,0:T(8,128)(2,1)} collective-permute-done((bf16[2,512,512]{2,1,0:T(8,128)(2,1)}, bf16[2,512,512]{2,1,0:T(8,128)(2,1)}, u32[]{:S(2)}, u32[]{:S(2)}) %collective-permute-start.18) | collective-permute-done | bytes 1048608 | tf_op jit(solution)/shard_map/ppermute | solution.py:475
  406.8 2.8 add_convert_fusion
  409.6 3.4 collective-permute-start.19
  413.0 2.5 add_convert_fusion.1
  415.5 2.4 collective-permute-start.14
  418.0 8.5 %layer_part.4 = bf16[1024,1024]{1,0:T(8,128)(2,1)} custom-call(s32[8]{0:T(128)} %stack.105.ids, s32[2]{0:T(128)} %pad_add_fusion.5.wanted, bf16[1024,1024]{1,0:T(8,128)(2,1)} %copy-done.3, bf16[1024,512]{1,0:T(8,128)(2,1)} %refs_0_.7, bf16[1024,512]{1,0:T(8,128)(2,1)} %collective-permute-done.6.refs_1_, bf16[1024,512]{1,0:T(8,128)(2,1)} %copy-done.7, ...), custom_call_target="tpu_custom_call" | custom-call | flops 2147483648 | bytes 6291456 | tf_op jit(solution)/shard_map/layer_part/pallas_call | solution.py:211
  428.6 5.2 %proj_part.11 = (bf16[1,512,512]{2,1,0:T(8,128)(2,1)}, bf16[1,512,512]{2,1,0:T(8,128)(2,1)}) custom-call(s32[2]{0:T(128)} %pad_add_fusion.8.order, bf16[1024,512]{1,0:T(8,128)(2,1)} %copy-done.1, bf16[1024,4096]{1,0:T(8,128)(2,1)} %grad_ref.12, bf16[2,512,512]{2,1,0:T(8,128)(2,1)} %collective-permute-done.15.refs_0_), custom_call_target="tpu_custom_call" | custom-call | flops 1073741824 | bytes 5242880 | tf_op jit(solution)/shard_map/proj_part/pallas_call | solution.py:265
  435.2 2.7 collective-permute-done.19
  437.9 2.1 fusion
  440.0 3.5 collective-permute-start.20
  443.5 15.5 %collective-permute-done.14 = bf16[2,512,512]{2,1,0:T(8,128)(2,1)} collective-permute-done((bf16[2,512,512]{2,1,0:T(8,128)(2,1)}, bf16[2,512,512]{2,1,0:T(8,128)(2,1)}, u32[]{:S(2)}, u32[]{:S(2)}) %collective-permute-start.14) | collective-permute-done | bytes 1048608 | tf_op jit(solution)/shard_map/ppermute | solution.py:475
  459.0 2.1 fusion.4
  461.2 2.1 collective-permute-start.16
  463.9 1.8 fusion.2
  465.7 7.5 %collective-permute-done.16 = bf16[512,512]{1,0:T(8,128)(2,1)} collective-permute-done((bf16[512,512]{1,0:T(8,128)(2,1)}, bf16[512,512]{1,0:T(8,128)(2,1)}, u32[]{:S(2)}, u32[]{:S(2)}) %collective-permute-start.16) | collective-permute-done | bytes 524320 | tf_op jit(solution)/shard_map/ppermute | solution.py:475
  476.0 9.2 %layer_part.5 = bf16[1024,1024]{1,0:T(8,128)(2,1)} custom-call(s32[8]{0:T(128)} %stack.105.ids, s32[2]{0:T(128)} %pad_add_fusion.wanted, bf16[1024,1024]{1,0:T(8,128)(2,1)} %copy-done.3, bf16[1024,512]{1,0:T(8,128)(2,1)} %refs_0_.7, bf16[1024,512]{1,0:T(8,128)(2,1)} %collective-permute-done.6.refs_1_, bf16[1024,512]{1,0:T(8,128)(2,1)} %copy-done.7, ...), custom_call_target="tpu_custom_call" | custom-call | flops 2147483648 | bytes 6291456 | tf_op jit(solution)/shard_map/layer_part/pallas_call | solution.py:211
  486.9 7.3 %join_gradients.1 = (bf16[1024,8,128]{2,1,0:T(8,128)(2,1)}, bf16[1024,8,128]{2,1,0:T(8,128)(2,1)}, bf16[1024,8,128]{2,1,0:T(8,128)(2,1)}) custom-call(bf16[8,3,4,2,64,128]{5,4,3,2,1,0:T(8,128)(2,1)} %copy-done.5, bf16[4,1024,128]{2,1,0:T(8,128)(2,1)} %get-tuple-element.71.refs_0_, bf16[4,1024,128]{2,1,0:T(8,128)(2,1)} %get-tuple-element.72.refs_1_, ...), custom_call_target="tpu_custom_call" | custom-call | tf_op jit(solution)/shard_map/join_gradients/pallas_call | solution.py:78
  (63 shorter events, 27.0 us)
Async XLA Ops:
  0.6 25.2 %collective-permute-start = (bf16[1024,512]{1,0:T(8,128)(2,1)}, bf16[1024,512]{1,0:T(8,128)(2,1)S(1)}, u32[]{:S(2)}, u32[]{:S(2)}) collective-permute-start(bf16[1024,512]{1,0:T(8,128)(2,1)} %refs_0_.7), channel_id=1, source_target_pairs={{0,8},{4,12},{8,0},{12,4},{16,24},{20,28},{24,16},{28,20},{1,9},{5... | collective-permute-start | bytes 3145736 | tf_op jit(solution)/shard_map/ppermute | solution.py:475
  0.7 30.1 %collective-permute-start.3 = (bf16[1024,512]{1,0:T(8,128)(2,1)}, bf16[1024,512]{1,0:T(8,128)(2,1)S(1)}, u32[]{:S(2)}, u32[]{:S(2)}) collective-permute-start(bf16[1024,512]{1,0:T(8,128)(2,1)} %refs_0_.7), channel_id=1, source_target_pairs={{8,16},{12,20},{16,8},{20,12},{9,17},{13,21},{17,9},{21,13},{10,18... | collective-permute-start | bytes 3145736 | tf_op jit(solution)/shard_map/ppermute | solution.py:475
  25.8 17.2 %copy-start.7 = (bf16[1024,512]{1,0:T(8,128)(2,1)}, bf16[1024,512]{1,0:T(8,128)(2,1)S(1)}, u32[]{:S(2)}) copy-start(bf16[1024,512]{1,0:T(8,128)(2,1)S(1)} %collective-permute-done.refs_2_) | copy-start | bytes 3145732
  25.8 24.9 %collective-permute-start.1 = (bf16[1024,512]{1,0:T(8,128)(2,1)S(1)}, bf16[1024,512]{1,0:T(8,128)(2,1)S(1)}, u32[]{:S(2)}, u32[]{:S(2)}) collective-permute-start(bf16[1024,512]{1,0:T(8,128)(2,1)S(1)} %collective-permute-done.refs_2_), channel_id=1, source_target_pairs={{0,4},{4,0},{8,12},{12,8},{16,20},{20,16},{24,28},{28,24},{1,5},{5... | collective-permute-start | bytes 3145736 | tf_op jit(solution)/shard_map/ppermute | solution.py:475
  27.3 25.7 %collective-permute-start.2 = (bf16[1024,512]{1,0:T(8,128)(2,1)S(1)}, bf16[1024,512]{1,0:T(8,128)(2,1)}, u32[]{:S(2)}, u32[]{:S(2)}) collective-permute-start(bf16[1024,512]{1,0:T(8,128)(2,1)S(1)} %collective-permute-done.refs_2_), channel_id=1, source_target_pairs={{8,16},{12,20},{16,8},{20,12},{9,17},{13,21},{17,9},{21,13},{10,18... | collective-permute-start | bytes 3145736 | tf_op jit(solution)/shard_map/ppermute | solution.py:475
  30.8 12.2 %copy-start.10 = (bf16[1024,512]{1,0:T(8,128)(2,1)}, bf16[1024,512]{1,0:T(8,128)(2,1)S(1)}, u32[]{:S(2)}) copy-start(bf16[1024,512]{1,0:T(8,128)(2,1)S(1)} %collective-permute-done.3) | copy-start | bytes 3145732
  30.8 22.5 %collective-permute-start.4 = (bf16[1024,512]{1,0:T(8,128)(2,1)S(1)}, bf16[1024,512]{1,0:T(8,128)(2,1)}, u32[]{:S(2)}, u32[]{:S(2)}) collective-permute-start(bf16[1024,512]{1,0:T(8,128)(2,1)S(1)} %collective-permute-done.3), channel_id=1, source_target_pairs={{8,0},{12,4},{16,24},{20,28},{9,1},{13,5},{17,25},{21,29},{10,2},{... | collective-permute-start | bytes 3145736 | tf_op jit(solution)/shard_map/ppermute | solution.py:475
  50.7 2.7 copy-start.8
  53.4 97.7 %all-to-all-start = ((bf16[8,3,4,2,64,128]{5,4,3,2,1,0:T(8,128)(2,1)}), bf16[8,3,4,2,64,128]{5,4,3,2,1,0:T(8,128)(2,1)S(1)}, u32[]{:S(2)}, u32[]{:S(2)}) async-start(bf16[8,3,4,2,64,128]{5,4,3,2,1,0:T(8,128)(2,1)} %get-tuple-element.54), calls=%async_computation | async-start | bytes 6291456 | tf_op jit(solution)/shard_map/all_to_all | solution.py:487
  60.0 54.1 %collective-permute-start.6 = (bf16[1024,512]{1,0:T(8,128)(2,1)}, bf16[1024,512]{1,0:T(8,128)(2,1)}, u32[]{:S(2)}, u32[]{:S(2)}) collective-permute-start(bf16[1024,512]{1,0:T(8,128)(2,1)} %refs_0_.7), channel_id=1, source_target_pairs={{0,4},{4,0},{8,12},{12,8},{16,20},{20,16},{24,28},{28,24},{1,5},{5... | collective-permute-start | bytes 3145736 | tf_op jit(solution)/shard_map/ppermute | solution.py:475
  114.1 34.6 %collective-permute-start.7 = (bf16[1024,512]{1,0:T(8,128)(2,1)}, bf16[1024,512]{1,0:T(8,128)(2,1)}, u32[]{:S(2)}, u32[]{:S(2)}) collective-permute-start(bf16[1024,512]{1,0:T(8,128)(2,1)} %collective-permute-done.2), channel_id=1, source_target_pairs={{8,0},{12,4},{16,24},{20,28},{9,1},{13,5},{17,25},{21,29},{10,2},{... | collective-permute-start | bytes 3145736 | tf_op jit(solution)/shard_map/ppermute | solution.py:475
  120.8 30.3 %copy-start.6 = (bf16[1024,512]{1,0:T(8,128)(2,1)}, bf16[1024,512]{1,0:T(8,128)(2,1)S(1)}, u32[]{:S(2)}) copy-start(bf16[1024,512]{1,0:T(8,128)(2,1)S(1)} %broadcast_select_fusion.1.refs_4_) | copy-start | bytes 3145732
  120.8 30.3 %collective-permute-start.5 = (bf16[1024,512]{1,0:T(8,128)(2,1)S(1)}, bf16[1024,512]{1,0:T(8,128)(2,1)}, u32[]{:S(2)}, u32[]{:S(2)}) collective-permute-start(bf16[1024,512]{1,0:T(8,128)(2,1)S(1)} %broadcast_select_fusion.1.refs_4_), channel_id=1, source_target_pairs={{0,4},{4,0},{8,12},{12,8},{16,20},{20,16},{24,28},{28,24},{1,5},{5... | collective-permute-start | bytes 3145736 | tf_op jit(solution)/shard_map/ppermute | solution.py:475
  120.9 120.8 %collective-permute-start.9 = (bf16[4,512,512]{2,1,0:T(8,128)(2,1)}, bf16[4,512,512]{2,1,0:T(8,128)(2,1)}, u32[]{:S(2)}, u32[]{:S(2)}) collective-permute-start(bf16[4,512,512]{2,1,0:T(8,128)(2,1)} %proj_part.6), channel_id=1, source_target_pairs={{0,4},{4,0},{8,12},{12,8},{16,20},{20,16},{24,28},{28,24},{1,5},{5... | collective-permute-start | bytes 6291464 | tf_op jit(solution)/shard_map/ppermute | solution.py:475
  151.1 69.5 %collective-permute-start.8 = (bf16[1024,512]{1,0:T(8,128)(2,1)}, bf16[1024,512]{1,0:T(8,128)(2,1)}, u32[]{:S(2)}, u32[]{:S(2)}) collective-permute-start(bf16[1024,512]{1,0:T(8,128)(2,1)} %broadcast_select_fusion.refs_6_), channel_id=1, source_target_pairs={{0,4},{4,0},{8,12},{12,8},{16,20},{20,16},{24,28},{28,24},{1,5},{5... | collective-permute-start | bytes 3145736 | tf_op jit(solution)/shard_map/ppermute | solution.py:475
  159.8 1.0 copy-start.4
  160.7 80.9 %all-to-all-start.1 = ((bf16[8,4,2,64,128]{4,3,2,1,0:T(8,128)(2,1)}), bf16[8,4,2,64,128]{4,3,2,1,0:T(8,128)(2,1)}, u32[]{:S(2)}, u32[]{:S(2)}) async-start(bf16[8,4,2,64,128]{4,3,2,1,0:T(8,128)(2,1)} %copy-done.4), calls=%async_computation.1 | async-start | bytes 2097152 | tf_op jit(solution)/shard_map/all_to_all | solution.py:487
  241.6 35.1 %all-to-all-start.2 = ((bf16[8,4,2,64,128]{4,3,2,1,0:T(8,128)(2,1)}), bf16[8,4,2,64,128]{4,3,2,1,0:T(8,128)(2,1)}, u32[]{:S(2)}, u32[]{:S(2)}) async-start(bf16[8,4,2,64,128]{4,3,2,1,0:T(8,128)(2,1)} %get-tuple-element.63), calls=%async_computation.2 | async-start | bytes 2097152 | tf_op jit(solution)/shard_map/all_to_all | solution.py:487
  248.7 1.2 copy-start
  251.8 1.0 copy-start.1
  252.8 1.3 copy-start.3
  265.8 152.2 %collective-permute-start.10 = (bf16[1024,2048]{1,0:T(8,128)(2,1)}, bf16[1024,2048]{1,0:T(8,128)(2,1)}, u32[]{:S(2)}, u32[]{:S(2)}) collective-permute-start(bf16[1024,2048]{1,0:T(8,128)(2,1)} %layer_part.3), channel_id=1, source_target_pairs={{0,1},{1,0},{2,3},{3,2},{4,5},{5,4},{6,7},{7,6},{8,9},{9,8},{10,11... | collective-permute-start | bytes 12582920 | tf_op jit(solution)/shard_map/ppermute | solution.py:503
  289.7 1.7 copy-start.2
  291.4 193.9 %all-to-all-start.3 = ((bf16[8,3,4,2,64,128]{5,4,3,2,1,0:T(8,128)(2,1)}), bf16[8,3,4,2,64,128]{5,4,3,2,1,0:T(8,128)(2,1)S(1)}, u32[]{:S(2)}, u32[]{:S(2)}) async-start(bf16[8,3,4,2,64,128]{5,4,3,2,1,0:T(8,128)(2,1)} %copy-done.2), calls=%async_computation.3 | async-start | bytes 6291456 | tf_op jit(solution)/shard_map/all_to_all | solution.py:487
  297.4 56.8 %collective-permute-start.12 = (bf16[2,512,512]{2,1,0:T(8,128)(2,1)}, bf16[2,512,512]{2,1,0:T(8,128)(2,1)}, u32[]{:S(2)}, u32[]{:S(2)}) collective-permute-start(bf16[2,512,512]{2,1,0:T(8,128)(2,1)} %proj_part.7), channel_id=1, source_target_pairs={{0,4},{4,0},{8,12},{12,8},{16,20},{20,16},{24,28},{28,24},{1,5},{5... | collective-permute-start | bytes 3145736 | tf_op jit(solution)/shard_map/ppermute | solution.py:475
  307.2 105.9 %collective-permute-start.13 = (bf16[3,512,512]{2,1,0:T(8,128)(2,1)}, bf16[3,512,512]{2,1,0:T(8,128)(2,1)}, u32[]{:S(2)}, u32[]{:S(2)}) collective-permute-start(bf16[3,512,512]{2,1,0:T(8,128)(2,1)} %get-tuple-element.80), channel_id=1, source_target_pairs={{0,8},{4,12},{24,16},{28,20},{1,9},{5,13},{25,17},{29,21},{2,10},{... | collective-permute-start | bytes 4718600 | tf_op jit(solution)/shard_map/ppermute | solution.py:475
  359.2 47.6 %collective-permute-start.18 = (bf16[2,512,512]{2,1,0:T(8,128)(2,1)}, bf16[2,512,512]{2,1,0:T(8,128)(2,1)}, u32[]{:S(2)}, u32[]{:S(2)}) collective-permute-start(bf16[2,512,512]{2,1,0:T(8,128)(2,1)} %proj_part.9), channel_id=1, source_target_pairs={{0,8},{4,12},{24,16},{28,20},{1,9},{5,13},{25,17},{29,21},{2,10},{... | collective-permute-start | bytes 3145736 | tf_op jit(solution)/shard_map/ppermute | solution.py:475
  361.1 67.5 %collective-permute-start.15 = (bf16[2,512,512]{2,1,0:T(8,128)(2,1)}, bf16[2,512,512]{2,1,0:T(8,128)(2,1)}, u32[]{:S(2)}, u32[]{:S(2)}) collective-permute-start(bf16[2,512,512]{2,1,0:T(8,128)(2,1)} %proj_part.8), channel_id=1, source_target_pairs={{0,4},{4,0},{8,12},{12,8},{16,20},{20,16},{24,28},{28,24},{1,5},{5... | collective-permute-start | bytes 3145736 | tf_op jit(solution)/shard_map/ppermute | solution.py:475
  377.2 35.8 %copy-start.9 = (bf16[3,512,512]{2,1,0:T(8,128)(2,1)S(1)}, bf16[3,512,512]{2,1,0:T(8,128)(2,1)}, u32[]{:S(2)}) copy-start(bf16[3,512,512]{2,1,0:T(8,128)(2,1)} %get-tuple-element.80) | copy-start | bytes 4718596
  409.6 28.3 %collective-permute-start.19 = (bf16[2,512,512]{2,1,0:T(8,128)(2,1)}, bf16[2,512,512]{2,1,0:T(8,128)(2,1)}, u32[]{:S(2)}, u32[]{:S(2)}) collective-permute-start(bf16[2,512,512]{2,1,0:T(8,128)(2,1)} %add_convert_fusion), channel_id=1, source_target_pairs={{8,16},{12,20},{16,8},{20,12},{9,17},{13,21},{17,9},{21,13},{10,18... | collective-permute-start | bytes 3145736 | tf_op jit(solution)/shard_map/ppermute | solution.py:475
  415.5 43.5 %collective-permute-start.14 = (bf16[2,512,512]{2,1,0:T(8,128)(2,1)}, bf16[2,512,512]{2,1,0:T(8,128)(2,1)}, u32[]{:S(2)}, u32[]{:S(2)}) collective-permute-start(bf16[2,512,512]{2,1,0:T(8,128)(2,1)} %add_convert_fusion.1), channel_id=1, source_target_pairs={{8,16},{12,20},{16,8},{20,12},{9,17},{13,21},{17,9},{21,13},{10,18... | collective-permute-start | bytes 3145736 | tf_op jit(solution)/shard_map/ppermute | solution.py:475
  426.4 49.6 %collective-permute-start.11 = (bf16[1024,1024]{1,0:T(8,128)(2,1)}, bf16[1024,1024]{1,0:T(8,128)(2,1)}, u32[]{:S(2)}, u32[]{:S(2)}) collective-permute-start(bf16[1024,1024]{1,0:T(8,128)(2,1)} %layer_part.4), channel_id=1, source_target_pairs={{0,2},{1,3},{2,0},{3,1},{4,6},{5,7},{6,4},{7,5},{8,10},{9,11},{10,... | collective-permute-start | bytes 6291464 | tf_op jit(solution)/shard_map/ppermute | solution.py:503
  433.9 30.0 %collective-permute-start.17 = (bf16[512,512]{1,0:T(8,128)(2,1)}, bf16[512,512]{1,0:T(8,128)(2,1)}, u32[]{:S(2)}, u32[]{:S(2)}) collective-permute-start(bf16[512,512]{1,0:T(8,128)(2,1)} %bitcast.43), channel_id=1, source_target_pairs={{0,8},{4,12},{24,16},{28,20},{1,9},{5,13},{25,17},{29,21},{2,10},{... | collective-permute-start | bytes 1572872 | tf_op jit(solution)/shard_map/ppermute | solution.py:475
  440.0 23.9 %collective-permute-start.20 = (bf16[512,512]{1,0:T(8,128)(2,1)}, bf16[512,512]{1,0:T(8,128)(2,1)}, u32[]{:S(2)}, u32[]{:S(2)}) collective-permute-start(bf16[512,512]{1,0:T(8,128)(2,1)} %fusion), channel_id=1, source_target_pairs={{8,0},{12,4},{16,24},{20,28},{9,1},{13,5},{17,25},{21,29},{10,2},{... | collective-permute-start | bytes 1572872 | tf_op jit(solution)/shard_map/ppermute | solution.py:475
  461.2 12.0 %collective-permute-start.16 = (bf16[512,512]{1,0:T(8,128)(2,1)}, bf16[512,512]{1,0:T(8,128)(2,1)}, u32[]{:S(2)}, u32[]{:S(2)}) collective-permute-start(bf16[512,512]{1,0:T(8,128)(2,1)} %fusion.4), channel_id=1, source_target_pairs={{8,0},{12,4},{16,24},{20,28},{9,1},{13,5},{17,25},{21,29},{10,2},{... | collective-permute-start | bytes 1572872 | tf_op jit(solution)/shard_map/ppermute | solution.py:475
  463.3 9.9 %copy-start.11 = (bf16[1,512,512]{2,1,0:T(8,128)(2,1)S(1)}, bf16[1,512,512]{2,1,0:T(8,128)(2,1)}, u32[]{:S(2)}) copy-start(bf16[1,512,512]{2,1,0:T(8,128)(2,1)} %get-tuple-element.78) | copy-start | bytes 1572868
  485.2 1.6 copy-start.5

commit v6 on v5

--- a/solution.py
+++ b/solution.py
@@ -508,7 +508,8 @@
 
     def turn(self, done):
         self.flat = after(self.flat, done)
-        self.far = [self.move(self.part([g], [self.near], [g // 2 * self.per]), g) for g in self.even[1:]]
+        self.parts = [self.part([g], [self.near], [g // 2 * self.per]) for g in self.even[1:]]
+        self.far = [self.move(part, g) for part, g in zip(self.parts, self.even[1:])]
 
     def finish(self):
         return self.part([0], [self.near] + self.far, [0] * (1 + len(self.far)))
@@ -541,54 +542,58 @@
     def add(*terms):
         return sum(term.astype(F32) for term in terms).astype(BF16)
 
-    everyone = [line ^ 1, *far, line]
     near = links.along(wo, PAIRS)
     cross_own = links.along(wo, CROSS)
     own_blocks = around(wo)
     chunks, by_head = split_inputs(queries, keys, values, n)
     row_out = row_forward(*by_head)
-    row_theirs = leaving(row_out, everyone)
-    near = after(near, chunks)
+    row_far, row_close = leaving(row_out, far), leaving(row_out, close)
+    near = after(near, chunks, *own_blocks[1:])
     near_blocks = around(near)
     cross_near = links.along(near, CROSS)
     out_own = links.along(cross_own, OUTWARD)
-    chunks = swap(after(chunks, *near_blocks, cross_near, out_own, *row_theirs))
+    chunks = swap(after(chunks, *near_blocks, cross_near, out_own, *row_far, *row_close))
+    out_near = links.along(cross_near, OUTWARD)
     far_own = jnp.where(middle, cross_own, out_own)
     far_own_blocks = around(far_own)
-    far_near = jnp.where(middle, cross_near, links.along(cross_near, OUTWARD))
+    far_near = jnp.where(middle, cross_near, out_near)
     far_near_blocks = around(far_near)
     blocks = own_blocks + near_blocks + far_own_blocks + far_near_blocks
     ids = [owner * inner + (spot ^ e) for owner in (line, line ^ 1, *far) for e in range(inner)]
     ids = jnp.stack(ids).astype(jnp.int32)
 
-    row_theirs = exchanged(row_theirs)
     outs = column_forward(after(chunks, *far_own_blocks))
     column_part = swap(outs)
     grad_row, grads = attn_grad(ids, after(out_grad, outs), blocks, dim)
-    grads = swap(after(grads, column_part, *row_theirs))
+    row_far = exchanged([after(part, *far_near_blocks) for part in row_far])
+    row_close = exchanged(row_close)
+    grads = swap(after(grads, column_part, *row_far))
+    (row_far,) = summed(after(row_out, outs), far, row_far, 0)
+    row_far_in = links.along(row_far, INWARD)
     column_out, flat = collect(row_out, column_part)
     column_far, column_close = leaving(column_out, far), leaving(column_out, close)
+    column_far = exchanged(column_far)
     layer = LayerSum(ids, flat, blocks, heads_n)
     layer.start()
-    gradients = column_backward(chunks, after(grads, *column_far, *column_close, layer.first))
-    column_far, column_close = exchanged(column_far), exchanged(column_close)
-    column_grads = swap(gradients)
-
-    row_lead, row_own = summed(after(row_out, gradients), everyone, row_theirs, 3)
-    row_in = links.along(row_lead, INWARD)
-    layer.turn(gradients)
+    gradients = column_backward(chunks, after(grads, *column_close, row_far, layer.first))
+    column_grads = swap(after(gradients, *column_far, row_far_in, *row_close))
+
+    column_close = exchanged(column_close)
+    row_cross = links.along(add(row_far, row_far_in), CROSS)
+    row_near, row_own = summed(after(row_out, gradients), close, row_close, 1)
+    row_near_in = links.along(row_near[0], INWARD)
     (column_far,) = summed(after(column_out, gradients), far, column_far, 0)
     column_far_in = links.along(column_far, INWARD)
+    layer.turn(gradients)
     row_grads = row_backward(*by_head, after(grad_row, column_far))
-    column_near, column_own = summed(after(column_out, gradients), close, column_close, 1)
-    row_cross = links.along(add(row_lead[1:], row_in[1:]), CROSS)
+    column_near, column_own = summed(after(column_out, *layer.parts), close, column_close, 1)
+    column_near_in = links.along(column_near[0], INWARD)
     column_cross = links.along(add(column_far, after(column_far_in, row_grads[0])), CROSS)
-    column_near_in = links.along(column_near[0], INWARD)
-    row_back = links.along(add(row_lead[0], row_cross[1]), OUTWARD)
+    row_back = links.along(add(row_near[0], row_cross[1]), OUTWARD)
     column_back = links.along(add(column_near[0], column_cross[1]), OUTWARD)
 
     gradients = join_gradients(column_grads, row_grads)
-    proj_row = add(row_own[0], row_in[0], row_cross[0], row_back)
+    proj_row = add(row_own[0], row_near_in, row_cross[0], row_back)
     proj_column = add(column_own[0], column_near_in, column_cross[0], column_back)
     shape = (half, dim, depth)
     proj_grad = jnp.stack([proj_row.reshape(shape), proj_column.reshape(shape)], axis=1)

time: 499 us -> 422 us (0.85)
  waiting for transfers between devices: 247 us -> 165 us
  Pallas kernels: 146 us -> 151 us
    ppermute x19 -> x21, waiting for transfers between devices: 247 us -> 165 us  [send(): out = lax.ppermute(value, 'ctx', pairs)]
    ppermute x19 -> x21, starting transfers between devices: 40.5 us -> 46.8 us  [send(): out = lax.ppermute(value, 'ctx', pairs)]
    pallas_call x6 -> x8, Pallas kernels: 34.7 us -> 40.3 us  [proj_part(): pl.pallas_call(functools.partial(proj_kernel, lead, len(extra), dim), gri...]
  transfers between devices with their start and end apart: 25 -> 27, of which waited for: 11 -> 12; matrix products, arithmetic and copies ran while one was open for 5% -> 6% of each run, Pallas kernels for 28% -> 34%
where the time goes in v6:
time: 422 us; the launch traced here: 420 us
  waiting for transfers between devices  165 us (39%)
  Pallas kernels  151 us (36%)
  starting transfers between devices  72.5 us (17%)
  other arithmetic  21.4 us (5%)
  local copies, waits for them, and re-layouts  9.19 us (2%)
    ppermute x21, waiting for transfers between devices, send(): out = lax.ppermute(value, 'ctx', pairs)  165 us
    ppermute x21, starting transfers between devices, send(): out = lax.ppermute(value, 'ctx', pairs)  46.8 us
    pallas_call x8, Pallas kernels, proj_part(): pl.pallas_call(functools.partial(proj_kernel, lead, len(extra), dim), gri...  40.3 us
    pallas_call x3, Pallas kernels, layer_part(): pl.pallas_call(functools.partial(layer_kernel, n, count, len(extra)), gri...  29.3 us
    all_to_all x4, starting transfers between devices, swap(): lax.all_to_all(chunks, 'ctx', split_axis=0, concat_axis=0, tiled=True)  24 us
    pallas_call x1, Pallas kernels, attn_grad(): pl.pallas_call(functools.partial(attn_grad_kernel, n, dim), grid_spec=plt...  21.1 us
    pallas_call x1, Pallas kernels, row_backward(): pl.pallas_call(functools.partial(row_backward_kernel, dim ** (-0.5)), gri...  13.6 us
    convert_element_type x6, other arithmetic, add(): return sum((term.astype(F32) for term in terms)).astype(BF16)  13.3 us
  transfers between devices with their start and end apart: 27, of which 12 were waited for; matrix products, arithmetic and copies ran while one was open for 6% of the time, Pallas kernels for 34%

profile of v6, /device:TPU:8, one launch (start us, length us, event | category | flops | bytes accessed | tf_op | source)
XLA Modules:
  0.0 420.2 jit_solution(13378624981763476449)
XLA Ops:
  0.6 3.5 collective-permute-start.4
  5.8 7.1 %split_inputs.1 = (bf16[8,3,4,2,64,128]{5,4,3,2,1,0:T(8,128)(2,1)}, bf16[4,1024,128]{2,1,0:T(8,128)(2,1)}, bf16[4,1024,128]{2,1,0:T(8,128)(2,1)}, bf16[4,1024,128]{2,1,0:T(8,128)(2,1)}) custom-call(bf16[1024,8,128]{2,1,0:T(8,128)(2,1)} %q_ref.1, bf16[1024,8,128]{2,1,0:T(8,128)(2,1)} %k_ref.1, bf16[1024,8,128]{2,1,0:T(8,128)(2,1)} %v_ref.1), custom_call_target="tpu_custom_call" | custom-call | tf_op jit(solution)/shard_map/split_inputs/pallas_call | solution.py:48
  12.9 14.9 %collective-permute-done.4 = bf16[1024,512]{1,0:T(8,128)(2,1)} collective-permute-done((bf16[1024,512]{1,0:T(8,128)(2,1)}, bf16[1024,512]{1,0:T(8,128)(2,1)}, u32[]{:S(2)}, u32[]{:S(2)}) %collective-permute-start.4) | collective-permute-done | bytes 1048608 | tf_op jit(solution)/shard_map/ppermute | solution.py:475
  29.0 3.2 collective-permute-start.5
  32.2 3.1 collective-permute-start.3
  36.9 9.9 %row_forward.1.flat_ref.row_ref = bf16[1024,512]{1,0:T(8,128)(2,1)} custom-call(bf16[4,1024,128]{2,1,0:T(8,128)(2,1)} %get-tuple-element.54.q_ref, bf16[4,1024,128]{2,1,0:T(8,128)(2,1)} %get-tuple-element.55.k_ref, bf16[4,1024,128]{2,1,0:T(8,128)(2,1)} %get-tuple-element.56.v_ref), custom_call_target="tpu_custom_call" | custom-call | flops 1073741824 | bytes 4194304 | tf_op jit(solution)/shard_map/row_forward/pallas_call | solution.py:311
  47.5 4.8 %proj_part.9 = bf16[2,512,512]{2,1,0:T(8,128)(2,1)} custom-call(s32[2]{0:T(128)} %pad_add_fusion.2.order, bf16[1024,512]{1,0:T(8,128)(2,1)} %row_forward.1.flat_ref.row_ref, bf16[1024,4096]{1,0:T(8,128)(2,1)} %grad_ref.16), custom_call_target="tpu_custom_call" | custom-call | flops 1073741824 | bytes 4194304 | tf_op jit(solution)/shard_map/proj_part/pallas_call | solution.py:265
  53.0 4.9 %proj_part.8 = bf16[2,512,512]{2,1,0:T(8,128)(2,1)} custom-call(s32[2]{0:T(128)} %pad_add_fusion.1.order, bf16[1024,512]{1,0:T(8,128)(2,1)} %row_forward.1.flat_ref.row_ref, bf16[1024,4096]{1,0:T(8,128)(2,1)} %grad_ref.16), custom_call_target="tpu_custom_call" | custom-call | flops 1073741824 | bytes 4194304 | tf_op jit(solution)/shard_map/proj_part/pallas_call | solution.py:265
  59.9 4.5 %all-to-all-start = ((bf16[8,3,4,2,64,128]{5,4,3,2,1,0:T(8,128)(2,1)}), bf16[8,3,4,2,64,128]{5,4,3,2,1,0:T(8,128)(2,1)S(1)}, u32[]{:S(2)}, u32[]{:S(2)}) async-start(bf16[8,3,4,2,64,128]{5,4,3,2,1,0:T(8,128)(2,1)} %get-tuple-element.60), calls=%async_computation | async-start | bytes 6291456 | tf_op jit(solution)/shard_map/all_to_all | solution.py:487
  64.3 2.9 collective-permute-start.7
  68.6 2.1 collective-permute-start.6
  70.7 64.5 %collective-permute-done.7 = bf16[1024,512]{1,0:T(8,128)(2,1)} collective-permute-done((bf16[1024,512]{1,0:T(8,128)(2,1)}, bf16[1024,512]{1,0:T(8,128)(2,1)}, u32[]{:S(2)}, u32[]{:S(2)}) %collective-permute-start.7) | collective-permute-done | bytes 1048608 | tf_op jit(solution)/shard_map/ppermute | solution.py:475
  135.1 2.3 broadcast_select_fusion.refs_6_
  138.9 8.7 %column_forward.1 = bf16[8,4,2,64,128]{4,3,2,1,0:T(8,128)(2,1)S(1)} custom-call(bf16[8,3,4,2,64,128]{5,4,3,2,1,0:T(8,128)(2,1)S(1)} %all-to-all-done.chunk_ref), custom_call_target="tpu_custom_call" | custom-call | flops 536870912 | bytes 4194304 | tf_op jit(solution)/shard_map/column_forward/pallas_call | solution.py:403
  148.6 6.2 %all-to-all-start.1 = ((bf16[8,4,2,64,128]{4,3,2,1,0:T(8,128)(2,1)}), bf16[8,4,2,64,128]{4,3,2,1,0:T(8,128)(2,1)S(1)}, u32[]{:S(2)}, u32[]{:S(2)}) async-start(bf16[8,4,2,64,128]{4,3,2,1,0:T(8,128)(2,1)} %copy-done.6), calls=%async_computation.1 | async-start | bytes 2097152 | tf_op jit(solution)/shard_map/all_to_all | solution.py:487
  154.7 15.2 %collective-permute-done.8.refs_7_ = bf16[1024,512]{1,0:T(8,128)(2,1)} collective-permute-done((bf16[1024,512]{1,0:T(8,128)(2,1)}, bf16[1024,512]{1,0:T(8,128)(2,1)}, u32[]{:S(2)}, u32[]{:S(2)}) %collective-permute-start.8) | collective-permute-done | bytes 1048608 | tf_op jit(solution)/shard_map/ppermute | solution.py:475
  170.0 3.0 collective-permute-start.9
  173.6 21.1 %attn_grad.1 = (bf16[1024,512]{1,0:T(8,128)(2,1)}, bf16[8,4,2,64,128]{4,3,2,1,0:T(8,128)(2,1)}) custom-call(s32[8]{0:T(128)} %stack.103.ids, bf16[1024,4096]{1,0:T(8,128)(2,1)} %grad_ref.16, bf16[1024,512]{1,0:T(8,128)(2,1)} %refs_0_.7, bf16[1024,512]{1,0:T(8,128)(2,1)} %copy-done.10, bf16[1024,512]{1,0:T(8,128)(2,1)} %copy-done.9, ...), custom_call_target="tpu_custom_call" | custom-call | flops 8589934592 | bytes 18874368 | tf_op jit(solution)/shard_map/attn_grad/pallas_call | solution.py:153
  194.7 8.4 %all-to-all-start.2 = ((bf16[8,4,2,64,128]{4,3,2,1,0:T(8,128)(2,1)}), bf16[8,4,2,64,128]{4,3,2,1,0:T(8,128)(2,1)}, u32[]{:S(2)}, u32[]{:S(2)}) async-start(bf16[8,4,2,64,128]{4,3,2,1,0:T(8,128)(2,1)} %get-tuple-element.70), calls=%async_computation.2 | async-start | bytes 2097152 | tf_op jit(solution)/shard_map/all_to_all | solution.py:487
  208.8 11.7 %layer_part.3 = bf16[1024,2048]{1,0:T(8,128)(2,1)} custom-call(s32[8]{0:T(128)} %stack.103.ids, s32[4]{0:T(128)} %pad_add_fusion.4.wanted, bf16[1024,1024]{1,0:T(8,128)(2,1)} %copy-done.5, bf16[1024,512]{1,0:T(8,128)(2,1)} %refs_0_.7, bf16[1024,512]{1,0:T(8,128)(2,1)} %copy-done.10, bf16[1024,512]{1,0:T(8,128)(2,1)} %copy-done.9, ...), custom_call_target="tpu_custom_call" | custom-call | flops 4294967296 | bytes 10485760 | tf_op jit(solution)/shard_map/layer_part/pallas_call | solution.py:211
  220.5 5.1 %proj_part.11 = bf16[2,512,512]{2,1,0:T(8,128)(2,1)} custom-call(s32[2]{0:T(128)} %pad_add_fusion.3.order, bf16[1024,512]{1,0:T(8,128)(2,1)} %row_forward.1.flat_ref.row_ref, bf16[1024,4096]{1,0:T(8,128)(2,1)} %grad_ref.16, bf16[2,512,512]{2,1,0:T(8,128)(2,1)} %copy-done.12), custom_call_target="tpu_custom_call" | custom-call | flops 1073741824 | bytes 5242880 | tf_op jit(solution)/shard_map/proj_part/pallas_call | solution.py:265
  227.1 4.9 %proj_part.12 = bf16[2,512,512]{2,1,0:T(8,128)(2,1)} custom-call(s32[2]{0:T(128)} %pad_add_fusion.1.order, bf16[1024,512]{1,0:T(8,128)(2,1)} %copy-done.3, bf16[1024,4096]{1,0:T(8,128)(2,1)} %grad_ref.16), custom_call_target="tpu_custom_call" | custom-call | flops 1073741824 | bytes 4194304 | tf_op jit(solution)/shard_map/proj_part/pallas_call | solution.py:265
  232.5 5.1 %proj_part.10 = bf16[2,512,512]{2,1,0:T(8,128)(2,1)} custom-call(s32[2]{0:T(128)} %pad_add_fusion.2.order, bf16[1024,512]{1,0:T(8,128)(2,1)} %copy-done.3, bf16[1024,4096]{1,0:T(8,128)(2,1)} %grad_ref.16), custom_call_target="tpu_custom_call" | custom-call | flops 1073741824 | bytes 4194304 | tf_op jit(solution)/shard_map/proj_part/pallas_call | solution.py:265
  237.6 12.9 %column_backward.1 = bf16[8,3,4,2,64,128]{5,4,3,2,1,0:T(8,128)(2,1)S(1)} custom-call(bf16[8,3,4,2,64,128]{5,4,3,2,1,0:T(8,128)(2,1)S(1)} %copy-done.2, bf16[8,4,2,64,128]{4,3,2,1,0:T(8,128)(2,1)} %all-to-all-done.2.grad_ref), custom_call_target="tpu_custom_call" | custom-call | flops 1342177280 | bytes 7340032 | tf_op jit(solution)/shard_map/column_backward/pallas_call | solution.py:441
  253.4 7.5 %collective-permute-done.12.refs_0_ = bf16[2,512,512]{2,1,0:T(8,128)(2,1)} collective-permute-done((bf16[2,512,512]{2,1,0:T(8,128)(2,1)}, bf16[2,512,512]{2,1,0:T(8,128)(2,1)}, u32[]{:S(2)}, u32[]{:S(2)}) %collective-permute-start.12) | collective-permute-done | bytes 1048608 | tf_op jit(solution)/shard_map/ppermute | solution.py:475
  260.9 5.0 %all-to-all-start.3 = ((bf16[8,3,4,2,64,128]{5,4,3,2,1,0:T(8,128)(2,1)}), bf16[8,3,4,2,64,128]{5,4,3,2,1,0:T(8,128)(2,1)S(1)}, u32[]{:S(2)}, u32[]{:S(2)}) async-start(bf16[8,3,4,2,64,128]{5,4,3,2,1,0:T(8,128)(2,1)} %copy-done.4), calls=%async_computation.3 | async-start | bytes 6291456 | tf_op jit(solution)/shard_map/all_to_all | solution.py:487
  265.8 5.0 %proj_part.13 = bf16[2,512,512]{2,1,0:T(8,128)(2,1)} custom-call(s32[2]{0:T(128)} %pad_add_fusion.3.order, bf16[1024,512]{1,0:T(8,128)(2,1)} %copy-done.3, bf16[1024,4096]{1,0:T(8,128)(2,1)} %grad_ref.16, bf16[2,512,512]{2,1,0:T(8,128)(2,1)} %collective-permute-done.12.refs_0_), custom_call_target="tpu_custom_call" | custom-call | flops 1073741824 | bytes 5242880 | tf_op jit(solution)/shard_map/proj_part/pallas_call | solution.py:265
  274.3 2.9 add_convert_fusion.1
  277.1 3.4 collective-permute-start.16
  280.5 13.6 %row_backward.1 = (bf16[4,1024,128]{2,1,0:T(8,128)(2,1)}, bf16[4,1024,128]{2,1,0:T(8,128)(2,1)}, bf16[4,1024,128]{2,1,0:T(8,128)(2,1)}) custom-call(bf16[4,1024,128]{2,1,0:T(8,128)(2,1)} %get-tuple-element.54.q_ref, bf16[4,1024,128]{2,1,0:T(8,128)(2,1)} %get-tuple-element.55.k_ref, bf16[4,1024,128]{2,1,0:T(8,128)(2,1)} %get-tuple-element.56.v_ref, ...), custom_call_target="tpu_custom_call" | custom-call | flops 2684354560 | bytes 7340032 | tf_op jit(solution)/shard_map/row_backward/pallas_call | solution.py:345
  294.1 46.4 %collective-permute-done.20 = bf16[2,512,512]{2,1,0:T(8,128)(2,1)} collective-permute-done((bf16[2,512,512]{2,1,0:T(8,128)(2,1)}, bf16[2,512,512]{2,1,0:T(8,128)(2,1)}, u32[]{:S(2)}, u32[]{:S(2)}) %collective-permute-start.20) | collective-permute-done | bytes 1048608 | tf_op jit(solution)/shard_map/ppermute | solution.py:475
  340.5 2.8 add_convert_fusion
  343.3 3.7 collective-permute-start.21
  347.0 8.5 %layer_part.4 = bf16[1024,1024]{1,0:T(8,128)(2,1)} custom-call(s32[8]{0:T(128)} %stack.103.ids, s32[2]{0:T(128)} %pad_add_fusion.5.wanted, bf16[1024,1024]{1,0:T(8,128)(2,1)} %copy-done.5, bf16[1024,512]{1,0:T(8,128)(2,1)} %refs_0_.7, bf16[1024,512]{1,0:T(8,128)(2,1)} %copy-done.10, bf16[1024,512]{1,0:T(8,128)(2,1)} %copy-done.9, ...), custom_call_target="tpu_custom_call" | custom-call | flops 2147483648 | bytes 6291456 | tf_op jit(solution)/shard_map/layer_part/pallas_call | solution.py:211
  357.7 5.2 %proj_part.14 = (bf16[1,512,512]{2,1,0:T(8,128)(2,1)}, bf16[1,512,512]{2,1,0:T(8,128)(2,1)}) custom-call(s32[2]{0:T(128)} %pad_add_fusion.6.order, bf16[1024,512]{1,0:T(8,128)(2,1)} %row_forward.1.flat_ref.row_ref, bf16[1024,4096]{1,0:T(8,128)(2,1)} %grad_ref.16, bf16[2,512,512]{2,1,0:T(8,128)(2,1)} %collective-permute-done.14.refs_0_), custom_call_target="tpu_custom_call" | custom-call | flops 1073741824 | bytes 5242880 | tf_op jit(solution)/shard_map/proj_part/pallas_call | solution.py:265
  364.2 2.1 fusion.3
  366.3 6.2 %collective-permute-start.18 = (bf16[512,512]{1,0:T(8,128)(2,1)}, bf16[512,512]{1,0:T(8,128)(2,1)}, u32[]{:S(2)}, u32[]{:S(2)}) collective-permute-start(bf16[512,512]{1,0:T(8,128)(2,1)} %fusion.3), channel_id=1, source_target_pairs={{8,0},{12,4},{16,24},{20,28},{9,1},{13,5},{17,25},{21,29},{10,2},{... | collective-permute-start | bytes 1572872 | tf_op jit(solution)/shard_map/ppermute | solution.py:475
  372.5 5.2 %proj_part.15 = (bf16[1,512,512]{2,1,0:T(8,128)(2,1)}, bf16[1,512,512]{2,1,0:T(8,128)(2,1)}) custom-call(s32[2]{0:T(128)} %pad_add_fusion.6.order, bf16[1024,512]{1,0:T(8,128)(2,1)} %copy-done.3, bf16[1024,4096]{1,0:T(8,128)(2,1)} %grad_ref.16, bf16[2,512,512]{2,1,0:T(8,128)(2,1)} %collective-permute-done.17.refs_0_), custom_call_target="tpu_custom_call" | custom-call | flops 1073741824 | bytes 5242880 | tf_op jit(solution)/shard_map/proj_part/pallas_call | solution.py:265
  377.7 2.3 collective-permute-done.21
  380.0 2.1 fusion
  382.2 2.1 collective-permute-start.22
  386.5 1.8 fusion.5
  388.2 6.0 %collective-permute-done.22 = bf16[512,512]{1,0:T(8,128)(2,1)} collective-permute-done((bf16[512,512]{1,0:T(8,128)(2,1)}, bf16[512,512]{1,0:T(8,128)(2,1)}, u32[]{:S(2)}, u32[]{:S(2)}) %collective-permute-start.22) | collective-permute-done | bytes 524320 | tf_op jit(solution)/shard_map/ppermute | solution.py:475
  394.3 4.9 %collective-permute-done.19 = bf16[512,512]{1,0:T(8,128)(2,1)} collective-permute-done((bf16[512,512]{1,0:T(8,128)(2,1)}, bf16[512,512]{1,0:T(8,128)(2,1)}, u32[]{:S(2)}, u32[]{:S(2)}) %collective-permute-start.19) | collective-permute-done | bytes 524320 | tf_op jit(solution)/shard_map/ppermute | solution.py:475
  399.2 1.6 fusion.2
  402.1 9.2 %layer_part.5 = bf16[1024,1024]{1,0:T(8,128)(2,1)} custom-call(s32[8]{0:T(128)} %stack.103.ids, s32[2]{0:T(128)} %pad_add_fusion.wanted, bf16[1024,1024]{1,0:T(8,128)(2,1)} %copy-done.5, bf16[1024,512]{1,0:T(8,128)(2,1)} %refs_0_.7, bf16[1024,512]{1,0:T(8,128)(2,1)} %copy-done.10, bf16[1024,512]{1,0:T(8,128)(2,1)} %copy-done.9, ...), custom_call_target="tpu_custom_call" | custom-call | flops 2147483648 | bytes 6291456 | tf_op jit(solution)/shard_map/layer_part/pallas_call | solution.py:211
  411.3 1.6 copy-done.7
  412.9 7.3 %join_gradients.1 = (bf16[1024,8,128]{2,1,0:T(8,128)(2,1)}, bf16[1024,8,128]{2,1,0:T(8,128)(2,1)}, bf16[1024,8,128]{2,1,0:T(8,128)(2,1)}) custom-call(bf16[8,3,4,2,64,128]{5,4,3,2,1,0:T(8,128)(2,1)} %copy-done.7, bf16[4,1024,128]{2,1,0:T(8,128)(2,1)} %get-tuple-element.82.refs_0_, bf16[4,1024,128]{2,1,0:T(8,128)(2,1)} %get-tuple-element.83.refs_1_, ...), custom_call_target="tpu_custom_call" | custom-call | tf_op jit(solution)/shard_map/join_gradients/pallas_call | solution.py:78
  (71 shorter events, 32.9 us)
Async XLA Ops:
  0.6 27.1 %collective-permute-start.4 = (bf16[1024,512]{1,0:T(8,128)(2,1)}, bf16[1024,512]{1,0:T(8,128)(2,1)}, u32[]{:S(2)}, u32[]{:S(2)}) collective-permute-start(bf16[1024,512]{1,0:T(8,128)(2,1)} %refs_0_.7), channel_id=1, source_target_pairs={{8,16},{12,20},{16,8},{20,12},{9,17},{13,21},{17,9},{21,13},{10,18... | collective-permute-start | bytes 3145736 | tf_op jit(solution)/shard_map/ppermute | solution.py:475
  4.1 24.9 %collective-permute-start = (bf16[1024,512]{1,0:T(8,128)(2,1)}, bf16[1024,512]{1,0:T(8,128)(2,1)S(1)}, u32[]{:S(2)}, u32[]{:S(2)}) collective-permute-start(bf16[1024,512]{1,0:T(8,128)(2,1)} %refs_0_.7), channel_id=1, source_target_pairs={{0,8},{4,12},{8,0},{12,4},{16,24},{20,28},{24,16},{28,20},{1,9},{5... | collective-permute-start | bytes 3145736 | tf_op jit(solution)/shard_map/ppermute | solution.py:475
  4.2 28.0 %collective-permute-start.1 = (bf16[1024,512]{1,0:T(8,128)(2,1)}, bf16[1024,512]{1,0:T(8,128)(2,1)S(1)}, u32[]{:S(2)}, u32[]{:S(2)}) collective-permute-start(bf16[1024,512]{1,0:T(8,128)(2,1)} %refs_0_.7), channel_id=1, source_target_pairs={{0,4},{4,0},{8,12},{12,8},{16,20},{20,16},{24,28},{28,24},{1,5},{5... | collective-permute-start | bytes 3145736 | tf_op jit(solution)/shard_map/ppermute | solution.py:475
  29.0 17.8 %copy-start.9 = (bf16[1024,512]{1,0:T(8,128)(2,1)}, bf16[1024,512]{1,0:T(8,128)(2,1)S(1)}, u32[]{:S(2)}) copy-start(bf16[1024,512]{1,0:T(8,128)(2,1)S(1)} %collective-permute-done.refs_2_) | copy-start | bytes 3145732
  29.0 28.8 %collective-permute-start.5 = (bf16[1024,512]{1,0:T(8,128)(2,1)}, bf16[1024,512]{1,0:T(8,128)(2,1)}, u32[]{:S(2)}, u32[]{:S(2)}) collective-permute-start(bf16[1024,512]{1,0:T(8,128)(2,1)} %collective-permute-done.4), channel_id=1, source_target_pairs={{8,0},{12,4},{16,24},{20,28},{9,1},{13,5},{17,25},{21,29},{10,2},{... | collective-permute-start | bytes 3145736 | tf_op jit(solution)/shard_map/ppermute | solution.py:475
  32.2 14.6 %copy-start.10 = (bf16[1024,512]{1,0:T(8,128)(2,1)}, bf16[1024,512]{1,0:T(8,128)(2,1)S(1)}, u32[]{:S(2)}) copy-start(bf16[1024,512]{1,0:T(8,128)(2,1)S(1)} %collective-permute-done.1.refs_1_) | copy-start | bytes 3145732
  32.2 25.7 %collective-permute-start.3 = (bf16[1024,512]{1,0:T(8,128)(2,1)S(1)}, bf16[1024,512]{1,0:T(8,128)(2,1)}, u32[]{:S(2)}, u32[]{:S(2)}) collective-permute-start(bf16[1024,512]{1,0:T(8,128)(2,1)S(1)} %collective-permute-done.refs_2_), channel_id=1, source_target_pairs={{8,16},{12,20},{16,8},{20,12},{9,17},{13,21},{17,9},{21,13},{10,18... | collective-permute-start | bytes 3145736 | tf_op jit(solution)/shard_map/ppermute | solution.py:475
  35.4 23.5 %collective-permute-start.2 = (bf16[1024,512]{1,0:T(8,128)(2,1)S(1)}, bf16[1024,512]{1,0:T(8,128)(2,1)S(1)}, u32[]{:S(2)}, u32[]{:S(2)}) collective-permute-start(bf16[1024,512]{1,0:T(8,128)(2,1)S(1)} %collective-permute-done.refs_2_), channel_id=1, source_target_pairs={{0,4},{4,0},{8,12},{12,8},{16,20},{20,16},{24,28},{28,24},{1,5},{5... | collective-permute-start | bytes 3145736 | tf_op jit(solution)/shard_map/ppermute | solution.py:475
  58.9 1.0 copy-start.11
  59.9 79.0 %all-to-all-start = ((bf16[8,3,4,2,64,128]{5,4,3,2,1,0:T(8,128)(2,1)}), bf16[8,3,4,2,64,128]{5,4,3,2,1,0:T(8,128)(2,1)S(1)}, u32[]{:S(2)}, u32[]{:S(2)}) async-start(bf16[8,3,4,2,64,128]{5,4,3,2,1,0:T(8,128)(2,1)} %get-tuple-element.60), calls=%async_computation | async-start | bytes 6291456 | tf_op jit(solution)/shard_map/all_to_all | solution.py:487
  64.3 70.8 %collective-permute-start.7 = (bf16[1024,512]{1,0:T(8,128)(2,1)}, bf16[1024,512]{1,0:T(8,128)(2,1)}, u32[]{:S(2)}, u32[]{:S(2)}) collective-permute-start(bf16[1024,512]{1,0:T(8,128)(2,1)} %collective-permute-done.3), channel_id=1, source_target_pairs={{8,0},{12,4},{16,24},{20,28},{9,1},{13,5},{17,25},{21,29},{10,2},{... | collective-permute-start | bytes 3145736 | tf_op jit(solution)/shard_map/ppermute | solution.py:475
  68.6 70.3 %copy-start.8 = (bf16[1024,512]{1,0:T(8,128)(2,1)}, bf16[1024,512]{1,0:T(8,128)(2,1)S(1)}, u32[]{:S(2)}) copy-start(bf16[1024,512]{1,0:T(8,128)(2,1)S(1)} %broadcast_select_fusion.1.refs_4_) | copy-start | bytes 3145732
  68.6 70.3 %collective-permute-start.6 = (bf16[1024,512]{1,0:T(8,128)(2,1)S(1)}, bf16[1024,512]{1,0:T(8,128)(2,1)}, u32[]{:S(2)}, u32[]{:S(2)}) collective-permute-start(bf16[1024,512]{1,0:T(8,128)(2,1)S(1)} %broadcast_select_fusion.1.refs_4_), channel_id=1, source_target_pairs={{0,4},{4,0},{8,12},{12,8},{16,20},{20,16},{24,28},{28,24},{1,5},{5... | collective-permute-start | bytes 3145736 | tf_op jit(solution)/shard_map/ppermute | solution.py:475
  137.5 32.5 %collective-permute-start.8 = (bf16[1024,512]{1,0:T(8,128)(2,1)}, bf16[1024,512]{1,0:T(8,128)(2,1)}, u32[]{:S(2)}, u32[]{:S(2)}) collective-permute-start(bf16[1024,512]{1,0:T(8,128)(2,1)} %broadcast_select_fusion.refs_6_), channel_id=1, source_target_pairs={{0,4},{4,0},{8,12},{12,8},{16,20},{20,16},{24,28},{28,24},{1,5},{5... | collective-permute-start | bytes 3145736 | tf_op jit(solution)/shard_map/ppermute | solution.py:475
  138.9 8.7 %copy-start.1 = (bf16[8,3,4,2,64,128]{5,4,3,2,1,0:T(8,128)(2,1)}, bf16[8,3,4,2,64,128]{5,4,3,2,1,0:T(8,128)(2,1)S(1)}, u32[]{:S(2)}) copy-start(bf16[8,3,4,2,64,128]{5,4,3,2,1,0:T(8,128)(2,1)S(1)} %all-to-all-done.chunk_ref) | copy-start | bytes 9437188
  147.6 1.0 copy-start.6
  148.6 46.1 %all-to-all-start.1 = ((bf16[8,4,2,64,128]{4,3,2,1,0:T(8,128)(2,1)}), bf16[8,4,2,64,128]{4,3,2,1,0:T(8,128)(2,1)S(1)}, u32[]{:S(2)}, u32[]{:S(2)}) async-start(bf16[8,4,2,64,128]{4,3,2,1,0:T(8,128)(2,1)} %copy-done.6), calls=%async_computation.1 | async-start | bytes 2097152 | tf_op jit(solution)/shard_map/all_to_all | solution.py:487
  170.0 24.7 %collective-permute-start.9 = (bf16[2,512,512]{2,1,0:T(8,128)(2,1)}, bf16[2,512,512]{2,1,0:T(8,128)(2,1)S(1)}, u32[]{:S(2)}, u32[]{:S(2)}) collective-permute-start(bf16[2,512,512]{2,1,0:T(8,128)(2,1)} %proj_part.8), channel_id=1, source_target_pairs={{0,4},{4,0},{8,12},{12,8},{16,20},{20,16},{24,28},{28,24},{1,5},{5... | collective-permute-start | bytes 3145736 | tf_op jit(solution)/shard_map/ppermute | solution.py:475
  194.6 11.2 %copy-start = (bf16[1024,512]{1,0:T(8,128)(2,1)S(1)}, bf16[1024,512]{1,0:T(8,128)(2,1)}, u32[]{:S(2)}) copy-start(bf16[1024,512]{1,0:T(8,128)(2,1)} %row_forward.1.flat_ref.row_ref) | copy-start | bytes 3145732
  194.7 11.8 %copy-start.12 = (bf16[2,512,512]{2,1,0:T(8,128)(2,1)}, bf16[2,512,512]{2,1,0:T(8,128)(2,1)S(1)}, u32[]{:S(2)}) copy-start(bf16[2,512,512]{2,1,0:T(8,128)(2,1)S(1)} %collective-permute-done.9.refs_0_) | copy-start | bytes 3145732
  194.7 42.9 %all-to-all-start.2 = ((bf16[8,4,2,64,128]{4,3,2,1,0:T(8,128)(2,1)}), bf16[8,4,2,64,128]{4,3,2,1,0:T(8,128)(2,1)}, u32[]{:S(2)}, u32[]{:S(2)}) async-start(bf16[8,4,2,64,128]{4,3,2,1,0:T(8,128)(2,1)} %get-tuple-element.70), calls=%async_computation.2 | async-start | bytes 2097152 | tf_op jit(solution)/shard_map/all_to_all | solution.py:487
  204.4 47.8 %collective-permute-start.14 = (bf16[2,512,512]{2,1,0:T(8,128)(2,1)}, bf16[2,512,512]{2,1,0:T(8,128)(2,1)}, u32[]{:S(2)}, u32[]{:S(2)}) collective-permute-start(bf16[2,512,512]{2,1,0:T(8,128)(2,1)} %proj_part.9), channel_id=1, source_target_pairs={{0,4},{4,0},{8,12},{12,8},{16,20},{20,16},{24,28},{28,24},{1,5},{5... | collective-permute-start | bytes 3145736 | tf_op jit(solution)/shard_map/ppermute | solution.py:475
  206.5 1.0 copy-start.3
  207.5 1.3 copy-start.5
  220.5 126.6 %collective-permute-start.10 = (bf16[1024,2048]{1,0:T(8,128)(2,1)}, bf16[1024,2048]{1,0:T(8,128)(2,1)}, u32[]{:S(2)}, u32[]{:S(2)}) collective-permute-start(bf16[1024,2048]{1,0:T(8,128)(2,1)} %layer_part.3), channel_id=1, source_target_pairs={{0,1},{1,0},{2,3},{3,2},{4,5},{5,4},{6,7},{7,6},{8,9},{9,8},{10,11... | collective-permute-start | bytes 12582920 | tf_op jit(solution)/shard_map/ppermute | solution.py:503
  225.6 27.7 %collective-permute-start.13 = (bf16[2,512,512]{2,1,0:T(8,128)(2,1)}, bf16[2,512,512]{2,1,0:T(8,128)(2,1)}, u32[]{:S(2)}, u32[]{:S(2)}) collective-permute-start(bf16[2,512,512]{2,1,0:T(8,128)(2,1)} %proj_part.11), channel_id=1, source_target_pairs={{0,8},{4,12},{24,16},{28,20},{1,9},{5,13},{25,17},{29,21},{2,10},{... | collective-permute-start | bytes 3145736 | tf_op jit(solution)/shard_map/ppermute | solution.py:475
  232.0 28.9 %collective-permute-start.12 = (bf16[2,512,512]{2,1,0:T(8,128)(2,1)}, bf16[2,512,512]{2,1,0:T(8,128)(2,1)}, u32[]{:S(2)}, u32[]{:S(2)}) collective-permute-start(bf16[2,512,512]{2,1,0:T(8,128)(2,1)} %proj_part.12), channel_id=1, source_target_pairs={{0,4},{4,0},{8,12},{12,8},{16,20},{20,16},{24,28},{28,24},{1,5},{5... | collective-permute-start | bytes 3145736 | tf_op jit(solution)/shard_map/ppermute | solution.py:475
  232.5 5.1 %copy-start.2 = (bf16[8,3,4,2,64,128]{5,4,3,2,1,0:T(8,128)(2,1)S(1)}, bf16[8,3,4,2,64,128]{5,4,3,2,1,0:T(8,128)(2,1)}, u32[]{:S(2)}) copy-start(bf16[8,3,4,2,64,128]{5,4,3,2,1,0:T(8,128)(2,1)} %copy-done.1) | copy-start | bytes 9437188
  250.5 1.6 copy-start.4
  260.9 150.4 %all-to-all-start.3 = ((bf16[8,3,4,2,64,128]{5,4,3,2,1,0:T(8,128)(2,1)}), bf16[8,3,4,2,64,128]{5,4,3,2,1,0:T(8,128)(2,1)S(1)}, u32[]{:S(2)}, u32[]{:S(2)}) async-start(bf16[8,3,4,2,64,128]{5,4,3,2,1,0:T(8,128)(2,1)} %copy-done.4), calls=%async_computation.3 | async-start | bytes 6291456 | tf_op jit(solution)/shard_map/all_to_all | solution.py:487
  270.9 69.6 %collective-permute-start.20 = (bf16[2,512,512]{2,1,0:T(8,128)(2,1)}, bf16[2,512,512]{2,1,0:T(8,128)(2,1)}, u32[]{:S(2)}, u32[]{:S(2)}) collective-permute-start(bf16[2,512,512]{2,1,0:T(8,128)(2,1)} %proj_part.13), channel_id=1, source_target_pairs={{0,8},{4,12},{24,16},{28,20},{1,9},{5,13},{25,17},{29,21},{2,10},{... | collective-permute-start | bytes 3145736 | tf_op jit(solution)/shard_map/ppermute | solution.py:475
  272.2 71.1 %collective-permute-start.17 = (bf16[2,512,512]{2,1,0:T(8,128)(2,1)}, bf16[2,512,512]{2,1,0:T(8,128)(2,1)}, u32[]{:S(2)}, u32[]{:S(2)}) collective-permute-start(bf16[2,512,512]{2,1,0:T(8,128)(2,1)} %proj_part.10), channel_id=1, source_target_pairs={{0,4},{4,0},{8,12},{12,8},{16,20},{20,16},{24,28},{28,24},{1,5},{5... | collective-permute-start | bytes 3145736 | tf_op jit(solution)/shard_map/ppermute | solution.py:475
  277.1 87.0 %collective-permute-start.16 = (bf16[2,512,512]{2,1,0:T(8,128)(2,1)}, bf16[2,512,512]{2,1,0:T(8,128)(2,1)}, u32[]{:S(2)}, u32[]{:S(2)}) collective-permute-start(bf16[2,512,512]{2,1,0:T(8,128)(2,1)} %add_convert_fusion.1), channel_id=1, source_target_pairs={{8,16},{12,20},{16,8},{20,12},{9,17},{13,21},{17,9},{21,13},{10,18... | collective-permute-start | bytes 3145736 | tf_op jit(solution)/shard_map/ppermute | solution.py:475
  343.3 36.7 %collective-permute-start.21 = (bf16[2,512,512]{2,1,0:T(8,128)(2,1)}, bf16[2,512,512]{2,1,0:T(8,128)(2,1)}, u32[]{:S(2)}, u32[]{:S(2)}) collective-permute-start(bf16[2,512,512]{2,1,0:T(8,128)(2,1)} %add_convert_fusion), channel_id=1, source_target_pairs={{8,16},{12,20},{16,8},{20,12},{9,17},{13,21},{17,9},{21,13},{10,18... | collective-permute-start | bytes 3145736 | tf_op jit(solution)/shard_map/ppermute | solution.py:475
  355.5 46.5 %collective-permute-start.11 = (bf16[1024,1024]{1,0:T(8,128)(2,1)}, bf16[1024,1024]{1,0:T(8,128)(2,1)}, u32[]{:S(2)}, u32[]{:S(2)}) collective-permute-start(bf16[1024,1024]{1,0:T(8,128)(2,1)} %layer_part.4), channel_id=1, source_target_pairs={{0,2},{1,3},{2,0},{3,1},{4,6},{5,7},{6,4},{7,5},{8,10},{9,11},{10,... | collective-permute-start | bytes 6291464 | tf_op jit(solution)/shard_map/ppermute | solution.py:503
  362.9 19.3 %collective-permute-start.15 = (bf16[512,512]{1,0:T(8,128)(2,1)}, bf16[512,512]{1,0:T(8,128)(2,1)}, u32[]{:S(2)}, u32[]{:S(2)}) collective-permute-start(bf16[512,512]{1,0:T(8,128)(2,1)} %bitcast.53), channel_id=1, source_target_pairs={{0,8},{4,12},{24,16},{28,20},{1,9},{5,13},{25,17},{29,21},{2,10},{... | collective-permute-start | bytes 1572872 | tf_op jit(solution)/shard_map/ppermute | solution.py:475
  366.3 20.1 %collective-permute-start.18 = (bf16[512,512]{1,0:T(8,128)(2,1)}, bf16[512,512]{1,0:T(8,128)(2,1)}, u32[]{:S(2)}, u32[]{:S(2)}) collective-permute-start(bf16[512,512]{1,0:T(8,128)(2,1)} %fusion.3), channel_id=1, source_target_pairs={{8,0},{12,4},{16,24},{20,28},{9,1},{13,5},{17,25},{21,29},{10,2},{... | collective-permute-start | bytes 1572872 | tf_op jit(solution)/shard_map/ppermute | solution.py:475
  382.2 12.1 %collective-permute-start.22 = (bf16[512,512]{1,0:T(8,128)(2,1)}, bf16[512,512]{1,0:T(8,128)(2,1)}, u32[]{:S(2)}, u32[]{:S(2)}) collective-permute-start(bf16[512,512]{1,0:T(8,128)(2,1)} %fusion), channel_id=1, source_target_pairs={{8,0},{12,4},{16,24},{20,28},{9,1},{13,5},{17,25},{21,29},{10,2},{... | collective-permute-start | bytes 1572872 | tf_op jit(solution)/shard_map/ppermute | solution.py:475
  384.3 14.9 %collective-permute-start.19 = (bf16[512,512]{1,0:T(8,128)(2,1)}, bf16[512,512]{1,0:T(8,128)(2,1)}, u32[]{:S(2)}, u32[]{:S(2)}) collective-permute-start(bf16[512,512]{1,0:T(8,128)(2,1)} %bitcast.52), channel_id=1, source_target_pairs={{0,8},{4,12},{24,16},{28,20},{1,9},{5,13},{25,17},{29,21},{2,10},{... | collective-permute-start | bytes 1572872 | tf_op jit(solution)/shard_map/ppermute | solution.py:475
  385.8 13.4 %copy-start.13 = (bf16[1,512,512]{2,1,0:T(8,128)(2,1)S(1)}, bf16[1,512,512]{2,1,0:T(8,128)(2,1)}, u32[]{:S(2)}) copy-start(bf16[1,512,512]{2,1,0:T(8,128)(2,1)} %get-tuple-element.96) | copy-start | bytes 1572868
  411.3 1.6 copy-start.7

commit v7 on v6

--- a/solution.py
+++ b/solution.py
@@ -59,33 +59,33 @@
     return out[0], out[1:]
 
 
-def join_kernel(chunk_ref, *refs):
+def join_kernel(query_ref, rest_ref, *refs):
     row_refs, outs, wide = refs[:3], refs[3:6], refs[6]
-    n, width = chunk_ref.shape[0], chunk_ref.shape[3]
+    n, width = query_ref.shape[0], query_ref.shape[3]
     span, heads, dim = outs[0].shape
     for array in range(3):
         for head in range(heads // 2):
             wide[pl.ds(2 * head, span, stride=heads), :] = row_refs[array][head].astype(F32)
             for d in range(n):
-                part = chunk_ref[d, array, head].astype(F32)
+                part = (query_ref if array == 0 else rest_ref)[d, max(array - 1, 0), head].astype(F32)
                 wide[pl.ds(d * width * heads + 2 * head + 1, width, stride=heads), :] = part
         outs[array][...] = wide[...].reshape(span, heads, dim).astype(BF16)
 
 
 def join_gradients(chunks, by_head):
-    n, _, half, rows, width, dim = chunks.shape
+    n, _, half, rows, width, dim = chunks[0].shape
     tokens, heads = by_head[0].shape[1], 2 * half
     return pl.pallas_call(
         join_kernel,
         grid=(rows,),
-        in_specs=[pl.BlockSpec((n, 3, half, pl.squeezed, width, dim), lambda r: (0, 0, 0, r, 0, 0))]
+        in_specs=[pl.BlockSpec((n, k, half, pl.squeezed, width, dim), lambda r: (0, 0, 0, r, 0, 0)) for k in (1, 2)]
         + [pl.BlockSpec((half, C, dim), lambda r: (0, r, 0))] * 3,
         out_specs=[pl.BlockSpec((C, heads, dim), lambda r: (r, 0, 0))] * 3,
         scratch_shapes=[pltpu.VMEM((C * heads, dim), F32)],
         out_shape=[jax.ShapeDtypeStruct((tokens, heads, dim), BF16)] * 3,
         compiler_params=params(60),
         name="join_gradients",
-    )(chunks, *by_head)
+    )(*chunks, *by_head)
 
 
 def collect_kernel(row_ref, chunk_ref, flat_ref, both_ref):
@@ -115,18 +115,21 @@
     )(row_out, chunks)
 
 
-def attn_grad_kernel(n, dim, ids, grad_ref, *refs):
-    blocks, (row_ref, chunk_ref, weight, total, sem) = refs[:n], refs[n:]
+def attn_grad_kernel(n, dim, last, ids, grad_ref, *refs):
+    blocks, refs = refs[:n], refs[n:]
     step = pl.program_id(0)
-    _, half, rows, width, _ = chunk_ref.shape
+    if last:
+        so_far, row_ref, chunk_ref, weight, sem, total = refs
+    else:
+        total, weight, sem = refs
     tokens = grad_ref.shape[0]
     tile = tokens // 4
 
     @pl.when(step == 0)
     def _():
         for d in range(n):
-            pltpu.make_async_copy(blocks[d], weight.at[ids[d]], sem.at[ids[d]]).start()
-        total[...] = jnp.zeros_like(total)
+            pltpu.make_async_copy(blocks[d], weight.at[d], sem.at[d]).start()
+        total[...] = so_far[...] if last else jnp.zeros_like(total)
 
     pltpu.make_async_copy(blocks[0], weight.at[step], sem.at[step]).wait()
 
@@ -135,46 +138,53 @@
         at = pl.multiple_of(at, tile)
         total[pl.ds(at, tile)] += dot(grad_ref[pl.ds(at, tile)], weight[step], ((1,), (1,)))
 
-    @pl.when(step == n - 1)
-    def _():
-        for head in range(half):
-            row_ref[:, head * dim : (head + 1) * dim] = total[:, 2 * head * dim : (2 * head + 1) * dim].astype(BF16)
-            for d in range(n):
-                for row in range(rows):
-                    at = row * C + d * width
-                    part = total[at : at + width, (2 * head + 1) * dim : (2 * head + 2) * dim]
-                    chunk_ref[d, head, row] = part.astype(BF16)
-
-
-def attn_grad(ids, out_grad, blocks, dim):
-    n, (span, depth) = len(blocks), blocks[0].shape
-    tokens, half = out_grad.shape[0], span // dim // 2
+    if last:
+
+        @pl.when(step == n - 1)
+        def _():
+            places, half, rows, width, _ = chunk_ref.shape
+            for head in range(half):
+                row_ref[:, head * dim : (head + 1) * dim] = total[:, 2 * head * dim : (2 * head + 1) * dim].astype(BF16)
+                for d in range(places):
+                    for row in range(rows):
+                        at = row * C + d * width
+                        part = total[at : at + width, (2 * head + 1) * dim : (2 * head + 2) * dim]
+                        chunk_ref[d, head, row] = part.astype(BF16)
+
+
+def attn_grad(ids, out_grad, blocks, so_far, dim):
+    m, (span, depth), last = len(blocks), blocks[0].shape, so_far is not None
+    tokens, model = out_grad.shape
+    n, half = model // depth, span // dim // 2
+    total = jax.ShapeDtypeStruct((tokens, span), F32)
+    whole = pl.BlockSpec((tokens, span), lambda b, ids: (0, 0))
     chunk = jax.ShapeDtypeStruct((n, half, tokens // C, C // n, dim), BF16)
-    return pl.pallas_call(
-        functools.partial(attn_grad_kernel, n, dim),
+    scratch = [pltpu.VMEM((m, span, depth), BF16), pltpu.SemaphoreType.DMA((m,))]
+    return pl.pallas_call(
+        functools.partial(attn_grad_kernel, m, dim, last),
         grid_spec=pltpu.PrefetchScalarGridSpec(
             num_scalar_prefetch=1,
-            grid=(n,),
-            in_specs=[pl.BlockSpec((tokens, depth), lambda b, ids: (0, b))] + [pl.BlockSpec(memory_space=pl.ANY)] * n,
+            grid=(m,),
+            in_specs=[pl.BlockSpec((tokens, depth), lambda b, ids: (0, ids[b]))]
+            + [pl.BlockSpec(memory_space=pl.ANY)] * m
+            + [whole] * last,
             out_specs=[
                 pl.BlockSpec((tokens, half * dim), lambda b, ids: (0, 0)),
                 pl.BlockSpec(chunk.shape, lambda b, ids: (0, 0, 0, 0, 0)),
-            ],
-            scratch_shapes=[
-                pltpu.VMEM((n, span, depth), BF16),
-                pltpu.VMEM((tokens, span), F32),
-                pltpu.SemaphoreType.DMA((n,)),
-            ],
-        ),
-        out_shape=[jax.ShapeDtypeStruct((tokens, half * dim), BF16), chunk],
+            ]
+            if last
+            else whole,
+            scratch_shapes=scratch + [pltpu.VMEM(total.shape, F32)] * last,
+        ),
+        out_shape=[jax.ShapeDtypeStruct((tokens, half * dim), BF16), chunk] if last else total,
         compiler_params=params(60),
         cost_estimate=pl.CostEstimate(
-            flops=2 * tokens * span * depth * n,
-            bytes_accessed=2 * n * depth * (tokens + span) + 2 * tokens * span,
+            flops=2 * tokens * span * depth * m,
+            bytes_accessed=2 * m * depth * (tokens + span) + 4 * tokens * span,
             transcendentals=0,
         ),
         name="attn_grad",
-    )(ids, out_grad, *blocks)
+    )(ids, out_grad, *blocks, *([so_far] if last else []))
 
 
 def layer_kernel(n, count, adds, ids, wanted, flat_ref, *refs):
@@ -416,7 +426,7 @@
     )(chunks)
 
 
-def column_backward_kernel(scale, chunk_ref, grad_ref, out_ref, bias):
+def column_backward_kernel(scale, chunk_ref, grad_ref, query_ref, rest_ref, bias):
     half, width = chunk_ref.shape[2], chunk_ref.shape[4]
     bias[...] = jnp.where(column_mask(bias.shape[0]), 0.0, -jnp.inf)
     blocks = width // LANE
@@ -430,9 +440,9 @@
         prob_grad = dot(grad, v, ((1,), (1,)))
         inner = jnp.sum(probs * prob_grad, axis=-1, keepdims=True)
         score_low = (probs * (prob_grad - inner)).astype(BF16)
-        scattered(out_ref, (0, head), at, (dot(score_low, k, ((1,), (0,))) * scale).astype(BF16))
-        scattered(out_ref, (1, head), at, (dot(score_low, q, ((0,), (0,))) * scale).astype(BF16))
-        scattered(out_ref, (2, head), at, dot(probs.astype(BF16), grad, ((0,), (0,))).astype(BF16))
+        scattered(query_ref, (0, head), at, (dot(score_low, k, ((1,), (0,))) * scale).astype(BF16))
+        scattered(rest_ref, (0, head), at, (dot(score_low, q, ((0,), (0,))) * scale).astype(BF16))
+        scattered(rest_ref, (1, head), at, dot(probs.astype(BF16), grad, ((0,), (0,))).astype(BF16))
 
 
 def column_backward(chunks, grads):
@@ -441,8 +451,8 @@
     return pl.pallas_call(
         functools.partial(column_backward_kernel, dim**-0.5),
         in_specs=[VMEM] * 2,
-        out_specs=VMEM,
-        out_shape=jax.ShapeDtypeStruct(chunks.shape, BF16),
+        out_specs=[VMEM] * 2,
+        out_shape=[jax.ShapeDtypeStruct((n, k, half, rows, width, dim), BF16) for k in (1, 2)],
         scratch_shapes=[pltpu.VMEM((size, size), F32)],
         compiler_params=params(24),
         cost_estimate=pl.CostEstimate(
@@ -561,38 +571,42 @@
     blocks = own_blocks + near_blocks + far_own_blocks + far_near_blocks
     ids = [owner * inner + (spot ^ e) for owner in (line, line ^ 1, *far) for e in range(inner)]
     ids = jnp.stack(ids).astype(jnp.int32)
+    early = n - inner
 
     outs = column_forward(after(chunks, *far_own_blocks))
     column_part = swap(outs)
-    grad_row, grads = attn_grad(ids, after(out_grad, outs), blocks, dim)
+    so_far = attn_grad(ids[:early], after(out_grad, outs), blocks[:early], None, dim)
+    grad_row, grads = attn_grad(ids[early:], out_grad, blocks[early:], so_far, dim)
     row_far = exchanged([after(part, *far_near_blocks) for part in row_far])
     row_close = exchanged(row_close)
     grads = swap(after(grads, column_part, *row_far))
     (row_far,) = summed(after(row_out, outs), far, row_far, 0)
     row_far_in = links.along(row_far, INWARD)
-    column_out, flat = collect(row_out, column_part)
+    column_out, flat = collect(row_out, after(column_part, row_far))
     column_far, column_close = leaving(column_out, far), leaving(column_out, close)
     column_far = exchanged(column_far)
-    layer = LayerSum(ids, flat, blocks, heads_n)
+    grad_query, grad_rest = column_backward(chunks, after(grads, *column_close, row_far))
+    grad_query = swap(after(grad_query, *column_far))
+
+    layer = LayerSum(ids, after(flat, grad_rest), blocks, heads_n)
+    (column_far,) = summed(after(column_out, grad_rest), far, column_far, 0)
+    column_far_in = links.along(column_far, INWARD)
+    row_cross = links.along(add(row_far, after(row_far_in, grad_rest)), CROSS)
+    column_close = exchanged(column_close)
+    row_near, row_own = summed(after(row_out, grad_rest), close, row_close, 1)
+    row_near_in = links.along(row_near[0], INWARD)
     layer.start()
-    gradients = column_backward(chunks, after(grads, *column_close, row_far, layer.first))
-    column_grads = swap(after(gradients, *column_far, row_far_in, *row_close))
-
-    column_close = exchanged(column_close)
-    row_cross = links.along(add(row_far, row_far_in), CROSS)
-    row_near, row_own = summed(after(row_out, gradients), close, row_close, 1)
-    row_near_in = links.along(row_near[0], INWARD)
-    (column_far,) = summed(after(column_out, gradients), far, column_far, 0)
-    column_far_in = links.along(column_far, INWARD)
-    layer.turn(gradients)
-    row_grads = row_backward(*by_head, after(grad_row, column_far))
+    grad_rest = swap(after(grad_rest, grad_query, column_far_in, row_cross, layer.first))
+    column_cross = links.along(add(column_far, column_far_in), CROSS)
+    layer.turn(layer.near)
+    row_grads = row_backward(*by_head, after(grad_row, column_far_in))
     column_near, column_own = summed(after(column_out, *layer.parts), close, column_close, 1)
     column_near_in = links.along(column_near[0], INWARD)
-    column_cross = links.along(add(column_far, after(column_far_in, row_grads[0])), CROSS)
+    column_cross = after(column_cross, row_grads[0])
     row_back = links.along(add(row_near[0], row_cross[1]), OUTWARD)
     column_back = links.along(add(column_near[0], column_cross[1]), OUTWARD)
 
-    gradients = join_gradients(column_grads, row_grads)
+    gradients = join_gradients([grad_query, grad_rest], row_grads)
     proj_row = add(row_own[0], row_near_in, row_cross[0], row_back)
     proj_column = add(column_own[0], column_near_in, column_cross[0], column_back)
     shape = (half, dim, depth)

time: 422 us -> 446 us (1.057)
  waiting for transfers between devices: 165 us -> 179 us
  Pallas kernels: 151 us -> 158 us
    ppermute x21, waiting for transfers between devices: 165 us -> 179 us  [send(): out = lax.ppermute(value, 'ctx', pairs)]
    pallas_call x2 -> x3, Pallas kernels: 28.4 us -> 34.1 us  [the longest x2 26.7 us: attn_grad(): pl.pallas_call(functools.partial(attn_grad_kernel, m, dim, last), grid_sp...]
    all_to_all x4 -> x5, starting transfers between devices: 24 us -> 27.2 us  [swap(): lax.all_to_all(chunks, 'ctx', split_axis=0, concat_axis=0, tiled=True)]
  transfers between devices with their start and end apart: 27 -> 28, of which waited for: 12 -> 12; matrix products, arithmetic and copies ran while one was open for 6% -> 5% of each run, Pallas kernels for 34% -> 34%
where the time goes in v7:
time: 446 us; the launch traced here: 444 us
  waiting for transfers between devices  179 us (40%)
  Pallas kernels  158 us (35%)
  starting transfers between devices  74.6 us (17%)
  other arithmetic  19.8 us (4%)
  local copies, waits for them, and re-layouts  10.4 us (2%)
    ppermute x21, waiting for transfers between devices, send(): out = lax.ppermute(value, 'ctx', pairs)  179 us
    ppermute x21, starting transfers between devices, send(): out = lax.ppermute(value, 'ctx', pairs)  45.8 us
    pallas_call x8, Pallas kernels, proj_part(): pl.pallas_call(functools.partial(proj_kernel, lead, len(extra), dim), gri...  40.5 us
    pallas_call x3, Pallas kernels, layer_part(): pl.pallas_call(functools.partial(layer_kernel, n, count, len(extra)), gri...  29.5 us
    all_to_all x5, starting transfers between devices, swap(): lax.all_to_all(chunks, 'ctx', split_axis=0, concat_axis=0, tiled=True)  27.2 us
    pallas_call x2, Pallas kernels, attn_grad(): pl.pallas_call(functools.partial(attn_grad_kernel, m, dim, last), grid_sp...  26.7 us
    pallas_call x1, Pallas kernels, column_backward(): pl.pallas_call(functools.partial(column_backward_kernel, dim ** (-0.5)),...  14.5 us
    pallas_call x1, Pallas kernels, row_backward(): pl.pallas_call(functools.partial(row_backward_kernel, dim ** (-0.5)), gri...  13.6 us
  transfers between devices with their start and end apart: 28, of which 12 were waited for; matrix products, arithmetic and copies ran while one was open for 5% of the time, Pallas kernels for 34%

profile of v7, /device:TPU:8, one launch (start us, length us, event | category | flops | bytes accessed | tf_op | source)
XLA Modules:
  0.0 443.7 jit_solution(8766495821092136748)
XLA Ops:
  0.6 3.5 collective-permute-start.4
  5.8 7.1 %split_inputs.1 = (bf16[8,3,4,2,64,128]{5,4,3,2,1,0:T(8,128)(2,1)}, bf16[4,1024,128]{2,1,0:T(8,128)(2,1)}, bf16[4,1024,128]{2,1,0:T(8,128)(2,1)}, bf16[4,1024,128]{2,1,0:T(8,128)(2,1)}) custom-call(bf16[1024,8,128]{2,1,0:T(8,128)(2,1)} %q_ref.1, bf16[1024,8,128]{2,1,0:T(8,128)(2,1)} %k_ref.1, bf16[1024,8,128]{2,1,0:T(8,128)(2,1)} %v_ref.1), custom_call_target="tpu_custom_call" | custom-call | tf_op jit(solution)/shard_map/split_inputs/pallas_call | solution.py:48
  12.9 14.9 %collective-permute-done.4 = bf16[1024,512]{1,0:T(8,128)(2,1)} collective-permute-done((bf16[1024,512]{1,0:T(8,128)(2,1)}, bf16[1024,512]{1,0:T(8,128)(2,1)}, u32[]{:S(2)}, u32[]{:S(2)}) %collective-permute-start.4) | collective-permute-done | bytes 1048608 | tf_op jit(solution)/shard_map/ppermute | solution.py:485
  29.0 3.2 collective-permute-start.5
  32.2 3.1 collective-permute-start.3
  36.9 9.9 %row_forward.1.flat_ref.row_ref = bf16[1024,512]{1,0:T(8,128)(2,1)} custom-call(bf16[4,1024,128]{2,1,0:T(8,128)(2,1)} %get-tuple-element.60.q_ref, bf16[4,1024,128]{2,1,0:T(8,128)(2,1)} %get-tuple-element.61.k_ref, bf16[4,1024,128]{2,1,0:T(8,128)(2,1)} %get-tuple-element.62.v_ref), custom_call_target="tpu_custom_call" | custom-call | flops 1073741824 | bytes 4194304 | tf_op jit(solution)/shard_map/row_forward/pallas_call | solution.py:321
  47.4 4.9 %proj_part.9 = bf16[2,512,512]{2,1,0:T(8,128)(2,1)} custom-call(s32[2]{0:T(128)} %pad_add_fusion.2.order, bf16[1024,512]{1,0:T(8,128)(2,1)} %row_forward.1.flat_ref.row_ref, bf16[1024,4096]{1,0:T(8,128)(2,1)} %grad_ref.18), custom_call_target="tpu_custom_call" | custom-call | flops 1073741824 | bytes 4194304 | tf_op jit(solution)/shard_map/proj_part/pallas_call | solution.py:275
  52.8 4.9 %proj_part.8 = bf16[2,512,512]{2,1,0:T(8,128)(2,1)} custom-call(s32[2]{0:T(128)} %pad_add_fusion.1.order, bf16[1024,512]{1,0:T(8,128)(2,1)} %row_forward.1.flat_ref.row_ref, bf16[1024,4096]{1,0:T(8,128)(2,1)} %grad_ref.18), custom_call_target="tpu_custom_call" | custom-call | flops 1073741824 | bytes 4194304 | tf_op jit(solution)/shard_map/proj_part/pallas_call | solution.py:275
  59.8 4.5 %all-to-all-start = ((bf16[8,3,4,2,64,128]{5,4,3,2,1,0:T(8,128)(2,1)}), bf16[8,3,4,2,64,128]{5,4,3,2,1,0:T(8,128)(2,1)S(1)}, u32[]{:S(2)}, u32[]{:S(2)}) async-start(bf16[8,3,4,2,64,128]{5,4,3,2,1,0:T(8,128)(2,1)} %get-tuple-element.66), calls=%async_computation | async-start | bytes 6291456 | tf_op jit(solution)/shard_map/all_to_all | solution.py:497
  64.3 2.9 collective-permute-start.7
  68.5 2.1 collective-permute-start.6
  70.6 64.5 %collective-permute-done.7 = bf16[1024,512]{1,0:T(8,128)(2,1)} collective-permute-done((bf16[1024,512]{1,0:T(8,128)(2,1)}, bf16[1024,512]{1,0:T(8,128)(2,1)}, u32[]{:S(2)}, u32[]{:S(2)}) %collective-permute-start.7) | collective-permute-done | bytes 1048608 | tf_op jit(solution)/shard_map/ppermute | solution.py:485
  135.1 2.3 broadcast_select_fusion.refs_0_.refs_6_
  138.9 8.7 %column_forward.1 = bf16[8,4,2,64,128]{4,3,2,1,0:T(8,128)(2,1)S(1)} custom-call(bf16[8,3,4,2,64,128]{5,4,3,2,1,0:T(8,128)(2,1)S(1)} %all-to-all-done.chunk_ref), custom_call_target="tpu_custom_call" | custom-call | flops 536870912 | bytes 4194304 | tf_op jit(solution)/shard_map/column_forward/pallas_call | solution.py:413
  148.6 6.2 %all-to-all-start.1 = ((bf16[8,4,2,64,128]{4,3,2,1,0:T(8,128)(2,1)}), bf16[8,4,2,64,128]{4,3,2,1,0:T(8,128)(2,1)S(1)}, u32[]{:S(2)}, u32[]{:S(2)}) async-start(bf16[8,4,2,64,128]{4,3,2,1,0:T(8,128)(2,1)} %copy-done.5), calls=%async_computation.1 | async-start | bytes 2097152 | tf_op jit(solution)/shard_map/all_to_all | solution.py:497
  154.7 15.2 %collective-permute-done.8.refs_1_.refs_7_ = bf16[1024,512]{1,0:T(8,128)(2,1)} collective-permute-done((bf16[1024,512]{1,0:T(8,128)(2,1)}, bf16[1024,512]{1,0:T(8,128)(2,1)}, u32[]{:S(2)}, u32[]{:S(2)}) %collective-permute-start.8) | collective-permute-done | bytes 1048608 | tf_op jit(solution)/shard_map/ppermute | solution.py:485
  169.9 3.0 collective-permute-start.9
  174.2 16.6 %attn_grad.2.refs_2_ = f32[1024,1024]{1,0:T(8,128)} custom-call(s32[6]{0:T(128)} %stack.115.ids, bf16[1024,4096]{1,0:T(8,128)(2,1)} %grad_ref.18, bf16[1024,512]{1,0:T(8,128)(2,1)} %refs_0_.7, bf16[1024,512]{1,0:T(8,128)(2,1)} %copy-done.9, bf16[1024,512]{1,0:T(8,128)(2,1)} %copy-done.8, bf16[1024,512]{1,0:T(8,128)(2,1)} %copy-done.10, ...), custom_call_target="tpu_custom_call" | custom-call | flops 6442450944 | bytes 16777216 | tf_op jit(solution)/shard_map/attn_grad/pallas_call | solution.py:163
  190.8 10.1 %attn_grad.3 = (bf16[1024,512]{1,0:T(8,128)(2,1)}, bf16[8,4,2,64,128]{4,3,2,1,0:T(8,128)(2,1)}) custom-call(s32[2]{0:T(128)} %pad_add_fusion.4.ids, bf16[1024,4096]{1,0:T(8,128)(2,1)} %grad_ref.18, bf16[1024,512]{1,0:T(8,128)(2,1)} %broadcast_select_fusion.refs_0_.refs_6_, bf16[1024,512]{1,0:T(8,128)(2,1)} %collective-permute-done.8.refs_1_.refs_7_, ...), custom_call_target="tpu_custom_call" | custom-call | flops 2147483648 | bytes 8388608 | tf_op jit(solution)/shard_map/attn_grad/pallas_call | solution.py:163
  200.9 6.6 %all-to-all-start.2 = ((bf16[8,4,2,64,128]{4,3,2,1,0:T(8,128)(2,1)}), bf16[8,4,2,64,128]{4,3,2,1,0:T(8,128)(2,1)}, u32[]{:S(2)}, u32[]{:S(2)}) async-start(bf16[8,4,2,64,128]{4,3,2,1,0:T(8,128)(2,1)} %get-tuple-element.78), calls=%async_computation.2 | async-start | bytes 2097152 | tf_op jit(solution)/shard_map/all_to_all | solution.py:497
  209.4 5.4 %proj_part.10 = bf16[2,512,512]{2,1,0:T(8,128)(2,1)} custom-call(s32[2]{0:T(128)} %pad_add_fusion.3.order, bf16[1024,512]{1,0:T(8,128)(2,1)} %row_forward.1.flat_ref.row_ref, bf16[1024,4096]{1,0:T(8,128)(2,1)} %grad_ref.18, bf16[2,512,512]{2,1,0:T(8,128)(2,1)} %copy-done.16), custom_call_target="tpu_custom_call" | custom-call | flops 1073741824 | bytes 5242880 | tf_op jit(solution)/shard_map/proj_part/pallas_call | solution.py:275
  217.8 4.8 %proj_part.12 = bf16[2,512,512]{2,1,0:T(8,128)(2,1)} custom-call(s32[2]{0:T(128)} %pad_add_fusion.1.order, bf16[1024,512]{1,0:T(8,128)(2,1)} %copy-done.1, bf16[1024,4096]{1,0:T(8,128)(2,1)} %grad_ref.18), custom_call_target="tpu_custom_call" | custom-call | flops 1073741824 | bytes 4194304 | tf_op jit(solution)/shard_map/proj_part/pallas_call | solution.py:275
  224.1 4.8 %proj_part.11 = bf16[2,512,512]{2,1,0:T(8,128)(2,1)} custom-call(s32[2]{0:T(128)} %pad_add_fusion.2.order, bf16[1024,512]{1,0:T(8,128)(2,1)} %copy-done.1, bf16[1024,4096]{1,0:T(8,128)(2,1)} %grad_ref.18), custom_call_target="tpu_custom_call" | custom-call | flops 1073741824 | bytes 4194304 | tf_op jit(solution)/shard_map/proj_part/pallas_call | solution.py:275
  229.6 14.5 %column_backward.1 = (bf16[8,1,4,2,64,128]{5,4,3,2,1,0:T(8,128)(2,1)}, bf16[8,2,4,2,64,128]{5,4,3,2,1,0:T(8,128)(2,1)}) custom-call(bf16[8,3,4,2,64,128]{5,4,3,2,1,0:T(8,128)(2,1)S(1)} %copy-done.3, bf16[8,4,2,64,128]{4,3,2,1,0:T(8,128)(2,1)} %all-to-all-done.2.grad_ref), custom_call_target="tpu_custom_call" | custom-call | flops 1342177280 | bytes 7340032 | tf_op jit(solution)/shard_map/column_backward/pallas_call | solution.py:451
  244.1 11.8 %layer_part.3 = bf16[1024,2048]{1,0:T(8,128)(2,1)} custom-call(s32[8]{0:T(128)} %stack.107.ids, s32[4]{0:T(128)} %pad_add_fusion.5.wanted, bf16[1024,1024]{1,0:T(8,128)(2,1)} %copy-done.4, bf16[1024,512]{1,0:T(8,128)(2,1)} %refs_0_.7, bf16[1024,512]{1,0:T(8,128)(2,1)} %copy-done.9, bf16[1024,512]{1,0:T(8,128)(2,1)} %copy-done.8, ...), custom_call_target="tpu_custom_call" | custom-call | flops 4294967296 | bytes 10485760 | tf_op jit(solution)/shard_map/layer_part/pallas_call | solution.py:221
  257.3 6.2 %all-to-all-start.3 = ((bf16[8,1,4,2,64,128]{5,4,3,2,1,0:T(8,128)(2,1)}), bf16[8,1,4,2,64,128]{5,4,3,2,1,0:T(8,128)(2,1)S(1)}, u32[]{:S(2)}, u32[]{:S(2)}) async-start(bf16[8,1,4,2,64,128]{5,4,3,2,1,0:T(8,128)(2,1)} %get-tuple-element.86), calls=%async_computation.3 | async-start | bytes 2097152 | tf_op jit(solution)/shard_map/all_to_all | solution.py:497
  263.5 20.4 %collective-permute-done.14 = bf16[2,512,512]{2,1,0:T(8,128)(2,1)S(1)} collective-permute-done((bf16[2,512,512]{2,1,0:T(8,128)(2,1)S(1)}, bf16[2,512,512]{2,1,0:T(8,128)(2,1)S(1)}, u32[]{:S(2)}, u32[]{:S(2)}) %collective-permute-start.14) | collective-permute-done | bytes 1048608 | tf_op jit(solution)/shard_map/ppermute | solution.py:485
  285.1 5.0 %proj_part.13 = bf16[2,512,512]{2,1,0:T(8,128)(2,1)} custom-call(s32[2]{0:T(128)} %pad_add_fusion.3.order, bf16[1024,512]{1,0:T(8,128)(2,1)} %copy-done.1, bf16[1024,4096]{1,0:T(8,128)(2,1)} %grad_ref.18, bf16[2,512,512]{2,1,0:T(8,128)(2,1)} %collective-permute-done.12.refs_0_), custom_call_target="tpu_custom_call" | custom-call | flops 1073741824 | bytes 5242880 | tf_op jit(solution)/shard_map/proj_part/pallas_call | solution.py:275
  291.6 2.8 collective-permute-start.15
  295.1 27.7 %collective-permute-done.13 = bf16[2,512,512]{2,1,0:T(8,128)(2,1)S(1)} collective-permute-done((bf16[2,512,512]{2,1,0:T(8,128)(2,1)}, bf16[2,512,512]{2,1,0:T(8,128)(2,1)S(1)}, u32[]{:S(2)}, u32[]{:S(2)}) %collective-permute-start.13) | collective-permute-done | bytes 1048608 | tf_op jit(solution)/shard_map/ppermute | solution.py:485
  325.2 3.8 all-to-all-start.4
  330.5 2.5 add_convert_fusion
  333.0 3.4 collective-permute-start.21
  337.0 8.5 %layer_part.4 = bf16[1024,1024]{1,0:T(8,128)(2,1)} custom-call(s32[8]{0:T(128)} %stack.107.ids, s32[2]{0:T(128)} %pad_add_fusion.6.wanted, bf16[1024,1024]{1,0:T(8,128)(2,1)} %copy-done.4, bf16[1024,512]{1,0:T(8,128)(2,1)} %refs_0_.7, bf16[1024,512]{1,0:T(8,128)(2,1)} %copy-done.9, bf16[1024,512]{1,0:T(8,128)(2,1)} %copy-done.8, ...), custom_call_target="tpu_custom_call" | custom-call | flops 2147483648 | bytes 6291456 | tf_op jit(solution)/shard_map/layer_part/pallas_call | solution.py:221
  347.6 5.4 %proj_part.14 = (bf16[1,512,512]{2,1,0:T(8,128)(2,1)}, bf16[1,512,512]{2,1,0:T(8,128)(2,1)}) custom-call(s32[2]{0:T(128)} %pad_add_fusion.7.order, bf16[1024,512]{1,0:T(8,128)(2,1)} %row_forward.1.flat_ref.row_ref, bf16[1024,4096]{1,0:T(8,128)(2,1)} %grad_ref.18, bf16[2,512,512]{2,1,0:T(8,128)(2,1)} %collective-permute-done.16.refs_0_), custom_call_target="tpu_custom_call" | custom-call | flops 1073741824 | bytes 5242880 | tf_op jit(solution)/shard_map/proj_part/pallas_call | solution.py:275
  354.3 2.0 fusion.3
  356.3 6.3 %collective-permute-start.18 = (bf16[512,512]{1,0:T(8,128)(2,1)}, bf16[512,512]{1,0:T(8,128)(2,1)}, u32[]{:S(2)}, u32[]{:S(2)}) collective-permute-start(bf16[512,512]{1,0:T(8,128)(2,1)} %fusion.3), channel_id=1, source_target_pairs={{8,0},{12,4},{16,24},{20,28},{9,1},{13,5},{17,25},{21,29},{10,2},{... | collective-permute-start | bytes 1572872 | tf_op jit(solution)/shard_map/ppermute | solution.py:485
  362.6 13.6 %row_backward.1 = (bf16[4,1024,128]{2,1,0:T(8,128)(2,1)}, bf16[4,1024,128]{2,1,0:T(8,128)(2,1)}, bf16[4,1024,128]{2,1,0:T(8,128)(2,1)}) custom-call(bf16[4,1024,128]{2,1,0:T(8,128)(2,1)} %get-tuple-element.60.q_ref, bf16[4,1024,128]{2,1,0:T(8,128)(2,1)} %get-tuple-element.61.k_ref, bf16[4,1024,128]{2,1,0:T(8,128)(2,1)} %get-tuple-element.62.v_ref, ...), custom_call_target="tpu_custom_call" | custom-call | flops 2684354560 | bytes 7340032 | tf_op jit(solution)/shard_map/row_backward/pallas_call | solution.py:355
  376.2 22.2 %collective-permute-done.21 = bf16[2,512,512]{2,1,0:T(8,128)(2,1)} collective-permute-done((bf16[2,512,512]{2,1,0:T(8,128)(2,1)}, bf16[2,512,512]{2,1,0:T(8,128)(2,1)}, u32[]{:S(2)}, u32[]{:S(2)}) %collective-permute-start.21) | collective-permute-done | bytes 1048608 | tf_op jit(solution)/shard_map/ppermute | solution.py:485
  398.4 5.2 %proj_part.15 = (bf16[1,512,512]{2,1,0:T(8,128)(2,1)}, bf16[1,512,512]{2,1,0:T(8,128)(2,1)}) custom-call(s32[2]{0:T(128)} %pad_add_fusion.7.order, bf16[1024,512]{1,0:T(8,128)(2,1)} %copy-done.1, bf16[1024,4096]{1,0:T(8,128)(2,1)} %grad_ref.18, bf16[2,512,512]{2,1,0:T(8,128)(2,1)} %collective-permute-done.19.refs_0_), custom_call_target="tpu_custom_call" | custom-call | flops 1073741824 | bytes 5242880 | tf_op jit(solution)/shard_map/proj_part/pallas_call | solution.py:275
  403.6 2.1 fusion
  405.8 2.1 collective-permute-start.22
  409.8 1.6 fusion.5
  411.5 6.5 %collective-permute-done.22 = bf16[512,512]{1,0:T(8,128)(2,1)} collective-permute-done((bf16[512,512]{1,0:T(8,128)(2,1)}, bf16[512,512]{1,0:T(8,128)(2,1)}, u32[]{:S(2)}, u32[]{:S(2)}) %collective-permute-start.22) | collective-permute-done | bytes 524320 | tf_op jit(solution)/shard_map/ppermute | solution.py:485
  417.9 4.9 %collective-permute-done.20 = bf16[512,512]{1,0:T(8,128)(2,1)} collective-permute-done((bf16[512,512]{1,0:T(8,128)(2,1)}, bf16[512,512]{1,0:T(8,128)(2,1)}, u32[]{:S(2)}, u32[]{:S(2)}) %collective-permute-start.20) | collective-permute-done | bytes 524320 | tf_op jit(solution)/shard_map/ppermute | solution.py:485
  422.8 1.6 fusion.2
  427.0 7.3 %join_gradients.1 = (bf16[1024,8,128]{2,1,0:T(8,128)(2,1)}, bf16[1024,8,128]{2,1,0:T(8,128)(2,1)}, bf16[1024,8,128]{2,1,0:T(8,128)(2,1)}) custom-call(bf16[8,1,4,2,64,128]{5,4,3,2,1,0:T(8,128)(2,1)} %copy-done.13, bf16[8,2,4,2,64,128]{5,4,3,2,1,0:T(8,128)(2,1)} %copy-done.7, bf16[4,1024,128]{2,1,0:T(8,128)(2,1)} %get-tuple-element.95.refs_0_, ...), custom_call_target="tpu_custom_call" | custom-call | tf_op jit(solution)/shard_map/join_gradients/pallas_call | solution.py:78
  434.3 9.2 %layer_part.5 = bf16[1024,1024]{1,0:T(8,128)(2,1)} custom-call(s32[8]{0:T(128)} %stack.107.ids, s32[2]{0:T(128)} %pad_add_fusion.wanted, bf16[1024,1024]{1,0:T(8,128)(2,1)} %copy-done.4, bf16[1024,512]{1,0:T(8,128)(2,1)} %refs_0_.7, bf16[1024,512]{1,0:T(8,128)(2,1)} %copy-done.9, bf16[1024,512]{1,0:T(8,128)(2,1)} %copy-done.8, bf16[1024,512]{1,0:T(8,128)(2,1)} %copy-done.10, ...), custom_call_target="tpu_custom_call" | custom-call | flops 2147483648 | bytes 6291456 | tf_op jit(solution)/shard_map/layer_part/pallas_call | solution.py:221
  (86 shorter events, 37.0 us)
Async XLA Ops:
  0.6 27.1 %collective-permute-start.4 = (bf16[1024,512]{1,0:T(8,128)(2,1)}, bf16[1024,512]{1,0:T(8,128)(2,1)}, u32[]{:S(2)}, u32[]{:S(2)}) collective-permute-start(bf16[1024,512]{1,0:T(8,128)(2,1)} %refs_0_.7), channel_id=1, source_target_pairs={{8,16},{12,20},{16,8},{20,12},{9,17},{13,21},{17,9},{21,13},{10,18... | collective-permute-start | bytes 3145736 | tf_op jit(solution)/shard_map/ppermute | solution.py:485
  4.1 24.9 %collective-permute-start = (bf16[1024,512]{1,0:T(8,128)(2,1)}, bf16[1024,512]{1,0:T(8,128)(2,1)S(1)}, u32[]{:S(2)}, u32[]{:S(2)}) collective-permute-start(bf16[1024,512]{1,0:T(8,128)(2,1)} %refs_0_.7), channel_id=1, source_target_pairs={{0,8},{4,12},{8,0},{12,4},{16,24},{20,28},{24,16},{28,20},{1,9},{5... | collective-permute-start | bytes 3145736 | tf_op jit(solution)/shard_map/ppermute | solution.py:485
  4.2 28.0 %collective-permute-start.1 = (bf16[1024,512]{1,0:T(8,128)(2,1)}, bf16[1024,512]{1,0:T(8,128)(2,1)S(1)}, u32[]{:S(2)}, u32[]{:S(2)}) collective-permute-start(bf16[1024,512]{1,0:T(8,128)(2,1)} %refs_0_.7), channel_id=1, source_target_pairs={{0,4},{4,0},{8,12},{12,8},{16,20},{20,16},{24,28},{28,24},{1,5},{5... | collective-permute-start | bytes 3145736 | tf_op jit(solution)/shard_map/ppermute | solution.py:485
  29.0 17.8 %copy-start.8 = (bf16[1024,512]{1,0:T(8,128)(2,1)}, bf16[1024,512]{1,0:T(8,128)(2,1)S(1)}, u32[]{:S(2)}) copy-start(bf16[1024,512]{1,0:T(8,128)(2,1)S(1)} %collective-permute-done.refs_2_) | copy-start | bytes 3145732
  29.0 28.7 %collective-permute-start.5 = (bf16[1024,512]{1,0:T(8,128)(2,1)}, bf16[1024,512]{1,0:T(8,128)(2,1)}, u32[]{:S(2)}, u32[]{:S(2)}) collective-permute-start(bf16[1024,512]{1,0:T(8,128)(2,1)} %collective-permute-done.4), channel_id=1, source_target_pairs={{8,0},{12,4},{16,24},{20,28},{9,1},{13,5},{17,25},{21,29},{10,2},{... | collective-permute-start | bytes 3145736 | tf_op jit(solution)/shard_map/ppermute | solution.py:485
  32.2 14.6 %copy-start.9 = (bf16[1024,512]{1,0:T(8,128)(2,1)}, bf16[1024,512]{1,0:T(8,128)(2,1)S(1)}, u32[]{:S(2)}) copy-start(bf16[1024,512]{1,0:T(8,128)(2,1)S(1)} %collective-permute-done.1.refs_1_) | copy-start | bytes 3145732
  32.2 25.7 %collective-permute-start.3 = (bf16[1024,512]{1,0:T(8,128)(2,1)S(1)}, bf16[1024,512]{1,0:T(8,128)(2,1)}, u32[]{:S(2)}, u32[]{:S(2)}) collective-permute-start(bf16[1024,512]{1,0:T(8,128)(2,1)S(1)} %collective-permute-done.refs_2_), channel_id=1, source_target_pairs={{8,16},{12,20},{16,8},{20,12},{9,17},{13,21},{17,9},{21,13},{10,18... | collective-permute-start | bytes 3145736 | tf_op jit(solution)/shard_map/ppermute | solution.py:485
  35.3 23.5 %collective-permute-start.2 = (bf16[1024,512]{1,0:T(8,128)(2,1)S(1)}, bf16[1024,512]{1,0:T(8,128)(2,1)S(1)}, u32[]{:S(2)}, u32[]{:S(2)}) collective-permute-start(bf16[1024,512]{1,0:T(8,128)(2,1)S(1)} %collective-permute-done.refs_2_), channel_id=1, source_target_pairs={{0,4},{4,0},{8,12},{12,8},{16,20},{20,16},{24,28},{28,24},{1,5},{5... | collective-permute-start | bytes 3145736 | tf_op jit(solution)/shard_map/ppermute | solution.py:485
  58.9 1.0 copy-start.10
  59.8 79.0 %all-to-all-start = ((bf16[8,3,4,2,64,128]{5,4,3,2,1,0:T(8,128)(2,1)}), bf16[8,3,4,2,64,128]{5,4,3,2,1,0:T(8,128)(2,1)S(1)}, u32[]{:S(2)}, u32[]{:S(2)}) async-start(bf16[8,3,4,2,64,128]{5,4,3,2,1,0:T(8,128)(2,1)} %get-tuple-element.66), calls=%async_computation | async-start | bytes 6291456 | tf_op jit(solution)/shard_map/all_to_all | solution.py:497
  64.3 70.8 %collective-permute-start.7 = (bf16[1024,512]{1,0:T(8,128)(2,1)}, bf16[1024,512]{1,0:T(8,128)(2,1)}, u32[]{:S(2)}, u32[]{:S(2)}) collective-permute-start(bf16[1024,512]{1,0:T(8,128)(2,1)} %collective-permute-done.3), channel_id=1, source_target_pairs={{8,0},{12,4},{16,24},{20,28},{9,1},{13,5},{17,25},{21,29},{10,2},{... | collective-permute-start | bytes 3145736 | tf_op jit(solution)/shard_map/ppermute | solution.py:485
  68.5 70.3 %copy-start.6 = (bf16[1024,512]{1,0:T(8,128)(2,1)}, bf16[1024,512]{1,0:T(8,128)(2,1)S(1)}, u32[]{:S(2)}) copy-start(bf16[1024,512]{1,0:T(8,128)(2,1)S(1)} %broadcast_select_fusion.1.refs_4_) | copy-start | bytes 3145732
  68.5 70.3 %collective-permute-start.6 = (bf16[1024,512]{1,0:T(8,128)(2,1)S(1)}, bf16[1024,512]{1,0:T(8,128)(2,1)}, u32[]{:S(2)}, u32[]{:S(2)}) collective-permute-start(bf16[1024,512]{1,0:T(8,128)(2,1)S(1)} %broadcast_select_fusion.1.refs_4_), channel_id=1, source_target_pairs={{0,4},{4,0},{8,12},{12,8},{16,20},{20,16},{24,28},{28,24},{1,5},{5... | collective-permute-start | bytes 3145736 | tf_op jit(solution)/shard_map/ppermute | solution.py:485
  137.4 32.5 %collective-permute-start.8 = (bf16[1024,512]{1,0:T(8,128)(2,1)}, bf16[1024,512]{1,0:T(8,128)(2,1)}, u32[]{:S(2)}, u32[]{:S(2)}) collective-permute-start(bf16[1024,512]{1,0:T(8,128)(2,1)} %broadcast_select_fusion.refs_0_.refs_6_), channel_id=1, source_target_pairs={{0,4},{4,0},{8,12},{12,8},{16,20},{20,16},{24,28},{28,24},{1,5},{5... | collective-permute-start | bytes 3145736 | tf_op jit(solution)/shard_map/ppermute | solution.py:485
  138.9 8.7 %copy-start.2 = (bf16[8,3,4,2,64,128]{5,4,3,2,1,0:T(8,128)(2,1)}, bf16[8,3,4,2,64,128]{5,4,3,2,1,0:T(8,128)(2,1)S(1)}, u32[]{:S(2)}) copy-start(bf16[8,3,4,2,64,128]{5,4,3,2,1,0:T(8,128)(2,1)S(1)} %all-to-all-done.chunk_ref) | copy-start | bytes 9437188
  147.6 1.0 copy-start.5
  148.6 52.4 %all-to-all-start.1 = ((bf16[8,4,2,64,128]{4,3,2,1,0:T(8,128)(2,1)}), bf16[8,4,2,64,128]{4,3,2,1,0:T(8,128)(2,1)S(1)}, u32[]{:S(2)}, u32[]{:S(2)}) async-start(bf16[8,4,2,64,128]{4,3,2,1,0:T(8,128)(2,1)} %copy-done.5), calls=%async_computation.1 | async-start | bytes 2097152 | tf_op jit(solution)/shard_map/all_to_all | solution.py:497
  169.9 31.0 %collective-permute-start.9 = (bf16[2,512,512]{2,1,0:T(8,128)(2,1)}, bf16[2,512,512]{2,1,0:T(8,128)(2,1)S(1)}, u32[]{:S(2)}, u32[]{:S(2)}) collective-permute-start(bf16[2,512,512]{2,1,0:T(8,128)(2,1)} %proj_part.8), channel_id=1, source_target_pairs={{0,4},{4,0},{8,12},{12,8},{16,20},{20,16},{24,28},{28,24},{1,5},{5... | collective-permute-start | bytes 3145736 | tf_op jit(solution)/shard_map/ppermute | solution.py:485
  200.9 8.5 %copy-start.16 = (bf16[2,512,512]{2,1,0:T(8,128)(2,1)}, bf16[2,512,512]{2,1,0:T(8,128)(2,1)S(1)}, u32[]{:S(2)}) copy-start(bf16[2,512,512]{2,1,0:T(8,128)(2,1)S(1)} %collective-permute-done.9.refs_0_) | copy-start | bytes 3145732
  200.9 28.7 %all-to-all-start.2 = ((bf16[8,4,2,64,128]{4,3,2,1,0:T(8,128)(2,1)}), bf16[8,4,2,64,128]{4,3,2,1,0:T(8,128)(2,1)}, u32[]{:S(2)}, u32[]{:S(2)}) async-start(bf16[8,4,2,64,128]{4,3,2,1,0:T(8,128)(2,1)} %get-tuple-element.78), calls=%async_computation.2 | async-start | bytes 2097152 | tf_op jit(solution)/shard_map/all_to_all | solution.py:497
  209.4 5.4 %copy-start = (bf16[1024,512]{1,0:T(8,128)(2,1)S(1)}, bf16[1024,512]{1,0:T(8,128)(2,1)}, u32[]{:S(2)}) copy-start(bf16[1024,512]{1,0:T(8,128)(2,1)} %row_forward.1.flat_ref.row_ref) | copy-start | bytes 3145732
  215.5 1.0 copy-start.1
  216.5 1.3 copy-start.4
  222.7 7.0 %copy-start.3 = (bf16[8,3,4,2,64,128]{5,4,3,2,1,0:T(8,128)(2,1)S(1)}, bf16[8,3,4,2,64,128]{5,4,3,2,1,0:T(8,128)(2,1)}, u32[]{:S(2)}) copy-start(bf16[8,3,4,2,64,128]{5,4,3,2,1,0:T(8,128)(2,1)} %copy-done.2) | copy-start | bytes 9437188
  222.7 34.7 %collective-permute-start.12 = (bf16[2,512,512]{2,1,0:T(8,128)(2,1)}, bf16[2,512,512]{2,1,0:T(8,128)(2,1)}, u32[]{:S(2)}, u32[]{:S(2)}) collective-permute-start(bf16[2,512,512]{2,1,0:T(8,128)(2,1)} %proj_part.12), channel_id=1, source_target_pairs={{0,4},{4,0},{8,12},{12,8},{16,20},{20,16},{24,28},{28,24},{1,5},{5... | collective-permute-start | bytes 3145736 | tf_op jit(solution)/shard_map/ppermute | solution.py:485
  244.1 11.9 %copy-start.11 = (bf16[2,512,512]{2,1,0:T(8,128)(2,1)S(1)}, bf16[2,512,512]{2,1,0:T(8,128)(2,1)}, u32[]{:S(2)}) copy-start(bf16[2,512,512]{2,1,0:T(8,128)(2,1)} %proj_part.10) | copy-start | bytes 3145732
  255.9 81.0 %collective-permute-start.10 = (bf16[1024,2048]{1,0:T(8,128)(2,1)}, bf16[1024,2048]{1,0:T(8,128)(2,1)}, u32[]{:S(2)}, u32[]{:S(2)}) collective-permute-start(bf16[1024,2048]{1,0:T(8,128)(2,1)} %layer_part.3), channel_id=1, source_target_pairs={{0,1},{1,0},{2,3},{3,2},{4,5},{5,4},{6,7},{7,6},{8,9},{9,8},{10,11... | collective-permute-start | bytes 12582920 | tf_op jit(solution)/shard_map/ppermute | solution.py:513
  256.0 27.9 %collective-permute-start.14 = (bf16[2,512,512]{2,1,0:T(8,128)(2,1)S(1)}, bf16[2,512,512]{2,1,0:T(8,128)(2,1)S(1)}, u32[]{:S(2)}, u32[]{:S(2)}) collective-permute-start(bf16[2,512,512]{2,1,0:T(8,128)(2,1)S(1)} %copy-done.11), channel_id=1, source_target_pairs={{0,8},{4,12},{24,16},{28,20},{1,9},{5,13},{25,17},{29,21},{2,10},{... | collective-permute-start | bytes 3145736 | tf_op jit(solution)/shard_map/ppermute | solution.py:485
  257.3 66.5 %all-to-all-start.3 = ((bf16[8,1,4,2,64,128]{5,4,3,2,1,0:T(8,128)(2,1)}), bf16[8,1,4,2,64,128]{5,4,3,2,1,0:T(8,128)(2,1)S(1)}, u32[]{:S(2)}, u32[]{:S(2)}) async-start(bf16[8,1,4,2,64,128]{5,4,3,2,1,0:T(8,128)(2,1)} %get-tuple-element.86), calls=%async_computation.3 | async-start | bytes 2097152 | tf_op jit(solution)/shard_map/all_to_all | solution.py:497
  290.2 40.3 %copy-start.12 = (bf16[2,512,512]{2,1,0:T(8,128)(2,1)S(1)}, bf16[2,512,512]{2,1,0:T(8,128)(2,1)}, u32[]{:S(2)}) copy-start(bf16[2,512,512]{2,1,0:T(8,128)(2,1)} %proj_part.13) | copy-start | bytes 3145732
  290.2 32.7 %collective-permute-start.13 = (bf16[2,512,512]{2,1,0:T(8,128)(2,1)}, bf16[2,512,512]{2,1,0:T(8,128)(2,1)S(1)}, u32[]{:S(2)}, u32[]{:S(2)}) collective-permute-start(bf16[2,512,512]{2,1,0:T(8,128)(2,1)} %proj_part.13), channel_id=1, source_target_pairs={{0,8},{4,12},{24,16},{28,20},{1,9},{5,13},{25,17},{29,21},{2,10},{... | collective-permute-start | bytes 3145736 | tf_op jit(solution)/shard_map/ppermute | solution.py:485
  291.6 32.3 %collective-permute-start.15 = (bf16[2,512,512]{2,1,0:T(8,128)(2,1)}, bf16[2,512,512]{2,1,0:T(8,128)(2,1)S(1)}, u32[]{:S(2)}, u32[]{:S(2)}) collective-permute-start(bf16[2,512,512]{2,1,0:T(8,128)(2,1)} %add_convert_fusion.1), channel_id=1, source_target_pairs={{8,16},{12,20},{16,8},{20,12},{9,17},{13,21},{17,9},{21,13},{10,18... | collective-permute-start | bytes 3145736 | tf_op jit(solution)/shard_map/ppermute | solution.py:485
  294.4 34.7 %collective-permute-start.16 = (bf16[2,512,512]{2,1,0:T(8,128)(2,1)}, bf16[2,512,512]{2,1,0:T(8,128)(2,1)}, u32[]{:S(2)}, u32[]{:S(2)}) collective-permute-start(bf16[2,512,512]{2,1,0:T(8,128)(2,1)} %proj_part.9), channel_id=1, source_target_pairs={{0,4},{4,0},{8,12},{12,8},{16,20},{20,16},{24,28},{28,24},{1,5},{5... | collective-permute-start | bytes 3145736 | tf_op jit(solution)/shard_map/ppermute | solution.py:485
  322.8 1.0 copy-start.17
  323.9 1.0 copy-start.14
  323.9 1.4 copy-start.13
  325.2 100.4 %all-to-all-start.4 = ((bf16[8,2,4,2,64,128]{5,4,3,2,1,0:T(8,128)(2,1)}), bf16[8,2,4,2,64,128]{5,4,3,2,1,0:T(8,128)(2,1)S(1)}, u32[]{:S(2)}, u32[]{:S(2)}) async-start(bf16[8,2,4,2,64,128]{5,4,3,2,1,0:T(8,128)(2,1)} %get-tuple-element.92), calls=%async_computation.4 | async-start | bytes 4194304 | tf_op jit(solution)/shard_map/all_to_all | solution.py:497
  329.0 69.4 %collective-permute-start.19 = (bf16[2,512,512]{2,1,0:T(8,128)(2,1)}, bf16[2,512,512]{2,1,0:T(8,128)(2,1)}, u32[]{:S(2)}, u32[]{:S(2)}) collective-permute-start(bf16[2,512,512]{2,1,0:T(8,128)(2,1)} %proj_part.11), channel_id=1, source_target_pairs={{0,4},{4,0},{8,12},{12,8},{16,20},{20,16},{24,28},{28,24},{1,5},{5... | collective-permute-start | bytes 3145736 | tf_op jit(solution)/shard_map/ppermute | solution.py:485
  333.0 65.4 %collective-permute-start.21 = (bf16[2,512,512]{2,1,0:T(8,128)(2,1)}, bf16[2,512,512]{2,1,0:T(8,128)(2,1)}, u32[]{:S(2)}, u32[]{:S(2)}) collective-permute-start(bf16[2,512,512]{2,1,0:T(8,128)(2,1)} %add_convert_fusion), channel_id=1, source_target_pairs={{8,16},{12,20},{16,8},{20,12},{9,17},{13,21},{17,9},{21,13},{10,18... | collective-permute-start | bytes 3145736 | tf_op jit(solution)/shard_map/ppermute | solution.py:485
  345.4 88.9 %collective-permute-start.11 = (bf16[1024,1024]{1,0:T(8,128)(2,1)}, bf16[1024,1024]{1,0:T(8,128)(2,1)}, u32[]{:S(2)}, u32[]{:S(2)}) collective-permute-start(bf16[1024,1024]{1,0:T(8,128)(2,1)} %layer_part.4), channel_id=1, source_target_pairs={{0,2},{1,3},{2,0},{3,1},{4,6},{5,7},{6,4},{7,5},{8,10},{9,11},{10,... | collective-permute-start | bytes 6291464 | tf_op jit(solution)/shard_map/ppermute | solution.py:513
  347.6 6.7 %copy-start.15 = (bf16[2,512,512]{2,1,0:T(8,128)(2,1)S(1)}, bf16[2,512,512]{2,1,0:T(8,128)(2,1)}, u32[]{:S(2)}) copy-start(bf16[2,512,512]{2,1,0:T(8,128)(2,1)} %copy-done.14) | copy-start | bytes 3145732
  353.0 56.8 %collective-permute-start.17 = (bf16[512,512]{1,0:T(8,128)(2,1)}, bf16[512,512]{1,0:T(8,128)(2,1)}, u32[]{:S(2)}, u32[]{:S(2)}) collective-permute-start(bf16[512,512]{1,0:T(8,128)(2,1)} %bitcast.48), channel_id=1, source_target_pairs={{0,8},{4,12},{24,16},{28,20},{1,9},{5,13},{25,17},{29,21},{2,10},{... | collective-permute-start | bytes 1572872 | tf_op jit(solution)/shard_map/ppermute | solution.py:485
  356.3 53.5 %collective-permute-start.18 = (bf16[512,512]{1,0:T(8,128)(2,1)}, bf16[512,512]{1,0:T(8,128)(2,1)}, u32[]{:S(2)}, u32[]{:S(2)}) collective-permute-start(bf16[512,512]{1,0:T(8,128)(2,1)} %fusion.3), channel_id=1, source_target_pairs={{8,0},{12,4},{16,24},{20,28},{9,1},{13,5},{17,25},{21,29},{10,2},{... | collective-permute-start | bytes 1572872 | tf_op jit(solution)/shard_map/ppermute | solution.py:485
  405.8 12.1 %collective-permute-start.22 = (bf16[512,512]{1,0:T(8,128)(2,1)}, bf16[512,512]{1,0:T(8,128)(2,1)}, u32[]{:S(2)}, u32[]{:S(2)}) collective-permute-start(bf16[512,512]{1,0:T(8,128)(2,1)} %fusion), channel_id=1, source_target_pairs={{8,0},{12,4},{16,24},{20,28},{9,1},{13,5},{17,25},{21,29},{10,2},{... | collective-permute-start | bytes 1572872 | tf_op jit(solution)/shard_map/ppermute | solution.py:485
  407.8 15.0 %collective-permute-start.20 = (bf16[512,512]{1,0:T(8,128)(2,1)}, bf16[512,512]{1,0:T(8,128)(2,1)}, u32[]{:S(2)}, u32[]{:S(2)}) collective-permute-start(bf16[512,512]{1,0:T(8,128)(2,1)} %bitcast.49), channel_id=1, source_target_pairs={{0,8},{4,12},{24,16},{28,20},{1,9},{5,13},{25,17},{29,21},{2,10},{... | collective-permute-start | bytes 1572872 | tf_op jit(solution)/shard_map/ppermute | solution.py:485
  409.1 13.7 %copy-start.18 = (bf16[1,512,512]{2,1,0:T(8,128)(2,1)S(1)}, bf16[1,512,512]{2,1,0:T(8,128)(2,1)}, u32[]{:S(2)}) copy-start(bf16[1,512,512]{2,1,0:T(8,128)(2,1)} %get-tuple-element.109) | copy-start | bytes 1572868
  425.6 1.4 copy-start.7

commit v8 on v7

--- a/solution.py
+++ b/solution.py
@@ -59,33 +59,33 @@
     return out[0], out[1:]
 
 
-def join_kernel(query_ref, rest_ref, *refs):
+def join_kernel(chunk_ref, *refs):
     row_refs, outs, wide = refs[:3], refs[3:6], refs[6]
-    n, width = query_ref.shape[0], query_ref.shape[3]
+    n, width = chunk_ref.shape[0], chunk_ref.shape[3]
     span, heads, dim = outs[0].shape
     for array in range(3):
         for head in range(heads // 2):
             wide[pl.ds(2 * head, span, stride=heads), :] = row_refs[array][head].astype(F32)
             for d in range(n):
-                part = (query_ref if array == 0 else rest_ref)[d, max(array - 1, 0), head].astype(F32)
+                part = chunk_ref[d, array, head].astype(F32)
                 wide[pl.ds(d * width * heads + 2 * head + 1, width, stride=heads), :] = part
         outs[array][...] = wide[...].reshape(span, heads, dim).astype(BF16)
 
 
 def join_gradients(chunks, by_head):
-    n, _, half, rows, width, dim = chunks[0].shape
+    n, _, half, rows, width, dim = chunks.shape
     tokens, heads = by_head[0].shape[1], 2 * half
     return pl.pallas_call(
         join_kernel,
         grid=(rows,),
-        in_specs=[pl.BlockSpec((n, k, half, pl.squeezed, width, dim), lambda r: (0, 0, 0, r, 0, 0)) for k in (1, 2)]
+        in_specs=[pl.BlockSpec((n, 3, half, pl.squeezed, width, dim), lambda r: (0, 0, 0, r, 0, 0))]
         + [pl.BlockSpec((half, C, dim), lambda r: (0, r, 0))] * 3,
         out_specs=[pl.BlockSpec((C, heads, dim), lambda r: (r, 0, 0))] * 3,
         scratch_shapes=[pltpu.VMEM((C * heads, dim), F32)],
         out_shape=[jax.ShapeDtypeStruct((tokens, heads, dim), BF16)] * 3,
         compiler_params=params(60),
         name="join_gradients",
-    )(*chunks, *by_head)
+    )(chunks, *by_head)
 
 
 def collect_kernel(row_ref, chunk_ref, flat_ref, both_ref):
@@ -426,7 +426,7 @@
     )(chunks)
 
 
-def column_backward_kernel(scale, chunk_ref, grad_ref, query_ref, rest_ref, bias):
+def column_backward_kernel(scale, chunk_ref, grad_ref, out_ref, bias):
     half, width = chunk_ref.shape[2], chunk_ref.shape[4]
     bias[...] = jnp.where(column_mask(bias.shape[0]), 0.0, -jnp.inf)
     blocks = width // LANE
@@ -440,9 +440,9 @@
         prob_grad = dot(grad, v, ((1,), (1,)))
         inner = jnp.sum(probs * prob_grad, axis=-1, keepdims=True)
         score_low = (probs * (prob_grad - inner)).astype(BF16)
-        scattered(query_ref, (0, head), at, (dot(score_low, k, ((1,), (0,))) * scale).astype(BF16))
-        scattered(rest_ref, (0, head), at, (dot(score_low, q, ((0,), (0,))) * scale).astype(BF16))
-        scattered(rest_ref, (1, head), at, dot(probs.astype(BF16), grad, ((0,), (0,))).astype(BF16))
+        scattered(out_ref, (0, head), at, (dot(score_low, k, ((1,), (0,))) * scale).astype(BF16))
+        scattered(out_ref, (1, head), at, (dot(score_low, q, ((0,), (0,))) * scale).astype(BF16))
+        scattered(out_ref, (2, head), at, dot(probs.astype(BF16), grad, ((0,), (0,))).astype(BF16))
 
 
 def column_backward(chunks, grads):
@@ -451,8 +451,8 @@
     return pl.pallas_call(
         functools.partial(column_backward_kernel, dim**-0.5),
         in_specs=[VMEM] * 2,
-        out_specs=[VMEM] * 2,
-        out_shape=[jax.ShapeDtypeStruct((n, k, half, rows, width, dim), BF16) for k in (1, 2)],
+        out_specs=VMEM,
+        out_shape=jax.ShapeDtypeStruct(chunks.shape, BF16),
         scratch_shapes=[pltpu.VMEM((size, size), F32)],
         compiler_params=params(24),
         cost_estimate=pl.CostEstimate(
@@ -577,7 +577,7 @@
     column_part = swap(outs)
     so_far = attn_grad(ids[:early], after(out_grad, outs), blocks[:early], None, dim)
     grad_row, grads = attn_grad(ids[early:], out_grad, blocks[early:], so_far, dim)
-    row_far = exchanged([after(part, *far_near_blocks) for part in row_far])
+    row_far = exchanged([after(part, so_far, *far_near_blocks) for part in row_far])
     row_close = exchanged(row_close)
     grads = swap(after(grads, column_part, *row_far))
     (row_far,) = summed(after(row_out, outs), far, row_far, 0)
@@ -585,33 +585,34 @@
     column_out, flat = collect(row_out, after(column_part, row_far))
     column_far, column_close = leaving(column_out, far), leaving(column_out, close)
     column_far = exchanged(column_far)
-    grad_query, grad_rest = column_backward(chunks, after(grads, *column_close, row_far))
-    grad_query = swap(after(grad_query, *column_far))
-
-    layer = LayerSum(ids, after(flat, grad_rest), blocks, heads_n)
-    (column_far,) = summed(after(column_out, grad_rest), far, column_far, 0)
+    gradients = column_backward(chunks, after(grads, *column_close, row_far))
+    column_grads = swap(after(gradients, *column_far, row_far_in, *row_close))
+
+    layer = LayerSum(ids, after(flat, gradients), blocks, heads_n)
+    layer.start()
+    column_close = exchanged(column_close)
+    (column_far,) = summed(after(column_out, gradients), far, column_far, 0)
     column_far_in = links.along(column_far, INWARD)
-    row_cross = links.along(add(row_far, after(row_far_in, grad_rest)), CROSS)
-    column_close = exchanged(column_close)
-    row_near, row_own = summed(after(row_out, grad_rest), close, row_close, 1)
+    row_cross = links.along(add(row_far, row_far_in), CROSS)
+    row_near, row_own = summed(after(row_out, gradients), close, row_close, 1)
     row_near_in = links.along(row_near[0], INWARD)
-    layer.start()
-    grad_rest = swap(after(grad_rest, grad_query, column_far_in, row_cross, layer.first))
-    column_cross = links.along(add(column_far, column_far_in), CROSS)
-    layer.turn(layer.near)
-    row_grads = row_backward(*by_head, after(grad_row, column_far_in))
-    column_near, column_own = summed(after(column_out, *layer.parts), close, column_close, 1)
+    row_grads = row_backward(*by_head, after(grad_row, column_far))
+    column_near, column_own = summed(after(column_out, gradients), close, column_close, 1)
     column_near_in = links.along(column_near[0], INWARD)
-    column_cross = after(column_cross, row_grads[0])
-    row_back = links.along(add(row_near[0], row_cross[1]), OUTWARD)
-    column_back = links.along(add(column_near[0], column_cross[1]), OUTWARD)
-
-    gradients = join_gradients([grad_query, grad_rest], row_grads)
+    layer.turn(gradients)
+    first = after(column_far_in, row_grads[0], row_near[0], column_near[0], *layer.parts)
+    column_cross = links.along(add(column_far, first), CROSS)
+    row_back = links.along(add(row_near[0], after(row_cross, row_near_in)[1]), OUTWARD)
+    gradients = join_gradients(column_grads, row_grads)
+    layer_out = layer.finish()
+    last = after(column_cross, column_near_in, gradients[0], layer_out)
+    column_back = links.along(add(column_near[0], last[1]), OUTWARD)
+
     proj_row = add(row_own[0], row_near_in, row_cross[0], row_back)
     proj_column = add(column_own[0], column_near_in, column_cross[0], column_back)
     shape = (half, dim, depth)
     proj_grad = jnp.stack([proj_row.reshape(shape), proj_column.reshape(shape)], axis=1)
-    return (layer.finish(), *gradients, proj_grad.reshape(heads * dim, depth))
+    return (layer_out, *gradients, proj_grad.reshape(heads * dim, depth))
 
 
 def solution(mesh):

time: 446 us -> 404 us (0.906)
  waiting for transfers between devices: 179 us -> 147 us
  starting transfers between devices: 74.6 us -> 63 us
    ppermute x21, waiting for transfers between devices: 179 us -> 147 us  [send(): out = lax.ppermute(value, 'ctx', pairs)]
    all_to_all x5 -> x4, starting transfers between devices: 27.2 us -> 20.6 us  [swap(): lax.all_to_all(chunks, 'ctx', split_axis=0, concat_axis=0, tiled=True)]
    ppermute x21, starting transfers between devices: 45.8 us -> 40.8 us  [send(): out = lax.ppermute(value, 'ctx', pairs)]
  transfers between devices with their start and end apart: 28 -> 27, of which waited for: 12 -> 12; matrix products, arithmetic and copies ran while one was open for 5% -> 5% of each run, Pallas kernels for 34% -> 40%
where the time goes in v8:
time: 404 us; the launch traced here: 399 us
  Pallas kernels  158 us (39%)
  waiting for transfers between devices  147 us (36%)
  starting transfers between devices  63 us (16%)
  other arithmetic  20.6 us (5%)
  local copies, waits for them, and re-layouts  8.25 us (2%)
    ppermute x21, waiting for transfers between devices, send(): out = lax.ppermute(value, 'ctx', pairs)  147 us
    ppermute x21, starting transfers between devices, send(): out = lax.ppermute(value, 'ctx', pairs)  40.8 us
    pallas_call x8, Pallas kernels, proj_part(): pl.pallas_call(functools.partial(proj_kernel, lead, len(extra), dim), gri...  40.3 us
    pallas_call x3, Pallas kernels, layer_part(): pl.pallas_call(functools.partial(layer_kernel, n, count, len(extra)), gri...  29.5 us
    pallas_call x2, Pallas kernels, attn_grad(): pl.pallas_call(functools.partial(attn_grad_kernel, m, dim, last), grid_sp...  26.9 us
    all_to_all x4, starting transfers between devices, swap(): lax.all_to_all(chunks, 'ctx', split_axis=0, concat_axis=0, tiled=True)  20.6 us
    pallas_call x1, Pallas kernels, column_backward(): pl.pallas_call(functools.partial(column_backward_kernel, dim ** (-0.5)),...  14.5 us
    pallas_call x1, Pallas kernels, row_backward(): pl.pallas_call(functools.partial(row_backward_kernel, dim ** (-0.5)), gri...  13.6 us
  transfers between devices with their start and end apart: 27, of which 12 were waited for; matrix products, arithmetic and copies ran while one was open for 5% of the time, Pallas kernels for 40%

profile of v8, /device:TPU:8, one launch (start us, length us, event | category | flops | bytes accessed | tf_op | source)
XLA Modules:
  0.0 398.7 jit_solution(2937599507380756254)
XLA Ops:
  0.6 3.5 collective-permute-start.4
  4.2 1.6 collective-permute-start.1
  5.8 7.1 %split_inputs.1 = (bf16[8,3,4,2,64,128]{5,4,3,2,1,0:T(8,128)(2,1)}, bf16[4,1024,128]{2,1,0:T(8,128)(2,1)}, bf16[4,1024,128]{2,1,0:T(8,128)(2,1)}, bf16[4,1024,128]{2,1,0:T(8,128)(2,1)}) custom-call(bf16[1024,8,128]{2,1,0:T(8,128)(2,1)} %q_ref.1, bf16[1024,8,128]{2,1,0:T(8,128)(2,1)} %k_ref.1, bf16[1024,8,128]{2,1,0:T(8,128)(2,1)} %v_ref.1), custom_call_target="tpu_custom_call" | custom-call | tf_op jit(solution)/shard_map/split_inputs/pallas_call | solution.py:48
  12.9 14.9 %collective-permute-done.4 = bf16[1024,512]{1,0:T(8,128)(2,1)} collective-permute-done((bf16[1024,512]{1,0:T(8,128)(2,1)}, bf16[1024,512]{1,0:T(8,128)(2,1)}, u32[]{:S(2)}, u32[]{:S(2)}) %collective-permute-start.4) | collective-permute-done | bytes 1048608 | tf_op jit(solution)/shard_map/ppermute | solution.py:485
  29.0 3.2 collective-permute-start.5
  32.2 3.2 collective-permute-start.3
  35.4 1.6 collective-permute-start.2
  37.0 9.9 %row_forward.1.flat_ref.row_ref = bf16[1024,512]{1,0:T(8,128)(2,1)} custom-call(bf16[4,1024,128]{2,1,0:T(8,128)(2,1)} %get-tuple-element.57.q_ref, bf16[4,1024,128]{2,1,0:T(8,128)(2,1)} %get-tuple-element.58.k_ref, bf16[4,1024,128]{2,1,0:T(8,128)(2,1)} %get-tuple-element.59.v_ref), custom_call_target="tpu_custom_call" | custom-call | flops 1073741824 | bytes 4194304 | tf_op jit(solution)/shard_map/row_forward/pallas_call | solution.py:321
  47.4 4.9 %proj_part.9 = bf16[2,512,512]{2,1,0:T(8,128)(2,1)} custom-call(s32[2]{0:T(128)} %pad_add_fusion.2.order, bf16[1024,512]{1,0:T(8,128)(2,1)} %row_forward.1.flat_ref.row_ref, bf16[1024,4096]{1,0:T(8,128)(2,1)} %grad_ref.18), custom_call_target="tpu_custom_call" | custom-call | flops 1073741824 | bytes 4194304 | tf_op jit(solution)/shard_map/proj_part/pallas_call | solution.py:275
  52.9 4.8 %proj_part.8 = bf16[2,512,512]{2,1,0:T(8,128)(2,1)} custom-call(s32[2]{0:T(128)} %pad_add_fusion.1.order, bf16[1024,512]{1,0:T(8,128)(2,1)} %row_forward.1.flat_ref.row_ref, bf16[1024,4096]{1,0:T(8,128)(2,1)} %grad_ref.18), custom_call_target="tpu_custom_call" | custom-call | flops 1073741824 | bytes 4194304 | tf_op jit(solution)/shard_map/proj_part/pallas_call | solution.py:275
  59.9 4.4 %all-to-all-start = ((bf16[8,3,4,2,64,128]{5,4,3,2,1,0:T(8,128)(2,1)}), bf16[8,3,4,2,64,128]{5,4,3,2,1,0:T(8,128)(2,1)S(1)}, u32[]{:S(2)}, u32[]{:S(2)}) async-start(bf16[8,3,4,2,64,128]{5,4,3,2,1,0:T(8,128)(2,1)} %get-tuple-element.63), calls=%async_computation | async-start | bytes 6291456 | tf_op jit(solution)/shard_map/all_to_all | solution.py:497
  64.3 2.9 collective-permute-start.7
  68.6 2.1 collective-permute-start.6
  70.7 64.4 %collective-permute-done.7 = bf16[1024,512]{1,0:T(8,128)(2,1)} collective-permute-done((bf16[1024,512]{1,0:T(8,128)(2,1)}, bf16[1024,512]{1,0:T(8,128)(2,1)}, u32[]{:S(2)}, u32[]{:S(2)}) %collective-permute-start.7) | collective-permute-done | bytes 1048608 | tf_op jit(solution)/shard_map/ppermute | solution.py:485
  135.1 2.3 broadcast_select_fusion.refs_0_.refs_6_
  138.9 8.7 %column_forward.1 = bf16[8,4,2,64,128]{4,3,2,1,0:T(8,128)(2,1)S(1)} custom-call(bf16[8,3,4,2,64,128]{5,4,3,2,1,0:T(8,128)(2,1)S(1)} %all-to-all-done.chunk_ref), custom_call_target="tpu_custom_call" | custom-call | flops 536870912 | bytes 4194304 | tf_op jit(solution)/shard_map/column_forward/pallas_call | solution.py:413
  148.6 6.2 %all-to-all-start.1 = ((bf16[8,4,2,64,128]{4,3,2,1,0:T(8,128)(2,1)}), bf16[8,4,2,64,128]{4,3,2,1,0:T(8,128)(2,1)S(1)}, u32[]{:S(2)}, u32[]{:S(2)}) async-start(bf16[8,4,2,64,128]{4,3,2,1,0:T(8,128)(2,1)} %copy-done.5), calls=%async_computation.1 | async-start | bytes 2097152 | tf_op jit(solution)/shard_map/all_to_all | solution.py:497
  155.3 16.8 %attn_grad.2.refs_2_ = f32[1024,1024]{1,0:T(8,128)} custom-call(s32[6]{0:T(128)} %stack.114.ids, bf16[1024,4096]{1,0:T(8,128)(2,1)} %grad_ref.18, bf16[1024,512]{1,0:T(8,128)(2,1)} %refs_0_.7, bf16[1024,512]{1,0:T(8,128)(2,1)} %copy-done.9, bf16[1024,512]{1,0:T(8,128)(2,1)} %copy-done.8, bf16[1024,512]{1,0:T(8,128)(2,1)} %copy-done.10, ...), custom_call_target="tpu_custom_call" | custom-call | flops 6442450944 | bytes 16777216 | tf_op jit(solution)/shard_map/attn_grad/pallas_call | solution.py:163
  174.3 10.1 %attn_grad.3 = (bf16[1024,512]{1,0:T(8,128)(2,1)}, bf16[8,4,2,64,128]{4,3,2,1,0:T(8,128)(2,1)}) custom-call(s32[2]{0:T(128)} %pad_add_fusion.4.ids, bf16[1024,4096]{1,0:T(8,128)(2,1)} %grad_ref.18, bf16[1024,512]{1,0:T(8,128)(2,1)} %broadcast_select_fusion.refs_0_.refs_6_, bf16[1024,512]{1,0:T(8,128)(2,1)} %collective-permute-done.8.refs_1_.refs_7_, ...), custom_call_target="tpu_custom_call" | custom-call | flops 2147483648 | bytes 8388608 | tf_op jit(solution)/shard_map/attn_grad/pallas_call | solution.py:163
  184.4 13.6 %collective-permute-done.9.refs_0_ = bf16[2,512,512]{2,1,0:T(8,128)(2,1)S(1)} collective-permute-done((bf16[2,512,512]{2,1,0:T(8,128)(2,1)S(1)}, bf16[2,512,512]{2,1,0:T(8,128)(2,1)S(1)}, u32[]{:S(2)}, u32[]{:S(2)}) %collective-permute-start.9) | collective-permute-done | bytes 1048608 | tf_op jit(solution)/shard_map/ppermute | solution.py:485
  198.0 5.1 %all-to-all-start.2 = ((bf16[8,4,2,64,128]{4,3,2,1,0:T(8,128)(2,1)}), bf16[8,4,2,64,128]{4,3,2,1,0:T(8,128)(2,1)}, u32[]{:S(2)}, u32[]{:S(2)}) async-start(bf16[8,4,2,64,128]{4,3,2,1,0:T(8,128)(2,1)} %get-tuple-element.75), calls=%async_computation.2 | async-start | bytes 2097152 | tf_op jit(solution)/shard_map/all_to_all | solution.py:497
  206.4 5.0 %proj_part.10 = bf16[2,512,512]{2,1,0:T(8,128)(2,1)} custom-call(s32[2]{0:T(128)} %pad_add_fusion.3.order, bf16[1024,512]{1,0:T(8,128)(2,1)} %row_forward.1.flat_ref.row_ref, bf16[1024,4096]{1,0:T(8,128)(2,1)} %grad_ref.18, bf16[2,512,512]{2,1,0:T(8,128)(2,1)} %copy-done.11), custom_call_target="tpu_custom_call" | custom-call | flops 1073741824 | bytes 5242880 | tf_op jit(solution)/shard_map/proj_part/pallas_call | solution.py:275
  215.9 4.8 %proj_part.12 = bf16[2,512,512]{2,1,0:T(8,128)(2,1)} custom-call(s32[2]{0:T(128)} %pad_add_fusion.1.order, bf16[1024,512]{1,0:T(8,128)(2,1)} %copy-done.3, bf16[1024,4096]{1,0:T(8,128)(2,1)} %grad_ref.18), custom_call_target="tpu_custom_call" | custom-call | flops 1073741824 | bytes 4194304 | tf_op jit(solution)/shard_map/proj_part/pallas_call | solution.py:275
  221.3 5.2 %proj_part.11 = bf16[2,512,512]{2,1,0:T(8,128)(2,1)} custom-call(s32[2]{0:T(128)} %pad_add_fusion.2.order, bf16[1024,512]{1,0:T(8,128)(2,1)} %copy-done.3, bf16[1024,4096]{1,0:T(8,128)(2,1)} %grad_ref.18), custom_call_target="tpu_custom_call" | custom-call | flops 1073741824 | bytes 4194304 | tf_op jit(solution)/shard_map/proj_part/pallas_call | solution.py:275
  226.5 14.5 %column_backward.1 = bf16[8,3,4,2,64,128]{5,4,3,2,1,0:T(8,128)(2,1)} custom-call(bf16[8,3,4,2,64,128]{5,4,3,2,1,0:T(8,128)(2,1)S(1)} %copy-done.2, bf16[8,4,2,64,128]{4,3,2,1,0:T(8,128)(2,1)} %all-to-all-done.2.grad_ref), custom_call_target="tpu_custom_call" | custom-call | flops 1342177280 | bytes 7340032 | tf_op jit(solution)/shard_map/column_backward/pallas_call | solution.py:451
  241.0 11.7 %layer_part.3 = bf16[1024,2048]{1,0:T(8,128)(2,1)} custom-call(s32[8]{0:T(128)} %stack.107.ids, s32[4]{0:T(128)} %pad_add_fusion.5.wanted, bf16[1024,1024]{1,0:T(8,128)(2,1)} %copy-done.4, bf16[1024,512]{1,0:T(8,128)(2,1)} %refs_0_.7, bf16[1024,512]{1,0:T(8,128)(2,1)} %copy-done.9, bf16[1024,512]{1,0:T(8,128)(2,1)} %copy-done.8, ...), custom_call_target="tpu_custom_call" | custom-call | flops 4294967296 | bytes 10485760 | tf_op jit(solution)/shard_map/layer_part/pallas_call | solution.py:221
  252.8 8.3 %collective-permute-done.12.refs_0_ = bf16[2,512,512]{2,1,0:T(8,128)(2,1)} collective-permute-done((bf16[2,512,512]{2,1,0:T(8,128)(2,1)}, bf16[2,512,512]{2,1,0:T(8,128)(2,1)}, u32[]{:S(2)}, u32[]{:S(2)}) %collective-permute-start.12) | collective-permute-done | bytes 1048608 | tf_op jit(solution)/shard_map/ppermute | solution.py:485
  261.2 4.9 %all-to-all-start.3 = ((bf16[8,3,4,2,64,128]{5,4,3,2,1,0:T(8,128)(2,1)}), bf16[8,3,4,2,64,128]{5,4,3,2,1,0:T(8,128)(2,1)S(1)}, u32[]{:S(2)}, u32[]{:S(2)}) async-start(bf16[8,3,4,2,64,128]{5,4,3,2,1,0:T(8,128)(2,1)} %column_backward.1), calls=%async_computation.3 | async-start | bytes 6291456 | tf_op jit(solution)/shard_map/all_to_all | solution.py:497
  268.2 5.0 %proj_part.13 = bf16[2,512,512]{2,1,0:T(8,128)(2,1)} custom-call(s32[2]{0:T(128)} %pad_add_fusion.3.order, bf16[1024,512]{1,0:T(8,128)(2,1)} %copy-done.3, bf16[1024,4096]{1,0:T(8,128)(2,1)} %grad_ref.18, bf16[2,512,512]{2,1,0:T(8,128)(2,1)} %collective-permute-done.12.refs_0_), custom_call_target="tpu_custom_call" | custom-call | flops 1073741824 | bytes 5242880 | tf_op jit(solution)/shard_map/proj_part/pallas_call | solution.py:275
  274.5 8.5 %layer_part.4 = bf16[1024,1024]{1,0:T(8,128)(2,1)} custom-call(s32[8]{0:T(128)} %stack.107.ids, s32[2]{0:T(128)} %pad_add_fusion.6.wanted, bf16[1024,1024]{1,0:T(8,128)(2,1)} %copy-done.4, bf16[1024,512]{1,0:T(8,128)(2,1)} %refs_0_.7, bf16[1024,512]{1,0:T(8,128)(2,1)} %copy-done.9, bf16[1024,512]{1,0:T(8,128)(2,1)} %copy-done.8, ...), custom_call_target="tpu_custom_call" | custom-call | flops 2147483648 | bytes 6291456 | tf_op jit(solution)/shard_map/layer_part/pallas_call | solution.py:221
  285.1 2.8 add_convert_fusion.1
  287.9 3.4 collective-permute-start.16
  291.3 13.6 %row_backward.1 = (bf16[4,1024,128]{2,1,0:T(8,128)(2,1)}, bf16[4,1024,128]{2,1,0:T(8,128)(2,1)}, bf16[4,1024,128]{2,1,0:T(8,128)(2,1)}) custom-call(bf16[4,1024,128]{2,1,0:T(8,128)(2,1)} %get-tuple-element.57.q_ref, bf16[4,1024,128]{2,1,0:T(8,128)(2,1)} %get-tuple-element.58.k_ref, bf16[4,1024,128]{2,1,0:T(8,128)(2,1)} %get-tuple-element.59.v_ref, ...), custom_call_target="tpu_custom_call" | custom-call | flops 2684354560 | bytes 7340032 | tf_op jit(solution)/shard_map/row_backward/pallas_call | solution.py:355
  304.9 5.2 %proj_part.14 = (bf16[1,512,512]{2,1,0:T(8,128)(2,1)}, bf16[1,512,512]{2,1,0:T(8,128)(2,1)}) custom-call(s32[2]{0:T(128)} %pad_add_fusion.7.order, bf16[1024,512]{1,0:T(8,128)(2,1)} %row_forward.1.flat_ref.row_ref, bf16[1024,4096]{1,0:T(8,128)(2,1)} %grad_ref.18, bf16[2,512,512]{2,1,0:T(8,128)(2,1)} %collective-permute-done.14.refs_0_), custom_call_target="tpu_custom_call" | custom-call | flops 1073741824 | bytes 5242880 | tf_op jit(solution)/shard_map/proj_part/pallas_call | solution.py:275
  310.1 11.8 %collective-permute-done.17.refs_0_ = bf16[2,512,512]{2,1,0:T(8,128)(2,1)} collective-permute-done((bf16[2,512,512]{2,1,0:T(8,128)(2,1)}, bf16[2,512,512]{2,1,0:T(8,128)(2,1)}, u32[]{:S(2)}, u32[]{:S(2)}) %collective-permute-start.17) | collective-permute-done | bytes 1048608 | tf_op jit(solution)/shard_map/ppermute | solution.py:485
  321.9 5.2 %proj_part.15 = (bf16[1,512,512]{2,1,0:T(8,128)(2,1)}, bf16[1,512,512]{2,1,0:T(8,128)(2,1)}) custom-call(s32[2]{0:T(128)} %pad_add_fusion.7.order, bf16[1024,512]{1,0:T(8,128)(2,1)} %copy-done.3, bf16[1024,4096]{1,0:T(8,128)(2,1)} %grad_ref.18, bf16[2,512,512]{2,1,0:T(8,128)(2,1)} %collective-permute-done.17.refs_0_), custom_call_target="tpu_custom_call" | custom-call | flops 1073741824 | bytes 5242880 | tf_op jit(solution)/shard_map/proj_part/pallas_call | solution.py:275
  327.1 13.3 %collective-permute-done.18 = bf16[2,512,512]{2,1,0:T(8,128)(2,1)} collective-permute-done((bf16[2,512,512]{2,1,0:T(8,128)(2,1)}, bf16[2,512,512]{2,1,0:T(8,128)(2,1)}, u32[]{:S(2)}, u32[]{:S(2)}) %collective-permute-start.18) | collective-permute-done | bytes 1048608 | tf_op jit(solution)/shard_map/ppermute | solution.py:485
  340.4 2.8 add_convert_fusion
  343.2 3.8 collective-permute-start.21
  350.4 8.9 %collective-permute-done.16 = bf16[2,512,512]{2,1,0:T(8,128)(2,1)} collective-permute-done((bf16[2,512,512]{2,1,0:T(8,128)(2,1)}, bf16[2,512,512]{2,1,0:T(8,128)(2,1)}, u32[]{:S(2)}, u32[]{:S(2)}) %collective-permute-start.16) | collective-permute-done | bytes 1048608 | tf_op jit(solution)/shard_map/ppermute | solution.py:485
  359.3 4.7 %collective-permute-done.15 = bf16[512,512]{1,0:T(8,128)(2,1)} collective-permute-done((bf16[512,512]{1,0:T(8,128)(2,1)}, bf16[512,512]{1,0:T(8,128)(2,1)}, u32[]{:S(2)}, u32[]{:S(2)}) %collective-permute-start.15) | collective-permute-done | bytes 524320 | tf_op jit(solution)/shard_map/ppermute | solution.py:485
  364.1 2.2 fusion.3
  366.2 2.2 collective-permute-start.19
  368.5 1.6 copy-done.6
  370.1 7.3 %join_gradients.1 = (bf16[1024,8,128]{2,1,0:T(8,128)(2,1)}, bf16[1024,8,128]{2,1,0:T(8,128)(2,1)}, bf16[1024,8,128]{2,1,0:T(8,128)(2,1)}) custom-call(bf16[8,3,4,2,64,128]{5,4,3,2,1,0:T(8,128)(2,1)} %copy-done.6, bf16[4,1024,128]{2,1,0:T(8,128)(2,1)} %get-tuple-element.87.refs_0_, bf16[4,1024,128]{2,1,0:T(8,128)(2,1)} %get-tuple-element.88.refs_1_, ...), custom_call_target="tpu_custom_call" | custom-call | tf_op jit(solution)/shard_map/join_gradients/pallas_call | solution.py:78
  377.5 9.3 %layer_part.5 = bf16[1024,1024]{1,0:T(8,128)(2,1)} custom-call(s32[8]{0:T(128)} %stack.107.ids, s32[2]{0:T(128)} %pad_add_fusion.wanted, bf16[1024,1024]{1,0:T(8,128)(2,1)} %copy-done.4, bf16[1024,512]{1,0:T(8,128)(2,1)} %refs_0_.7, bf16[1024,512]{1,0:T(8,128)(2,1)} %copy-done.9, bf16[1024,512]{1,0:T(8,128)(2,1)} %copy-done.8, bf16[1024,512]{1,0:T(8,128)(2,1)} %copy-done.10, ...), custom_call_target="tpu_custom_call" | custom-call | flops 2147483648 | bytes 6291456 | tf_op jit(solution)/shard_map/layer_part/pallas_call | solution.py:221
  389.4 1.6 fusion.5
  391.1 5.0 %collective-permute-done.22 = bf16[512,512]{1,0:T(8,128)(2,1)S(1)} collective-permute-done((bf16[512,512]{1,0:T(8,128)(2,1)S(1)}, bf16[512,512]{1,0:T(8,128)(2,1)S(1)}, u32[]{:S(2)}, u32[]{:S(2)}) %collective-permute-start.22) | collective-permute-done | bytes 524320 | tf_op jit(solution)/shard_map/ppermute | solution.py:485
  (78 shorter events, 33.7 us)
Async XLA Ops:
  0.6 27.1 %collective-permute-start.4 = (bf16[1024,512]{1,0:T(8,128)(2,1)}, bf16[1024,512]{1,0:T(8,128)(2,1)}, u32[]{:S(2)}, u32[]{:S(2)}) collective-permute-start(bf16[1024,512]{1,0:T(8,128)(2,1)} %refs_0_.7), channel_id=1, source_target_pairs={{8,16},{12,20},{16,8},{20,12},{9,17},{13,21},{17,9},{21,13},{10,18... | collective-permute-start | bytes 3145736 | tf_op jit(solution)/shard_map/ppermute | solution.py:485
  4.1 24.9 %collective-permute-start = (bf16[1024,512]{1,0:T(8,128)(2,1)}, bf16[1024,512]{1,0:T(8,128)(2,1)S(1)}, u32[]{:S(2)}, u32[]{:S(2)}) collective-permute-start(bf16[1024,512]{1,0:T(8,128)(2,1)} %refs_0_.7), channel_id=1, source_target_pairs={{0,8},{4,12},{8,0},{12,4},{16,24},{20,28},{24,16},{28,20},{1,9},{5... | collective-permute-start | bytes 3145736 | tf_op jit(solution)/shard_map/ppermute | solution.py:485
  4.2 28.0 %collective-permute-start.1 = (bf16[1024,512]{1,0:T(8,128)(2,1)}, bf16[1024,512]{1,0:T(8,128)(2,1)S(1)}, u32[]{:S(2)}, u32[]{:S(2)}) collective-permute-start(bf16[1024,512]{1,0:T(8,128)(2,1)} %refs_0_.7), channel_id=1, source_target_pairs={{0,4},{4,0},{8,12},{12,8},{16,20},{20,16},{24,28},{28,24},{1,5},{5... | collective-permute-start | bytes 3145736 | tf_op jit(solution)/shard_map/ppermute | solution.py:485
  29.0 17.8 %copy-start.8 = (bf16[1024,512]{1,0:T(8,128)(2,1)}, bf16[1024,512]{1,0:T(8,128)(2,1)S(1)}, u32[]{:S(2)}) copy-start(bf16[1024,512]{1,0:T(8,128)(2,1)S(1)} %collective-permute-done.refs_2_) | copy-start | bytes 3145732
  29.0 28.7 %collective-permute-start.5 = (bf16[1024,512]{1,0:T(8,128)(2,1)}, bf16[1024,512]{1,0:T(8,128)(2,1)}, u32[]{:S(2)}, u32[]{:S(2)}) collective-permute-start(bf16[1024,512]{1,0:T(8,128)(2,1)} %collective-permute-done.4), channel_id=1, source_target_pairs={{8,0},{12,4},{16,24},{20,28},{9,1},{13,5},{17,25},{21,29},{10,2},{... | collective-permute-start | bytes 3145736 | tf_op jit(solution)/shard_map/ppermute | solution.py:485
  32.2 14.7 %copy-start.9 = (bf16[1024,512]{1,0:T(8,128)(2,1)}, bf16[1024,512]{1,0:T(8,128)(2,1)S(1)}, u32[]{:S(2)}) copy-start(bf16[1024,512]{1,0:T(8,128)(2,1)S(1)} %collective-permute-done.1.refs_1_) | copy-start | bytes 3145732
  32.2 25.7 %collective-permute-start.3 = (bf16[1024,512]{1,0:T(8,128)(2,1)S(1)}, bf16[1024,512]{1,0:T(8,128)(2,1)}, u32[]{:S(2)}, u32[]{:S(2)}) collective-permute-start(bf16[1024,512]{1,0:T(8,128)(2,1)S(1)} %collective-permute-done.refs_2_), channel_id=1, source_target_pairs={{8,16},{12,20},{16,8},{20,12},{9,17},{13,21},{17,9},{21,13},{10,18... | collective-permute-start | bytes 3145736 | tf_op jit(solution)/shard_map/ppermute | solution.py:485
  35.4 23.5 %collective-permute-start.2 = (bf16[1024,512]{1,0:T(8,128)(2,1)S(1)}, bf16[1024,512]{1,0:T(8,128)(2,1)S(1)}, u32[]{:S(2)}, u32[]{:S(2)}) collective-permute-start(bf16[1024,512]{1,0:T(8,128)(2,1)S(1)} %collective-permute-done.refs_2_), channel_id=1, source_target_pairs={{0,4},{4,0},{8,12},{12,8},{16,20},{20,16},{24,28},{28,24},{1,5},{5... | collective-permute-start | bytes 3145736 | tf_op jit(solution)/shard_map/ppermute | solution.py:485
  58.9 1.0 copy-start.10
  59.9 79.0 %all-to-all-start = ((bf16[8,3,4,2,64,128]{5,4,3,2,1,0:T(8,128)(2,1)}), bf16[8,3,4,2,64,128]{5,4,3,2,1,0:T(8,128)(2,1)S(1)}, u32[]{:S(2)}, u32[]{:S(2)}) async-start(bf16[8,3,4,2,64,128]{5,4,3,2,1,0:T(8,128)(2,1)} %get-tuple-element.63), calls=%async_computation | async-start | bytes 6291456 | tf_op jit(solution)/shard_map/all_to_all | solution.py:497
  64.3 70.8 %collective-permute-start.7 = (bf16[1024,512]{1,0:T(8,128)(2,1)}, bf16[1024,512]{1,0:T(8,128)(2,1)}, u32[]{:S(2)}, u32[]{:S(2)}) collective-permute-start(bf16[1024,512]{1,0:T(8,128)(2,1)} %collective-permute-done.3), channel_id=1, source_target_pairs={{8,0},{12,4},{16,24},{20,28},{9,1},{13,5},{17,25},{21,29},{10,2},{... | collective-permute-start | bytes 3145736 | tf_op jit(solution)/shard_map/ppermute | solution.py:485
  68.6 70.3 %copy-start.7 = (bf16[1024,512]{1,0:T(8,128)(2,1)}, bf16[1024,512]{1,0:T(8,128)(2,1)S(1)}, u32[]{:S(2)}) copy-start(bf16[1024,512]{1,0:T(8,128)(2,1)S(1)} %broadcast_select_fusion.1.refs_4_) | copy-start | bytes 3145732
  68.6 70.3 %collective-permute-start.6 = (bf16[1024,512]{1,0:T(8,128)(2,1)S(1)}, bf16[1024,512]{1,0:T(8,128)(2,1)}, u32[]{:S(2)}, u32[]{:S(2)}) collective-permute-start(bf16[1024,512]{1,0:T(8,128)(2,1)S(1)} %broadcast_select_fusion.1.refs_4_), channel_id=1, source_target_pairs={{0,4},{4,0},{8,12},{12,8},{16,20},{20,16},{24,28},{28,24},{1,5},{5... | collective-permute-start | bytes 3145736 | tf_op jit(solution)/shard_map/ppermute | solution.py:485
  137.5 34.7 %collective-permute-start.8 = (bf16[1024,512]{1,0:T(8,128)(2,1)}, bf16[1024,512]{1,0:T(8,128)(2,1)}, u32[]{:S(2)}, u32[]{:S(2)}) collective-permute-start(bf16[1024,512]{1,0:T(8,128)(2,1)} %broadcast_select_fusion.refs_0_.refs_6_), channel_id=1, source_target_pairs={{0,4},{4,0},{8,12},{12,8},{16,20},{20,16},{24,28},{28,24},{1,5},{5... | collective-permute-start | bytes 3145736 | tf_op jit(solution)/shard_map/ppermute | solution.py:485
  138.9 8.7 %copy-start.1 = (bf16[8,3,4,2,64,128]{5,4,3,2,1,0:T(8,128)(2,1)}, bf16[8,3,4,2,64,128]{5,4,3,2,1,0:T(8,128)(2,1)S(1)}, u32[]{:S(2)}) copy-start(bf16[8,3,4,2,64,128]{5,4,3,2,1,0:T(8,128)(2,1)S(1)} %all-to-all-done.chunk_ref) | copy-start | bytes 9437188
  147.6 1.0 copy-start.5
  148.6 49.4 %all-to-all-start.1 = ((bf16[8,4,2,64,128]{4,3,2,1,0:T(8,128)(2,1)}), bf16[8,4,2,64,128]{4,3,2,1,0:T(8,128)(2,1)S(1)}, u32[]{:S(2)}, u32[]{:S(2)}) async-start(bf16[8,4,2,64,128]{4,3,2,1,0:T(8,128)(2,1)} %copy-done.5), calls=%async_computation.1 | async-start | bytes 2097152 | tf_op jit(solution)/shard_map/all_to_all | solution.py:497
  155.3 16.8 %copy-start.12 = (bf16[2,512,512]{2,1,0:T(8,128)(2,1)S(1)}, bf16[2,512,512]{2,1,0:T(8,128)(2,1)}, u32[]{:S(2)}) copy-start(bf16[2,512,512]{2,1,0:T(8,128)(2,1)} %proj_part.8) | copy-start | bytes 3145732
  172.2 25.8 %collective-permute-start.9 = (bf16[2,512,512]{2,1,0:T(8,128)(2,1)S(1)}, bf16[2,512,512]{2,1,0:T(8,128)(2,1)S(1)}, u32[]{:S(2)}, u32[]{:S(2)}) collective-permute-start(bf16[2,512,512]{2,1,0:T(8,128)(2,1)S(1)} %copy-done.12), channel_id=1, source_target_pairs={{0,4},{4,0},{8,12},{12,8},{16,20},{20,16},{24,28},{28,24},{1,5},{5... | collective-permute-start | bytes 3145736 | tf_op jit(solution)/shard_map/ppermute | solution.py:485
  198.0 8.4 %copy-start.11 = (bf16[2,512,512]{2,1,0:T(8,128)(2,1)}, bf16[2,512,512]{2,1,0:T(8,128)(2,1)S(1)}, u32[]{:S(2)}) copy-start(bf16[2,512,512]{2,1,0:T(8,128)(2,1)S(1)} %collective-permute-done.9.refs_0_) | copy-start | bytes 3145732
  198.0 28.5 %all-to-all-start.2 = ((bf16[8,4,2,64,128]{4,3,2,1,0:T(8,128)(2,1)}), bf16[8,4,2,64,128]{4,3,2,1,0:T(8,128)(2,1)}, u32[]{:S(2)}, u32[]{:S(2)}) async-start(bf16[8,4,2,64,128]{4,3,2,1,0:T(8,128)(2,1)} %get-tuple-element.75), calls=%async_computation.2 | async-start | bytes 2097152 | tf_op jit(solution)/shard_map/all_to_all | solution.py:497
  204.9 8.0 %copy-start = (bf16[1024,512]{1,0:T(8,128)(2,1)S(1)}, bf16[1024,512]{1,0:T(8,128)(2,1)}, u32[]{:S(2)}) copy-start(bf16[1024,512]{1,0:T(8,128)(2,1)} %row_forward.1.flat_ref.row_ref) | copy-start | bytes 3145732
  204.9 47.9 %collective-permute-start.14 = (bf16[2,512,512]{2,1,0:T(8,128)(2,1)}, bf16[2,512,512]{2,1,0:T(8,128)(2,1)}, u32[]{:S(2)}, u32[]{:S(2)}) collective-permute-start(bf16[2,512,512]{2,1,0:T(8,128)(2,1)} %proj_part.9), channel_id=1, source_target_pairs={{0,4},{4,0},{8,12},{12,8},{16,20},{20,16},{24,28},{28,24},{1,5},{5... | collective-permute-start | bytes 3145736 | tf_op jit(solution)/shard_map/ppermute | solution.py:485
  211.4 41.4 %collective-permute-start.13 = (bf16[2,512,512]{2,1,0:T(8,128)(2,1)}, bf16[2,512,512]{2,1,0:T(8,128)(2,1)}, u32[]{:S(2)}, u32[]{:S(2)}) collective-permute-start(bf16[2,512,512]{2,1,0:T(8,128)(2,1)} %proj_part.10), channel_id=1, source_target_pairs={{0,8},{4,12},{24,16},{28,20},{1,9},{5,13},{25,17},{29,21},{2,10},{... | collective-permute-start | bytes 3145736 | tf_op jit(solution)/shard_map/ppermute | solution.py:485
  213.5 1.0 copy-start.3
  214.5 1.4 copy-start.4
  220.8 40.4 %collective-permute-start.12 = (bf16[2,512,512]{2,1,0:T(8,128)(2,1)}, bf16[2,512,512]{2,1,0:T(8,128)(2,1)}, u32[]{:S(2)}, u32[]{:S(2)}) collective-permute-start(bf16[2,512,512]{2,1,0:T(8,128)(2,1)} %proj_part.12), channel_id=1, source_target_pairs={{0,4},{4,0},{8,12},{12,8},{16,20},{20,16},{24,28},{28,24},{1,5},{5... | collective-permute-start | bytes 3145736 | tf_op jit(solution)/shard_map/ppermute | solution.py:485
  221.3 5.2 %copy-start.2 = (bf16[8,3,4,2,64,128]{5,4,3,2,1,0:T(8,128)(2,1)S(1)}, bf16[8,3,4,2,64,128]{5,4,3,2,1,0:T(8,128)(2,1)}, u32[]{:S(2)}) copy-start(bf16[8,3,4,2,64,128]{5,4,3,2,1,0:T(8,128)(2,1)} %copy-done.1) | copy-start | bytes 9437188
  252.7 21.7 %collective-permute-start.10 = (bf16[1024,2048]{1,0:T(8,128)(2,1)}, bf16[1024,2048]{1,0:T(8,128)(2,1)}, u32[]{:S(2)}, u32[]{:S(2)}) collective-permute-start(bf16[1024,2048]{1,0:T(8,128)(2,1)} %layer_part.3), channel_id=1, source_target_pairs={{0,1},{1,0},{2,3},{3,2},{4,5},{5,4},{6,7},{7,6},{8,9},{9,8},{10,11... | collective-permute-start | bytes 12582920 | tf_op jit(solution)/shard_map/ppermute | solution.py:513
  261.2 107.3 %all-to-all-start.3 = ((bf16[8,3,4,2,64,128]{5,4,3,2,1,0:T(8,128)(2,1)}), bf16[8,3,4,2,64,128]{5,4,3,2,1,0:T(8,128)(2,1)S(1)}, u32[]{:S(2)}, u32[]{:S(2)}) async-start(bf16[8,3,4,2,64,128]{5,4,3,2,1,0:T(8,128)(2,1)} %column_backward.1), calls=%async_computation.3 | async-start | bytes 6291456 | tf_op jit(solution)/shard_map/all_to_all | solution.py:497
  266.7 55.2 %collective-permute-start.17 = (bf16[2,512,512]{2,1,0:T(8,128)(2,1)}, bf16[2,512,512]{2,1,0:T(8,128)(2,1)}, u32[]{:S(2)}, u32[]{:S(2)}) collective-permute-start(bf16[2,512,512]{2,1,0:T(8,128)(2,1)} %proj_part.11), channel_id=1, source_target_pairs={{0,4},{4,0},{8,12},{12,8},{16,20},{20,16},{24,28},{28,24},{1,5},{5... | collective-permute-start | bytes 3145736 | tf_op jit(solution)/shard_map/ppermute | solution.py:485
  273.2 67.2 %collective-permute-start.18 = (bf16[2,512,512]{2,1,0:T(8,128)(2,1)}, bf16[2,512,512]{2,1,0:T(8,128)(2,1)}, u32[]{:S(2)}, u32[]{:S(2)}) collective-permute-start(bf16[2,512,512]{2,1,0:T(8,128)(2,1)} %proj_part.13), channel_id=1, source_target_pairs={{0,8},{4,12},{24,16},{28,20},{1,9},{5,13},{25,17},{29,21},{2,10},{... | collective-permute-start | bytes 3145736 | tf_op jit(solution)/shard_map/ppermute | solution.py:485
  283.0 94.5 %collective-permute-start.11 = (bf16[1024,1024]{1,0:T(8,128)(2,1)}, bf16[1024,1024]{1,0:T(8,128)(2,1)}, u32[]{:S(2)}, u32[]{:S(2)}) collective-permute-start(bf16[1024,1024]{1,0:T(8,128)(2,1)} %layer_part.4), channel_id=1, source_target_pairs={{0,2},{1,3},{2,0},{3,1},{4,6},{5,7},{6,4},{7,5},{8,10},{9,11},{10,... | collective-permute-start | bytes 6291464 | tf_op jit(solution)/shard_map/ppermute | solution.py:513
  287.9 71.4 %collective-permute-start.16 = (bf16[2,512,512]{2,1,0:T(8,128)(2,1)}, bf16[2,512,512]{2,1,0:T(8,128)(2,1)}, u32[]{:S(2)}, u32[]{:S(2)}) collective-permute-start(bf16[2,512,512]{2,1,0:T(8,128)(2,1)} %add_convert_fusion.1), channel_id=1, source_target_pairs={{8,16},{12,20},{16,8},{20,12},{9,17},{13,21},{17,9},{21,13},{10,18... | collective-permute-start | bytes 3145736 | tf_op jit(solution)/shard_map/ppermute | solution.py:485
  343.2 43.6 %collective-permute-start.21 = (bf16[2,512,512]{2,1,0:T(8,128)(2,1)}, bf16[2,512,512]{2,1,0:T(8,128)(2,1)}, u32[]{:S(2)}, u32[]{:S(2)}) collective-permute-start(bf16[2,512,512]{2,1,0:T(8,128)(2,1)} %add_convert_fusion), channel_id=1, source_target_pairs={{8,16},{12,20},{16,8},{20,12},{9,17},{13,21},{17,9},{21,13},{10,18... | collective-permute-start | bytes 3145736 | tf_op jit(solution)/shard_map/ppermute | solution.py:485
  347.0 17.1 %collective-permute-start.15 = (bf16[512,512]{1,0:T(8,128)(2,1)}, bf16[512,512]{1,0:T(8,128)(2,1)}, u32[]{:S(2)}, u32[]{:S(2)}) collective-permute-start(bf16[512,512]{1,0:T(8,128)(2,1)} %bitcast.17), channel_id=1, source_target_pairs={{0,8},{4,12},{24,16},{28,20},{1,9},{5,13},{25,17},{29,21},{2,10},{... | collective-permute-start | bytes 1572872 | tf_op jit(solution)/shard_map/ppermute | solution.py:485
  348.3 38.5 %collective-permute-start.20 = (bf16[512,512]{1,0:T(8,128)(2,1)}, bf16[512,512]{1,0:T(8,128)(2,1)}, u32[]{:S(2)}, u32[]{:S(2)}) collective-permute-start(bf16[512,512]{1,0:T(8,128)(2,1)} %bitcast.48), channel_id=1, source_target_pairs={{0,8},{4,12},{24,16},{28,20},{1,9},{5,13},{25,17},{29,21},{2,10},{... | collective-permute-start | bytes 1572872 | tf_op jit(solution)/shard_map/ppermute | solution.py:485
  366.2 23.2 %collective-permute-start.19 = (bf16[512,512]{1,0:T(8,128)(2,1)}, bf16[512,512]{1,0:T(8,128)(2,1)}, u32[]{:S(2)}, u32[]{:S(2)}) collective-permute-start(bf16[512,512]{1,0:T(8,128)(2,1)} %fusion.3), channel_id=1, source_target_pairs={{8,0},{12,4},{16,24},{20,28},{9,1},{13,5},{17,25},{21,29},{10,2},{... | collective-permute-start | bytes 1572872 | tf_op jit(solution)/shard_map/ppermute | solution.py:485
  368.5 1.6 copy-start.6
  377.4 9.4 %copy-start.15 = (bf16[1,512,512]{2,1,0:T(8,128)(2,1)S(1)}, bf16[1,512,512]{2,1,0:T(8,128)(2,1)}, u32[]{:S(2)}) copy-start(bf16[1,512,512]{2,1,0:T(8,128)(2,1)} %get-tuple-element.103) | copy-start | bytes 1572868
  377.4 12.0 %copy-start.13 = (bf16[1,512,512]{2,1,0:T(8,128)(2,1)S(1)}, bf16[1,512,512]{2,1,0:T(8,128)(2,1)}, u32[]{:S(2)}) copy-start(bf16[1,512,512]{2,1,0:T(8,128)(2,1)} %get-tuple-element.94) | copy-start | bytes 1572868
  386.8 9.2 %copy-start.14 = (bf16[1,512,512]{2,1,0:T(8,128)(2,1)S(1)}, bf16[1,512,512]{2,1,0:T(8,128)(2,1)}, u32[]{:S(2)}) copy-start(bf16[1,512,512]{2,1,0:T(8,128)(2,1)} %get-tuple-element.102) | copy-start | bytes 1572868
  388.1 8.0 %collective-permute-start.22 = (bf16[512,512]{1,0:T(8,128)(2,1)S(1)}, bf16[512,512]{1,0:T(8,128)(2,1)S(1)}, u32[]{:S(2)}, u32[]{:S(2)}) collective-permute-start(bf16[512,512]{1,0:T(8,128)(2,1)S(1)} %fusion), channel_id=1, source_target_pairs={{8,0},{12,4},{16,24},{20,28},{9,1},{13,5},{17,25},{21,29},{10,2},{... | collective-permute-start | bytes 1572872 | tf_op jit(solution)/shard_map/ppermute | solution.py:485

commit v9 on v8

--- a/solution.py
+++ b/solution.py
@@ -578,19 +578,18 @@
     so_far = attn_grad(ids[:early], after(out_grad, outs), blocks[:early], None, dim)
     grad_row, grads = attn_grad(ids[early:], out_grad, blocks[early:], so_far, dim)
     row_far = exchanged([after(part, so_far, *far_near_blocks) for part in row_far])
-    row_close = exchanged(row_close)
-    grads = swap(after(grads, column_part, *row_far))
-    (row_far,) = summed(after(row_out, outs), far, row_far, 0)
-    row_far_in = links.along(row_far, INWARD)
-    column_out, flat = collect(row_out, after(column_part, row_far))
+    grads = swap(after(grads, column_part))
+    column_out, flat = collect(row_out, column_part)
     column_far, column_close = leaving(column_out, far), leaving(column_out, close)
     column_far = exchanged(column_far)
+    (row_far,) = summed(after(row_out, *column_close), far, row_far, 0)
+    row_far_in = links.along(row_far, INWARD)
     gradients = column_backward(chunks, after(grads, *column_close, row_far))
-    column_grads = swap(after(gradients, *column_far, row_far_in, *row_close))
+    column_grads = swap(after(gradients, *column_far, row_far_in))
 
     layer = LayerSum(ids, after(flat, gradients), blocks, heads_n)
     layer.start()
-    column_close = exchanged(column_close)
+    row_close, column_close = exchanged(row_close), exchanged(column_close)
     (column_far,) = summed(after(column_out, gradients), far, column_far, 0)
     column_far_in = links.along(column_far, INWARD)
     row_cross = links.along(add(row_far, row_far_in), CROSS)
@@ -602,11 +601,10 @@
     layer.turn(gradients)
     first = after(column_far_in, row_grads[0], row_near[0], column_near[0], *layer.parts)
     column_cross = links.along(add(column_far, first), CROSS)
-    row_back = links.along(add(row_near[0], after(row_cross, row_near_in)[1]), OUTWARD)
     gradients = join_gradients(column_grads, row_grads)
     layer_out = layer.finish()
-    last = after(column_cross, column_near_in, gradients[0], layer_out)
-    column_back = links.along(add(column_near[0], last[1]), OUTWARD)
+    row_back = links.along(add(row_near[0], after(row_cross, gradients[0], layer_out)[1]), OUTWARD)
+    column_back = links.along(add(column_near[0], after(column_cross, gradients[0], layer_out)[1]), OUTWARD)
 
     proj_row = add(row_own[0], row_near_in, row_cross[0], row_back)
     proj_column = add(column_own[0], column_near_in, column_cross[0], column_back)

time: 404 us -> 438 us (1.084)
  waiting for transfers between devices: 147 us -> 175 us
  starting transfers between devices: 63 us -> 71.2 us
    ppermute x21, waiting for transfers between devices: 147 us -> 164 us  [send(): out = lax.ppermute(value, 'ctx', pairs)]
    all_to_all x4, waiting for transfers between devices: 0.01 us -> 11.6 us  [swap(): lax.all_to_all(chunks, 'ctx', split_axis=0, concat_axis=0, tiled=True)]
    ppermute x21, starting transfers between devices: 40.8 us -> 45.8 us  [send(): out = lax.ppermute(value, 'ctx', pairs)]
  transfers between devices with their start and end apart: 27 -> 27, of which waited for: 12 -> 13; matrix products, arithmetic and copies ran while one was open for 5% -> 4% of each run, Pallas kernels for 40% -> 36%
where the time goes in v9:
time: 438 us; the launch traced here: 433 us
  waiting for transfers between devices  175 us (40%)
  Pallas kernels  158 us (36%)
  starting transfers between devices  71.2 us (16%)
  other arithmetic  18.3 us (4%)
  local copies, waits for them, and re-layouts  9.33 us (2%)
    ppermute x21, waiting for transfers between devices, send(): out = lax.ppermute(value, 'ctx', pairs)  164 us
    ppermute x21, starting transfers between devices, send(): out = lax.ppermute(value, 'ctx', pairs)  45.8 us
    pallas_call x8, Pallas kernels, proj_part(): pl.pallas_call(functools.partial(proj_kernel, lead, len(extra), dim), gri...  40.1 us
    pallas_call x3, Pallas kernels, layer_part(): pl.pallas_call(functools.partial(layer_kernel, n, count, len(extra)), gri...  29.5 us
    pallas_call x2, Pallas kernels, attn_grad(): pl.pallas_call(functools.partial(attn_grad_kernel, m, dim, last), grid_sp...  26.8 us
    all_to_all x4, starting transfers between devices, swap(): lax.all_to_all(chunks, 'ctx', split_axis=0, concat_axis=0, tiled=True)  23.8 us
    pallas_call x1, Pallas kernels, column_backward(): pl.pallas_call(functools.partial(column_backward_kernel, dim ** (-0.5)),...  14.5 us
    pallas_call x1, Pallas kernels, row_backward(): pl.pallas_call(functools.partial(row_backward_kernel, dim ** (-0.5)), gri...  13.6 us
  transfers between devices with their start and end apart: 27, of which 13 were waited for; matrix products, arithmetic and copies ran while one was open for 4% of the time, Pallas kernels for 36%

profile of v9, /device:TPU:8, one launch (start us, length us, event | category | flops | bytes accessed | tf_op | source)
XLA Modules:
  0.0 433.5 jit_solution(14289898742305426793)
XLA Ops:
  0.6 3.5 collective-permute-start.4
  4.2 1.6 collective-permute-start.1
  5.8 7.1 %split_inputs.1 = (bf16[8,3,4,2,64,128]{5,4,3,2,1,0:T(8,128)(2,1)}, bf16[4,1024,128]{2,1,0:T(8,128)(2,1)}, bf16[4,1024,128]{2,1,0:T(8,128)(2,1)}, bf16[4,1024,128]{2,1,0:T(8,128)(2,1)}) custom-call(bf16[1024,8,128]{2,1,0:T(8,128)(2,1)} %q_ref.1, bf16[1024,8,128]{2,1,0:T(8,128)(2,1)} %k_ref.1, bf16[1024,8,128]{2,1,0:T(8,128)(2,1)} %v_ref.1), custom_call_target="tpu_custom_call" | custom-call | tf_op jit(solution)/shard_map/split_inputs/pallas_call | solution.py:48
  12.9 14.9 %collective-permute-done.4 = bf16[1024,512]{1,0:T(8,128)(2,1)} collective-permute-done((bf16[1024,512]{1,0:T(8,128)(2,1)}, bf16[1024,512]{1,0:T(8,128)(2,1)}, u32[]{:S(2)}, u32[]{:S(2)}) %collective-permute-start.4) | collective-permute-done | bytes 1048608 | tf_op jit(solution)/shard_map/ppermute | solution.py:485
  29.0 3.2 collective-permute-start.5
  32.2 3.1 collective-permute-start.3
  35.3 1.6 collective-permute-start.2
  36.9 9.9 %row_forward.1.flat_ref.row_ref = bf16[1024,512]{1,0:T(8,128)(2,1)} custom-call(bf16[4,1024,128]{2,1,0:T(8,128)(2,1)} %get-tuple-element.56.q_ref, bf16[4,1024,128]{2,1,0:T(8,128)(2,1)} %get-tuple-element.57.k_ref, bf16[4,1024,128]{2,1,0:T(8,128)(2,1)} %get-tuple-element.58.v_ref), custom_call_target="tpu_custom_call" | custom-call | flops 1073741824 | bytes 4194304 | tf_op jit(solution)/shard_map/row_forward/pallas_call | solution.py:321
  47.4 4.8 %proj_part.9 = bf16[2,512,512]{2,1,0:T(8,128)(2,1)} custom-call(s32[2]{0:T(128)} %pad_add_fusion.2.order, bf16[1024,512]{1,0:T(8,128)(2,1)} %row_forward.1.flat_ref.row_ref, bf16[1024,4096]{1,0:T(8,128)(2,1)} %grad_ref.18), custom_call_target="tpu_custom_call" | custom-call | flops 1073741824 | bytes 4194304 | tf_op jit(solution)/shard_map/proj_part/pallas_call | solution.py:275
  52.9 4.8 %proj_part.8 = bf16[2,512,512]{2,1,0:T(8,128)(2,1)} custom-call(s32[2]{0:T(128)} %pad_add_fusion.1.order, bf16[1024,512]{1,0:T(8,128)(2,1)} %row_forward.1.flat_ref.row_ref, bf16[1024,4096]{1,0:T(8,128)(2,1)} %grad_ref.18), custom_call_target="tpu_custom_call" | custom-call | flops 1073741824 | bytes 4194304 | tf_op jit(solution)/shard_map/proj_part/pallas_call | solution.py:275
  59.8 4.5 %all-to-all-start = ((bf16[8,3,4,2,64,128]{5,4,3,2,1,0:T(8,128)(2,1)}), bf16[8,3,4,2,64,128]{5,4,3,2,1,0:T(8,128)(2,1)S(1)}, u32[]{:S(2)}, u32[]{:S(2)}) async-start(bf16[8,3,4,2,64,128]{5,4,3,2,1,0:T(8,128)(2,1)} %get-tuple-element.62), calls=%async_computation | async-start | bytes 6291456 | tf_op jit(solution)/shard_map/all_to_all | solution.py:497
  65.7 1.5 collective-permute-start.6
  67.2 3.4 collective-permute-start.7
  70.7 47.5 %collective-permute-done.6.refs_5_ = bf16[1024,512]{1,0:T(8,128)(2,1)} collective-permute-done((bf16[1024,512]{1,0:T(8,128)(2,1)S(1)}, bf16[1024,512]{1,0:T(8,128)(2,1)}, u32[]{:S(2)}, u32[]{:S(2)}) %collective-permute-start.6) | collective-permute-done | bytes 1048608 | tf_op jit(solution)/shard_map/ppermute | solution.py:485
  118.1 11.6 %all-to-all-done.chunk_ref = bf16[8,3,4,2,64,128]{5,4,3,2,1,0:T(8,128)(2,1)S(1)} async-done(((bf16[8,3,4,2,64,128]{5,4,3,2,1,0:T(8,128)(2,1)}), bf16[8,3,4,2,64,128]{5,4,3,2,1,0:T(8,128)(2,1)S(1)}, u32[]{:S(2)}, u32[]{:S(2)}) %all-to-all-start) | async-done | bytes 3145760 | tf_op jit(solution)/shard_map/all_to_all | solution.py:497
  129.8 8.7 %column_forward.1 = bf16[8,4,2,64,128]{4,3,2,1,0:T(8,128)(2,1)S(1)} custom-call(bf16[8,3,4,2,64,128]{5,4,3,2,1,0:T(8,128)(2,1)S(1)} %all-to-all-done.chunk_ref), custom_call_target="tpu_custom_call" | custom-call | flops 536870912 | bytes 4194304 | tf_op jit(solution)/shard_map/column_forward/pallas_call | solution.py:413
  139.4 6.8 %all-to-all-start.1 = ((bf16[8,4,2,64,128]{4,3,2,1,0:T(8,128)(2,1)}), bf16[8,4,2,64,128]{4,3,2,1,0:T(8,128)(2,1)S(1)}, u32[]{:S(2)}, u32[]{:S(2)}) async-start(bf16[8,4,2,64,128]{4,3,2,1,0:T(8,128)(2,1)} %copy-done.5), calls=%async_computation.1 | async-start | bytes 2097152 | tf_op jit(solution)/shard_map/all_to_all | solution.py:497
  147.6 1.5 collective-permute-start.8
  150.4 16.6 %attn_grad.2.refs_2_ = f32[1024,1024]{1,0:T(8,128)} custom-call(s32[6]{0:T(128)} %stack.114.ids, bf16[1024,4096]{1,0:T(8,128)(2,1)} %grad_ref.18, bf16[1024,512]{1,0:T(8,128)(2,1)} %refs_0_.7, bf16[1024,512]{1,0:T(8,128)(2,1)} %copy-done.11, bf16[1024,512]{1,0:T(8,128)(2,1)} %copy-done.10, bf16[1024,512]{1,0:T(8,128)(2,1)} %copy-done.12, ...), custom_call_target="tpu_custom_call" | custom-call | flops 6442450944 | bytes 16777216 | tf_op jit(solution)/shard_map/attn_grad/pallas_call | solution.py:163
  167.0 14.8 %collective-permute-done.8.refs_1_.refs_7_ = bf16[1024,512]{1,0:T(8,128)(2,1)S(1)} collective-permute-done((bf16[1024,512]{1,0:T(8,128)(2,1)S(1)}, bf16[1024,512]{1,0:T(8,128)(2,1)S(1)}, u32[]{:S(2)}, u32[]{:S(2)}) %collective-permute-start.8) | collective-permute-done | bytes 1048608 | tf_op jit(solution)/shard_map/ppermute | solution.py:485
  182.8 10.1 %attn_grad.3 = (bf16[1024,512]{1,0:T(8,128)(2,1)}, bf16[8,4,2,64,128]{4,3,2,1,0:T(8,128)(2,1)}) custom-call(s32[2]{0:T(128)} %pad_add_fusion.3.ids, bf16[1024,4096]{1,0:T(8,128)(2,1)} %grad_ref.18, bf16[1024,512]{1,0:T(8,128)(2,1)} %copy-done.6, bf16[1024,512]{1,0:T(8,128)(2,1)} %copy-done.8, f32[1024,1024]{1,0:T(8,128)} %attn_grad.2.refs_2_), custom_call_target="tpu_custom_call" | custom-call | flops 2147483648 | bytes 8388608 | tf_op jit(solution)/shard_map/attn_grad/pallas_call | solution.py:163
  193.0 5.2 %all-to-all-start.2 = ((bf16[8,4,2,64,128]{4,3,2,1,0:T(8,128)(2,1)}), bf16[8,4,2,64,128]{4,3,2,1,0:T(8,128)(2,1)}, u32[]{:S(2)}, u32[]{:S(2)}) async-start(bf16[8,4,2,64,128]{4,3,2,1,0:T(8,128)(2,1)} %get-tuple-element.70), calls=%async_computation.2 | async-start | bytes 2097152 | tf_op jit(solution)/shard_map/all_to_all | solution.py:497
  204.6 4.8 %proj_part.10 = bf16[2,512,512]{2,1,0:T(8,128)(2,1)} custom-call(s32[2]{0:T(128)} %pad_add_fusion.2.order, bf16[1024,512]{1,0:T(8,128)(2,1)} %copy-done.3, bf16[1024,4096]{1,0:T(8,128)(2,1)} %grad_ref.18), custom_call_target="tpu_custom_call" | custom-call | flops 1073741824 | bytes 4194304 | tf_op jit(solution)/shard_map/proj_part/pallas_call | solution.py:275
  209.4 4.8 %proj_part.12 = bf16[2,512,512]{2,1,0:T(8,128)(2,1)} custom-call(s32[2]{0:T(128)} %pad_add_fusion.1.order, bf16[1024,512]{1,0:T(8,128)(2,1)} %copy-done.3, bf16[1024,4096]{1,0:T(8,128)(2,1)} %grad_ref.18), custom_call_target="tpu_custom_call" | custom-call | flops 1073741824 | bytes 4194304 | tf_op jit(solution)/shard_map/proj_part/pallas_call | solution.py:275
  214.8 20.5 %collective-permute-done.9.refs_0_ = bf16[2,512,512]{2,1,0:T(8,128)(2,1)} collective-permute-done((bf16[2,512,512]{2,1,0:T(8,128)(2,1)S(1)}, bf16[2,512,512]{2,1,0:T(8,128)(2,1)}, u32[]{:S(2)}, u32[]{:S(2)}) %collective-permute-start.9) | collective-permute-done | bytes 1048608 | tf_op jit(solution)/shard_map/ppermute | solution.py:485
  235.3 5.3 %proj_part.11 = bf16[2,512,512]{2,1,0:T(8,128)(2,1)} custom-call(s32[2]{0:T(128)} %pad_add_fusion.4.order, bf16[1024,512]{1,0:T(8,128)(2,1)} %row_forward.1.flat_ref.row_ref, bf16[1024,4096]{1,0:T(8,128)(2,1)} %grad_ref.18, bf16[2,512,512]{2,1,0:T(8,128)(2,1)} %collective-permute-done.9.refs_0_), custom_call_target="tpu_custom_call" | custom-call | flops 1073741824 | bytes 5242880 | tf_op jit(solution)/shard_map/proj_part/pallas_call | solution.py:275
  241.9 14.5 %column_backward.1 = bf16[8,3,4,2,64,128]{5,4,3,2,1,0:T(8,128)(2,1)} custom-call(bf16[8,3,4,2,64,128]{5,4,3,2,1,0:T(8,128)(2,1)S(1)} %copy-done.2, bf16[8,4,2,64,128]{4,3,2,1,0:T(8,128)(2,1)} %all-to-all-done.2.grad_ref), custom_call_target="tpu_custom_call" | custom-call | flops 1342177280 | bytes 7340032 | tf_op jit(solution)/shard_map/column_backward/pallas_call | solution.py:451
  256.4 11.7 %layer_part.3 = bf16[1024,2048]{1,0:T(8,128)(2,1)} custom-call(s32[8]{0:T(128)} %stack.107.ids, s32[4]{0:T(128)} %pad_add_fusion.5.wanted, bf16[1024,1024]{1,0:T(8,128)(2,1)} %copy-done.4, bf16[1024,512]{1,0:T(8,128)(2,1)} %refs_0_.7, bf16[1024,512]{1,0:T(8,128)(2,1)} %copy-done.11, bf16[1024,512]{1,0:T(8,128)(2,1)} %copy-done.10, ...), custom_call_target="tpu_custom_call" | custom-call | flops 4294967296 | bytes 10485760 | tf_op jit(solution)/shard_map/layer_part/pallas_call | solution.py:221
  268.2 7.2 %all-to-all-start.3 = ((bf16[8,3,4,2,64,128]{5,4,3,2,1,0:T(8,128)(2,1)}), bf16[8,3,4,2,64,128]{5,4,3,2,1,0:T(8,128)(2,1)S(1)}, u32[]{:S(2)}, u32[]{:S(2)}) async-start(bf16[8,3,4,2,64,128]{5,4,3,2,1,0:T(8,128)(2,1)} %column_backward.1), calls=%async_computation.3 | async-start | bytes 6291456 | tf_op jit(solution)/shard_map/all_to_all | solution.py:497
  278.1 8.5 %layer_part.4 = bf16[1024,1024]{1,0:T(8,128)(2,1)} custom-call(s32[8]{0:T(128)} %stack.107.ids, s32[2]{0:T(128)} %pad_add_fusion.6.wanted, bf16[1024,1024]{1,0:T(8,128)(2,1)} %copy-done.4, bf16[1024,512]{1,0:T(8,128)(2,1)} %refs_0_.7, bf16[1024,512]{1,0:T(8,128)(2,1)} %copy-done.11, bf16[1024,512]{1,0:T(8,128)(2,1)} %copy-done.10, ...), custom_call_target="tpu_custom_call" | custom-call | flops 2147483648 | bytes 6291456 | tf_op jit(solution)/shard_map/layer_part/pallas_call | solution.py:221
  286.5 1.6 collective-permute-start.11
  288.1 5.0 %proj_part.13 = bf16[2,512,512]{2,1,0:T(8,128)(2,1)} custom-call(s32[2]{0:T(128)} %pad_add_fusion.4.order, bf16[1024,512]{1,0:T(8,128)(2,1)} %copy-done.3, bf16[1024,4096]{1,0:T(8,128)(2,1)} %grad_ref.18, bf16[2,512,512]{2,1,0:T(8,128)(2,1)} %collective-permute-done.12.refs_0_), custom_call_target="tpu_custom_call" | custom-call | flops 1073741824 | bytes 5242880 | tf_op jit(solution)/shard_map/proj_part/pallas_call | solution.py:275
  295.0 2.8 add_convert_fusion.1
  297.7 3.6 collective-permute-start.16
  301.3 31.6 %collective-permute-done.17.refs_0_ = bf16[2,512,512]{2,1,0:T(8,128)(2,1)} collective-permute-done((bf16[2,512,512]{2,1,0:T(8,128)(2,1)}, bf16[2,512,512]{2,1,0:T(8,128)(2,1)}, u32[]{:S(2)}, u32[]{:S(2)}) %collective-permute-start.17) | collective-permute-done | bytes 1048608 | tf_op jit(solution)/shard_map/ppermute | solution.py:485
  332.9 5.2 %proj_part.15 = (bf16[1,512,512]{2,1,0:T(8,128)(2,1)}, bf16[1,512,512]{2,1,0:T(8,128)(2,1)}) custom-call(s32[2]{0:T(128)} %pad_add_fusion.7.order, bf16[1024,512]{1,0:T(8,128)(2,1)} %copy-done.3, bf16[1024,4096]{1,0:T(8,128)(2,1)} %grad_ref.18, bf16[2,512,512]{2,1,0:T(8,128)(2,1)} %collective-permute-done.17.refs_0_), custom_call_target="tpu_custom_call" | custom-call | flops 1073741824 | bytes 5242880 | tf_op jit(solution)/shard_map/proj_part/pallas_call | solution.py:275
  338.2 18.7 %collective-permute-done.14.refs_0_ = bf16[2,512,512]{2,1,0:T(8,128)(2,1)} collective-permute-done((bf16[2,512,512]{2,1,0:T(8,128)(2,1)}, bf16[2,512,512]{2,1,0:T(8,128)(2,1)}, u32[]{:S(2)}, u32[]{:S(2)}) %collective-permute-start.14) | collective-permute-done | bytes 1048608 | tf_op jit(solution)/shard_map/ppermute | solution.py:485
  356.9 5.2 %proj_part.14 = (bf16[1,512,512]{2,1,0:T(8,128)(2,1)}, bf16[1,512,512]{2,1,0:T(8,128)(2,1)}) custom-call(s32[2]{0:T(128)} %pad_add_fusion.7.order, bf16[1024,512]{1,0:T(8,128)(2,1)} %row_forward.1.flat_ref.row_ref, bf16[1024,4096]{1,0:T(8,128)(2,1)} %grad_ref.18, bf16[2,512,512]{2,1,0:T(8,128)(2,1)} %collective-permute-done.14.refs_0_), custom_call_target="tpu_custom_call" | custom-call | flops 1073741824 | bytes 5242880 | tf_op jit(solution)/shard_map/proj_part/pallas_call | solution.py:275
  362.1 13.6 %row_backward.1 = (bf16[4,1024,128]{2,1,0:T(8,128)(2,1)}, bf16[4,1024,128]{2,1,0:T(8,128)(2,1)}, bf16[4,1024,128]{2,1,0:T(8,128)(2,1)}) custom-call(bf16[4,1024,128]{2,1,0:T(8,128)(2,1)} %get-tuple-element.56.q_ref, bf16[4,1024,128]{2,1,0:T(8,128)(2,1)} %get-tuple-element.57.k_ref, bf16[4,1024,128]{2,1,0:T(8,128)(2,1)} %get-tuple-element.58.v_ref, ...), custom_call_target="tpu_custom_call" | custom-call | flops 2684354560 | bytes 7340032 | tf_op jit(solution)/shard_map/row_backward/pallas_call | solution.py:355
  375.7 2.8 add_convert_fusion
  378.5 3.4 collective-permute-start.21
  383.8 1.6 copy-done.7
  385.4 7.3 %join_gradients.1 = (bf16[1024,8,128]{2,1,0:T(8,128)(2,1)}, bf16[1024,8,128]{2,1,0:T(8,128)(2,1)}, bf16[1024,8,128]{2,1,0:T(8,128)(2,1)}) custom-call(bf16[8,3,4,2,64,128]{5,4,3,2,1,0:T(8,128)(2,1)} %copy-done.7, bf16[4,1024,128]{2,1,0:T(8,128)(2,1)} %get-tuple-element.84.refs_0_, bf16[4,1024,128]{2,1,0:T(8,128)(2,1)} %get-tuple-element.85.refs_1_, ...), custom_call_target="tpu_custom_call" | custom-call | tf_op jit(solution)/shard_map/join_gradients/pallas_call | solution.py:78
  392.8 9.3 %layer_part.5 = bf16[1024,1024]{1,0:T(8,128)(2,1)} custom-call(s32[8]{0:T(128)} %stack.107.ids, s32[2]{0:T(128)} %pad_add_fusion.wanted, bf16[1024,1024]{1,0:T(8,128)(2,1)} %copy-done.4, bf16[1024,512]{1,0:T(8,128)(2,1)} %refs_0_.7, bf16[1024,512]{1,0:T(8,128)(2,1)} %copy-done.11, bf16[1024,512]{1,0:T(8,128)(2,1)} %copy-done.10, ...), custom_call_target="tpu_custom_call" | custom-call | flops 2147483648 | bytes 6291456 | tf_op jit(solution)/shard_map/layer_part/pallas_call | solution.py:221
  403.4 5.5 %collective-permute-start.19 = (bf16[512,512]{1,0:T(8,128)(2,1)S(1)}, bf16[512,512]{1,0:T(8,128)(2,1)S(1)}, u32[]{:S(2)}, u32[]{:S(2)}) collective-permute-start(bf16[512,512]{1,0:T(8,128)(2,1)S(1)} %fusion.3), channel_id=1, source_target_pairs={{8,0},{12,4},{16,24},{20,28},{9,1},{13,5},{17,25},{21,29},{10,2},{... | collective-permute-start | bytes 1572872 | tf_op jit(solution)/shard_map/ppermute | solution.py:485
  411.4 4.6 %collective-permute-start.22 = (bf16[512,512]{1,0:T(8,128)(2,1)S(1)}, bf16[512,512]{1,0:T(8,128)(2,1)S(1)}, u32[]{:S(2)}, u32[]{:S(2)}) collective-permute-start(bf16[512,512]{1,0:T(8,128)(2,1)S(1)} %fusion), channel_id=1, source_target_pairs={{8,0},{12,4},{16,24},{20,28},{9,1},{13,5},{17,25},{21,29},{10,2},{... | collective-permute-start | bytes 1572872 | tf_op jit(solution)/shard_map/ppermute | solution.py:485
  416.1 5.2 %collective-permute-done.19 = bf16[512,512]{1,0:T(8,128)(2,1)S(1)} collective-permute-done((bf16[512,512]{1,0:T(8,128)(2,1)S(1)}, bf16[512,512]{1,0:T(8,128)(2,1)S(1)}, u32[]{:S(2)}, u32[]{:S(2)}) %collective-permute-start.19) | collective-permute-done | bytes 524320 | tf_op jit(solution)/shard_map/ppermute | solution.py:485
  423.9 7.1 %collective-permute-done.22 = bf16[512,512]{1,0:T(8,128)(2,1)S(1)} collective-permute-done((bf16[512,512]{1,0:T(8,128)(2,1)S(1)}, bf16[512,512]{1,0:T(8,128)(2,1)S(1)}, u32[]{:S(2)}, u32[]{:S(2)}) %collective-permute-start.22) | collective-permute-done | bytes 524320 | tf_op jit(solution)/shard_map/ppermute | solution.py:485
  (82 shorter events, 34.0 us)
Async XLA Ops:
  0.6 27.1 %collective-permute-start.4 = (bf16[1024,512]{1,0:T(8,128)(2,1)}, bf16[1024,512]{1,0:T(8,128)(2,1)}, u32[]{:S(2)}, u32[]{:S(2)}) collective-permute-start(bf16[1024,512]{1,0:T(8,128)(2,1)} %refs_0_.7), channel_id=1, source_target_pairs={{8,16},{12,20},{16,8},{20,12},{9,17},{13,21},{17,9},{21,13},{10,18... | collective-permute-start | bytes 3145736 | tf_op jit(solution)/shard_map/ppermute | solution.py:485
  4.1 24.9 %collective-permute-start = (bf16[1024,512]{1,0:T(8,128)(2,1)}, bf16[1024,512]{1,0:T(8,128)(2,1)S(1)}, u32[]{:S(2)}, u32[]{:S(2)}) collective-permute-start(bf16[1024,512]{1,0:T(8,128)(2,1)} %refs_0_.7), channel_id=1, source_target_pairs={{0,8},{4,12},{8,0},{12,4},{16,24},{20,28},{24,16},{28,20},{1,9},{5... | collective-permute-start | bytes 3145736 | tf_op jit(solution)/shard_map/ppermute | solution.py:485
  4.2 28.0 %collective-permute-start.1 = (bf16[1024,512]{1,0:T(8,128)(2,1)}, bf16[1024,512]{1,0:T(8,128)(2,1)S(1)}, u32[]{:S(2)}, u32[]{:S(2)}) collective-permute-start(bf16[1024,512]{1,0:T(8,128)(2,1)} %refs_0_.7), channel_id=1, source_target_pairs={{0,4},{4,0},{8,12},{12,8},{16,20},{20,16},{24,28},{28,24},{1,5},{5... | collective-permute-start | bytes 3145736 | tf_op jit(solution)/shard_map/ppermute | solution.py:485
  29.0 17.8 %copy-start.10 = (bf16[1024,512]{1,0:T(8,128)(2,1)}, bf16[1024,512]{1,0:T(8,128)(2,1)S(1)}, u32[]{:S(2)}) copy-start(bf16[1024,512]{1,0:T(8,128)(2,1)S(1)} %collective-permute-done.refs_2_) | copy-start | bytes 3145732
  29.0 28.7 %collective-permute-start.5 = (bf16[1024,512]{1,0:T(8,128)(2,1)}, bf16[1024,512]{1,0:T(8,128)(2,1)}, u32[]{:S(2)}, u32[]{:S(2)}) collective-permute-start(bf16[1024,512]{1,0:T(8,128)(2,1)} %collective-permute-done.4), channel_id=1, source_target_pairs={{8,0},{12,4},{16,24},{20,28},{9,1},{13,5},{17,25},{21,29},{10,2},{... | collective-permute-start | bytes 3145736 | tf_op jit(solution)/shard_map/ppermute | solution.py:485
  32.2 14.6 %copy-start.11 = (bf16[1024,512]{1,0:T(8,128)(2,1)}, bf16[1024,512]{1,0:T(8,128)(2,1)S(1)}, u32[]{:S(2)}) copy-start(bf16[1024,512]{1,0:T(8,128)(2,1)S(1)} %collective-permute-done.1.refs_1_) | copy-start | bytes 3145732
  32.2 25.7 %collective-permute-start.3 = (bf16[1024,512]{1,0:T(8,128)(2,1)S(1)}, bf16[1024,512]{1,0:T(8,128)(2,1)}, u32[]{:S(2)}, u32[]{:S(2)}) collective-permute-start(bf16[1024,512]{1,0:T(8,128)(2,1)S(1)} %collective-permute-done.refs_2_), channel_id=1, source_target_pairs={{8,16},{12,20},{16,8},{20,12},{9,17},{13,21},{17,9},{21,13},{10,18... | collective-permute-start | bytes 3145736 | tf_op jit(solution)/shard_map/ppermute | solution.py:485
  35.3 23.5 %collective-permute-start.2 = (bf16[1024,512]{1,0:T(8,128)(2,1)S(1)}, bf16[1024,512]{1,0:T(8,128)(2,1)S(1)}, u32[]{:S(2)}, u32[]{:S(2)}) collective-permute-start(bf16[1024,512]{1,0:T(8,128)(2,1)S(1)} %collective-permute-done.refs_2_), channel_id=1, source_target_pairs={{0,4},{4,0},{8,12},{12,8},{16,20},{20,16},{24,28},{28,24},{1,5},{5... | collective-permute-start | bytes 3145736 | tf_op jit(solution)/shard_map/ppermute | solution.py:485
  58.9 1.0 copy-start.12
  59.8 69.9 %all-to-all-start = ((bf16[8,3,4,2,64,128]{5,4,3,2,1,0:T(8,128)(2,1)}), bf16[8,3,4,2,64,128]{5,4,3,2,1,0:T(8,128)(2,1)S(1)}, u32[]{:S(2)}, u32[]{:S(2)}) async-start(bf16[8,3,4,2,64,128]{5,4,3,2,1,0:T(8,128)(2,1)} %get-tuple-element.62), calls=%async_computation | async-start | bytes 6291456 | tf_op jit(solution)/shard_map/all_to_all | solution.py:497
  65.7 5.0 %copy-start.9 = (bf16[1024,512]{1,0:T(8,128)(2,1)}, bf16[1024,512]{1,0:T(8,128)(2,1)S(1)}, u32[]{:S(2)}) copy-start(bf16[1024,512]{1,0:T(8,128)(2,1)S(1)} %broadcast_select_fusion.1.refs_4_) | copy-start | bytes 3145732
  65.7 52.5 %collective-permute-start.6 = (bf16[1024,512]{1,0:T(8,128)(2,1)S(1)}, bf16[1024,512]{1,0:T(8,128)(2,1)}, u32[]{:S(2)}, u32[]{:S(2)}) collective-permute-start(bf16[1024,512]{1,0:T(8,128)(2,1)S(1)} %broadcast_select_fusion.1.refs_4_), channel_id=1, source_target_pairs={{0,4},{4,0},{8,12},{12,8},{16,20},{20,16},{24,28},{28,24},{1,5},{5... | collective-permute-start | bytes 3145736 | tf_op jit(solution)/shard_map/ppermute | solution.py:485
  67.2 79.0 %collective-permute-start.7 = (bf16[1024,512]{1,0:T(8,128)(2,1)}, bf16[1024,512]{1,0:T(8,128)(2,1)}, u32[]{:S(2)}, u32[]{:S(2)}) collective-permute-start(bf16[1024,512]{1,0:T(8,128)(2,1)} %collective-permute-done.3), channel_id=1, source_target_pairs={{8,0},{12,4},{16,24},{20,28},{9,1},{13,5},{17,25},{21,29},{10,2},{... | collective-permute-start | bytes 3145736 | tf_op jit(solution)/shard_map/ppermute | solution.py:485
  129.8 8.7 %copy-start.1 = (bf16[8,3,4,2,64,128]{5,4,3,2,1,0:T(8,128)(2,1)}, bf16[8,3,4,2,64,128]{5,4,3,2,1,0:T(8,128)(2,1)S(1)}, u32[]{:S(2)}) copy-start(bf16[8,3,4,2,64,128]{5,4,3,2,1,0:T(8,128)(2,1)S(1)} %all-to-all-done.chunk_ref) | copy-start | bytes 9437188
  138.5 1.0 copy-start.5
  139.4 53.6 %all-to-all-start.1 = ((bf16[8,4,2,64,128]{4,3,2,1,0:T(8,128)(2,1)}), bf16[8,4,2,64,128]{4,3,2,1,0:T(8,128)(2,1)S(1)}, u32[]{:S(2)}, u32[]{:S(2)}) async-start(bf16[8,4,2,64,128]{4,3,2,1,0:T(8,128)(2,1)} %copy-done.5), calls=%async_computation.1 | async-start | bytes 2097152 | tf_op jit(solution)/shard_map/all_to_all | solution.py:497
  147.6 19.4 %copy-start.6 = (bf16[1024,512]{1,0:T(8,128)(2,1)}, bf16[1024,512]{1,0:T(8,128)(2,1)S(1)}, u32[]{:S(2)}) copy-start(bf16[1024,512]{1,0:T(8,128)(2,1)S(1)} %broadcast_select_fusion.refs_0_.refs_6_) | copy-start | bytes 3145732
  147.6 34.3 %collective-permute-start.8 = (bf16[1024,512]{1,0:T(8,128)(2,1)S(1)}, bf16[1024,512]{1,0:T(8,128)(2,1)S(1)}, u32[]{:S(2)}, u32[]{:S(2)}) collective-permute-start(bf16[1024,512]{1,0:T(8,128)(2,1)S(1)} %broadcast_select_fusion.refs_0_.refs_6_), channel_id=1, source_target_pairs={{0,4},{4,0},{8,12},{12,8},{16,20},{20,16},{24,28},{28,24},{1,5},{5... | collective-permute-start | bytes 3145736 | tf_op jit(solution)/shard_map/ppermute | solution.py:485
  181.9 1.0 copy-start.8
  193.0 5.3 %copy-start.13 = (bf16[2,512,512]{2,1,0:T(8,128)(2,1)S(1)}, bf16[2,512,512]{2,1,0:T(8,128)(2,1)}, u32[]{:S(2)}) copy-start(bf16[2,512,512]{2,1,0:T(8,128)(2,1)} %proj_part.8) | copy-start | bytes 3145732
  193.0 8.6 %copy-start = (bf16[1024,512]{1,0:T(8,128)(2,1)S(1)}, bf16[1024,512]{1,0:T(8,128)(2,1)}, u32[]{:S(2)}) copy-start(bf16[1024,512]{1,0:T(8,128)(2,1)} %row_forward.1.flat_ref.row_ref) | copy-start | bytes 3145732
  193.0 48.9 %all-to-all-start.2 = ((bf16[8,4,2,64,128]{4,3,2,1,0:T(8,128)(2,1)}), bf16[8,4,2,64,128]{4,3,2,1,0:T(8,128)(2,1)}, u32[]{:S(2)}, u32[]{:S(2)}) async-start(bf16[8,4,2,64,128]{4,3,2,1,0:T(8,128)(2,1)} %get-tuple-element.70), calls=%async_computation.2 | async-start | bytes 2097152 | tf_op jit(solution)/shard_map/all_to_all | solution.py:497
  198.2 37.1 %collective-permute-start.9 = (bf16[2,512,512]{2,1,0:T(8,128)(2,1)S(1)}, bf16[2,512,512]{2,1,0:T(8,128)(2,1)}, u32[]{:S(2)}, u32[]{:S(2)}) collective-permute-start(bf16[2,512,512]{2,1,0:T(8,128)(2,1)S(1)} %copy-done.13), channel_id=1, source_target_pairs={{0,4},{4,0},{8,12},{12,8},{16,20},{20,16},{24,28},{28,24},{1,5},{5... | collective-permute-start | bytes 3145736 | tf_op jit(solution)/shard_map/ppermute | solution.py:485
  202.3 1.0 copy-start.3
  203.2 1.4 copy-start.4
  214.3 53.9 %collective-permute-start.12 = (bf16[2,512,512]{2,1,0:T(8,128)(2,1)}, bf16[2,512,512]{2,1,0:T(8,128)(2,1)}, u32[]{:S(2)}, u32[]{:S(2)}) collective-permute-start(bf16[2,512,512]{2,1,0:T(8,128)(2,1)} %proj_part.12), channel_id=1, source_target_pairs={{0,4},{4,0},{8,12},{12,8},{16,20},{20,16},{24,28},{28,24},{1,5},{5... | collective-permute-start | bytes 3145736 | tf_op jit(solution)/shard_map/ppermute | solution.py:485
  235.3 6.6 %copy-start.2 = (bf16[8,3,4,2,64,128]{5,4,3,2,1,0:T(8,128)(2,1)S(1)}, bf16[8,3,4,2,64,128]{5,4,3,2,1,0:T(8,128)(2,1)}, u32[]{:S(2)}) copy-start(bf16[8,3,4,2,64,128]{5,4,3,2,1,0:T(8,128)(2,1)} %copy-done.1) | copy-start | bytes 9437188
  240.6 27.6 %collective-permute-start.13 = (bf16[2,512,512]{2,1,0:T(8,128)(2,1)}, bf16[2,512,512]{2,1,0:T(8,128)(2,1)}, u32[]{:S(2)}, u32[]{:S(2)}) collective-permute-start(bf16[2,512,512]{2,1,0:T(8,128)(2,1)} %proj_part.11), channel_id=1, source_target_pairs={{0,8},{4,12},{24,16},{28,20},{1,9},{5,13},{25,17},{29,21},{2,10},{... | collective-permute-start | bytes 3145736 | tf_op jit(solution)/shard_map/ppermute | solution.py:485
  268.1 10.0 %collective-permute-start.10 = (bf16[1024,2048]{1,0:T(8,128)(2,1)}, bf16[1024,2048]{1,0:T(8,128)(2,1)}, u32[]{:S(2)}, u32[]{:S(2)}) collective-permute-start(bf16[1024,2048]{1,0:T(8,128)(2,1)} %layer_part.3), channel_id=1, source_target_pairs={{0,1},{1,0},{2,3},{3,2},{4,5},{5,4},{6,7},{7,6},{8,9},{9,8},{10,11... | collective-permute-start | bytes 12582920 | tf_op jit(solution)/shard_map/ppermute | solution.py:513
  268.2 115.6 %all-to-all-start.3 = ((bf16[8,3,4,2,64,128]{5,4,3,2,1,0:T(8,128)(2,1)}), bf16[8,3,4,2,64,128]{5,4,3,2,1,0:T(8,128)(2,1)S(1)}, u32[]{:S(2)}, u32[]{:S(2)}) async-start(bf16[8,3,4,2,64,128]{5,4,3,2,1,0:T(8,128)(2,1)} %column_backward.1), calls=%async_computation.3 | async-start | bytes 6291456 | tf_op jit(solution)/shard_map/all_to_all | solution.py:497
  275.4 57.5 %collective-permute-start.17 = (bf16[2,512,512]{2,1,0:T(8,128)(2,1)}, bf16[2,512,512]{2,1,0:T(8,128)(2,1)}, u32[]{:S(2)}, u32[]{:S(2)}) collective-permute-start(bf16[2,512,512]{2,1,0:T(8,128)(2,1)} %proj_part.10), channel_id=1, source_target_pairs={{0,4},{4,0},{8,12},{12,8},{16,20},{20,16},{24,28},{28,24},{1,5},{5... | collective-permute-start | bytes 3145736 | tf_op jit(solution)/shard_map/ppermute | solution.py:485
  277.5 79.4 %collective-permute-start.14 = (bf16[2,512,512]{2,1,0:T(8,128)(2,1)}, bf16[2,512,512]{2,1,0:T(8,128)(2,1)}, u32[]{:S(2)}, u32[]{:S(2)}) collective-permute-start(bf16[2,512,512]{2,1,0:T(8,128)(2,1)} %proj_part.9), channel_id=1, source_target_pairs={{0,4},{4,0},{8,12},{12,8},{16,20},{20,16},{24,28},{28,24},{1,5},{5... | collective-permute-start | bytes 3145736 | tf_op jit(solution)/shard_map/ppermute | solution.py:485
  286.5 106.2 %collective-permute-start.11 = (bf16[1024,1024]{1,0:T(8,128)(2,1)}, bf16[1024,1024]{1,0:T(8,128)(2,1)}, u32[]{:S(2)}, u32[]{:S(2)}) collective-permute-start(bf16[1024,1024]{1,0:T(8,128)(2,1)} %layer_part.4), channel_id=1, source_target_pairs={{0,2},{1,3},{2,0},{3,1},{4,6},{5,7},{6,4},{7,5},{8,10},{9,11},{10,... | collective-permute-start | bytes 6291464 | tf_op jit(solution)/shard_map/ppermute | solution.py:513
  293.1 82.6 %collective-permute-start.18 = (bf16[2,512,512]{2,1,0:T(8,128)(2,1)}, bf16[2,512,512]{2,1,0:T(8,128)(2,1)}, u32[]{:S(2)}, u32[]{:S(2)}) collective-permute-start(bf16[2,512,512]{2,1,0:T(8,128)(2,1)} %proj_part.13), channel_id=1, source_target_pairs={{0,8},{4,12},{24,16},{28,20},{1,9},{5,13},{25,17},{29,21},{2,10},{... | collective-permute-start | bytes 3145736 | tf_op jit(solution)/shard_map/ppermute | solution.py:485
  297.7 104.4 %collective-permute-start.16 = (bf16[2,512,512]{2,1,0:T(8,128)(2,1)}, bf16[2,512,512]{2,1,0:T(8,128)(2,1)}, u32[]{:S(2)}, u32[]{:S(2)}) collective-permute-start(bf16[2,512,512]{2,1,0:T(8,128)(2,1)} %add_convert_fusion.1), channel_id=1, source_target_pairs={{8,16},{12,20},{16,8},{20,12},{9,17},{13,21},{17,9},{21,13},{10,18... | collective-permute-start | bytes 3145736 | tf_op jit(solution)/shard_map/ppermute | solution.py:485
  378.5 31.7 %collective-permute-start.21 = (bf16[2,512,512]{2,1,0:T(8,128)(2,1)}, bf16[2,512,512]{2,1,0:T(8,128)(2,1)}, u32[]{:S(2)}, u32[]{:S(2)}) collective-permute-start(bf16[2,512,512]{2,1,0:T(8,128)(2,1)} %add_convert_fusion), channel_id=1, source_target_pairs={{8,16},{12,20},{16,8},{20,12},{9,17},{13,21},{17,9},{21,13},{10,18... | collective-permute-start | bytes 3145736 | tf_op jit(solution)/shard_map/ppermute | solution.py:485
  382.5 33.6 %collective-permute-start.15 = (bf16[512,512]{1,0:T(8,128)(2,1)}, bf16[512,512]{1,0:T(8,128)(2,1)}, u32[]{:S(2)}, u32[]{:S(2)}) collective-permute-start(bf16[512,512]{1,0:T(8,128)(2,1)} %bitcast.49), channel_id=1, source_target_pairs={{0,8},{4,12},{24,16},{28,20},{1,9},{5,13},{25,17},{29,21},{2,10},{... | collective-permute-start | bytes 1572872 | tf_op jit(solution)/shard_map/ppermute | solution.py:485
  383.8 1.6 copy-start.7
  392.8 9.4 %copy-start.17 = (bf16[1,512,512]{2,1,0:T(8,128)(2,1)S(1)}, bf16[1,512,512]{2,1,0:T(8,128)(2,1)}, u32[]{:S(2)}) copy-start(bf16[1,512,512]{2,1,0:T(8,128)(2,1)} %get-tuple-element.93) | copy-start | bytes 1572868
  392.8 16.2 %copy-start.15 = (bf16[1,512,512]{2,1,0:T(8,128)(2,1)S(1)}, bf16[1,512,512]{2,1,0:T(8,128)(2,1)}, u32[]{:S(2)}) copy-start(bf16[1,512,512]{2,1,0:T(8,128)(2,1)} %get-tuple-element.101) | copy-start | bytes 1572868
  402.1 19.2 %copy-start.16 = (bf16[1,512,512]{2,1,0:T(8,128)(2,1)S(1)}, bf16[1,512,512]{2,1,0:T(8,128)(2,1)}, u32[]{:S(2)}) copy-start(bf16[1,512,512]{2,1,0:T(8,128)(2,1)} %get-tuple-element.92) | copy-start | bytes 1572868
  403.4 27.6 %copy-start.14 = (bf16[1,512,512]{2,1,0:T(8,128)(2,1)S(1)}, bf16[1,512,512]{2,1,0:T(8,128)(2,1)}, u32[]{:S(2)}) copy-start(bf16[1,512,512]{2,1,0:T(8,128)(2,1)} %get-tuple-element.100) | copy-start | bytes 1572868
  403.4 17.9 %collective-permute-start.19 = (bf16[512,512]{1,0:T(8,128)(2,1)S(1)}, bf16[512,512]{1,0:T(8,128)(2,1)S(1)}, u32[]{:S(2)}, u32[]{:S(2)}) collective-permute-start(bf16[512,512]{1,0:T(8,128)(2,1)S(1)} %fusion.3), channel_id=1, source_target_pairs={{8,0},{12,4},{16,24},{20,28},{9,1},{13,5},{17,25},{21,29},{10,2},{... | collective-permute-start | bytes 1572872 | tf_op jit(solution)/shard_map/ppermute | solution.py:485
  408.9 14.9 %collective-permute-start.20 = (bf16[512,512]{1,0:T(8,128)(2,1)S(1)}, bf16[512,512]{1,0:T(8,128)(2,1)S(1)}, u32[]{:S(2)}, u32[]{:S(2)}) collective-permute-start(bf16[512,512]{1,0:T(8,128)(2,1)S(1)} %bitcast.48), channel_id=1, source_target_pairs={{0,8},{4,12},{24,16},{28,20},{1,9},{5,13},{25,17},{29,21},{2,10},{... | collective-permute-start | bytes 1572872 | tf_op jit(solution)/shard_map/ppermute | solution.py:485
  411.4 19.5 %collective-permute-start.22 = (bf16[512,512]{1,0:T(8,128)(2,1)S(1)}, bf16[512,512]{1,0:T(8,128)(2,1)S(1)}, u32[]{:S(2)}, u32[]{:S(2)}) collective-permute-start(bf16[512,512]{1,0:T(8,128)(2,1)S(1)} %fusion), channel_id=1, source_target_pairs={{8,0},{12,4},{16,24},{20,28},{9,1},{13,5},{17,25},{21,29},{10,2},{... | collective-permute-start | bytes 1572872 | tf_op jit(solution)/shard_map/ppermute | solution.py:485

commit v10 on v9

--- a/solution.py
+++ b/solution.py
@@ -578,33 +578,35 @@
     so_far = attn_grad(ids[:early], after(out_grad, outs), blocks[:early], None, dim)
     grad_row, grads = attn_grad(ids[early:], out_grad, blocks[early:], so_far, dim)
     row_far = exchanged([after(part, so_far, *far_near_blocks) for part in row_far])
-    grads = swap(after(grads, column_part))
     column_out, flat = collect(row_out, column_part)
     column_far, column_close = leaving(column_out, far), leaving(column_out, close)
+    grads = swap(after(grads, column_part, *row_far, *column_far, *column_close))
     column_far = exchanged(column_far)
     (row_far,) = summed(after(row_out, *column_close), far, row_far, 0)
     row_far_in = links.along(row_far, INWARD)
-    gradients = column_backward(chunks, after(grads, *column_close, row_far))
-    column_grads = swap(after(gradients, *column_far, row_far_in))
-
-    layer = LayerSum(ids, after(flat, gradients), blocks, heads_n)
+    layer = LayerSum(ids, after(flat, row_far), blocks, heads_n)
     layer.start()
-    row_close, column_close = exchanged(row_close), exchanged(column_close)
-    (column_far,) = summed(after(column_out, gradients), far, column_far, 0)
+    row_close = exchanged([after(part, *column_far) for part in row_close])
+    (column_far,) = summed(column_out, far, column_far, 0)
     column_far_in = links.along(column_far, INWARD)
-    row_cross = links.along(add(row_far, row_far_in), CROSS)
+    row_middle = add(row_far, row_far_in)
+    row_cross = links.along(row_middle, CROSS)
+    gradients = column_backward(chunks, after(grads, column_far, row_middle, layer.first))
+    column_close = exchanged(column_close)
+    column_cross = links.along(add(column_far, column_far_in), CROSS)
+    column_grads = swap(after(gradients, row_cross, column_cross, *row_close, *column_close))
+
+    layer.turn(gradients)
     row_near, row_own = summed(after(row_out, gradients), close, row_close, 1)
     row_near_in = links.along(row_near[0], INWARD)
-    row_grads = row_backward(*by_head, after(grad_row, column_far))
     column_near, column_own = summed(after(column_out, gradients), close, column_close, 1)
     column_near_in = links.along(column_near[0], INWARD)
-    layer.turn(gradients)
-    first = after(column_far_in, row_grads[0], row_near[0], column_near[0], *layer.parts)
-    column_cross = links.along(add(column_far, first), CROSS)
-    gradients = join_gradients(column_grads, row_grads)
+    row_grads = row_backward(*by_head, after(grad_row, gradients))
+    row_back = links.along(add(row_near[0], row_cross[1]), OUTWARD)
+    column_back = links.along(add(column_near[0], column_cross[1]), OUTWARD)
     layer_out = layer.finish()
-    row_back = links.along(add(row_near[0], after(row_cross, gradients[0], layer_out)[1]), OUTWARD)
-    column_back = links.along(add(column_near[0], after(column_cross, gradients[0], layer_out)[1]), OUTWARD)
+    ahead = after(row_grads[0], layer_out, row_back, column_back, row_near_in, column_near_in)
+    gradients = join_gradients(column_grads, [ahead, *row_grads[1:]])
 
     proj_row = add(row_own[0], row_near_in, row_cross[0], row_back)
     proj_column = add(column_own[0], column_near_in, column_cross[0], column_back)

time: 438 us -> 428 us (0.977)
  waiting for transfers between devices: 175 us -> 167 us
    ppermute x21, waiting for transfers between devices: 164 us -> 155 us  [send(): out = lax.ppermute(value, 'ctx', pairs)]
  transfers between devices with their start and end apart: 27 -> 27, of which waited for: 13 -> 15; matrix products, arithmetic and copies ran while one was open for 4% -> 5% of each run, Pallas kernels for 36% -> 35%
where the time goes in v10:
time: 428 us; the launch traced here: 424 us
  waiting for transfers between devices  167 us (39%)
  Pallas kernels  156 us (36%)
  starting transfers between devices  70.2 us (16%)
  other arithmetic  19 us (4%)
  local copies, waits for them, and re-layouts  10.8 us (3%)
    ppermute x21, waiting for transfers between devices, send(): out = lax.ppermute(value, 'ctx', pairs)  155 us
    ppermute x21, starting transfers between devices, send(): out = lax.ppermute(value, 'ctx', pairs)  44.7 us
    pallas_call x8, Pallas kernels, proj_part(): pl.pallas_call(functools.partial(proj_kernel, lead, len(extra), dim), gri...  40 us
    pallas_call x3, Pallas kernels, layer_part(): pl.pallas_call(functools.partial(layer_kernel, n, count, len(extra)), gri...  29.4 us
    pallas_call x2, Pallas kernels, attn_grad(): pl.pallas_call(functools.partial(attn_grad_kernel, m, dim, last), grid_sp...  26.9 us
    all_to_all x4, starting transfers between devices, swap(): lax.all_to_all(chunks, 'ctx', split_axis=0, concat_axis=0, tiled=True)  23.8 us
    pallas_call x1, Pallas kernels, row_backward(): pl.pallas_call(functools.partial(row_backward_kernel, dim ** (-0.5)), gri...  13.6 us
    pallas_call x1, Pallas kernels, column_backward(): pl.pallas_call(functools.partial(column_backward_kernel, dim ** (-0.5)),...  12.9 us
  transfers between devices with their start and end apart: 27, of which 15 were waited for; matrix products, arithmetic and copies ran while one was open for 5% of the time, Pallas kernels for 35%

profile of v10, /device:TPU:8, one launch (start us, length us, event | category | flops | bytes accessed | tf_op | source)
XLA Modules:
  0.0 424.0 jit_solution(15421800380478103951)
XLA Ops:
  0.6 3.5 collective-permute-start.4
  5.8 7.1 %split_inputs.1 = (bf16[8,3,4,2,64,128]{5,4,3,2,1,0:T(8,128)(2,1)}, bf16[4,1024,128]{2,1,0:T(8,128)(2,1)}, bf16[4,1024,128]{2,1,0:T(8,128)(2,1)}, bf16[4,1024,128]{2,1,0:T(8,128)(2,1)}) custom-call(bf16[1024,8,128]{2,1,0:T(8,128)(2,1)} %q_ref.1, bf16[1024,8,128]{2,1,0:T(8,128)(2,1)} %k_ref.1, bf16[1024,8,128]{2,1,0:T(8,128)(2,1)} %v_ref.1), custom_call_target="tpu_custom_call" | custom-call | tf_op jit(solution)/shard_map/split_inputs/pallas_call | solution.py:48
  12.9 14.9 %collective-permute-done.4 = bf16[1024,512]{1,0:T(8,128)(2,1)} collective-permute-done((bf16[1024,512]{1,0:T(8,128)(2,1)}, bf16[1024,512]{1,0:T(8,128)(2,1)}, u32[]{:S(2)}, u32[]{:S(2)}) %collective-permute-start.4) | collective-permute-done | bytes 1048608 | tf_op jit(solution)/shard_map/ppermute | solution.py:485
  29.0 3.2 collective-permute-start.5
  32.2 3.1 collective-permute-start.3
  36.9 9.9 %row_forward.1.flat_ref.row_ref = bf16[1024,512]{1,0:T(8,128)(2,1)} custom-call(bf16[4,1024,128]{2,1,0:T(8,128)(2,1)} %get-tuple-element.55.q_ref, bf16[4,1024,128]{2,1,0:T(8,128)(2,1)} %get-tuple-element.56.k_ref, bf16[4,1024,128]{2,1,0:T(8,128)(2,1)} %get-tuple-element.57.v_ref), custom_call_target="tpu_custom_call" | custom-call | flops 1073741824 | bytes 4194304 | tf_op jit(solution)/shard_map/row_forward/pallas_call | solution.py:321
  47.5 4.8 %proj_part.9 = bf16[2,512,512]{2,1,0:T(8,128)(2,1)} custom-call(s32[2]{0:T(128)} %pad_add_fusion.2.order, bf16[1024,512]{1,0:T(8,128)(2,1)} %row_forward.1.flat_ref.row_ref, bf16[1024,4096]{1,0:T(8,128)(2,1)} %grad_ref.18), custom_call_target="tpu_custom_call" | custom-call | flops 1073741824 | bytes 4194304 | tf_op jit(solution)/shard_map/proj_part/pallas_call | solution.py:275
  52.9 4.8 %proj_part.8 = bf16[2,512,512]{2,1,0:T(8,128)(2,1)} custom-call(s32[2]{0:T(128)} %pad_add_fusion.1.order, bf16[1024,512]{1,0:T(8,128)(2,1)} %row_forward.1.flat_ref.row_ref, bf16[1024,4096]{1,0:T(8,128)(2,1)} %grad_ref.18), custom_call_target="tpu_custom_call" | custom-call | flops 1073741824 | bytes 4194304 | tf_op jit(solution)/shard_map/proj_part/pallas_call | solution.py:275
  59.9 4.5 %all-to-all-start = ((bf16[8,3,4,2,64,128]{5,4,3,2,1,0:T(8,128)(2,1)}), bf16[8,3,4,2,64,128]{5,4,3,2,1,0:T(8,128)(2,1)S(1)}, u32[]{:S(2)}, u32[]{:S(2)}) async-start(bf16[8,3,4,2,64,128]{5,4,3,2,1,0:T(8,128)(2,1)} %get-tuple-element.61), calls=%async_computation | async-start | bytes 6291456 | tf_op jit(solution)/shard_map/all_to_all | solution.py:497
  67.2 3.5 collective-permute-start.7
  70.7 47.5 %collective-permute-done.6.refs_5_ = bf16[1024,512]{1,0:T(8,128)(2,1)} collective-permute-done((bf16[1024,512]{1,0:T(8,128)(2,1)S(1)}, bf16[1024,512]{1,0:T(8,128)(2,1)}, u32[]{:S(2)}, u32[]{:S(2)}) %collective-permute-start.6) | collective-permute-done | bytes 1048608 | tf_op jit(solution)/shard_map/ppermute | solution.py:485
  118.1 11.6 %all-to-all-done.chunk_ref = bf16[8,3,4,2,64,128]{5,4,3,2,1,0:T(8,128)(2,1)S(1)} async-done(((bf16[8,3,4,2,64,128]{5,4,3,2,1,0:T(8,128)(2,1)}), bf16[8,3,4,2,64,128]{5,4,3,2,1,0:T(8,128)(2,1)S(1)}, u32[]{:S(2)}, u32[]{:S(2)}) %all-to-all-start) | async-done | bytes 3145760 | tf_op jit(solution)/shard_map/all_to_all | solution.py:497
  129.8 8.7 %column_forward.1 = bf16[8,4,2,64,128]{4,3,2,1,0:T(8,128)(2,1)S(1)} custom-call(bf16[8,3,4,2,64,128]{5,4,3,2,1,0:T(8,128)(2,1)S(1)} %all-to-all-done.chunk_ref), custom_call_target="tpu_custom_call" | custom-call | flops 536870912 | bytes 4194304 | tf_op jit(solution)/shard_map/column_forward/pallas_call | solution.py:413
  139.4 6.8 %all-to-all-start.1 = ((bf16[8,4,2,64,128]{4,3,2,1,0:T(8,128)(2,1)}), bf16[8,4,2,64,128]{4,3,2,1,0:T(8,128)(2,1)S(1)}, u32[]{:S(2)}, u32[]{:S(2)}) async-start(bf16[8,4,2,64,128]{4,3,2,1,0:T(8,128)(2,1)} %copy-done.6), calls=%async_computation.1 | async-start | bytes 2097152 | tf_op jit(solution)/shard_map/all_to_all | solution.py:497
  149.7 16.8 %attn_grad.2.refs_2_ = f32[1024,1024]{1,0:T(8,128)} custom-call(s32[6]{0:T(128)} %stack.114.ids, bf16[1024,4096]{1,0:T(8,128)(2,1)} %grad_ref.18, bf16[1024,512]{1,0:T(8,128)(2,1)} %refs_0_.7, bf16[1024,512]{1,0:T(8,128)(2,1)} %copy-done.11, bf16[1024,512]{1,0:T(8,128)(2,1)} %copy-done.10, bf16[1024,512]{1,0:T(8,128)(2,1)} %copy-done.12, ...), custom_call_target="tpu_custom_call" | custom-call | flops 6442450944 | bytes 16777216 | tf_op jit(solution)/shard_map/attn_grad/pallas_call | solution.py:163
  166.5 15.4 %collective-permute-done.8.refs_1_.refs_7_ = bf16[1024,512]{1,0:T(8,128)(2,1)} collective-permute-done((bf16[1024,512]{1,0:T(8,128)(2,1)S(1)}, bf16[1024,512]{1,0:T(8,128)(2,1)}, u32[]{:S(2)}, u32[]{:S(2)}) %collective-permute-start.8) | collective-permute-done | bytes 1048608 | tf_op jit(solution)/shard_map/ppermute | solution.py:485
  185.5 4.8 %proj_part.12 = bf16[2,512,512]{2,1,0:T(8,128)(2,1)} custom-call(s32[2]{0:T(128)} %pad_add_fusion.1.order, bf16[1024,512]{1,0:T(8,128)(2,1)} %copy-done.3, bf16[1024,4096]{1,0:T(8,128)(2,1)} %grad_ref.18), custom_call_target="tpu_custom_call" | custom-call | flops 1073741824 | bytes 4194304 | tf_op jit(solution)/shard_map/proj_part/pallas_call | solution.py:275
  192.4 4.8 %proj_part.10 = bf16[2,512,512]{2,1,0:T(8,128)(2,1)} custom-call(s32[2]{0:T(128)} %pad_add_fusion.2.order, bf16[1024,512]{1,0:T(8,128)(2,1)} %copy-done.3, bf16[1024,4096]{1,0:T(8,128)(2,1)} %grad_ref.18), custom_call_target="tpu_custom_call" | custom-call | flops 1073741824 | bytes 4194304 | tf_op jit(solution)/shard_map/proj_part/pallas_call | solution.py:275
  197.2 11.1 %collective-permute-done.9.refs_0_ = bf16[2,512,512]{2,1,0:T(8,128)(2,1)} collective-permute-done((bf16[2,512,512]{2,1,0:T(8,128)(2,1)}, bf16[2,512,512]{2,1,0:T(8,128)(2,1)}, u32[]{:S(2)}, u32[]{:S(2)}) %collective-permute-start.9) | collective-permute-done | bytes 1048608 | tf_op jit(solution)/shard_map/ppermute | solution.py:485
  208.4 5.1 %proj_part.11 = bf16[2,512,512]{2,1,0:T(8,128)(2,1)} custom-call(s32[2]{0:T(128)} %pad_add_fusion.3.order, bf16[1024,512]{1,0:T(8,128)(2,1)} %row_forward.1.flat_ref.row_ref, bf16[1024,4096]{1,0:T(8,128)(2,1)} %grad_ref.18, bf16[2,512,512]{2,1,0:T(8,128)(2,1)} %collective-permute-done.9.refs_0_), custom_call_target="tpu_custom_call" | custom-call | flops 1073741824 | bytes 5242880 | tf_op jit(solution)/shard_map/proj_part/pallas_call | solution.py:275
  214.7 13.8 %collective-permute-done.10.refs_0_ = bf16[2,512,512]{2,1,0:T(8,128)(2,1)S(1)} collective-permute-done((bf16[2,512,512]{2,1,0:T(8,128)(2,1)}, bf16[2,512,512]{2,1,0:T(8,128)(2,1)S(1)}, u32[]{:S(2)}, u32[]{:S(2)}) %collective-permute-start.10) | collective-permute-done | bytes 1048608 | tf_op jit(solution)/shard_map/ppermute | solution.py:485
  229.5 5.0 %proj_part.13 = bf16[2,512,512]{2,1,0:T(8,128)(2,1)} custom-call(s32[2]{0:T(128)} %pad_add_fusion.3.order, bf16[1024,512]{1,0:T(8,128)(2,1)} %copy-done.3, bf16[1024,4096]{1,0:T(8,128)(2,1)} %grad_ref.18, bf16[2,512,512]{2,1,0:T(8,128)(2,1)} %copy-done.15), custom_call_target="tpu_custom_call" | custom-call | flops 1073741824 | bytes 5242880 | tf_op jit(solution)/shard_map/proj_part/pallas_call | solution.py:275
  237.7 10.1 %attn_grad.3 = (bf16[1024,512]{1,0:T(8,128)(2,1)}, bf16[8,4,2,64,128]{4,3,2,1,0:T(8,128)(2,1)}) custom-call(s32[2]{0:T(128)} %pad_add_fusion.4.ids, bf16[1024,4096]{1,0:T(8,128)(2,1)} %grad_ref.18, bf16[1024,512]{1,0:T(8,128)(2,1)} %copy-done.7, bf16[1024,512]{1,0:T(8,128)(2,1)} %collective-permute-done.8.refs_1_.refs_7_, f32[1024,1024]{1,0:T(8,128)} %attn_grad.2.refs_2_), custom_call_target="tpu_custom_call" | custom-call | flops 2147483648 | bytes 8388608 | tf_op jit(solution)/shard_map/attn_grad/pallas_call | solution.py:163
  247.8 8.5 %all-to-all-start.2 = ((bf16[8,4,2,64,128]{4,3,2,1,0:T(8,128)(2,1)}), bf16[8,4,2,64,128]{4,3,2,1,0:T(8,128)(2,1)}, u32[]{:S(2)}, u32[]{:S(2)}) async-start(bf16[8,4,2,64,128]{4,3,2,1,0:T(8,128)(2,1)} %get-tuple-element.74), calls=%async_computation.2 | async-start | bytes 2097152 | tf_op jit(solution)/shard_map/all_to_all | solution.py:497
  256.3 11.8 %layer_part.3 = bf16[1024,2048]{1,0:T(8,128)(2,1)} custom-call(s32[8]{0:T(128)} %stack.107.ids, s32[4]{0:T(128)} %pad_add_fusion.5.wanted, bf16[1024,1024]{1,0:T(8,128)(2,1)} %copy-done.5, bf16[1024,512]{1,0:T(8,128)(2,1)} %refs_0_.7, bf16[1024,512]{1,0:T(8,128)(2,1)} %copy-done.11, bf16[1024,512]{1,0:T(8,128)(2,1)} %copy-done.10, ...), custom_call_target="tpu_custom_call" | custom-call | flops 4294967296 | bytes 10485760 | tf_op jit(solution)/shard_map/layer_part/pallas_call | solution.py:221
  271.0 3.6 collective-permute-start.14
  275.2 2.5 add_convert_fusion
  277.8 2.5 collective-permute-start.16
  280.2 12.9 %column_backward.1 = bf16[8,3,4,2,64,128]{5,4,3,2,1,0:T(8,128)(2,1)S(1)} custom-call(bf16[8,3,4,2,64,128]{5,4,3,2,1,0:T(8,128)(2,1)S(1)} %copy-done.2, bf16[8,4,2,64,128]{4,3,2,1,0:T(8,128)(2,1)} %all-to-all-done.2.grad_ref), custom_call_target="tpu_custom_call" | custom-call | flops 1342177280 | bytes 7340032 | tf_op jit(solution)/shard_map/column_backward/pallas_call | solution.py:451
  294.8 2.2 collective-permute-done.17.refs_0_
  297.0 5.4 %collective-permute-done.14 = bf16[2,512,512]{2,1,0:T(8,128)(2,1)} collective-permute-done((bf16[2,512,512]{2,1,0:T(8,128)(2,1)}, bf16[2,512,512]{2,1,0:T(8,128)(2,1)}, u32[]{:S(2)}, u32[]{:S(2)}) %collective-permute-start.14) | collective-permute-done | bytes 1048608 | tf_op jit(solution)/shard_map/ppermute | solution.py:485
  302.4 16.6 %collective-permute-done.18.refs_0_ = bf16[2,512,512]{2,1,0:T(8,128)(2,1)} collective-permute-done((bf16[2,512,512]{2,1,0:T(8,128)(2,1)}, bf16[2,512,512]{2,1,0:T(8,128)(2,1)}, u32[]{:S(2)}, u32[]{:S(2)}) %collective-permute-start.18) | collective-permute-done | bytes 1048608 | tf_op jit(solution)/shard_map/ppermute | solution.py:485
  319.0 5.8 %collective-permute-done.16 = bf16[2,512,512]{2,1,0:T(8,128)(2,1)} collective-permute-done((bf16[2,512,512]{2,1,0:T(8,128)(2,1)}, bf16[2,512,512]{2,1,0:T(8,128)(2,1)}, u32[]{:S(2)}, u32[]{:S(2)}) %collective-permute-start.16) | collective-permute-done | bytes 1048608 | tf_op jit(solution)/shard_map/ppermute | solution.py:485
  324.8 4.1 all-to-all-start.3
  329.5 8.5 %layer_part.4 = bf16[1024,1024]{1,0:T(8,128)(2,1)} custom-call(s32[8]{0:T(128)} %stack.107.ids, s32[2]{0:T(128)} %pad_add_fusion.6.wanted, bf16[1024,1024]{1,0:T(8,128)(2,1)} %copy-done.5, bf16[1024,512]{1,0:T(8,128)(2,1)} %refs_0_.7, bf16[1024,512]{1,0:T(8,128)(2,1)} %copy-done.11, bf16[1024,512]{1,0:T(8,128)(2,1)} %copy-done.10, ...), custom_call_target="tpu_custom_call" | custom-call | flops 2147483648 | bytes 6291456 | tf_op jit(solution)/shard_map/layer_part/pallas_call | solution.py:221
  340.7 5.3 %proj_part.14 = (bf16[1,512,512]{2,1,0:T(8,128)(2,1)}, bf16[1,512,512]{2,1,0:T(8,128)(2,1)}) custom-call(s32[2]{0:T(128)} %pad_add_fusion.7.order, bf16[1024,512]{1,0:T(8,128)(2,1)} %row_forward.1.flat_ref.row_ref, bf16[1024,4096]{1,0:T(8,128)(2,1)} %grad_ref.18, bf16[2,512,512]{2,1,0:T(8,128)(2,1)} %collective-permute-done.17.refs_0_), custom_call_target="tpu_custom_call" | custom-call | flops 1073741824 | bytes 5242880 | tf_op jit(solution)/shard_map/proj_part/pallas_call | solution.py:275
  346.0 2.1 fusion.5
  348.1 2.7 collective-permute-start.19
  352.1 5.3 %proj_part.15 = (bf16[1,512,512]{2,1,0:T(8,128)(2,1)}, bf16[1,512,512]{2,1,0:T(8,128)(2,1)}) custom-call(s32[2]{0:T(128)} %pad_add_fusion.7.order, bf16[1024,512]{1,0:T(8,128)(2,1)} %copy-done.3, bf16[1024,4096]{1,0:T(8,128)(2,1)} %grad_ref.18, bf16[2,512,512]{2,1,0:T(8,128)(2,1)} %collective-permute-done.18.refs_0_), custom_call_target="tpu_custom_call" | custom-call | flops 1073741824 | bytes 5242880 | tf_op jit(solution)/shard_map/proj_part/pallas_call | solution.py:275
  358.6 2.2 fusion.4
  360.8 7.0 %collective-permute-start.20 = (bf16[512,512]{1,0:T(8,128)(2,1)}, bf16[512,512]{1,0:T(8,128)(2,1)}, u32[]{:S(2)}, u32[]{:S(2)}) collective-permute-start(bf16[512,512]{1,0:T(8,128)(2,1)} %fusion.4), channel_id=1, source_target_pairs={{8,0},{12,4},{16,24},{20,28},{9,1},{13,5},{17,25},{21,29},{10,2},{... | collective-permute-start | bytes 1572872 | tf_op jit(solution)/shard_map/ppermute | solution.py:485
  367.8 13.6 %row_backward.1 = (bf16[4,1024,128]{2,1,0:T(8,128)(2,1)}, bf16[4,1024,128]{2,1,0:T(8,128)(2,1)}, bf16[4,1024,128]{2,1,0:T(8,128)(2,1)}) custom-call(bf16[4,1024,128]{2,1,0:T(8,128)(2,1)} %get-tuple-element.55.q_ref, bf16[4,1024,128]{2,1,0:T(8,128)(2,1)} %get-tuple-element.56.k_ref, bf16[4,1024,128]{2,1,0:T(8,128)(2,1)} %get-tuple-element.57.v_ref, ...), custom_call_target="tpu_custom_call" | custom-call | flops 2684354560 | bytes 7340032 | tf_op jit(solution)/shard_map/row_backward/pallas_call | solution.py:355
  381.4 12.0 %collective-permute-done.21 = bf16[512,512]{1,0:T(8,128)(2,1)} collective-permute-done((bf16[512,512]{1,0:T(8,128)(2,1)}, bf16[512,512]{1,0:T(8,128)(2,1)}, u32[]{:S(2)}, u32[]{:S(2)}) %collective-permute-start.21) | collective-permute-done | bytes 524320 | tf_op jit(solution)/shard_map/ppermute | solution.py:485
  393.5 1.6 fusion.3
  395.1 7.9 %collective-permute-done.22 = bf16[512,512]{1,0:T(8,128)(2,1)} collective-permute-done((bf16[512,512]{1,0:T(8,128)(2,1)}, bf16[512,512]{1,0:T(8,128)(2,1)}, u32[]{:S(2)}, u32[]{:S(2)}) %collective-permute-start.22) | collective-permute-done | bytes 524320 | tf_op jit(solution)/shard_map/ppermute | solution.py:485
  403.0 1.6 fusion.1
  405.8 9.2 %layer_part.5 = bf16[1024,1024]{1,0:T(8,128)(2,1)} custom-call(s32[8]{0:T(128)} %stack.107.ids, s32[2]{0:T(128)} %pad_add_fusion.wanted, bf16[1024,1024]{1,0:T(8,128)(2,1)} %copy-done.5, bf16[1024,512]{1,0:T(8,128)(2,1)} %refs_0_.7, bf16[1024,512]{1,0:T(8,128)(2,1)} %copy-done.11, bf16[1024,512]{1,0:T(8,128)(2,1)} %copy-done.10, ...), custom_call_target="tpu_custom_call" | custom-call | flops 2147483648 | bytes 6291456 | tf_op jit(solution)/shard_map/layer_part/pallas_call | solution.py:221
  416.6 7.3 %join_gradients.1 = (bf16[1024,8,128]{2,1,0:T(8,128)(2,1)}, bf16[1024,8,128]{2,1,0:T(8,128)(2,1)}, bf16[1024,8,128]{2,1,0:T(8,128)(2,1)}) custom-call(bf16[8,3,4,2,64,128]{5,4,3,2,1,0:T(8,128)(2,1)} %copy-done.8, bf16[4,1024,128]{2,1,0:T(8,128)(2,1)} %get-tuple-element.97.refs_0_, bf16[4,1024,128]{2,1,0:T(8,128)(2,1)} %get-tuple-element.98.refs_1_, ...), custom_call_target="tpu_custom_call" | custom-call | tf_op jit(solution)/shard_map/join_gradients/pallas_call | solution.py:78
  (82 shorter events, 40.0 us)
Async XLA Ops:
  0.6 27.1 %collective-permute-start.4 = (bf16[1024,512]{1,0:T(8,128)(2,1)}, bf16[1024,512]{1,0:T(8,128)(2,1)}, u32[]{:S(2)}, u32[]{:S(2)}) collective-permute-start(bf16[1024,512]{1,0:T(8,128)(2,1)} %refs_0_.7), channel_id=1, source_target_pairs={{8,16},{12,20},{16,8},{20,12},{9,17},{13,21},{17,9},{21,13},{10,18... | collective-permute-start | bytes 3145736 | tf_op jit(solution)/shard_map/ppermute | solution.py:485
  4.1 24.9 %collective-permute-start = (bf16[1024,512]{1,0:T(8,128)(2,1)}, bf16[1024,512]{1,0:T(8,128)(2,1)S(1)}, u32[]{:S(2)}, u32[]{:S(2)}) collective-permute-start(bf16[1024,512]{1,0:T(8,128)(2,1)} %refs_0_.7), channel_id=1, source_target_pairs={{0,8},{4,12},{8,0},{12,4},{16,24},{20,28},{24,16},{28,20},{1,9},{5... | collective-permute-start | bytes 3145736 | tf_op jit(solution)/shard_map/ppermute | solution.py:485
  4.2 28.0 %collective-permute-start.1 = (bf16[1024,512]{1,0:T(8,128)(2,1)}, bf16[1024,512]{1,0:T(8,128)(2,1)S(1)}, u32[]{:S(2)}, u32[]{:S(2)}) collective-permute-start(bf16[1024,512]{1,0:T(8,128)(2,1)} %refs_0_.7), channel_id=1, source_target_pairs={{0,4},{4,0},{8,12},{12,8},{16,20},{20,16},{24,28},{28,24},{1,5},{5... | collective-permute-start | bytes 3145736 | tf_op jit(solution)/shard_map/ppermute | solution.py:485
  29.0 17.8 %copy-start.10 = (bf16[1024,512]{1,0:T(8,128)(2,1)}, bf16[1024,512]{1,0:T(8,128)(2,1)S(1)}, u32[]{:S(2)}) copy-start(bf16[1024,512]{1,0:T(8,128)(2,1)S(1)} %collective-permute-done.refs_2_) | copy-start | bytes 3145732
  29.0 28.7 %collective-permute-start.5 = (bf16[1024,512]{1,0:T(8,128)(2,1)}, bf16[1024,512]{1,0:T(8,128)(2,1)}, u32[]{:S(2)}, u32[]{:S(2)}) collective-permute-start(bf16[1024,512]{1,0:T(8,128)(2,1)} %collective-permute-done.4), channel_id=1, source_target_pairs={{8,0},{12,4},{16,24},{20,28},{9,1},{13,5},{17,25},{21,29},{10,2},{... | collective-permute-start | bytes 3145736 | tf_op jit(solution)/shard_map/ppermute | solution.py:485
  32.2 14.6 %copy-start.11 = (bf16[1024,512]{1,0:T(8,128)(2,1)}, bf16[1024,512]{1,0:T(8,128)(2,1)S(1)}, u32[]{:S(2)}) copy-start(bf16[1024,512]{1,0:T(8,128)(2,1)S(1)} %collective-permute-done.1.refs_1_) | copy-start | bytes 3145732
  32.2 25.7 %collective-permute-start.3 = (bf16[1024,512]{1,0:T(8,128)(2,1)S(1)}, bf16[1024,512]{1,0:T(8,128)(2,1)}, u32[]{:S(2)}, u32[]{:S(2)}) collective-permute-start(bf16[1024,512]{1,0:T(8,128)(2,1)S(1)} %collective-permute-done.refs_2_), channel_id=1, source_target_pairs={{8,16},{12,20},{16,8},{20,12},{9,17},{13,21},{17,9},{21,13},{10,18... | collective-permute-start | bytes 3145736 | tf_op jit(solution)/shard_map/ppermute | solution.py:485
  35.4 23.5 %collective-permute-start.2 = (bf16[1024,512]{1,0:T(8,128)(2,1)S(1)}, bf16[1024,512]{1,0:T(8,128)(2,1)S(1)}, u32[]{:S(2)}, u32[]{:S(2)}) collective-permute-start(bf16[1024,512]{1,0:T(8,128)(2,1)S(1)} %collective-permute-done.refs_2_), channel_id=1, source_target_pairs={{0,4},{4,0},{8,12},{12,8},{16,20},{20,16},{24,28},{28,24},{1,5},{5... | collective-permute-start | bytes 3145736 | tf_op jit(solution)/shard_map/ppermute | solution.py:485
  58.9 1.0 copy-start.12
  59.9 69.9 %all-to-all-start = ((bf16[8,3,4,2,64,128]{5,4,3,2,1,0:T(8,128)(2,1)}), bf16[8,3,4,2,64,128]{5,4,3,2,1,0:T(8,128)(2,1)S(1)}, u32[]{:S(2)}, u32[]{:S(2)}) async-start(bf16[8,3,4,2,64,128]{5,4,3,2,1,0:T(8,128)(2,1)} %get-tuple-element.61), calls=%async_computation | async-start | bytes 6291456 | tf_op jit(solution)/shard_map/all_to_all | solution.py:497
  65.7 5.0 %copy-start.9 = (bf16[1024,512]{1,0:T(8,128)(2,1)}, bf16[1024,512]{1,0:T(8,128)(2,1)S(1)}, u32[]{:S(2)}) copy-start(bf16[1024,512]{1,0:T(8,128)(2,1)S(1)} %broadcast_select_fusion.1.refs_4_) | copy-start | bytes 3145732
  65.7 52.5 %collective-permute-start.6 = (bf16[1024,512]{1,0:T(8,128)(2,1)S(1)}, bf16[1024,512]{1,0:T(8,128)(2,1)}, u32[]{:S(2)}, u32[]{:S(2)}) collective-permute-start(bf16[1024,512]{1,0:T(8,128)(2,1)S(1)} %broadcast_select_fusion.1.refs_4_), channel_id=1, source_target_pairs={{0,4},{4,0},{8,12},{12,8},{16,20},{20,16},{24,28},{28,24},{1,5},{5... | collective-permute-start | bytes 3145736 | tf_op jit(solution)/shard_map/ppermute | solution.py:485
  67.2 79.0 %collective-permute-start.7 = (bf16[1024,512]{1,0:T(8,128)(2,1)}, bf16[1024,512]{1,0:T(8,128)(2,1)}, u32[]{:S(2)}, u32[]{:S(2)}) collective-permute-start(bf16[1024,512]{1,0:T(8,128)(2,1)} %collective-permute-done.3), channel_id=1, source_target_pairs={{8,0},{12,4},{16,24},{20,28},{9,1},{13,5},{17,25},{21,29},{10,2},{... | collective-permute-start | bytes 3145736 | tf_op jit(solution)/shard_map/ppermute | solution.py:485
  129.8 8.7 %copy-start.1 = (bf16[8,3,4,2,64,128]{5,4,3,2,1,0:T(8,128)(2,1)}, bf16[8,3,4,2,64,128]{5,4,3,2,1,0:T(8,128)(2,1)S(1)}, u32[]{:S(2)}) copy-start(bf16[8,3,4,2,64,128]{5,4,3,2,1,0:T(8,128)(2,1)S(1)} %all-to-all-done.chunk_ref) | copy-start | bytes 9437188
  138.4 1.0 copy-start.6
  139.4 43.1 %all-to-all-start.1 = ((bf16[8,4,2,64,128]{4,3,2,1,0:T(8,128)(2,1)}), bf16[8,4,2,64,128]{4,3,2,1,0:T(8,128)(2,1)S(1)}, u32[]{:S(2)}, u32[]{:S(2)}) async-start(bf16[8,4,2,64,128]{4,3,2,1,0:T(8,128)(2,1)} %copy-done.6), calls=%async_computation.1 | async-start | bytes 2097152 | tf_op jit(solution)/shard_map/all_to_all | solution.py:497
  147.6 18.9 %copy-start.7 = (bf16[1024,512]{1,0:T(8,128)(2,1)}, bf16[1024,512]{1,0:T(8,128)(2,1)S(1)}, u32[]{:S(2)}) copy-start(bf16[1024,512]{1,0:T(8,128)(2,1)S(1)} %broadcast_select_fusion.refs_0_.refs_6_) | copy-start | bytes 3145732
  147.6 34.4 %collective-permute-start.8 = (bf16[1024,512]{1,0:T(8,128)(2,1)S(1)}, bf16[1024,512]{1,0:T(8,128)(2,1)}, u32[]{:S(2)}, u32[]{:S(2)}) collective-permute-start(bf16[1024,512]{1,0:T(8,128)(2,1)S(1)} %broadcast_select_fusion.refs_0_.refs_6_), channel_id=1, source_target_pairs={{0,4},{4,0},{8,12},{12,8},{16,20},{20,16},{24,28},{28,24},{1,5},{5... | collective-permute-start | bytes 3145736 | tf_op jit(solution)/shard_map/ppermute | solution.py:485
  149.7 32.8 %copy-start = (bf16[1024,512]{1,0:T(8,128)(2,1)S(1)}, bf16[1024,512]{1,0:T(8,128)(2,1)}, u32[]{:S(2)}) copy-start(bf16[1024,512]{1,0:T(8,128)(2,1)} %row_forward.1.flat_ref.row_ref) | copy-start | bytes 3145732
  182.0 26.4 %collective-permute-start.9 = (bf16[2,512,512]{2,1,0:T(8,128)(2,1)}, bf16[2,512,512]{2,1,0:T(8,128)(2,1)}, u32[]{:S(2)}, u32[]{:S(2)}) collective-permute-start(bf16[2,512,512]{2,1,0:T(8,128)(2,1)} %proj_part.8), channel_id=1, source_target_pairs={{0,4},{4,0},{8,12},{12,8},{16,20},{20,16},{24,28},{28,24},{1,5},{5... | collective-permute-start | bytes 3145736 | tf_op jit(solution)/shard_map/ppermute | solution.py:485
  183.2 1.0 copy-start.3
  184.2 1.3 copy-start.5
  190.3 38.2 %collective-permute-start.10 = (bf16[2,512,512]{2,1,0:T(8,128)(2,1)}, bf16[2,512,512]{2,1,0:T(8,128)(2,1)S(1)}, u32[]{:S(2)}, u32[]{:S(2)}) collective-permute-start(bf16[2,512,512]{2,1,0:T(8,128)(2,1)} %proj_part.12), channel_id=1, source_target_pairs={{0,4},{4,0},{8,12},{12,8},{16,20},{20,16},{24,28},{28,24},{1,5},{5... | collective-permute-start | bytes 3145736 | tf_op jit(solution)/shard_map/ppermute | solution.py:485
  213.5 56.3 %collective-permute-start.11 = (bf16[2,512,512]{2,1,0:T(8,128)(2,1)}, bf16[2,512,512]{2,1,0:T(8,128)(2,1)S(1)}, u32[]{:S(2)}, u32[]{:S(2)}) collective-permute-start(bf16[2,512,512]{2,1,0:T(8,128)(2,1)} %proj_part.11), channel_id=1, source_target_pairs={{0,8},{4,12},{24,16},{28,20},{1,9},{5,13},{25,17},{29,21},{2,10},{... | collective-permute-start | bytes 3145736 | tf_op jit(solution)/shard_map/ppermute | solution.py:485
  228.5 1.0 copy-start.15
  234.5 40.8 %collective-permute-start.15 = (bf16[2,512,512]{2,1,0:T(8,128)(2,1)}, bf16[2,512,512]{2,1,0:T(8,128)(2,1)}, u32[]{:S(2)}, u32[]{:S(2)}) collective-permute-start(bf16[2,512,512]{2,1,0:T(8,128)(2,1)} %proj_part.13), channel_id=1, source_target_pairs={{0,8},{4,12},{24,16},{28,20},{1,9},{5,13},{25,17},{29,21},{2,10},{... | collective-permute-start | bytes 3145736 | tf_op jit(solution)/shard_map/ppermute | solution.py:485
  247.8 32.4 %all-to-all-start.2 = ((bf16[8,4,2,64,128]{4,3,2,1,0:T(8,128)(2,1)}), bf16[8,4,2,64,128]{4,3,2,1,0:T(8,128)(2,1)}, u32[]{:S(2)}, u32[]{:S(2)}) async-start(bf16[8,4,2,64,128]{4,3,2,1,0:T(8,128)(2,1)} %get-tuple-element.74), calls=%async_computation.2 | async-start | bytes 2097152 | tf_op jit(solution)/shard_map/all_to_all | solution.py:497
  256.3 13.4 %copy-start.14 = (bf16[2,512,512]{2,1,0:T(8,128)(2,1)S(1)}, bf16[2,512,512]{2,1,0:T(8,128)(2,1)}, u32[]{:S(2)}) copy-start(bf16[2,512,512]{2,1,0:T(8,128)(2,1)} %proj_part.11) | copy-start | bytes 3145732
  268.1 7.1 %copy-start.13 = (bf16[2,512,512]{2,1,0:T(8,128)(2,1)S(1)}, bf16[2,512,512]{2,1,0:T(8,128)(2,1)}, u32[]{:S(2)}) copy-start(bf16[2,512,512]{2,1,0:T(8,128)(2,1)} %proj_part.13) | copy-start | bytes 3145732
  268.1 61.4 %collective-permute-start.12 = (bf16[1024,2048]{1,0:T(8,128)(2,1)}, bf16[1024,2048]{1,0:T(8,128)(2,1)}, u32[]{:S(2)}, u32[]{:S(2)}) collective-permute-start(bf16[1024,2048]{1,0:T(8,128)(2,1)} %layer_part.3), channel_id=1, source_target_pairs={{0,1},{1,0},{2,3},{3,2},{4,5},{5,4},{6,7},{7,6},{8,9},{9,8},{10,11... | collective-permute-start | bytes 12582920 | tf_op jit(solution)/shard_map/ppermute | solution.py:513
  268.2 28.8 %collective-permute-start.17 = (bf16[2,512,512]{2,1,0:T(8,128)(2,1)}, bf16[2,512,512]{2,1,0:T(8,128)(2,1)}, u32[]{:S(2)}, u32[]{:S(2)}) collective-permute-start(bf16[2,512,512]{2,1,0:T(8,128)(2,1)} %proj_part.9), channel_id=1, source_target_pairs={{0,4},{4,0},{8,12},{12,8},{16,20},{20,16},{24,28},{28,24},{1,5},{5... | collective-permute-start | bytes 3145736 | tf_op jit(solution)/shard_map/ppermute | solution.py:485
  271.0 9.3 %copy-start.2 = (bf16[8,3,4,2,64,128]{5,4,3,2,1,0:T(8,128)(2,1)S(1)}, bf16[8,3,4,2,64,128]{5,4,3,2,1,0:T(8,128)(2,1)}, u32[]{:S(2)}) copy-start(bf16[8,3,4,2,64,128]{5,4,3,2,1,0:T(8,128)(2,1)} %copy-done.1) | copy-start | bytes 9437188
  271.0 31.4 %collective-permute-start.14 = (bf16[2,512,512]{2,1,0:T(8,128)(2,1)}, bf16[2,512,512]{2,1,0:T(8,128)(2,1)}, u32[]{:S(2)}, u32[]{:S(2)}) collective-permute-start(bf16[2,512,512]{2,1,0:T(8,128)(2,1)} %add_convert_fusion.1), channel_id=1, source_target_pairs={{8,16},{12,20},{16,8},{20,12},{9,17},{13,21},{17,9},{21,13},{10,18... | collective-permute-start | bytes 3145736 | tf_op jit(solution)/shard_map/ppermute | solution.py:485
  274.6 44.4 %collective-permute-start.18 = (bf16[2,512,512]{2,1,0:T(8,128)(2,1)}, bf16[2,512,512]{2,1,0:T(8,128)(2,1)}, u32[]{:S(2)}, u32[]{:S(2)}) collective-permute-start(bf16[2,512,512]{2,1,0:T(8,128)(2,1)} %proj_part.10), channel_id=1, source_target_pairs={{0,4},{4,0},{8,12},{12,8},{16,20},{20,16},{24,28},{28,24},{1,5},{5... | collective-permute-start | bytes 3145736 | tf_op jit(solution)/shard_map/ppermute | solution.py:485
  277.8 47.1 %collective-permute-start.16 = (bf16[2,512,512]{2,1,0:T(8,128)(2,1)}, bf16[2,512,512]{2,1,0:T(8,128)(2,1)}, u32[]{:S(2)}, u32[]{:S(2)}) collective-permute-start(bf16[2,512,512]{2,1,0:T(8,128)(2,1)} %add_convert_fusion), channel_id=1, source_target_pairs={{8,16},{12,20},{16,8},{20,12},{9,17},{13,21},{17,9},{21,13},{10,18... | collective-permute-start | bytes 3145736 | tf_op jit(solution)/shard_map/ppermute | solution.py:485
  293.1 1.6 copy-start.4
  324.8 90.2 %all-to-all-start.3 = ((bf16[8,3,4,2,64,128]{5,4,3,2,1,0:T(8,128)(2,1)}), bf16[8,3,4,2,64,128]{5,4,3,2,1,0:T(8,128)(2,1)S(1)}, u32[]{:S(2)}, u32[]{:S(2)}) async-start(bf16[8,3,4,2,64,128]{5,4,3,2,1,0:T(8,128)(2,1)} %copy-done.4), calls=%async_computation.3 | async-start | bytes 6291456 | tf_op jit(solution)/shard_map/all_to_all | solution.py:497
  338.0 67.8 %collective-permute-start.13 = (bf16[1024,1024]{1,0:T(8,128)(2,1)}, bf16[1024,1024]{1,0:T(8,128)(2,1)}, u32[]{:S(2)}, u32[]{:S(2)}) collective-permute-start(bf16[1024,1024]{1,0:T(8,128)(2,1)} %layer_part.4), channel_id=1, source_target_pairs={{0,2},{1,3},{2,0},{3,1},{4,6},{5,7},{6,4},{7,5},{8,10},{9,11},{10,... | collective-permute-start | bytes 6291464 | tf_op jit(solution)/shard_map/ppermute | solution.py:513
  348.1 33.3 %collective-permute-start.19 = (bf16[512,512]{1,0:T(8,128)(2,1)}, bf16[512,512]{1,0:T(8,128)(2,1)}, u32[]{:S(2)}, u32[]{:S(2)}) collective-permute-start(bf16[512,512]{1,0:T(8,128)(2,1)} %fusion.5), channel_id=1, source_target_pairs={{8,0},{12,4},{16,24},{20,28},{9,1},{13,5},{17,25},{21,29},{10,2},{... | collective-permute-start | bytes 1572872 | tf_op jit(solution)/shard_map/ppermute | solution.py:485
  350.8 42.7 %collective-permute-start.21 = (bf16[512,512]{1,0:T(8,128)(2,1)}, bf16[512,512]{1,0:T(8,128)(2,1)}, u32[]{:S(2)}, u32[]{:S(2)}) collective-permute-start(bf16[512,512]{1,0:T(8,128)(2,1)} %bitcast.52), channel_id=1, source_target_pairs={{0,8},{4,12},{24,16},{28,20},{1,9},{5,13},{25,17},{29,21},{2,10},{... | collective-permute-start | bytes 1572872 | tf_op jit(solution)/shard_map/ppermute | solution.py:485
  357.4 45.6 %collective-permute-start.22 = (bf16[512,512]{1,0:T(8,128)(2,1)}, bf16[512,512]{1,0:T(8,128)(2,1)}, u32[]{:S(2)}, u32[]{:S(2)}) collective-permute-start(bf16[512,512]{1,0:T(8,128)(2,1)} %bitcast.53), channel_id=1, source_target_pairs={{0,8},{4,12},{24,16},{28,20},{1,9},{5,13},{25,17},{29,21},{2,10},{... | collective-permute-start | bytes 1572872 | tf_op jit(solution)/shard_map/ppermute | solution.py:485
  360.8 32.7 %copy-start.16 = (bf16[1,512,512]{2,1,0:T(8,128)(2,1)S(1)}, bf16[1,512,512]{2,1,0:T(8,128)(2,1)}, u32[]{:S(2)}) copy-start(bf16[1,512,512]{2,1,0:T(8,128)(2,1)} %get-tuple-element.103) | copy-start | bytes 1572868
  360.8 42.2 %collective-permute-start.20 = (bf16[512,512]{1,0:T(8,128)(2,1)}, bf16[512,512]{1,0:T(8,128)(2,1)}, u32[]{:S(2)}, u32[]{:S(2)}) collective-permute-start(bf16[512,512]{1,0:T(8,128)(2,1)} %fusion.4), channel_id=1, source_target_pairs={{8,0},{12,4},{16,24},{20,28},{9,1},{13,5},{17,25},{21,29},{10,2},{... | collective-permute-start | bytes 1572872 | tf_op jit(solution)/shard_map/ppermute | solution.py:485
  381.4 21.5 %copy-start.17 = (bf16[1,512,512]{2,1,0:T(8,128)(2,1)S(1)}, bf16[1,512,512]{2,1,0:T(8,128)(2,1)}, u32[]{:S(2)}) copy-start(bf16[1,512,512]{2,1,0:T(8,128)(2,1)} %get-tuple-element.104) | copy-start | bytes 1572868
  415.0 1.6 copy-start.8

commit v11 on v10

--- a/solution.py
+++ b/solution.py
@@ -578,20 +578,20 @@
     so_far = attn_grad(ids[:early], after(out_grad, outs), blocks[:early], None, dim)
     grad_row, grads = attn_grad(ids[early:], out_grad, blocks[early:], so_far, dim)
     row_far = exchanged([after(part, so_far, *far_near_blocks) for part in row_far])
-    column_out, flat = collect(row_out, column_part)
+    column_out, flat = collect(row_out, after(column_part, grads))
     column_far, column_close = leaving(column_out, far), leaving(column_out, close)
     grads = swap(after(grads, column_part, *row_far, *column_far, *column_close))
     column_far = exchanged(column_far)
     (row_far,) = summed(after(row_out, *column_close), far, row_far, 0)
     row_far_in = links.along(row_far, INWARD)
-    layer = LayerSum(ids, after(flat, row_far), blocks, heads_n)
-    layer.start()
     row_close = exchanged([after(part, *column_far) for part in row_close])
     (column_far,) = summed(column_out, far, column_far, 0)
     column_far_in = links.along(column_far, INWARD)
     row_middle = add(row_far, row_far_in)
     row_cross = links.along(row_middle, CROSS)
-    gradients = column_backward(chunks, after(grads, column_far, row_middle, layer.first))
+    gradients = column_backward(chunks, after(grads, column_far, row_middle))
+    layer = LayerSum(ids, after(flat, gradients), blocks, heads_n)
+    layer.start()
     column_close = exchanged(column_close)
     column_cross = links.along(add(column_far, column_far_in), CROSS)
     column_grads = swap(after(gradients, row_cross, column_cross, *row_close, *column_close))

time: 428 us -> 414 us (0.967)
  waiting for transfers between devices: 167 us -> 155 us
    all_to_all x4, waiting for transfers between devices: 11.6 us -> 0.01 us  [swap(): lax.all_to_all(chunks, 'ctx', split_axis=0, concat_axis=0, tiled=True)]
    all_to_all x4, starting transfers between devices: 23.8 us -> 19.5 us  [swap(): lax.all_to_all(chunks, 'ctx', split_axis=0, concat_axis=0, tiled=True)]
  transfers between devices with their start and end apart: 27 -> 27, of which waited for: 15 -> 11; matrix products, arithmetic and copies ran while one was open for 5% -> 6% of each run, Pallas kernels for 35% -> 37%
where the time goes in v11:
time: 414 us; the launch traced here: 410 us
  Pallas kernels  158 us (38%)
  waiting for transfers between devices  155 us (37%)
  starting transfers between devices  66.6 us (16%)
  other arithmetic  20.4 us (5%)
  local copies, waits for them, and re-layouts  9.23 us (2%)
    ppermute x21, waiting for transfers between devices, send(): out = lax.ppermute(value, 'ctx', pairs)  155 us
    ppermute x21, starting transfers between devices, send(): out = lax.ppermute(value, 'ctx', pairs)  45.4 us
    pallas_call x8, Pallas kernels, proj_part(): pl.pallas_call(functools.partial(proj_kernel, lead, len(extra), dim), gri...  40 us
    pallas_call x3, Pallas kernels, layer_part(): pl.pallas_call(functools.partial(layer_kernel, n, count, len(extra)), gri...  29.4 us
    pallas_call x2, Pallas kernels, attn_grad(): pl.pallas_call(functools.partial(attn_grad_kernel, m, dim, last), grid_sp...  26.9 us
    all_to_all x4, starting transfers between devices, swap(): lax.all_to_all(chunks, 'ctx', split_axis=0, concat_axis=0, tiled=True)  19.5 us
    pallas_call x1, Pallas kernels, column_backward(): pl.pallas_call(functools.partial(column_backward_kernel, dim ** (-0.5)),...  14.5 us
    pallas_call x1, Pallas kernels, row_backward(): pl.pallas_call(functools.partial(row_backward_kernel, dim ** (-0.5)), gri...  13.6 us
  transfers between devices with their start and end apart: 27, of which 11 were waited for; matrix products, arithmetic and copies ran while one was open for 6% of the time, Pallas kernels for 37%

profile of v11, /device:TPU:8, one launch (start us, length us, event | category | flops | bytes accessed | tf_op | source)
XLA Modules:
  0.0 410.2 jit_solution(11736763183014486166)
XLA Ops:
  0.6 3.5 collective-permute-start.4
  4.2 1.6 collective-permute-start.1
  5.8 7.1 %split_inputs.1 = (bf16[8,3,4,2,64,128]{5,4,3,2,1,0:T(8,128)(2,1)}, bf16[4,1024,128]{2,1,0:T(8,128)(2,1)}, bf16[4,1024,128]{2,1,0:T(8,128)(2,1)}, bf16[4,1024,128]{2,1,0:T(8,128)(2,1)}) custom-call(bf16[1024,8,128]{2,1,0:T(8,128)(2,1)} %q_ref.1, bf16[1024,8,128]{2,1,0:T(8,128)(2,1)} %k_ref.1, bf16[1024,8,128]{2,1,0:T(8,128)(2,1)} %v_ref.1), custom_call_target="tpu_custom_call" | custom-call | tf_op jit(solution)/shard_map/split_inputs/pallas_call | solution.py:48
  12.9 14.9 %collective-permute-done.4 = bf16[1024,512]{1,0:T(8,128)(2,1)} collective-permute-done((bf16[1024,512]{1,0:T(8,128)(2,1)}, bf16[1024,512]{1,0:T(8,128)(2,1)}, u32[]{:S(2)}, u32[]{:S(2)}) %collective-permute-start.4) | collective-permute-done | bytes 1048608 | tf_op jit(solution)/shard_map/ppermute | solution.py:485
  29.0 3.2 collective-permute-start.5
  32.2 3.1 collective-permute-start.3
  35.4 1.6 collective-permute-start.2
  36.9 9.9 %row_forward.1.flat_ref.row_ref = bf16[1024,512]{1,0:T(8,128)(2,1)} custom-call(bf16[4,1024,128]{2,1,0:T(8,128)(2,1)} %get-tuple-element.56.q_ref, bf16[4,1024,128]{2,1,0:T(8,128)(2,1)} %get-tuple-element.57.k_ref, bf16[4,1024,128]{2,1,0:T(8,128)(2,1)} %get-tuple-element.58.v_ref), custom_call_target="tpu_custom_call" | custom-call | flops 1073741824 | bytes 4194304 | tf_op jit(solution)/shard_map/row_forward/pallas_call | solution.py:321
  47.4 4.8 %proj_part.9 = bf16[2,512,512]{2,1,0:T(8,128)(2,1)} custom-call(s32[2]{0:T(128)} %pad_add_fusion.2.order, bf16[1024,512]{1,0:T(8,128)(2,1)} %row_forward.1.flat_ref.row_ref, bf16[1024,4096]{1,0:T(8,128)(2,1)} %grad_ref.18), custom_call_target="tpu_custom_call" | custom-call | flops 1073741824 | bytes 4194304 | tf_op jit(solution)/shard_map/proj_part/pallas_call | solution.py:275
  52.8 4.8 %proj_part.8 = bf16[2,512,512]{2,1,0:T(8,128)(2,1)} custom-call(s32[2]{0:T(128)} %pad_add_fusion.1.order, bf16[1024,512]{1,0:T(8,128)(2,1)} %row_forward.1.flat_ref.row_ref, bf16[1024,4096]{1,0:T(8,128)(2,1)} %grad_ref.18), custom_call_target="tpu_custom_call" | custom-call | flops 1073741824 | bytes 4194304 | tf_op jit(solution)/shard_map/proj_part/pallas_call | solution.py:275
  59.9 4.5 %all-to-all-start = ((bf16[8,3,4,2,64,128]{5,4,3,2,1,0:T(8,128)(2,1)}), bf16[8,3,4,2,64,128]{5,4,3,2,1,0:T(8,128)(2,1)S(1)}, u32[]{:S(2)}, u32[]{:S(2)}) async-start(bf16[8,3,4,2,64,128]{5,4,3,2,1,0:T(8,128)(2,1)} %get-tuple-element.62), calls=%async_computation | async-start | bytes 6291456 | tf_op jit(solution)/shard_map/all_to_all | solution.py:497
  64.3 2.9 collective-permute-start.7
  68.6 2.1 collective-permute-start.6
  70.7 64.5 %collective-permute-done.7 = bf16[1024,512]{1,0:T(8,128)(2,1)} collective-permute-done((bf16[1024,512]{1,0:T(8,128)(2,1)}, bf16[1024,512]{1,0:T(8,128)(2,1)}, u32[]{:S(2)}, u32[]{:S(2)}) %collective-permute-start.7) | collective-permute-done | bytes 1048608 | tf_op jit(solution)/shard_map/ppermute | solution.py:485
  135.2 2.3 broadcast_select_fusion.refs_0_.refs_6_
  138.9 8.7 %column_forward.1 = bf16[8,4,2,64,128]{4,3,2,1,0:T(8,128)(2,1)S(1)} custom-call(bf16[8,3,4,2,64,128]{5,4,3,2,1,0:T(8,128)(2,1)S(1)} %all-to-all-done.chunk_ref), custom_call_target="tpu_custom_call" | custom-call | flops 536870912 | bytes 4194304 | tf_op jit(solution)/shard_map/column_forward/pallas_call | solution.py:413
  148.6 6.2 %all-to-all-start.1 = ((bf16[8,4,2,64,128]{4,3,2,1,0:T(8,128)(2,1)}), bf16[8,4,2,64,128]{4,3,2,1,0:T(8,128)(2,1)S(1)}, u32[]{:S(2)}, u32[]{:S(2)}) async-start(bf16[8,4,2,64,128]{4,3,2,1,0:T(8,128)(2,1)} %copy-done.5), calls=%async_computation.1 | async-start | bytes 2097152 | tf_op jit(solution)/shard_map/all_to_all | solution.py:497
  155.3 16.6 %attn_grad.2.refs_2_ = f32[1024,1024]{1,0:T(8,128)} custom-call(s32[6]{0:T(128)} %stack.114.ids, bf16[1024,4096]{1,0:T(8,128)(2,1)} %grad_ref.18, bf16[1024,512]{1,0:T(8,128)(2,1)} %refs_0_.7, bf16[1024,512]{1,0:T(8,128)(2,1)} %copy-done.9, bf16[1024,512]{1,0:T(8,128)(2,1)} %copy-done.8, bf16[1024,512]{1,0:T(8,128)(2,1)} %copy-done.10, ...), custom_call_target="tpu_custom_call" | custom-call | flops 6442450944 | bytes 16777216 | tf_op jit(solution)/shard_map/attn_grad/pallas_call | solution.py:163
  174.1 10.2 %attn_grad.3 = (bf16[1024,512]{1,0:T(8,128)(2,1)}, bf16[8,4,2,64,128]{4,3,2,1,0:T(8,128)(2,1)}) custom-call(s32[2]{0:T(128)} %pad_add_fusion.3.ids, bf16[1024,4096]{1,0:T(8,128)(2,1)} %grad_ref.18, bf16[1024,512]{1,0:T(8,128)(2,1)} %broadcast_select_fusion.refs_0_.refs_6_, bf16[1024,512]{1,0:T(8,128)(2,1)} %collective-permute-done.8.refs_1_.refs_7_, ...), custom_call_target="tpu_custom_call" | custom-call | flops 2147483648 | bytes 8388608 | tf_op jit(solution)/shard_map/attn_grad/pallas_call | solution.py:163
  187.3 4.9 %proj_part.11 = bf16[2,512,512]{2,1,0:T(8,128)(2,1)} custom-call(s32[2]{0:T(128)} %pad_add_fusion.2.order, bf16[1024,512]{1,0:T(8,128)(2,1)} %copy-done.3, bf16[1024,4096]{1,0:T(8,128)(2,1)} %grad_ref.18), custom_call_target="tpu_custom_call" | custom-call | flops 1073741824 | bytes 4194304 | tf_op jit(solution)/shard_map/proj_part/pallas_call | solution.py:275
  192.2 4.8 %proj_part.10 = bf16[2,512,512]{2,1,0:T(8,128)(2,1)} custom-call(s32[2]{0:T(128)} %pad_add_fusion.1.order, bf16[1024,512]{1,0:T(8,128)(2,1)} %copy-done.3, bf16[1024,4096]{1,0:T(8,128)(2,1)} %grad_ref.18), custom_call_target="tpu_custom_call" | custom-call | flops 1073741824 | bytes 4194304 | tf_op jit(solution)/shard_map/proj_part/pallas_call | solution.py:275
  198.0 5.1 %all-to-all-start.2 = ((bf16[8,4,2,64,128]{4,3,2,1,0:T(8,128)(2,1)}), bf16[8,4,2,64,128]{4,3,2,1,0:T(8,128)(2,1)}, u32[]{:S(2)}, u32[]{:S(2)}) async-start(bf16[8,4,2,64,128]{4,3,2,1,0:T(8,128)(2,1)} %get-tuple-element.74), calls=%async_computation.2 | async-start | bytes 2097152 | tf_op jit(solution)/shard_map/all_to_all | solution.py:497
  205.2 5.0 %proj_part.13 = bf16[2,512,512]{2,1,0:T(8,128)(2,1)} custom-call(s32[2]{0:T(128)} %pad_add_fusion.4.order, bf16[1024,512]{1,0:T(8,128)(2,1)} %row_forward.1.flat_ref.row_ref, bf16[1024,4096]{1,0:T(8,128)(2,1)} %grad_ref.18, bf16[2,512,512]{2,1,0:T(8,128)(2,1)} %copy-done.12), custom_call_target="tpu_custom_call" | custom-call | flops 1073741824 | bytes 5242880 | tf_op jit(solution)/shard_map/proj_part/pallas_call | solution.py:275
  211.6 26.6 %collective-permute-done.10.refs_0_ = bf16[2,512,512]{2,1,0:T(8,128)(2,1)S(1)} collective-permute-done((bf16[2,512,512]{2,1,0:T(8,128)(2,1)}, bf16[2,512,512]{2,1,0:T(8,128)(2,1)S(1)}, u32[]{:S(2)}, u32[]{:S(2)}) %collective-permute-start.10) | collective-permute-done | bytes 1048608 | tf_op jit(solution)/shard_map/ppermute | solution.py:485
  239.1 5.0 %proj_part.12 = bf16[2,512,512]{2,1,0:T(8,128)(2,1)} custom-call(s32[2]{0:T(128)} %pad_add_fusion.4.order, bf16[1024,512]{1,0:T(8,128)(2,1)} %copy-done.3, bf16[1024,4096]{1,0:T(8,128)(2,1)} %grad_ref.18, bf16[2,512,512]{2,1,0:T(8,128)(2,1)} %copy-done.13), custom_call_target="tpu_custom_call" | custom-call | flops 1073741824 | bytes 5242880 | tf_op jit(solution)/shard_map/proj_part/pallas_call | solution.py:275
  247.0 2.8 add_convert_fusion.1
  249.8 3.4 collective-permute-start.14
  255.2 14.5 %column_backward.1 = bf16[8,3,4,2,64,128]{5,4,3,2,1,0:T(8,128)(2,1)} custom-call(bf16[8,3,4,2,64,128]{5,4,3,2,1,0:T(8,128)(2,1)S(1)} %copy-done.2, bf16[8,4,2,64,128]{4,3,2,1,0:T(8,128)(2,1)} %all-to-all-done.2.grad_ref), custom_call_target="tpu_custom_call" | custom-call | flops 1342177280 | bytes 7340032 | tf_op jit(solution)/shard_map/column_backward/pallas_call | solution.py:451
  269.7 11.8 %layer_part.3 = bf16[1024,2048]{1,0:T(8,128)(2,1)} custom-call(s32[8]{0:T(128)} %stack.107.ids, s32[4]{0:T(128)} %pad_add_fusion.5.wanted, bf16[1024,1024]{1,0:T(8,128)(2,1)} %copy-done.4, bf16[1024,512]{1,0:T(8,128)(2,1)} %refs_0_.7, bf16[1024,512]{1,0:T(8,128)(2,1)} %copy-done.9, bf16[1024,512]{1,0:T(8,128)(2,1)} %copy-done.8, ...), custom_call_target="tpu_custom_call" | custom-call | flops 4294967296 | bytes 10485760 | tf_op jit(solution)/shard_map/layer_part/pallas_call | solution.py:221
  283.2 2.5 collective-permute-start.16
  285.7 14.8 %collective-permute-done.18.refs_0_ = bf16[2,512,512]{2,1,0:T(8,128)(2,1)} collective-permute-done((bf16[2,512,512]{2,1,0:T(8,128)(2,1)}, bf16[2,512,512]{2,1,0:T(8,128)(2,1)}, u32[]{:S(2)}, u32[]{:S(2)}) %collective-permute-start.18) | collective-permute-done | bytes 1048608 | tf_op jit(solution)/shard_map/ppermute | solution.py:485
  300.5 10.2 %collective-permute-done.16 = bf16[2,512,512]{2,1,0:T(8,128)(2,1)} collective-permute-done((bf16[2,512,512]{2,1,0:T(8,128)(2,1)S(1)}, bf16[2,512,512]{2,1,0:T(8,128)(2,1)}, u32[]{:S(2)}, u32[]{:S(2)}) %collective-permute-start.16) | collective-permute-done | bytes 1048608 | tf_op jit(solution)/shard_map/ppermute | solution.py:485
  310.7 3.8 all-to-all-start.3
  315.1 8.5 %layer_part.4 = bf16[1024,1024]{1,0:T(8,128)(2,1)} custom-call(s32[8]{0:T(128)} %stack.107.ids, s32[2]{0:T(128)} %pad_add_fusion.6.wanted, bf16[1024,1024]{1,0:T(8,128)(2,1)} %copy-done.4, bf16[1024,512]{1,0:T(8,128)(2,1)} %refs_0_.7, bf16[1024,512]{1,0:T(8,128)(2,1)} %copy-done.9, bf16[1024,512]{1,0:T(8,128)(2,1)} %copy-done.8, ...), custom_call_target="tpu_custom_call" | custom-call | flops 2147483648 | bytes 6291456 | tf_op jit(solution)/shard_map/layer_part/pallas_call | solution.py:221
  326.4 5.3 %proj_part.14 = (bf16[1,512,512]{2,1,0:T(8,128)(2,1)}, bf16[1,512,512]{2,1,0:T(8,128)(2,1)}) custom-call(s32[2]{0:T(128)} %pad_add_fusion.7.order, bf16[1024,512]{1,0:T(8,128)(2,1)} %row_forward.1.flat_ref.row_ref, bf16[1024,4096]{1,0:T(8,128)(2,1)} %grad_ref.18, bf16[2,512,512]{2,1,0:T(8,128)(2,1)} %collective-permute-done.17.refs_0_), custom_call_target="tpu_custom_call" | custom-call | flops 1073741824 | bytes 5242880 | tf_op jit(solution)/shard_map/proj_part/pallas_call | solution.py:275
  331.7 2.1 fusion.5
  333.8 2.7 collective-permute-start.19
  337.8 5.3 %proj_part.15 = (bf16[1,512,512]{2,1,0:T(8,128)(2,1)}, bf16[1,512,512]{2,1,0:T(8,128)(2,1)}) custom-call(s32[2]{0:T(128)} %pad_add_fusion.7.order, bf16[1024,512]{1,0:T(8,128)(2,1)} %copy-done.3, bf16[1024,4096]{1,0:T(8,128)(2,1)} %grad_ref.18, bf16[2,512,512]{2,1,0:T(8,128)(2,1)} %collective-permute-done.18.refs_0_), custom_call_target="tpu_custom_call" | custom-call | flops 1073741824 | bytes 5242880 | tf_op jit(solution)/shard_map/proj_part/pallas_call | solution.py:275
  344.3 2.2 fusion.4
  346.5 7.0 %collective-permute-start.20 = (bf16[512,512]{1,0:T(8,128)(2,1)}, bf16[512,512]{1,0:T(8,128)(2,1)}, u32[]{:S(2)}, u32[]{:S(2)}) collective-permute-start(bf16[512,512]{1,0:T(8,128)(2,1)} %fusion.4), channel_id=1, source_target_pairs={{8,0},{12,4},{16,24},{20,28},{9,1},{13,5},{17,25},{21,29},{10,2},{... | collective-permute-start | bytes 1572872 | tf_op jit(solution)/shard_map/ppermute | solution.py:485
  353.5 13.6 %row_backward.1 = (bf16[4,1024,128]{2,1,0:T(8,128)(2,1)}, bf16[4,1024,128]{2,1,0:T(8,128)(2,1)}, bf16[4,1024,128]{2,1,0:T(8,128)(2,1)}) custom-call(bf16[4,1024,128]{2,1,0:T(8,128)(2,1)} %get-tuple-element.56.q_ref, bf16[4,1024,128]{2,1,0:T(8,128)(2,1)} %get-tuple-element.57.k_ref, bf16[4,1024,128]{2,1,0:T(8,128)(2,1)} %get-tuple-element.58.v_ref, ...), custom_call_target="tpu_custom_call" | custom-call | flops 2684354560 | bytes 7340032 | tf_op jit(solution)/shard_map/row_backward/pallas_call | solution.py:355
  367.1 12.1 %collective-permute-done.21 = bf16[512,512]{1,0:T(8,128)(2,1)} collective-permute-done((bf16[512,512]{1,0:T(8,128)(2,1)}, bf16[512,512]{1,0:T(8,128)(2,1)}, u32[]{:S(2)}, u32[]{:S(2)}) %collective-permute-start.21) | collective-permute-done | bytes 524320 | tf_op jit(solution)/shard_map/ppermute | solution.py:485
  379.3 1.6 fusion.3
  380.9 8.3 %collective-permute-done.22 = bf16[512,512]{1,0:T(8,128)(2,1)} collective-permute-done((bf16[512,512]{1,0:T(8,128)(2,1)}, bf16[512,512]{1,0:T(8,128)(2,1)}, u32[]{:S(2)}, u32[]{:S(2)}) %collective-permute-start.22) | collective-permute-done | bytes 524320 | tf_op jit(solution)/shard_map/ppermute | solution.py:485
  389.2 1.6 fusion.1
  392.0 9.2 %layer_part.5 = bf16[1024,1024]{1,0:T(8,128)(2,1)} custom-call(s32[8]{0:T(128)} %stack.107.ids, s32[2]{0:T(128)} %pad_add_fusion.wanted, bf16[1024,1024]{1,0:T(8,128)(2,1)} %copy-done.4, bf16[1024,512]{1,0:T(8,128)(2,1)} %refs_0_.7, bf16[1024,512]{1,0:T(8,128)(2,1)} %copy-done.9, bf16[1024,512]{1,0:T(8,128)(2,1)} %copy-done.8, bf16[1024,512]{1,0:T(8,128)(2,1)} %copy-done.10, ...), custom_call_target="tpu_custom_call" | custom-call | flops 2147483648 | bytes 6291456 | tf_op jit(solution)/shard_map/layer_part/pallas_call | solution.py:221
  401.2 1.6 copy-done.6
  402.8 7.3 %join_gradients.1 = (bf16[1024,8,128]{2,1,0:T(8,128)(2,1)}, bf16[1024,8,128]{2,1,0:T(8,128)(2,1)}, bf16[1024,8,128]{2,1,0:T(8,128)(2,1)}) custom-call(bf16[8,3,4,2,64,128]{5,4,3,2,1,0:T(8,128)(2,1)} %copy-done.6, bf16[4,1024,128]{2,1,0:T(8,128)(2,1)} %get-tuple-element.99.refs_0_, bf16[4,1024,128]{2,1,0:T(8,128)(2,1)} %get-tuple-element.100.refs_1_, ...), custom_call_target="tpu_custom_call" | custom-call | tf_op jit(solution)/shard_map/join_gradients/pallas_call | solution.py:78
  (78 shorter events, 33.1 us)
Async XLA Ops:
  0.6 27.1 %collective-permute-start.4 = (bf16[1024,512]{1,0:T(8,128)(2,1)}, bf16[1024,512]{1,0:T(8,128)(2,1)}, u32[]{:S(2)}, u32[]{:S(2)}) collective-permute-start(bf16[1024,512]{1,0:T(8,128)(2,1)} %refs_0_.7), channel_id=1, source_target_pairs={{8,16},{12,20},{16,8},{20,12},{9,17},{13,21},{17,9},{21,13},{10,18... | collective-permute-start | bytes 3145736 | tf_op jit(solution)/shard_map/ppermute | solution.py:485
  4.1 24.9 %collective-permute-start = (bf16[1024,512]{1,0:T(8,128)(2,1)}, bf16[1024,512]{1,0:T(8,128)(2,1)S(1)}, u32[]{:S(2)}, u32[]{:S(2)}) collective-permute-start(bf16[1024,512]{1,0:T(8,128)(2,1)} %refs_0_.7), channel_id=1, source_target_pairs={{0,8},{4,12},{8,0},{12,4},{16,24},{20,28},{24,16},{28,20},{1,9},{5... | collective-permute-start | bytes 3145736 | tf_op jit(solution)/shard_map/ppermute | solution.py:485
  4.2 28.0 %collective-permute-start.1 = (bf16[1024,512]{1,0:T(8,128)(2,1)}, bf16[1024,512]{1,0:T(8,128)(2,1)S(1)}, u32[]{:S(2)}, u32[]{:S(2)}) collective-permute-start(bf16[1024,512]{1,0:T(8,128)(2,1)} %refs_0_.7), channel_id=1, source_target_pairs={{0,4},{4,0},{8,12},{12,8},{16,20},{20,16},{24,28},{28,24},{1,5},{5... | collective-permute-start | bytes 3145736 | tf_op jit(solution)/shard_map/ppermute | solution.py:485
  29.0 17.8 %copy-start.8 = (bf16[1024,512]{1,0:T(8,128)(2,1)}, bf16[1024,512]{1,0:T(8,128)(2,1)S(1)}, u32[]{:S(2)}) copy-start(bf16[1024,512]{1,0:T(8,128)(2,1)S(1)} %collective-permute-done.refs_2_) | copy-start | bytes 3145732
  29.0 28.7 %collective-permute-start.5 = (bf16[1024,512]{1,0:T(8,128)(2,1)}, bf16[1024,512]{1,0:T(8,128)(2,1)}, u32[]{:S(2)}, u32[]{:S(2)}) collective-permute-start(bf16[1024,512]{1,0:T(8,128)(2,1)} %collective-permute-done.4), channel_id=1, source_target_pairs={{8,0},{12,4},{16,24},{20,28},{9,1},{13,5},{17,25},{21,29},{10,2},{... | collective-permute-start | bytes 3145736 | tf_op jit(solution)/shard_map/ppermute | solution.py:485
  32.2 14.6 %copy-start.9 = (bf16[1024,512]{1,0:T(8,128)(2,1)}, bf16[1024,512]{1,0:T(8,128)(2,1)S(1)}, u32[]{:S(2)}) copy-start(bf16[1024,512]{1,0:T(8,128)(2,1)S(1)} %collective-permute-done.1.refs_1_) | copy-start | bytes 3145732
  32.2 25.7 %collective-permute-start.3 = (bf16[1024,512]{1,0:T(8,128)(2,1)S(1)}, bf16[1024,512]{1,0:T(8,128)(2,1)}, u32[]{:S(2)}, u32[]{:S(2)}) collective-permute-start(bf16[1024,512]{1,0:T(8,128)(2,1)S(1)} %collective-permute-done.refs_2_), channel_id=1, source_target_pairs={{8,16},{12,20},{16,8},{20,12},{9,17},{13,21},{17,9},{21,13},{10,18... | collective-permute-start | bytes 3145736 | tf_op jit(solution)/shard_map/ppermute | solution.py:485
  35.4 23.5 %collective-permute-start.2 = (bf16[1024,512]{1,0:T(8,128)(2,1)S(1)}, bf16[1024,512]{1,0:T(8,128)(2,1)S(1)}, u32[]{:S(2)}, u32[]{:S(2)}) collective-permute-start(bf16[1024,512]{1,0:T(8,128)(2,1)S(1)} %collective-permute-done.refs_2_), channel_id=1, source_target_pairs={{0,4},{4,0},{8,12},{12,8},{16,20},{20,16},{24,28},{28,24},{1,5},{5... | collective-permute-start | bytes 3145736 | tf_op jit(solution)/shard_map/ppermute | solution.py:485
  58.9 1.0 copy-start.10
  59.9 79.1 %all-to-all-start = ((bf16[8,3,4,2,64,128]{5,4,3,2,1,0:T(8,128)(2,1)}), bf16[8,3,4,2,64,128]{5,4,3,2,1,0:T(8,128)(2,1)S(1)}, u32[]{:S(2)}, u32[]{:S(2)}) async-start(bf16[8,3,4,2,64,128]{5,4,3,2,1,0:T(8,128)(2,1)} %get-tuple-element.62), calls=%async_computation | async-start | bytes 6291456 | tf_op jit(solution)/shard_map/all_to_all | solution.py:497
  64.3 70.8 %collective-permute-start.7 = (bf16[1024,512]{1,0:T(8,128)(2,1)}, bf16[1024,512]{1,0:T(8,128)(2,1)}, u32[]{:S(2)}, u32[]{:S(2)}) collective-permute-start(bf16[1024,512]{1,0:T(8,128)(2,1)} %collective-permute-done.3), channel_id=1, source_target_pairs={{8,0},{12,4},{16,24},{20,28},{9,1},{13,5},{17,25},{21,29},{10,2},{... | collective-permute-start | bytes 3145736 | tf_op jit(solution)/shard_map/ppermute | solution.py:485
  68.6 70.3 %copy-start.7 = (bf16[1024,512]{1,0:T(8,128)(2,1)}, bf16[1024,512]{1,0:T(8,128)(2,1)S(1)}, u32[]{:S(2)}) copy-start(bf16[1024,512]{1,0:T(8,128)(2,1)S(1)} %broadcast_select_fusion.1.refs_4_) | copy-start | bytes 3145732
  68.6 70.3 %collective-permute-start.6 = (bf16[1024,512]{1,0:T(8,128)(2,1)S(1)}, bf16[1024,512]{1,0:T(8,128)(2,1)}, u32[]{:S(2)}, u32[]{:S(2)}) collective-permute-start(bf16[1024,512]{1,0:T(8,128)(2,1)S(1)} %broadcast_select_fusion.1.refs_4_), channel_id=1, source_target_pairs={{0,4},{4,0},{8,12},{12,8},{16,20},{20,16},{24,28},{28,24},{1,5},{5... | collective-permute-start | bytes 3145736 | tf_op jit(solution)/shard_map/ppermute | solution.py:485
  137.5 34.5 %collective-permute-start.8 = (bf16[1024,512]{1,0:T(8,128)(2,1)}, bf16[1024,512]{1,0:T(8,128)(2,1)}, u32[]{:S(2)}, u32[]{:S(2)}) collective-permute-start(bf16[1024,512]{1,0:T(8,128)(2,1)} %broadcast_select_fusion.refs_0_.refs_6_), channel_id=1, source_target_pairs={{0,4},{4,0},{8,12},{12,8},{16,20},{20,16},{24,28},{28,24},{1,5},{5... | collective-permute-start | bytes 3145736 | tf_op jit(solution)/shard_map/ppermute | solution.py:485
  138.9 8.7 %copy-start.1 = (bf16[8,3,4,2,64,128]{5,4,3,2,1,0:T(8,128)(2,1)}, bf16[8,3,4,2,64,128]{5,4,3,2,1,0:T(8,128)(2,1)S(1)}, u32[]{:S(2)}) copy-start(bf16[8,3,4,2,64,128]{5,4,3,2,1,0:T(8,128)(2,1)S(1)} %all-to-all-done.chunk_ref) | copy-start | bytes 9437188
  147.6 1.0 copy-start.5
  148.6 35.8 %all-to-all-start.1 = ((bf16[8,4,2,64,128]{4,3,2,1,0:T(8,128)(2,1)}), bf16[8,4,2,64,128]{4,3,2,1,0:T(8,128)(2,1)S(1)}, u32[]{:S(2)}, u32[]{:S(2)}) async-start(bf16[8,4,2,64,128]{4,3,2,1,0:T(8,128)(2,1)} %copy-done.5), calls=%async_computation.1 | async-start | bytes 2097152 | tf_op jit(solution)/shard_map/all_to_all | solution.py:497
  172.0 26.0 %collective-permute-start.9 = (bf16[2,512,512]{2,1,0:T(8,128)(2,1)}, bf16[2,512,512]{2,1,0:T(8,128)(2,1)S(1)}, u32[]{:S(2)}, u32[]{:S(2)}) collective-permute-start(bf16[2,512,512]{2,1,0:T(8,128)(2,1)} %proj_part.8), channel_id=1, source_target_pairs={{0,4},{4,0},{8,12},{12,8},{16,20},{20,16},{24,28},{28,24},{1,5},{5... | collective-permute-start | bytes 3145736 | tf_op jit(solution)/shard_map/ppermute | solution.py:485
  174.1 10.3 %copy-start = (bf16[1024,512]{1,0:T(8,128)(2,1)S(1)}, bf16[1024,512]{1,0:T(8,128)(2,1)}, u32[]{:S(2)}) copy-start(bf16[1024,512]{1,0:T(8,128)(2,1)} %row_forward.1.flat_ref.row_ref) | copy-start | bytes 3145732
  185.0 1.0 copy-start.3
  186.0 1.3 copy-start.4
  198.0 7.2 %copy-start.12 = (bf16[2,512,512]{2,1,0:T(8,128)(2,1)}, bf16[2,512,512]{2,1,0:T(8,128)(2,1)S(1)}, u32[]{:S(2)}) copy-start(bf16[2,512,512]{2,1,0:T(8,128)(2,1)S(1)} %collective-permute-done.9.refs_0_) | copy-start | bytes 3145732
  198.0 57.2 %all-to-all-start.2 = ((bf16[8,4,2,64,128]{4,3,2,1,0:T(8,128)(2,1)}), bf16[8,4,2,64,128]{4,3,2,1,0:T(8,128)(2,1)}, u32[]{:S(2)}, u32[]{:S(2)}) async-start(bf16[8,4,2,64,128]{4,3,2,1,0:T(8,128)(2,1)} %get-tuple-element.74), calls=%async_computation.2 | async-start | bytes 2097152 | tf_op jit(solution)/shard_map/all_to_all | solution.py:497
  203.1 35.1 %collective-permute-start.10 = (bf16[2,512,512]{2,1,0:T(8,128)(2,1)}, bf16[2,512,512]{2,1,0:T(8,128)(2,1)S(1)}, u32[]{:S(2)}, u32[]{:S(2)}) collective-permute-start(bf16[2,512,512]{2,1,0:T(8,128)(2,1)} %proj_part.10), channel_id=1, source_target_pairs={{0,4},{4,0},{8,12},{12,8},{16,20},{20,16},{24,28},{28,24},{1,5},{5... | collective-permute-start | bytes 3145736 | tf_op jit(solution)/shard_map/ppermute | solution.py:485
  210.3 36.7 %collective-permute-start.11 = (bf16[2,512,512]{2,1,0:T(8,128)(2,1)}, bf16[2,512,512]{2,1,0:T(8,128)(2,1)}, u32[]{:S(2)}, u32[]{:S(2)}) collective-permute-start(bf16[2,512,512]{2,1,0:T(8,128)(2,1)} %proj_part.13), channel_id=1, source_target_pairs={{0,8},{4,12},{24,16},{28,20},{1,9},{5,13},{25,17},{29,21},{2,10},{... | collective-permute-start | bytes 3145736 | tf_op jit(solution)/shard_map/ppermute | solution.py:485
  238.2 1.0 copy-start.13
  244.1 11.1 %copy-start.2 = (bf16[8,3,4,2,64,128]{5,4,3,2,1,0:T(8,128)(2,1)S(1)}, bf16[8,3,4,2,64,128]{5,4,3,2,1,0:T(8,128)(2,1)}, u32[]{:S(2)}) copy-start(bf16[8,3,4,2,64,128]{5,4,3,2,1,0:T(8,128)(2,1)} %copy-done.1) | copy-start | bytes 9437188
  244.1 37.5 %collective-permute-start.15 = (bf16[2,512,512]{2,1,0:T(8,128)(2,1)}, bf16[2,512,512]{2,1,0:T(8,128)(2,1)}, u32[]{:S(2)}, u32[]{:S(2)}) collective-permute-start(bf16[2,512,512]{2,1,0:T(8,128)(2,1)} %proj_part.12), channel_id=1, source_target_pairs={{0,8},{4,12},{24,16},{28,20},{1,9},{5,13},{25,17},{29,21},{2,10},{... | collective-permute-start | bytes 3145736 | tf_op jit(solution)/shard_map/ppermute | solution.py:485
  249.8 35.9 %collective-permute-start.14 = (bf16[2,512,512]{2,1,0:T(8,128)(2,1)}, bf16[2,512,512]{2,1,0:T(8,128)(2,1)}, u32[]{:S(2)}, u32[]{:S(2)}) collective-permute-start(bf16[2,512,512]{2,1,0:T(8,128)(2,1)} %add_convert_fusion.1), channel_id=1, source_target_pairs={{8,16},{12,20},{16,8},{20,12},{9,17},{13,21},{17,9},{21,13},{10,18... | collective-permute-start | bytes 3145736 | tf_op jit(solution)/shard_map/ppermute | solution.py:485
  253.1 32.5 %collective-permute-start.17 = (bf16[2,512,512]{2,1,0:T(8,128)(2,1)}, bf16[2,512,512]{2,1,0:T(8,128)(2,1)}, u32[]{:S(2)}, u32[]{:S(2)}) collective-permute-start(bf16[2,512,512]{2,1,0:T(8,128)(2,1)} %proj_part.9), channel_id=1, source_target_pairs={{0,4},{4,0},{8,12},{12,8},{16,20},{20,16},{24,28},{28,24},{1,5},{5... | collective-permute-start | bytes 3145736 | tf_op jit(solution)/shard_map/ppermute | solution.py:485
  254.3 46.2 %collective-permute-start.18 = (bf16[2,512,512]{2,1,0:T(8,128)(2,1)}, bf16[2,512,512]{2,1,0:T(8,128)(2,1)}, u32[]{:S(2)}, u32[]{:S(2)}) collective-permute-start(bf16[2,512,512]{2,1,0:T(8,128)(2,1)} %proj_part.11), channel_id=1, source_target_pairs={{0,4},{4,0},{8,12},{12,8},{16,20},{20,16},{24,28},{28,24},{1,5},{5... | collective-permute-start | bytes 3145736 | tf_op jit(solution)/shard_map/ppermute | solution.py:485
  269.7 11.9 %copy-start.11 = (bf16[2,512,512]{2,1,0:T(8,128)(2,1)S(1)}, bf16[2,512,512]{2,1,0:T(8,128)(2,1)}, u32[]{:S(2)}) copy-start(bf16[2,512,512]{2,1,0:T(8,128)(2,1)} %proj_part.12) | copy-start | bytes 3145732
  281.6 33.6 %collective-permute-start.12 = (bf16[1024,2048]{1,0:T(8,128)(2,1)}, bf16[1024,2048]{1,0:T(8,128)(2,1)}, u32[]{:S(2)}, u32[]{:S(2)}) collective-permute-start(bf16[1024,2048]{1,0:T(8,128)(2,1)} %layer_part.3), channel_id=1, source_target_pairs={{0,1},{1,0},{2,3},{3,2},{4,5},{5,4},{6,7},{7,6},{8,9},{9,8},{10,11... | collective-permute-start | bytes 12582920 | tf_op jit(solution)/shard_map/ppermute | solution.py:513
  283.2 27.5 %collective-permute-start.16 = (bf16[2,512,512]{2,1,0:T(8,128)(2,1)S(1)}, bf16[2,512,512]{2,1,0:T(8,128)(2,1)}, u32[]{:S(2)}, u32[]{:S(2)}) collective-permute-start(bf16[2,512,512]{2,1,0:T(8,128)(2,1)S(1)} %add_convert_fusion), channel_id=1, source_target_pairs={{8,16},{12,20},{16,8},{20,12},{9,17},{13,21},{17,9},{21,13},{10,18... | collective-permute-start | bytes 3145736 | tf_op jit(solution)/shard_map/ppermute | solution.py:485
  310.7 90.5 %all-to-all-start.3 = ((bf16[8,3,4,2,64,128]{5,4,3,2,1,0:T(8,128)(2,1)}), bf16[8,3,4,2,64,128]{5,4,3,2,1,0:T(8,128)(2,1)S(1)}, u32[]{:S(2)}, u32[]{:S(2)}) async-start(bf16[8,3,4,2,64,128]{5,4,3,2,1,0:T(8,128)(2,1)} %column_backward.1), calls=%async_computation.3 | async-start | bytes 6291456 | tf_op jit(solution)/shard_map/all_to_all | solution.py:497
  323.6 68.4 %collective-permute-start.13 = (bf16[1024,1024]{1,0:T(8,128)(2,1)}, bf16[1024,1024]{1,0:T(8,128)(2,1)}, u32[]{:S(2)}, u32[]{:S(2)}) collective-permute-start(bf16[1024,1024]{1,0:T(8,128)(2,1)} %layer_part.4), channel_id=1, source_target_pairs={{0,2},{1,3},{2,0},{3,1},{4,6},{5,7},{6,4},{7,5},{8,10},{9,11},{10,... | collective-permute-start | bytes 6291464 | tf_op jit(solution)/shard_map/ppermute | solution.py:513
  333.8 33.3 %collective-permute-start.19 = (bf16[512,512]{1,0:T(8,128)(2,1)}, bf16[512,512]{1,0:T(8,128)(2,1)}, u32[]{:S(2)}, u32[]{:S(2)}) collective-permute-start(bf16[512,512]{1,0:T(8,128)(2,1)} %fusion.5), channel_id=1, source_target_pairs={{8,0},{12,4},{16,24},{20,28},{9,1},{13,5},{17,25},{21,29},{10,2},{... | collective-permute-start | bytes 1572872 | tf_op jit(solution)/shard_map/ppermute | solution.py:485
  336.5 42.8 %collective-permute-start.21 = (bf16[512,512]{1,0:T(8,128)(2,1)}, bf16[512,512]{1,0:T(8,128)(2,1)}, u32[]{:S(2)}, u32[]{:S(2)}) collective-permute-start(bf16[512,512]{1,0:T(8,128)(2,1)} %bitcast.52), channel_id=1, source_target_pairs={{0,8},{4,12},{24,16},{28,20},{1,9},{5,13},{25,17},{29,21},{2,10},{... | collective-permute-start | bytes 1572872 | tf_op jit(solution)/shard_map/ppermute | solution.py:485
  343.0 46.1 %collective-permute-start.22 = (bf16[512,512]{1,0:T(8,128)(2,1)}, bf16[512,512]{1,0:T(8,128)(2,1)}, u32[]{:S(2)}, u32[]{:S(2)}) collective-permute-start(bf16[512,512]{1,0:T(8,128)(2,1)} %bitcast.53), channel_id=1, source_target_pairs={{0,8},{4,12},{24,16},{28,20},{1,9},{5,13},{25,17},{29,21},{2,10},{... | collective-permute-start | bytes 1572872 | tf_op jit(solution)/shard_map/ppermute | solution.py:485
  346.5 32.8 %copy-start.14 = (bf16[1,512,512]{2,1,0:T(8,128)(2,1)S(1)}, bf16[1,512,512]{2,1,0:T(8,128)(2,1)}, u32[]{:S(2)}) copy-start(bf16[1,512,512]{2,1,0:T(8,128)(2,1)} %get-tuple-element.105) | copy-start | bytes 1572868
  346.5 42.7 %collective-permute-start.20 = (bf16[512,512]{1,0:T(8,128)(2,1)}, bf16[512,512]{1,0:T(8,128)(2,1)}, u32[]{:S(2)}, u32[]{:S(2)}) collective-permute-start(bf16[512,512]{1,0:T(8,128)(2,1)} %fusion.4), channel_id=1, source_target_pairs={{8,0},{12,4},{16,24},{20,28},{9,1},{13,5},{17,25},{21,29},{10,2},{... | collective-permute-start | bytes 1572872 | tf_op jit(solution)/shard_map/ppermute | solution.py:485
  367.1 22.1 %copy-start.15 = (bf16[1,512,512]{2,1,0:T(8,128)(2,1)S(1)}, bf16[1,512,512]{2,1,0:T(8,128)(2,1)}, u32[]{:S(2)}) copy-start(bf16[1,512,512]{2,1,0:T(8,128)(2,1)} %get-tuple-element.106) | copy-start | bytes 1572868
  401.2 1.6 copy-start.6

commit v12 on v11

--- a/solution.py
+++ b/solution.py
@@ -589,27 +589,27 @@
     column_far_in = links.along(column_far, INWARD)
     row_middle = add(row_far, row_far_in)
     row_cross = links.along(row_middle, CROSS)
-    gradients = column_backward(chunks, after(grads, column_far, row_middle))
+    gradients = column_backward(chunks, after(grads, row_far))
     layer = LayerSum(ids, after(flat, gradients), blocks, heads_n)
     layer.start()
     column_close = exchanged(column_close)
     column_cross = links.along(add(column_far, column_far_in), CROSS)
-    column_grads = swap(after(gradients, row_cross, column_cross, *row_close, *column_close))
-
-    layer.turn(gradients)
     row_near, row_own = summed(after(row_out, gradients), close, row_close, 1)
     row_near_in = links.along(row_near[0], INWARD)
+    row_back = links.along(add(row_near[0], row_cross[1]), OUTWARD)
+    column_grads = swap(after(gradients, column_cross, *column_close, row_near_in, row_back))
+
+    layer.turn(gradients)
     column_near, column_own = summed(after(column_out, gradients), close, column_close, 1)
     column_near_in = links.along(column_near[0], INWARD)
     row_grads = row_backward(*by_head, after(grad_row, gradients))
-    row_back = links.along(add(row_near[0], row_cross[1]), OUTWARD)
     column_back = links.along(add(column_near[0], column_cross[1]), OUTWARD)
     layer_out = layer.finish()
-    ahead = after(row_grads[0], layer_out, row_back, column_back, row_near_in, column_near_in)
+    ahead = after(row_grads[0], layer_out)
     gradients = join_gradients(column_grads, [ahead, *row_grads[1:]])
 
     proj_row = add(row_own[0], row_near_in, row_cross[0], row_back)
-    proj_column = add(column_own[0], column_near_in, column_cross[0], column_back)
+    proj_column = add(column_own[0], after(column_near_in, layer_out), column_cross[0], column_back)
     shape = (half, dim, depth)
     proj_grad = jnp.stack([proj_row.reshape(shape), proj_column.reshape(shape)], axis=1)
     return (layer_out, *gradients, proj_grad.reshape(heads * dim, depth))

time: 414 us -> 397 us (0.959)
  waiting for transfers between devices: 155 us -> 136 us
    ppermute x21, waiting for transfers between devices: 155 us -> 122 us  [send(): out = lax.ppermute(value, 'ctx', pairs)]
    ppermute x2, waiting for transfers between devices: 0.01 us -> 13.9 us  [move(): lax.ppermute(part, 'head', [(place, place ^ g) for place in range(self.he...]
  transfers between devices with their start and end apart: 27 -> 27, of which waited for: 11 -> 11; matrix products, arithmetic and copies ran while one was open for 6% -> 6% of each run, Pallas kernels for 37% -> 38%
where the time goes in v12:
time: 397 us; the launch traced here: 393 us
  Pallas kernels  158 us (40%)
  waiting for transfers between devices  136 us (34%)
  starting transfers between devices  67.9 us (17%)
  other arithmetic  20.1 us (5%)
  local copies, waits for them, and re-layouts  9.3 us (2%)
    ppermute x21, waiting for transfers between devices, send(): out = lax.ppermute(value, 'ctx', pairs)  122 us
    ppermute x21, starting transfers between devices, send(): out = lax.ppermute(value, 'ctx', pairs)  45.6 us
    pallas_call x8, Pallas kernels, proj_part(): pl.pallas_call(functools.partial(proj_kernel, lead, len(extra), dim), gri...  39.9 us
    pallas_call x3, Pallas kernels, layer_part(): pl.pallas_call(functools.partial(layer_kernel, n, count, len(extra)), gri...  29.4 us
    pallas_call x2, Pallas kernels, attn_grad(): pl.pallas_call(functools.partial(attn_grad_kernel, m, dim, last), grid_sp...  26.9 us
    all_to_all x4, starting transfers between devices, swap(): lax.all_to_all(chunks, 'ctx', split_axis=0, concat_axis=0, tiled=True)  20.6 us
    pallas_call x1, Pallas kernels, column_backward(): pl.pallas_call(functools.partial(column_backward_kernel, dim ** (-0.5)),...  14.5 us
    ppermute x2, waiting for transfers between devices, move(): lax.ppermute(part, 'head', [(place, place ^ g) for place in range(self.he...  13.9 us
  transfers between devices with their start and end apart: 27, of which 11 were waited for; matrix products, arithmetic and copies ran while one was open for 6% of the time, Pallas kernels for 38%

profile of v12, /device:TPU:8, one launch (start us, length us, event | category | flops | bytes accessed | tf_op | source)
XLA Modules:
  0.0 392.6 jit_solution(12185718838534177903)
XLA Ops:
  0.6 3.5 collective-permute-start.4
  4.2 1.6 collective-permute-start.1
  5.8 7.1 %split_inputs.1 = (bf16[8,3,4,2,64,128]{5,4,3,2,1,0:T(8,128)(2,1)}, bf16[4,1024,128]{2,1,0:T(8,128)(2,1)}, bf16[4,1024,128]{2,1,0:T(8,128)(2,1)}, bf16[4,1024,128]{2,1,0:T(8,128)(2,1)}) custom-call(bf16[1024,8,128]{2,1,0:T(8,128)(2,1)} %q_ref.1, bf16[1024,8,128]{2,1,0:T(8,128)(2,1)} %k_ref.1, bf16[1024,8,128]{2,1,0:T(8,128)(2,1)} %v_ref.1), custom_call_target="tpu_custom_call" | custom-call | tf_op jit(solution)/shard_map/split_inputs/pallas_call | solution.py:48
  12.9 14.9 %collective-permute-done.4 = bf16[1024,512]{1,0:T(8,128)(2,1)} collective-permute-done((bf16[1024,512]{1,0:T(8,128)(2,1)}, bf16[1024,512]{1,0:T(8,128)(2,1)}, u32[]{:S(2)}, u32[]{:S(2)}) %collective-permute-start.4) | collective-permute-done | bytes 1048608 | tf_op jit(solution)/shard_map/ppermute | solution.py:485
  29.0 3.2 collective-permute-start.5
  32.2 3.1 collective-permute-start.3
  35.3 1.6 collective-permute-start.2
  36.9 9.9 %row_forward.1.flat_ref.row_ref = bf16[1024,512]{1,0:T(8,128)(2,1)} custom-call(bf16[4,1024,128]{2,1,0:T(8,128)(2,1)} %get-tuple-element.57.q_ref, bf16[4,1024,128]{2,1,0:T(8,128)(2,1)} %get-tuple-element.58.k_ref, bf16[4,1024,128]{2,1,0:T(8,128)(2,1)} %get-tuple-element.59.v_ref), custom_call_target="tpu_custom_call" | custom-call | flops 1073741824 | bytes 4194304 | tf_op jit(solution)/shard_map/row_forward/pallas_call | solution.py:321
  47.4 4.8 %proj_part.9 = bf16[2,512,512]{2,1,0:T(8,128)(2,1)} custom-call(s32[2]{0:T(128)} %pad_add_fusion.2.order, bf16[1024,512]{1,0:T(8,128)(2,1)} %row_forward.1.flat_ref.row_ref, bf16[1024,4096]{1,0:T(8,128)(2,1)} %grad_ref.18), custom_call_target="tpu_custom_call" | custom-call | flops 1073741824 | bytes 4194304 | tf_op jit(solution)/shard_map/proj_part/pallas_call | solution.py:275
  52.9 4.8 %proj_part.8 = bf16[2,512,512]{2,1,0:T(8,128)(2,1)} custom-call(s32[2]{0:T(128)} %pad_add_fusion.1.order, bf16[1024,512]{1,0:T(8,128)(2,1)} %row_forward.1.flat_ref.row_ref, bf16[1024,4096]{1,0:T(8,128)(2,1)} %grad_ref.18), custom_call_target="tpu_custom_call" | custom-call | flops 1073741824 | bytes 4194304 | tf_op jit(solution)/shard_map/proj_part/pallas_call | solution.py:275
  59.8 4.5 %all-to-all-start = ((bf16[8,3,4,2,64,128]{5,4,3,2,1,0:T(8,128)(2,1)}), bf16[8,3,4,2,64,128]{5,4,3,2,1,0:T(8,128)(2,1)S(1)}, u32[]{:S(2)}, u32[]{:S(2)}) async-start(bf16[8,3,4,2,64,128]{5,4,3,2,1,0:T(8,128)(2,1)} %get-tuple-element.63), calls=%async_computation | async-start | bytes 6291456 | tf_op jit(solution)/shard_map/all_to_all | solution.py:497
  64.3 2.9 collective-permute-start.7
  68.6 2.1 collective-permute-start.6
  70.7 64.5 %collective-permute-done.7 = bf16[1024,512]{1,0:T(8,128)(2,1)} collective-permute-done((bf16[1024,512]{1,0:T(8,128)(2,1)}, bf16[1024,512]{1,0:T(8,128)(2,1)}, u32[]{:S(2)}, u32[]{:S(2)}) %collective-permute-start.7) | collective-permute-done | bytes 1048608 | tf_op jit(solution)/shard_map/ppermute | solution.py:485
  135.1 2.3 broadcast_select_fusion.refs_0_.refs_6_
  138.9 8.7 %column_forward.1 = bf16[8,4,2,64,128]{4,3,2,1,0:T(8,128)(2,1)S(1)} custom-call(bf16[8,3,4,2,64,128]{5,4,3,2,1,0:T(8,128)(2,1)S(1)} %all-to-all-done.chunk_ref), custom_call_target="tpu_custom_call" | custom-call | flops 536870912 | bytes 4194304 | tf_op jit(solution)/shard_map/column_forward/pallas_call | solution.py:413
  148.6 6.2 %all-to-all-start.1 = ((bf16[8,4,2,64,128]{4,3,2,1,0:T(8,128)(2,1)}), bf16[8,4,2,64,128]{4,3,2,1,0:T(8,128)(2,1)S(1)}, u32[]{:S(2)}, u32[]{:S(2)}) async-start(bf16[8,4,2,64,128]{4,3,2,1,0:T(8,128)(2,1)} %copy-done.5), calls=%async_computation.1 | async-start | bytes 2097152 | tf_op jit(solution)/shard_map/all_to_all | solution.py:497
  155.4 16.6 %attn_grad.2.refs_2_ = f32[1024,1024]{1,0:T(8,128)} custom-call(s32[6]{0:T(128)} %stack.114.ids, bf16[1024,4096]{1,0:T(8,128)(2,1)} %grad_ref.18, bf16[1024,512]{1,0:T(8,128)(2,1)} %refs_0_.7, bf16[1024,512]{1,0:T(8,128)(2,1)} %copy-done.9, bf16[1024,512]{1,0:T(8,128)(2,1)} %copy-done.8, bf16[1024,512]{1,0:T(8,128)(2,1)} %copy-done.10, ...), custom_call_target="tpu_custom_call" | custom-call | flops 6442450944 | bytes 16777216 | tf_op jit(solution)/shard_map/attn_grad/pallas_call | solution.py:163
  174.3 10.3 %attn_grad.3 = (bf16[1024,512]{1,0:T(8,128)(2,1)}, bf16[8,4,2,64,128]{4,3,2,1,0:T(8,128)(2,1)}) custom-call(s32[2]{0:T(128)} %pad_add_fusion.3.ids, bf16[1024,4096]{1,0:T(8,128)(2,1)} %grad_ref.18, bf16[1024,512]{1,0:T(8,128)(2,1)} %broadcast_select_fusion.refs_0_.refs_6_, bf16[1024,512]{1,0:T(8,128)(2,1)} %collective-permute-done.8.refs_1_.refs_7_, ...), custom_call_target="tpu_custom_call" | custom-call | flops 2147483648 | bytes 8388608 | tf_op jit(solution)/shard_map/attn_grad/pallas_call | solution.py:163
  187.5 4.8 %proj_part.11 = bf16[2,512,512]{2,1,0:T(8,128)(2,1)} custom-call(s32[2]{0:T(128)} %pad_add_fusion.2.order, bf16[1024,512]{1,0:T(8,128)(2,1)} %copy-done.3, bf16[1024,4096]{1,0:T(8,128)(2,1)} %grad_ref.18), custom_call_target="tpu_custom_call" | custom-call | flops 1073741824 | bytes 4194304 | tf_op jit(solution)/shard_map/proj_part/pallas_call | solution.py:275
  192.4 4.8 %proj_part.10 = bf16[2,512,512]{2,1,0:T(8,128)(2,1)} custom-call(s32[2]{0:T(128)} %pad_add_fusion.1.order, bf16[1024,512]{1,0:T(8,128)(2,1)} %copy-done.3, bf16[1024,4096]{1,0:T(8,128)(2,1)} %grad_ref.18), custom_call_target="tpu_custom_call" | custom-call | flops 1073741824 | bytes 4194304 | tf_op jit(solution)/shard_map/proj_part/pallas_call | solution.py:275
  198.1 5.2 %all-to-all-start.2 = ((bf16[8,4,2,64,128]{4,3,2,1,0:T(8,128)(2,1)}), bf16[8,4,2,64,128]{4,3,2,1,0:T(8,128)(2,1)}, u32[]{:S(2)}, u32[]{:S(2)}) async-start(bf16[8,4,2,64,128]{4,3,2,1,0:T(8,128)(2,1)} %get-tuple-element.75), calls=%async_computation.2 | async-start | bytes 2097152 | tf_op jit(solution)/shard_map/all_to_all | solution.py:497
  205.4 5.0 %proj_part.12 = bf16[2,512,512]{2,1,0:T(8,128)(2,1)} custom-call(s32[2]{0:T(128)} %pad_add_fusion.4.order, bf16[1024,512]{1,0:T(8,128)(2,1)} %row_forward.1.flat_ref.row_ref, bf16[1024,4096]{1,0:T(8,128)(2,1)} %grad_ref.18, bf16[2,512,512]{2,1,0:T(8,128)(2,1)} %copy-done.13), custom_call_target="tpu_custom_call" | custom-call | flops 1073741824 | bytes 5242880 | tf_op jit(solution)/shard_map/proj_part/pallas_call | solution.py:275
  212.9 25.2 %collective-permute-done.12.refs_0_ = bf16[2,512,512]{2,1,0:T(8,128)(2,1)S(1)} collective-permute-done((bf16[2,512,512]{2,1,0:T(8,128)(2,1)S(1)}, bf16[2,512,512]{2,1,0:T(8,128)(2,1)S(1)}, u32[]{:S(2)}, u32[]{:S(2)}) %collective-permute-start.12) | collective-permute-done | bytes 1048608 | tf_op jit(solution)/shard_map/ppermute | solution.py:485
  239.2 5.0 %proj_part.13 = bf16[2,512,512]{2,1,0:T(8,128)(2,1)} custom-call(s32[2]{0:T(128)} %pad_add_fusion.4.order, bf16[1024,512]{1,0:T(8,128)(2,1)} %copy-done.3, bf16[1024,4096]{1,0:T(8,128)(2,1)} %grad_ref.18, bf16[2,512,512]{2,1,0:T(8,128)(2,1)} %copy-done.12), custom_call_target="tpu_custom_call" | custom-call | flops 1073741824 | bytes 5242880 | tf_op jit(solution)/shard_map/proj_part/pallas_call | solution.py:275
  244.2 1.5 collective-permute-start.13
  245.7 2.8 add_convert_fusion
  248.5 3.4 collective-permute-start.19
  253.0 14.5 %column_backward.1 = bf16[8,3,4,2,64,128]{5,4,3,2,1,0:T(8,128)(2,1)} custom-call(bf16[8,3,4,2,64,128]{5,4,3,2,1,0:T(8,128)(2,1)S(1)} %copy-done.2, bf16[8,4,2,64,128]{4,3,2,1,0:T(8,128)(2,1)} %all-to-all-done.2.grad_ref), custom_call_target="tpu_custom_call" | custom-call | flops 1342177280 | bytes 7340032 | tf_op jit(solution)/shard_map/column_backward/pallas_call | solution.py:451
  267.5 11.8 %layer_part.3 = bf16[1024,2048]{1,0:T(8,128)(2,1)} custom-call(s32[8]{0:T(128)} %stack.107.ids, s32[4]{0:T(128)} %pad_add_fusion.5.wanted, bf16[1024,1024]{1,0:T(8,128)(2,1)} %copy-done.4, bf16[1024,512]{1,0:T(8,128)(2,1)} %refs_0_.7, bf16[1024,512]{1,0:T(8,128)(2,1)} %copy-done.9, bf16[1024,512]{1,0:T(8,128)(2,1)} %copy-done.8, ...), custom_call_target="tpu_custom_call" | custom-call | flops 4294967296 | bytes 10485760 | tf_op jit(solution)/shard_map/layer_part/pallas_call | solution.py:221
  282.0 2.7 collective-permute-start.15
  285.3 5.2 %proj_part.14 = (bf16[1,512,512]{2,1,0:T(8,128)(2,1)}, bf16[1,512,512]{2,1,0:T(8,128)(2,1)}) custom-call(s32[2]{0:T(128)} %pad_add_fusion.7.order, bf16[1024,512]{1,0:T(8,128)(2,1)} %row_forward.1.flat_ref.row_ref, bf16[1024,4096]{1,0:T(8,128)(2,1)} %grad_ref.18, bf16[2,512,512]{2,1,0:T(8,128)(2,1)} %collective-permute-done.17.refs_0_), custom_call_target="tpu_custom_call" | custom-call | flops 1073741824 | bytes 5242880 | tf_op jit(solution)/shard_map/proj_part/pallas_call | solution.py:275
  291.9 3.5 collective-permute-start.20
  296.7 8.4 %collective-permute-done.16.refs_0_ = bf16[2,512,512]{2,1,0:T(8,128)(2,1)} collective-permute-done((bf16[2,512,512]{2,1,0:T(8,128)(2,1)S(1)}, bf16[2,512,512]{2,1,0:T(8,128)(2,1)}, u32[]{:S(2)}, u32[]{:S(2)}) %collective-permute-start.16) | collective-permute-done | bytes 1048608 | tf_op jit(solution)/shard_map/ppermute | solution.py:485
  306.1 5.2 %collective-permute-done.18 = bf16[512,512]{1,0:T(8,128)(2,1)} collective-permute-done((bf16[512,512]{1,0:T(8,128)(2,1)}, bf16[512,512]{1,0:T(8,128)(2,1)}, u32[]{:S(2)}, u32[]{:S(2)}) %collective-permute-start.18) | collective-permute-done | bytes 524320 | tf_op jit(solution)/shard_map/ppermute | solution.py:485
  311.3 4.7 %all-to-all-start.3 = ((bf16[8,3,4,2,64,128]{5,4,3,2,1,0:T(8,128)(2,1)}), bf16[8,3,4,2,64,128]{5,4,3,2,1,0:T(8,128)(2,1)S(1)}, u32[]{:S(2)}, u32[]{:S(2)}) async-start(bf16[8,3,4,2,64,128]{5,4,3,2,1,0:T(8,128)(2,1)} %column_backward.1), calls=%async_computation.3 | async-start | bytes 6291456 | tf_op jit(solution)/shard_map/all_to_all | solution.py:497
  316.6 8.5 %layer_part.4 = bf16[1024,1024]{1,0:T(8,128)(2,1)} custom-call(s32[8]{0:T(128)} %stack.107.ids, s32[2]{0:T(128)} %pad_add_fusion.6.wanted, bf16[1024,1024]{1,0:T(8,128)(2,1)} %copy-done.4, bf16[1024,512]{1,0:T(8,128)(2,1)} %refs_0_.7, bf16[1024,512]{1,0:T(8,128)(2,1)} %copy-done.9, bf16[1024,512]{1,0:T(8,128)(2,1)} %copy-done.8, ...), custom_call_target="tpu_custom_call" | custom-call | flops 2147483648 | bytes 6291456 | tf_op jit(solution)/shard_map/layer_part/pallas_call | solution.py:221
  325.1 1.6 collective-permute-start.11
  327.2 5.3 %proj_part.15 = (bf16[1,512,512]{2,1,0:T(8,128)(2,1)}, bf16[1,512,512]{2,1,0:T(8,128)(2,1)}) custom-call(s32[2]{0:T(128)} %pad_add_fusion.7.order, bf16[1024,512]{1,0:T(8,128)(2,1)} %copy-done.3, bf16[1024,4096]{1,0:T(8,128)(2,1)} %grad_ref.18, bf16[2,512,512]{2,1,0:T(8,128)(2,1)} %collective-permute-done.16.refs_0_), custom_call_target="tpu_custom_call" | custom-call | flops 1073741824 | bytes 5242880 | tf_op jit(solution)/shard_map/proj_part/pallas_call | solution.py:275
  333.8 2.2 fusion
  336.0 6.1 %collective-permute-start.22 = (bf16[512,512]{1,0:T(8,128)(2,1)}, bf16[512,512]{1,0:T(8,128)(2,1)}, u32[]{:S(2)}, u32[]{:S(2)}) collective-permute-start(bf16[512,512]{1,0:T(8,128)(2,1)} %fusion), channel_id=1, source_target_pairs={{8,0},{12,4},{16,24},{20,28},{9,1},{13,5},{17,25},{21,29},{10,2},{... | collective-permute-start | bytes 1572872 | tf_op jit(solution)/shard_map/ppermute | solution.py:485
  342.1 13.6 %row_backward.1 = (bf16[4,1024,128]{2,1,0:T(8,128)(2,1)}, bf16[4,1024,128]{2,1,0:T(8,128)(2,1)}, bf16[4,1024,128]{2,1,0:T(8,128)(2,1)}) custom-call(bf16[4,1024,128]{2,1,0:T(8,128)(2,1)} %get-tuple-element.57.q_ref, bf16[4,1024,128]{2,1,0:T(8,128)(2,1)} %get-tuple-element.58.k_ref, bf16[4,1024,128]{2,1,0:T(8,128)(2,1)} %get-tuple-element.59.v_ref, ...), custom_call_target="tpu_custom_call" | custom-call | flops 2684354560 | bytes 7340032 | tf_op jit(solution)/shard_map/row_backward/pallas_call | solution.py:355
  355.7 1.8 fusion.4
  357.5 13.9 %collective-permute-done.11.refs_9_ = bf16[1024,1024]{1,0:T(8,128)(2,1)} collective-permute-done((bf16[1024,1024]{1,0:T(8,128)(2,1)}, bf16[1024,1024]{1,0:T(8,128)(2,1)}, u32[]{:S(2)}, u32[]{:S(2)}) %collective-permute-start.11) | collective-permute-done | bytes 2097184 | tf_op jit(solution)/shard_map/ppermute | solution.py:513
  371.4 9.2 %layer_part.5 = bf16[1024,1024]{1,0:T(8,128)(2,1)} custom-call(s32[8]{0:T(128)} %stack.107.ids, s32[2]{0:T(128)} %pad_add_fusion.wanted, bf16[1024,1024]{1,0:T(8,128)(2,1)} %copy-done.4, bf16[1024,512]{1,0:T(8,128)(2,1)} %refs_0_.7, bf16[1024,512]{1,0:T(8,128)(2,1)} %copy-done.9, bf16[1024,512]{1,0:T(8,128)(2,1)} %copy-done.8, bf16[1024,512]{1,0:T(8,128)(2,1)} %copy-done.10, ...), custom_call_target="tpu_custom_call" | custom-call | flops 2147483648 | bytes 6291456 | tf_op jit(solution)/shard_map/layer_part/pallas_call | solution.py:221
  380.6 1.8 fusion.2
  383.6 1.6 copy-done.6
  385.2 7.3 %join_gradients.1 = (bf16[1024,8,128]{2,1,0:T(8,128)(2,1)}, bf16[1024,8,128]{2,1,0:T(8,128)(2,1)}, bf16[1024,8,128]{2,1,0:T(8,128)(2,1)}) custom-call(bf16[8,3,4,2,64,128]{5,4,3,2,1,0:T(8,128)(2,1)} %copy-done.6, bf16[4,1024,128]{2,1,0:T(8,128)(2,1)} %get-tuple-element.96.refs_0_, bf16[4,1024,128]{2,1,0:T(8,128)(2,1)} %get-tuple-element.97.refs_1_, ...), custom_call_target="tpu_custom_call" | custom-call | tf_op jit(solution)/shard_map/join_gradients/pallas_call | solution.py:78
  (78 shorter events, 32.3 us)
Async XLA Ops:
  0.6 27.1 %collective-permute-start.4 = (bf16[1024,512]{1,0:T(8,128)(2,1)}, bf16[1024,512]{1,0:T(8,128)(2,1)}, u32[]{:S(2)}, u32[]{:S(2)}) collective-permute-start(bf16[1024,512]{1,0:T(8,128)(2,1)} %refs_0_.7), channel_id=1, source_target_pairs={{8,16},{12,20},{16,8},{20,12},{9,17},{13,21},{17,9},{21,13},{10,18... | collective-permute-start | bytes 3145736 | tf_op jit(solution)/shard_map/ppermute | solution.py:485
  4.1 24.9 %collective-permute-start = (bf16[1024,512]{1,0:T(8,128)(2,1)}, bf16[1024,512]{1,0:T(8,128)(2,1)S(1)}, u32[]{:S(2)}, u32[]{:S(2)}) collective-permute-start(bf16[1024,512]{1,0:T(8,128)(2,1)} %refs_0_.7), channel_id=1, source_target_pairs={{0,8},{4,12},{8,0},{12,4},{16,24},{20,28},{24,16},{28,20},{1,9},{5... | collective-permute-start | bytes 3145736 | tf_op jit(solution)/shard_map/ppermute | solution.py:485
  4.2 28.0 %collective-permute-start.1 = (bf16[1024,512]{1,0:T(8,128)(2,1)}, bf16[1024,512]{1,0:T(8,128)(2,1)S(1)}, u32[]{:S(2)}, u32[]{:S(2)}) collective-permute-start(bf16[1024,512]{1,0:T(8,128)(2,1)} %refs_0_.7), channel_id=1, source_target_pairs={{0,4},{4,0},{8,12},{12,8},{16,20},{20,16},{24,28},{28,24},{1,5},{5... | collective-permute-start | bytes 3145736 | tf_op jit(solution)/shard_map/ppermute | solution.py:485
  29.0 17.8 %copy-start.8 = (bf16[1024,512]{1,0:T(8,128)(2,1)}, bf16[1024,512]{1,0:T(8,128)(2,1)S(1)}, u32[]{:S(2)}) copy-start(bf16[1024,512]{1,0:T(8,128)(2,1)S(1)} %collective-permute-done.refs_2_) | copy-start | bytes 3145732
  29.0 28.7 %collective-permute-start.5 = (bf16[1024,512]{1,0:T(8,128)(2,1)}, bf16[1024,512]{1,0:T(8,128)(2,1)}, u32[]{:S(2)}, u32[]{:S(2)}) collective-permute-start(bf16[1024,512]{1,0:T(8,128)(2,1)} %collective-permute-done.4), channel_id=1, source_target_pairs={{8,0},{12,4},{16,24},{20,28},{9,1},{13,5},{17,25},{21,29},{10,2},{... | collective-permute-start | bytes 3145736 | tf_op jit(solution)/shard_map/ppermute | solution.py:485
  32.2 14.6 %copy-start.9 = (bf16[1024,512]{1,0:T(8,128)(2,1)}, bf16[1024,512]{1,0:T(8,128)(2,1)S(1)}, u32[]{:S(2)}) copy-start(bf16[1024,512]{1,0:T(8,128)(2,1)S(1)} %collective-permute-done.1.refs_1_) | copy-start | bytes 3145732
  32.2 25.7 %collective-permute-start.3 = (bf16[1024,512]{1,0:T(8,128)(2,1)S(1)}, bf16[1024,512]{1,0:T(8,128)(2,1)}, u32[]{:S(2)}, u32[]{:S(2)}) collective-permute-start(bf16[1024,512]{1,0:T(8,128)(2,1)S(1)} %collective-permute-done.refs_2_), channel_id=1, source_target_pairs={{8,16},{12,20},{16,8},{20,12},{9,17},{13,21},{17,9},{21,13},{10,18... | collective-permute-start | bytes 3145736 | tf_op jit(solution)/shard_map/ppermute | solution.py:485
  35.3 23.5 %collective-permute-start.2 = (bf16[1024,512]{1,0:T(8,128)(2,1)S(1)}, bf16[1024,512]{1,0:T(8,128)(2,1)S(1)}, u32[]{:S(2)}, u32[]{:S(2)}) collective-permute-start(bf16[1024,512]{1,0:T(8,128)(2,1)S(1)} %collective-permute-done.refs_2_), channel_id=1, source_target_pairs={{0,4},{4,0},{8,12},{12,8},{16,20},{20,16},{24,28},{28,24},{1,5},{5... | collective-permute-start | bytes 3145736 | tf_op jit(solution)/shard_map/ppermute | solution.py:485
  58.9 1.0 copy-start.10
  59.8 79.1 %all-to-all-start = ((bf16[8,3,4,2,64,128]{5,4,3,2,1,0:T(8,128)(2,1)}), bf16[8,3,4,2,64,128]{5,4,3,2,1,0:T(8,128)(2,1)S(1)}, u32[]{:S(2)}, u32[]{:S(2)}) async-start(bf16[8,3,4,2,64,128]{5,4,3,2,1,0:T(8,128)(2,1)} %get-tuple-element.63), calls=%async_computation | async-start | bytes 6291456 | tf_op jit(solution)/shard_map/all_to_all | solution.py:497
  64.3 70.8 %collective-permute-start.7 = (bf16[1024,512]{1,0:T(8,128)(2,1)}, bf16[1024,512]{1,0:T(8,128)(2,1)}, u32[]{:S(2)}, u32[]{:S(2)}) collective-permute-start(bf16[1024,512]{1,0:T(8,128)(2,1)} %collective-permute-done.3), channel_id=1, source_target_pairs={{8,0},{12,4},{16,24},{20,28},{9,1},{13,5},{17,25},{21,29},{10,2},{... | collective-permute-start | bytes 3145736 | tf_op jit(solution)/shard_map/ppermute | solution.py:485
  68.6 70.3 %copy-start.7 = (bf16[1024,512]{1,0:T(8,128)(2,1)}, bf16[1024,512]{1,0:T(8,128)(2,1)S(1)}, u32[]{:S(2)}) copy-start(bf16[1024,512]{1,0:T(8,128)(2,1)S(1)} %broadcast_select_fusion.1.refs_4_) | copy-start | bytes 3145732
  68.6 70.3 %collective-permute-start.6 = (bf16[1024,512]{1,0:T(8,128)(2,1)S(1)}, bf16[1024,512]{1,0:T(8,128)(2,1)}, u32[]{:S(2)}, u32[]{:S(2)}) collective-permute-start(bf16[1024,512]{1,0:T(8,128)(2,1)S(1)} %broadcast_select_fusion.1.refs_4_), channel_id=1, source_target_pairs={{0,4},{4,0},{8,12},{12,8},{16,20},{20,16},{24,28},{28,24},{1,5},{5... | collective-permute-start | bytes 3145736 | tf_op jit(solution)/shard_map/ppermute | solution.py:485
  137.5 34.6 %collective-permute-start.8 = (bf16[1024,512]{1,0:T(8,128)(2,1)}, bf16[1024,512]{1,0:T(8,128)(2,1)}, u32[]{:S(2)}, u32[]{:S(2)}) collective-permute-start(bf16[1024,512]{1,0:T(8,128)(2,1)} %broadcast_select_fusion.refs_0_.refs_6_), channel_id=1, source_target_pairs={{0,4},{4,0},{8,12},{12,8},{16,20},{20,16},{24,28},{28,24},{1,5},{5... | collective-permute-start | bytes 3145736 | tf_op jit(solution)/shard_map/ppermute | solution.py:485
  138.9 8.7 %copy-start.1 = (bf16[8,3,4,2,64,128]{5,4,3,2,1,0:T(8,128)(2,1)}, bf16[8,3,4,2,64,128]{5,4,3,2,1,0:T(8,128)(2,1)S(1)}, u32[]{:S(2)}) copy-start(bf16[8,3,4,2,64,128]{5,4,3,2,1,0:T(8,128)(2,1)S(1)} %all-to-all-done.chunk_ref) | copy-start | bytes 9437188
  147.6 1.0 copy-start.5
  148.6 36.0 %all-to-all-start.1 = ((bf16[8,4,2,64,128]{4,3,2,1,0:T(8,128)(2,1)}), bf16[8,4,2,64,128]{4,3,2,1,0:T(8,128)(2,1)S(1)}, u32[]{:S(2)}, u32[]{:S(2)}) async-start(bf16[8,4,2,64,128]{4,3,2,1,0:T(8,128)(2,1)} %copy-done.5), calls=%async_computation.1 | async-start | bytes 2097152 | tf_op jit(solution)/shard_map/all_to_all | solution.py:497
  172.1 26.0 %collective-permute-start.9 = (bf16[2,512,512]{2,1,0:T(8,128)(2,1)}, bf16[2,512,512]{2,1,0:T(8,128)(2,1)S(1)}, u32[]{:S(2)}, u32[]{:S(2)}) collective-permute-start(bf16[2,512,512]{2,1,0:T(8,128)(2,1)} %proj_part.8), channel_id=1, source_target_pairs={{0,4},{4,0},{8,12},{12,8},{16,20},{20,16},{24,28},{28,24},{1,5},{5... | collective-permute-start | bytes 3145736 | tf_op jit(solution)/shard_map/ppermute | solution.py:485
  174.3 10.3 %copy-start = (bf16[1024,512]{1,0:T(8,128)(2,1)S(1)}, bf16[1024,512]{1,0:T(8,128)(2,1)}, u32[]{:S(2)}) copy-start(bf16[1024,512]{1,0:T(8,128)(2,1)} %row_forward.1.flat_ref.row_ref) | copy-start | bytes 3145732
  185.2 1.0 copy-start.3
  186.2 1.3 copy-start.4
  197.2 6.7 %copy-start.15 = (bf16[2,512,512]{2,1,0:T(8,128)(2,1)S(1)}, bf16[2,512,512]{2,1,0:T(8,128)(2,1)}, u32[]{:S(2)}) copy-start(bf16[2,512,512]{2,1,0:T(8,128)(2,1)} %proj_part.10) | copy-start | bytes 3145732
  198.1 7.3 %copy-start.13 = (bf16[2,512,512]{2,1,0:T(8,128)(2,1)}, bf16[2,512,512]{2,1,0:T(8,128)(2,1)S(1)}, u32[]{:S(2)}) copy-start(bf16[2,512,512]{2,1,0:T(8,128)(2,1)S(1)} %collective-permute-done.9.refs_0_) | copy-start | bytes 3145732
  198.1 54.9 %all-to-all-start.2 = ((bf16[8,4,2,64,128]{4,3,2,1,0:T(8,128)(2,1)}), bf16[8,4,2,64,128]{4,3,2,1,0:T(8,128)(2,1)}, u32[]{:S(2)}, u32[]{:S(2)}) async-start(bf16[8,4,2,64,128]{4,3,2,1,0:T(8,128)(2,1)} %get-tuple-element.75), calls=%async_computation.2 | async-start | bytes 2097152 | tf_op jit(solution)/shard_map/all_to_all | solution.py:497
  203.9 34.2 %collective-permute-start.12 = (bf16[2,512,512]{2,1,0:T(8,128)(2,1)S(1)}, bf16[2,512,512]{2,1,0:T(8,128)(2,1)S(1)}, u32[]{:S(2)}, u32[]{:S(2)}) collective-permute-start(bf16[2,512,512]{2,1,0:T(8,128)(2,1)S(1)} %copy-done.15), channel_id=1, source_target_pairs={{0,4},{4,0},{8,12},{12,8},{16,20},{20,16},{24,28},{28,24},{1,5},{5... | collective-permute-start | bytes 3145736 | tf_op jit(solution)/shard_map/ppermute | solution.py:485
  210.4 35.3 %collective-permute-start.14 = (bf16[2,512,512]{2,1,0:T(8,128)(2,1)}, bf16[2,512,512]{2,1,0:T(8,128)(2,1)}, u32[]{:S(2)}, u32[]{:S(2)}) collective-permute-start(bf16[2,512,512]{2,1,0:T(8,128)(2,1)} %proj_part.12), channel_id=1, source_target_pairs={{0,8},{4,12},{24,16},{28,20},{1,9},{5,13},{25,17},{29,21},{2,10},{... | collective-permute-start | bytes 3145736 | tf_op jit(solution)/shard_map/ppermute | solution.py:485
  238.1 1.0 copy-start.12
  244.2 8.9 %copy-start.2 = (bf16[8,3,4,2,64,128]{5,4,3,2,1,0:T(8,128)(2,1)S(1)}, bf16[8,3,4,2,64,128]{5,4,3,2,1,0:T(8,128)(2,1)}, u32[]{:S(2)}) copy-start(bf16[8,3,4,2,64,128]{5,4,3,2,1,0:T(8,128)(2,1)} %copy-done.1) | copy-start | bytes 9437188
  244.2 36.3 %collective-permute-start.13 = (bf16[2,512,512]{2,1,0:T(8,128)(2,1)}, bf16[2,512,512]{2,1,0:T(8,128)(2,1)}, u32[]{:S(2)}, u32[]{:S(2)}) collective-permute-start(bf16[2,512,512]{2,1,0:T(8,128)(2,1)} %proj_part.13), channel_id=1, source_target_pairs={{0,8},{4,12},{24,16},{28,20},{1,9},{5,13},{25,17},{29,21},{2,10},{... | collective-permute-start | bytes 3145736 | tf_op jit(solution)/shard_map/ppermute | solution.py:485
  248.5 42.0 %collective-permute-start.19 = (bf16[2,512,512]{2,1,0:T(8,128)(2,1)}, bf16[2,512,512]{2,1,0:T(8,128)(2,1)}, u32[]{:S(2)}, u32[]{:S(2)}) collective-permute-start(bf16[2,512,512]{2,1,0:T(8,128)(2,1)} %add_convert_fusion), channel_id=1, source_target_pairs={{8,16},{12,20},{16,8},{20,12},{9,17},{13,21},{17,9},{21,13},{10,18... | collective-permute-start | bytes 3145736 | tf_op jit(solution)/shard_map/ppermute | solution.py:485
  251.9 33.4 %collective-permute-start.17 = (bf16[2,512,512]{2,1,0:T(8,128)(2,1)}, bf16[2,512,512]{2,1,0:T(8,128)(2,1)}, u32[]{:S(2)}, u32[]{:S(2)}) collective-permute-start(bf16[2,512,512]{2,1,0:T(8,128)(2,1)} %proj_part.9), channel_id=1, source_target_pairs={{0,4},{4,0},{8,12},{12,8},{16,20},{20,16},{24,28},{28,24},{1,5},{5... | collective-permute-start | bytes 3145736 | tf_op jit(solution)/shard_map/ppermute | solution.py:485
  267.5 11.9 %copy-start.14 = (bf16[2,512,512]{2,1,0:T(8,128)(2,1)S(1)}, bf16[2,512,512]{2,1,0:T(8,128)(2,1)}, u32[]{:S(2)}) copy-start(bf16[2,512,512]{2,1,0:T(8,128)(2,1)} %proj_part.11) | copy-start | bytes 3145732
  267.5 12.9 %copy-start.11 = (bf16[2,512,512]{2,1,0:T(8,128)(2,1)S(1)}, bf16[2,512,512]{2,1,0:T(8,128)(2,1)}, u32[]{:S(2)}) copy-start(bf16[2,512,512]{2,1,0:T(8,128)(2,1)} %proj_part.13) | copy-start | bytes 3145732
  279.4 37.2 %collective-permute-start.10 = (bf16[1024,2048]{1,0:T(8,128)(2,1)}, bf16[1024,2048]{1,0:T(8,128)(2,1)}, u32[]{:S(2)}, u32[]{:S(2)}) collective-permute-start(bf16[1024,2048]{1,0:T(8,128)(2,1)} %layer_part.3), channel_id=1, source_target_pairs={{0,1},{1,0},{2,3},{3,2},{4,5},{5,4},{6,7},{7,6},{8,9},{9,8},{10,11... | collective-permute-start | bytes 12582920 | tf_op jit(solution)/shard_map/ppermute | solution.py:513
  279.4 25.7 %collective-permute-start.16 = (bf16[2,512,512]{2,1,0:T(8,128)(2,1)S(1)}, bf16[2,512,512]{2,1,0:T(8,128)(2,1)}, u32[]{:S(2)}, u32[]{:S(2)}) collective-permute-start(bf16[2,512,512]{2,1,0:T(8,128)(2,1)S(1)} %copy-done.14), channel_id=1, source_target_pairs={{0,4},{4,0},{8,12},{12,8},{16,20},{20,16},{24,28},{28,24},{1,5},{5... | collective-permute-start | bytes 3145736 | tf_op jit(solution)/shard_map/ppermute | solution.py:485
  282.0 29.3 %collective-permute-start.15 = (bf16[2,512,512]{2,1,0:T(8,128)(2,1)S(1)}, bf16[2,512,512]{2,1,0:T(8,128)(2,1)}, u32[]{:S(2)}, u32[]{:S(2)}) collective-permute-start(bf16[2,512,512]{2,1,0:T(8,128)(2,1)S(1)} %add_convert_fusion.1), channel_id=1, source_target_pairs={{8,16},{12,20},{16,8},{20,12},{9,17},{13,21},{17,9},{21,13},{10,18... | collective-permute-start | bytes 3145736 | tf_op jit(solution)/shard_map/ppermute | solution.py:485
  291.9 14.2 %collective-permute-start.20 = (bf16[512,512]{1,0:T(8,128)(2,1)S(1)}, bf16[512,512]{1,0:T(8,128)(2,1)}, u32[]{:S(2)}, u32[]{:S(2)}) collective-permute-start(bf16[512,512]{1,0:T(8,128)(2,1)S(1)} %fusion.5), channel_id=1, source_target_pairs={{8,0},{12,4},{16,24},{20,28},{9,1},{13,5},{17,25},{21,29},{10,2},{... | collective-permute-start | bytes 1572872 | tf_op jit(solution)/shard_map/ppermute | solution.py:485
  295.4 15.9 %collective-permute-start.18 = (bf16[512,512]{1,0:T(8,128)(2,1)}, bf16[512,512]{1,0:T(8,128)(2,1)}, u32[]{:S(2)}, u32[]{:S(2)}) collective-permute-start(bf16[512,512]{1,0:T(8,128)(2,1)} %bitcast.53), channel_id=1, source_target_pairs={{0,8},{4,12},{24,16},{28,20},{1,9},{5,13},{25,17},{29,21},{2,10},{... | collective-permute-start | bytes 1572872 | tf_op jit(solution)/shard_map/ppermute | solution.py:485
  311.3 72.3 %all-to-all-start.3 = ((bf16[8,3,4,2,64,128]{5,4,3,2,1,0:T(8,128)(2,1)}), bf16[8,3,4,2,64,128]{5,4,3,2,1,0:T(8,128)(2,1)S(1)}, u32[]{:S(2)}, u32[]{:S(2)}) async-start(bf16[8,3,4,2,64,128]{5,4,3,2,1,0:T(8,128)(2,1)} %column_backward.1), calls=%async_computation.3 | async-start | bytes 6291456 | tf_op jit(solution)/shard_map/all_to_all | solution.py:497
  325.1 46.4 %collective-permute-start.11 = (bf16[1024,1024]{1,0:T(8,128)(2,1)}, bf16[1024,1024]{1,0:T(8,128)(2,1)}, u32[]{:S(2)}, u32[]{:S(2)}) collective-permute-start(bf16[1024,1024]{1,0:T(8,128)(2,1)} %layer_part.4), channel_id=1, source_target_pairs={{0,2},{1,3},{2,0},{3,1},{4,6},{5,7},{6,4},{7,5},{8,10},{9,11},{10,... | collective-permute-start | bytes 6291464 | tf_op jit(solution)/shard_map/ppermute | solution.py:513
  332.5 48.1 %collective-permute-start.21 = (bf16[512,512]{1,0:T(8,128)(2,1)}, bf16[512,512]{1,0:T(8,128)(2,1)}, u32[]{:S(2)}, u32[]{:S(2)}) collective-permute-start(bf16[512,512]{1,0:T(8,128)(2,1)} %bitcast.52), channel_id=1, source_target_pairs={{0,8},{4,12},{24,16},{28,20},{1,9},{5,13},{25,17},{29,21},{2,10},{... | collective-permute-start | bytes 1572872 | tf_op jit(solution)/shard_map/ppermute | solution.py:485
  336.0 44.7 %collective-permute-start.22 = (bf16[512,512]{1,0:T(8,128)(2,1)}, bf16[512,512]{1,0:T(8,128)(2,1)}, u32[]{:S(2)}, u32[]{:S(2)}) collective-permute-start(bf16[512,512]{1,0:T(8,128)(2,1)} %fusion), channel_id=1, source_target_pairs={{8,0},{12,4},{16,24},{20,28},{9,1},{13,5},{17,25},{21,29},{10,2},{... | collective-permute-start | bytes 1572872 | tf_op jit(solution)/shard_map/ppermute | solution.py:485
  383.6 1.6 copy-start.6

commit v13 on v12

--- a/solution.py
+++ b/solution.py
@@ -585,11 +585,10 @@
     (row_far,) = summed(after(row_out, *column_close), far, row_far, 0)
     row_far_in = links.along(row_far, INWARD)
     row_close = exchanged([after(part, *column_far) for part in row_close])
-    (column_far,) = summed(column_out, far, column_far, 0)
+    gradients = column_backward(chunks, after(grads, row_far))
+    (column_far,) = summed(after(column_out, gradients), far, column_far, 0)
     column_far_in = links.along(column_far, INWARD)
-    row_middle = add(row_far, row_far_in)
-    row_cross = links.along(row_middle, CROSS)
-    gradients = column_backward(chunks, after(grads, row_far))
+    row_cross = links.along(add(row_far, row_far_in), CROSS)
     layer = LayerSum(ids, after(flat, gradients), blocks, heads_n)
     layer.start()
     column_close = exchanged(column_close)
@@ -597,9 +596,9 @@
     row_near, row_own = summed(after(row_out, gradients), close, row_close, 1)
     row_near_in = links.along(row_near[0], INWARD)
     row_back = links.along(add(row_near[0], row_cross[1]), OUTWARD)
-    column_grads = swap(after(gradients, column_cross, *column_close, row_near_in, row_back))
-
     layer.turn(gradients)
+    column_grads = swap(after(gradients, *layer.parts, column_cross, *column_close, row_near_in, row_back))
+
     column_near, column_own = summed(after(column_out, gradients), close, column_close, 1)
     column_near_in = links.along(column_near[0], INWARD)
     row_grads = row_backward(*by_head, after(grad_row, gradients))

time: 397 us -> 427 us (1.076)
  waiting for transfers between devices: 136 us -> 163 us
    all_to_all x4, waiting for transfers between devices: 0.01 us -> 17.7 us  [swap(): lax.all_to_all(chunks, 'ctx', split_axis=0, concat_axis=0, tiled=True)]
    ppermute x21, waiting for transfers between devices: 122 us -> 133 us  [send(): out = lax.ppermute(value, 'ctx', pairs)]
  transfers between devices with their start and end apart: 27 -> 27, of which waited for: 11 -> 13; matrix products, arithmetic and copies ran while one was open for 6% -> 5% of each run, Pallas kernels for 38% -> 30%
where the time goes in v13:
time: 427 us; the launch traced here: 422 us
  waiting for transfers between devices  163 us (38%)
  Pallas kernels  158 us (37%)
  starting transfers between devices  70.4 us (16%)
  other arithmetic  18.5 us (4%)
  local copies, waits for them, and re-layouts  10.2 us (2%)
    ppermute x21, waiting for transfers between devices, send(): out = lax.ppermute(value, 'ctx', pairs)  133 us
    ppermute x21, starting transfers between devices, send(): out = lax.ppermute(value, 'ctx', pairs)  46.7 us
    pallas_call x8, Pallas kernels, proj_part(): pl.pallas_call(functools.partial(proj_kernel, lead, len(extra), dim), gri...  40.3 us
    pallas_call x3, Pallas kernels, layer_part(): pl.pallas_call(functools.partial(layer_kernel, n, count, len(extra)), gri...  29.5 us
    pallas_call x2, Pallas kernels, attn_grad(): pl.pallas_call(functools.partial(attn_grad_kernel, m, dim, last), grid_sp...  27 us
    all_to_all x4, starting transfers between devices, swap(): lax.all_to_all(chunks, 'ctx', split_axis=0, concat_axis=0, tiled=True)  22.1 us
    all_to_all x4, waiting for transfers between devices, swap(): lax.all_to_all(chunks, 'ctx', split_axis=0, concat_axis=0, tiled=True)  17.7 us
    pallas_call x1, Pallas kernels, column_backward(): pl.pallas_call(functools.partial(column_backward_kernel, dim ** (-0.5)),...  14.5 us
  transfers between devices with their start and end apart: 27, of which 13 were waited for; matrix products, arithmetic and copies ran while one was open for 5% of the time, Pallas kernels for 30%

profile of v13, /device:TPU:8, one launch (start us, length us, event | category | flops | bytes accessed | tf_op | source)
XLA Modules:
  0.0 422.0 jit_solution(4653525186581817206)
XLA Ops:
  0.6 3.5 collective-permute-start.4
  4.2 1.6 collective-permute-start.1
  5.8 7.1 %split_inputs.1 = (bf16[8,3,4,2,64,128]{5,4,3,2,1,0:T(8,128)(2,1)}, bf16[4,1024,128]{2,1,0:T(8,128)(2,1)}, bf16[4,1024,128]{2,1,0:T(8,128)(2,1)}, bf16[4,1024,128]{2,1,0:T(8,128)(2,1)}) custom-call(bf16[1024,8,128]{2,1,0:T(8,128)(2,1)} %q_ref.1, bf16[1024,8,128]{2,1,0:T(8,128)(2,1)} %k_ref.1, bf16[1024,8,128]{2,1,0:T(8,128)(2,1)} %v_ref.1), custom_call_target="tpu_custom_call" | custom-call | tf_op jit(solution)/shard_map/split_inputs/pallas_call | solution.py:48
  12.9 14.9 %collective-permute-done.4 = bf16[1024,512]{1,0:T(8,128)(2,1)} collective-permute-done((bf16[1024,512]{1,0:T(8,128)(2,1)}, bf16[1024,512]{1,0:T(8,128)(2,1)}, u32[]{:S(2)}, u32[]{:S(2)}) %collective-permute-start.4) | collective-permute-done | bytes 1048608 | tf_op jit(solution)/shard_map/ppermute | solution.py:485
  29.0 3.2 collective-permute-start.5
  32.2 3.1 collective-permute-start.3
  35.3 1.6 collective-permute-start.2
  36.9 9.9 %row_forward.1.flat_ref.row_ref = bf16[1024,512]{1,0:T(8,128)(2,1)} custom-call(bf16[4,1024,128]{2,1,0:T(8,128)(2,1)} %get-tuple-element.57.q_ref, bf16[4,1024,128]{2,1,0:T(8,128)(2,1)} %get-tuple-element.58.k_ref, bf16[4,1024,128]{2,1,0:T(8,128)(2,1)} %get-tuple-element.59.v_ref), custom_call_target="tpu_custom_call" | custom-call | flops 1073741824 | bytes 4194304 | tf_op jit(solution)/shard_map/row_forward/pallas_call | solution.py:321
  47.4 4.9 %proj_part.9 = bf16[2,512,512]{2,1,0:T(8,128)(2,1)} custom-call(s32[2]{0:T(128)} %pad_add_fusion.2.order, bf16[1024,512]{1,0:T(8,128)(2,1)} %row_forward.1.flat_ref.row_ref, bf16[1024,4096]{1,0:T(8,128)(2,1)} %grad_ref.18), custom_call_target="tpu_custom_call" | custom-call | flops 1073741824 | bytes 4194304 | tf_op jit(solution)/shard_map/proj_part/pallas_call | solution.py:275
  52.9 4.9 %proj_part.8 = bf16[2,512,512]{2,1,0:T(8,128)(2,1)} custom-call(s32[2]{0:T(128)} %pad_add_fusion.1.order, bf16[1024,512]{1,0:T(8,128)(2,1)} %row_forward.1.flat_ref.row_ref, bf16[1024,4096]{1,0:T(8,128)(2,1)} %grad_ref.18), custom_call_target="tpu_custom_call" | custom-call | flops 1073741824 | bytes 4194304 | tf_op jit(solution)/shard_map/proj_part/pallas_call | solution.py:275
  59.8 4.5 %all-to-all-start = ((bf16[8,3,4,2,64,128]{5,4,3,2,1,0:T(8,128)(2,1)}), bf16[8,3,4,2,64,128]{5,4,3,2,1,0:T(8,128)(2,1)S(1)}, u32[]{:S(2)}, u32[]{:S(2)}) async-start(bf16[8,3,4,2,64,128]{5,4,3,2,1,0:T(8,128)(2,1)} %get-tuple-element.63), calls=%async_computation | async-start | bytes 6291456 | tf_op jit(solution)/shard_map/all_to_all | solution.py:497
  64.3 2.9 collective-permute-start.7
  68.5 2.1 collective-permute-start.6
  70.6 64.5 %collective-permute-done.7 = bf16[1024,512]{1,0:T(8,128)(2,1)} collective-permute-done((bf16[1024,512]{1,0:T(8,128)(2,1)}, bf16[1024,512]{1,0:T(8,128)(2,1)}, u32[]{:S(2)}, u32[]{:S(2)}) %collective-permute-start.7) | collective-permute-done | bytes 1048608 | tf_op jit(solution)/shard_map/ppermute | solution.py:485
  135.1 2.3 broadcast_select_fusion.refs_0_.refs_6_
  138.9 8.7 %column_forward.1 = bf16[8,4,2,64,128]{4,3,2,1,0:T(8,128)(2,1)S(1)} custom-call(bf16[8,3,4,2,64,128]{5,4,3,2,1,0:T(8,128)(2,1)S(1)} %all-to-all-done.chunk_ref), custom_call_target="tpu_custom_call" | custom-call | flops 536870912 | bytes 4194304 | tf_op jit(solution)/shard_map/column_forward/pallas_call | solution.py:413
  148.6 6.2 %all-to-all-start.1 = ((bf16[8,4,2,64,128]{4,3,2,1,0:T(8,128)(2,1)}), bf16[8,4,2,64,128]{4,3,2,1,0:T(8,128)(2,1)S(1)}, u32[]{:S(2)}, u32[]{:S(2)}) async-start(bf16[8,4,2,64,128]{4,3,2,1,0:T(8,128)(2,1)} %copy-done.5), calls=%async_computation.1 | async-start | bytes 2097152 | tf_op jit(solution)/shard_map/all_to_all | solution.py:497
  155.4 16.7 %attn_grad.2.refs_2_ = f32[1024,1024]{1,0:T(8,128)} custom-call(s32[6]{0:T(128)} %stack.114.ids, bf16[1024,4096]{1,0:T(8,128)(2,1)} %grad_ref.18, bf16[1024,512]{1,0:T(8,128)(2,1)} %refs_0_.7, bf16[1024,512]{1,0:T(8,128)(2,1)} %copy-done.9, bf16[1024,512]{1,0:T(8,128)(2,1)} %copy-done.8, bf16[1024,512]{1,0:T(8,128)(2,1)} %copy-done.10, ...), custom_call_target="tpu_custom_call" | custom-call | flops 6442450944 | bytes 16777216 | tf_op jit(solution)/shard_map/attn_grad/pallas_call | solution.py:163
  174.3 10.3 %attn_grad.3 = (bf16[1024,512]{1,0:T(8,128)(2,1)}, bf16[8,4,2,64,128]{4,3,2,1,0:T(8,128)(2,1)}) custom-call(s32[2]{0:T(128)} %pad_add_fusion.3.ids, bf16[1024,4096]{1,0:T(8,128)(2,1)} %grad_ref.18, bf16[1024,512]{1,0:T(8,128)(2,1)} %broadcast_select_fusion.refs_0_.refs_6_, bf16[1024,512]{1,0:T(8,128)(2,1)} %collective-permute-done.8.refs_1_.refs_7_, ...), custom_call_target="tpu_custom_call" | custom-call | flops 2147483648 | bytes 8388608 | tf_op jit(solution)/shard_map/attn_grad/pallas_call | solution.py:163
  187.6 4.8 %proj_part.11 = bf16[2,512,512]{2,1,0:T(8,128)(2,1)} custom-call(s32[2]{0:T(128)} %pad_add_fusion.2.order, bf16[1024,512]{1,0:T(8,128)(2,1)} %copy-done.3, bf16[1024,4096]{1,0:T(8,128)(2,1)} %grad_ref.18), custom_call_target="tpu_custom_call" | custom-call | flops 1073741824 | bytes 4194304 | tf_op jit(solution)/shard_map/proj_part/pallas_call | solution.py:275
  192.4 4.8 %proj_part.10 = bf16[2,512,512]{2,1,0:T(8,128)(2,1)} custom-call(s32[2]{0:T(128)} %pad_add_fusion.1.order, bf16[1024,512]{1,0:T(8,128)(2,1)} %copy-done.3, bf16[1024,4096]{1,0:T(8,128)(2,1)} %grad_ref.18), custom_call_target="tpu_custom_call" | custom-call | flops 1073741824 | bytes 4194304 | tf_op jit(solution)/shard_map/proj_part/pallas_call | solution.py:275
  198.1 5.1 %all-to-all-start.2 = ((bf16[8,4,2,64,128]{4,3,2,1,0:T(8,128)(2,1)}), bf16[8,4,2,64,128]{4,3,2,1,0:T(8,128)(2,1)}, u32[]{:S(2)}, u32[]{:S(2)}) async-start(bf16[8,4,2,64,128]{4,3,2,1,0:T(8,128)(2,1)} %get-tuple-element.75), calls=%async_computation.2 | async-start | bytes 2097152 | tf_op jit(solution)/shard_map/all_to_all | solution.py:497
  205.1 5.3 %proj_part.12 = bf16[2,512,512]{2,1,0:T(8,128)(2,1)} custom-call(s32[2]{0:T(128)} %pad_add_fusion.4.order, bf16[1024,512]{1,0:T(8,128)(2,1)} %row_forward.1.flat_ref.row_ref, bf16[1024,4096]{1,0:T(8,128)(2,1)} %grad_ref.18, bf16[2,512,512]{2,1,0:T(8,128)(2,1)} %copy-done.15), custom_call_target="tpu_custom_call" | custom-call | flops 1073741824 | bytes 5242880 | tf_op jit(solution)/shard_map/proj_part/pallas_call | solution.py:275
  210.4 15.7 %all-to-all-done.2.grad_ref = bf16[8,4,2,64,128]{4,3,2,1,0:T(8,128)(2,1)} async-done(((bf16[8,4,2,64,128]{4,3,2,1,0:T(8,128)(2,1)}), bf16[8,4,2,64,128]{4,3,2,1,0:T(8,128)(2,1)}, u32[]{:S(2)}, u32[]{:S(2)}) %all-to-all-start.2) | async-done | bytes 1048608 | tf_op jit(solution)/shard_map/all_to_all | solution.py:497
  226.1 14.5 %column_backward.1 = bf16[8,3,4,2,64,128]{5,4,3,2,1,0:T(8,128)(2,1)} custom-call(bf16[8,3,4,2,64,128]{5,4,3,2,1,0:T(8,128)(2,1)S(1)} %copy-done.2, bf16[8,4,2,64,128]{4,3,2,1,0:T(8,128)(2,1)} %all-to-all-done.2.grad_ref), custom_call_target="tpu_custom_call" | custom-call | flops 1342177280 | bytes 7340032 | tf_op jit(solution)/shard_map/column_backward/pallas_call | solution.py:451
  240.6 11.8 %layer_part.3 = bf16[1024,2048]{1,0:T(8,128)(2,1)} custom-call(s32[8]{0:T(128)} %stack.107.ids, s32[4]{0:T(128)} %pad_add_fusion.5.wanted, bf16[1024,1024]{1,0:T(8,128)(2,1)} %copy-done.4, bf16[1024,512]{1,0:T(8,128)(2,1)} %refs_0_.7, bf16[1024,512]{1,0:T(8,128)(2,1)} %copy-done.9, bf16[1024,512]{1,0:T(8,128)(2,1)} %copy-done.8, ...), custom_call_target="tpu_custom_call" | custom-call | flops 4294967296 | bytes 10485760 | tf_op jit(solution)/shard_map/layer_part/pallas_call | solution.py:221
  254.3 24.0 %collective-permute-done.12.refs_0_ = bf16[2,512,512]{2,1,0:T(8,128)(2,1)S(1)} collective-permute-done((bf16[2,512,512]{2,1,0:T(8,128)(2,1)}, bf16[2,512,512]{2,1,0:T(8,128)(2,1)S(1)}, u32[]{:S(2)}, u32[]{:S(2)}) %collective-permute-start.12) | collective-permute-done | bytes 1048608 | tf_op jit(solution)/shard_map/ppermute | solution.py:485
  279.3 5.0 %proj_part.13 = bf16[2,512,512]{2,1,0:T(8,128)(2,1)} custom-call(s32[2]{0:T(128)} %pad_add_fusion.4.order, bf16[1024,512]{1,0:T(8,128)(2,1)} %copy-done.3, bf16[1024,4096]{1,0:T(8,128)(2,1)} %grad_ref.18, bf16[2,512,512]{2,1,0:T(8,128)(2,1)} %copy-done.16), custom_call_target="tpu_custom_call" | custom-call | flops 1073741824 | bytes 5242880 | tf_op jit(solution)/shard_map/proj_part/pallas_call | solution.py:275
  287.5 3.4 collective-permute-start.19
  292.4 19.7 %collective-permute-done.13 = bf16[2,512,512]{2,1,0:T(8,128)(2,1)S(1)} collective-permute-done((bf16[2,512,512]{2,1,0:T(8,128)(2,1)}, bf16[2,512,512]{2,1,0:T(8,128)(2,1)S(1)}, u32[]{:S(2)}, u32[]{:S(2)}) %collective-permute-start.13) | collective-permute-done | bytes 1048608 | tf_op jit(solution)/shard_map/ppermute | solution.py:485
  312.4 2.6 collective-permute-start.15
  315.6 5.3 %proj_part.14 = (bf16[1,512,512]{2,1,0:T(8,128)(2,1)}, bf16[1,512,512]{2,1,0:T(8,128)(2,1)}) custom-call(s32[2]{0:T(128)} %pad_add_fusion.7.order, bf16[1024,512]{1,0:T(8,128)(2,1)} %row_forward.1.flat_ref.row_ref, bf16[1024,4096]{1,0:T(8,128)(2,1)} %grad_ref.18, bf16[2,512,512]{2,1,0:T(8,128)(2,1)} %collective-permute-done.17.refs_0_), custom_call_target="tpu_custom_call" | custom-call | flops 1073741824 | bytes 5242880 | tf_op jit(solution)/shard_map/proj_part/pallas_call | solution.py:275
  322.2 2.4 fusion.5
  324.6 6.1 %collective-permute-start.20 = (bf16[512,512]{1,0:T(8,128)(2,1)}, bf16[512,512]{1,0:T(8,128)(2,1)}, u32[]{:S(2)}, u32[]{:S(2)}) collective-permute-start(bf16[512,512]{1,0:T(8,128)(2,1)} %fusion.5), channel_id=1, source_target_pairs={{8,0},{12,4},{16,24},{20,28},{9,1},{13,5},{17,25},{21,29},{10,2},{... | collective-permute-start | bytes 1572872 | tf_op jit(solution)/shard_map/ppermute | solution.py:485
  331.3 8.5 %layer_part.4 = bf16[1024,1024]{1,0:T(8,128)(2,1)} custom-call(s32[8]{0:T(128)} %stack.107.ids, s32[2]{0:T(128)} %pad_add_fusion.6.wanted, bf16[1024,1024]{1,0:T(8,128)(2,1)} %copy-done.4, bf16[1024,512]{1,0:T(8,128)(2,1)} %refs_0_.7, bf16[1024,512]{1,0:T(8,128)(2,1)} %copy-done.9, bf16[1024,512]{1,0:T(8,128)(2,1)} %copy-done.8, ...), custom_call_target="tpu_custom_call" | custom-call | flops 2147483648 | bytes 6291456 | tf_op jit(solution)/shard_map/layer_part/pallas_call | solution.py:221
  341.0 6.4 %all-to-all-start.3 = ((bf16[8,3,4,2,64,128]{5,4,3,2,1,0:T(8,128)(2,1)}), bf16[8,3,4,2,64,128]{5,4,3,2,1,0:T(8,128)(2,1)S(1)}, u32[]{:S(2)}, u32[]{:S(2)}) async-start(bf16[8,3,4,2,64,128]{5,4,3,2,1,0:T(8,128)(2,1)} %column_backward.1), calls=%async_computation.3 | async-start | bytes 6291456 | tf_op jit(solution)/shard_map/all_to_all | solution.py:497
  349.5 5.3 %proj_part.15 = (bf16[1,512,512]{2,1,0:T(8,128)(2,1)}, bf16[1,512,512]{2,1,0:T(8,128)(2,1)}) custom-call(s32[2]{0:T(128)} %pad_add_fusion.7.order, bf16[1024,512]{1,0:T(8,128)(2,1)} %copy-done.3, bf16[1024,4096]{1,0:T(8,128)(2,1)} %grad_ref.18, bf16[2,512,512]{2,1,0:T(8,128)(2,1)} %collective-permute-done.16.refs_0_), custom_call_target="tpu_custom_call" | custom-call | flops 1073741824 | bytes 5242880 | tf_op jit(solution)/shard_map/proj_part/pallas_call | solution.py:275
  356.1 2.1 fusion
  358.2 6.1 %collective-permute-start.22 = (bf16[512,512]{1,0:T(8,128)(2,1)}, bf16[512,512]{1,0:T(8,128)(2,1)}, u32[]{:S(2)}, u32[]{:S(2)}) collective-permute-start(bf16[512,512]{1,0:T(8,128)(2,1)} %fusion), channel_id=1, source_target_pairs={{8,0},{12,4},{16,24},{20,28},{9,1},{13,5},{17,25},{21,29},{10,2},{... | collective-permute-start | bytes 1572872 | tf_op jit(solution)/shard_map/ppermute | solution.py:485
  364.4 13.6 %row_backward.1 = (bf16[4,1024,128]{2,1,0:T(8,128)(2,1)}, bf16[4,1024,128]{2,1,0:T(8,128)(2,1)}, bf16[4,1024,128]{2,1,0:T(8,128)(2,1)}) custom-call(bf16[4,1024,128]{2,1,0:T(8,128)(2,1)} %get-tuple-element.57.q_ref, bf16[4,1024,128]{2,1,0:T(8,128)(2,1)} %get-tuple-element.58.k_ref, bf16[4,1024,128]{2,1,0:T(8,128)(2,1)} %get-tuple-element.59.v_ref, ...), custom_call_target="tpu_custom_call" | custom-call | flops 2684354560 | bytes 7340032 | tf_op jit(solution)/shard_map/row_backward/pallas_call | solution.py:355
  378.0 1.8 fusion.4
  379.8 12.7 %collective-permute-done.11.refs_9_ = bf16[1024,1024]{1,0:T(8,128)(2,1)} collective-permute-done((bf16[1024,1024]{1,0:T(8,128)(2,1)}, bf16[1024,1024]{1,0:T(8,128)(2,1)}, u32[]{:S(2)}, u32[]{:S(2)}) %collective-permute-start.11) | collective-permute-done | bytes 2097184 | tf_op jit(solution)/shard_map/ppermute | solution.py:513
  392.4 9.2 %layer_part.5 = bf16[1024,1024]{1,0:T(8,128)(2,1)} custom-call(s32[8]{0:T(128)} %stack.107.ids, s32[2]{0:T(128)} %pad_add_fusion.wanted, bf16[1024,1024]{1,0:T(8,128)(2,1)} %copy-done.4, bf16[1024,512]{1,0:T(8,128)(2,1)} %refs_0_.7, bf16[1024,512]{1,0:T(8,128)(2,1)} %copy-done.9, bf16[1024,512]{1,0:T(8,128)(2,1)} %copy-done.8, bf16[1024,512]{1,0:T(8,128)(2,1)} %copy-done.10, ...), custom_call_target="tpu_custom_call" | custom-call | flops 2147483648 | bytes 6291456 | tf_op jit(solution)/shard_map/layer_part/pallas_call | solution.py:221
  401.6 6.5 %collective-permute-done.21 = bf16[512,512]{1,0:T(8,128)(2,1)} collective-permute-done((bf16[512,512]{1,0:T(8,128)(2,1)}, bf16[512,512]{1,0:T(8,128)(2,1)}, u32[]{:S(2)}, u32[]{:S(2)}) %collective-permute-start.21) | collective-permute-done | bytes 524320 | tf_op jit(solution)/shard_map/ppermute | solution.py:485
  408.1 1.8 fusion.2
  411.1 1.9 all-to-all-done.3.chunk_ref
  413.0 1.6 copy-done.6
  414.7 7.3 %join_gradients.1 = (bf16[1024,8,128]{2,1,0:T(8,128)(2,1)}, bf16[1024,8,128]{2,1,0:T(8,128)(2,1)}, bf16[1024,8,128]{2,1,0:T(8,128)(2,1)}) custom-call(bf16[8,3,4,2,64,128]{5,4,3,2,1,0:T(8,128)(2,1)} %copy-done.6, bf16[4,1024,128]{2,1,0:T(8,128)(2,1)} %get-tuple-element.97.refs_0_, bf16[4,1024,128]{2,1,0:T(8,128)(2,1)} %get-tuple-element.98.refs_1_, ...), custom_call_target="tpu_custom_call" | custom-call | tf_op jit(solution)/shard_map/join_gradients/pallas_call | solution.py:78
  (80 shorter events, 33.1 us)
Async XLA Ops:
  0.6 27.1 %collective-permute-start.4 = (bf16[1024,512]{1,0:T(8,128)(2,1)}, bf16[1024,512]{1,0:T(8,128)(2,1)}, u32[]{:S(2)}, u32[]{:S(2)}) collective-permute-start(bf16[1024,512]{1,0:T(8,128)(2,1)} %refs_0_.7), channel_id=1, source_target_pairs={{8,16},{12,20},{16,8},{20,12},{9,17},{13,21},{17,9},{21,13},{10,18... | collective-permute-start | bytes 3145736 | tf_op jit(solution)/shard_map/ppermute | solution.py:485
  4.1 24.9 %collective-permute-start = (bf16[1024,512]{1,0:T(8,128)(2,1)}, bf16[1024,512]{1,0:T(8,128)(2,1)S(1)}, u32[]{:S(2)}, u32[]{:S(2)}) collective-permute-start(bf16[1024,512]{1,0:T(8,128)(2,1)} %refs_0_.7), channel_id=1, source_target_pairs={{0,8},{4,12},{8,0},{12,4},{16,24},{20,28},{24,16},{28,20},{1,9},{5... | collective-permute-start | bytes 3145736 | tf_op jit(solution)/shard_map/ppermute | solution.py:485
  4.2 28.0 %collective-permute-start.1 = (bf16[1024,512]{1,0:T(8,128)(2,1)}, bf16[1024,512]{1,0:T(8,128)(2,1)S(1)}, u32[]{:S(2)}, u32[]{:S(2)}) collective-permute-start(bf16[1024,512]{1,0:T(8,128)(2,1)} %refs_0_.7), channel_id=1, source_target_pairs={{0,4},{4,0},{8,12},{12,8},{16,20},{20,16},{24,28},{28,24},{1,5},{5... | collective-permute-start | bytes 3145736 | tf_op jit(solution)/shard_map/ppermute | solution.py:485
  29.0 17.8 %copy-start.8 = (bf16[1024,512]{1,0:T(8,128)(2,1)}, bf16[1024,512]{1,0:T(8,128)(2,1)S(1)}, u32[]{:S(2)}) copy-start(bf16[1024,512]{1,0:T(8,128)(2,1)S(1)} %collective-permute-done.refs_2_) | copy-start | bytes 3145732
  29.0 28.7 %collective-permute-start.5 = (bf16[1024,512]{1,0:T(8,128)(2,1)}, bf16[1024,512]{1,0:T(8,128)(2,1)}, u32[]{:S(2)}, u32[]{:S(2)}) collective-permute-start(bf16[1024,512]{1,0:T(8,128)(2,1)} %collective-permute-done.4), channel_id=1, source_target_pairs={{8,0},{12,4},{16,24},{20,28},{9,1},{13,5},{17,25},{21,29},{10,2},{... | collective-permute-start | bytes 3145736 | tf_op jit(solution)/shard_map/ppermute | solution.py:485
  32.2 14.6 %copy-start.9 = (bf16[1024,512]{1,0:T(8,128)(2,1)}, bf16[1024,512]{1,0:T(8,128)(2,1)S(1)}, u32[]{:S(2)}) copy-start(bf16[1024,512]{1,0:T(8,128)(2,1)S(1)} %collective-permute-done.1.refs_1_) | copy-start | bytes 3145732
  32.2 25.7 %collective-permute-start.3 = (bf16[1024,512]{1,0:T(8,128)(2,1)S(1)}, bf16[1024,512]{1,0:T(8,128)(2,1)}, u32[]{:S(2)}, u32[]{:S(2)}) collective-permute-start(bf16[1024,512]{1,0:T(8,128)(2,1)S(1)} %collective-permute-done.refs_2_), channel_id=1, source_target_pairs={{8,16},{12,20},{16,8},{20,12},{9,17},{13,21},{17,9},{21,13},{10,18... | collective-permute-start | bytes 3145736 | tf_op jit(solution)/shard_map/ppermute | solution.py:485
  35.3 23.5 %collective-permute-start.2 = (bf16[1024,512]{1,0:T(8,128)(2,1)S(1)}, bf16[1024,512]{1,0:T(8,128)(2,1)S(1)}, u32[]{:S(2)}, u32[]{:S(2)}) collective-permute-start(bf16[1024,512]{1,0:T(8,128)(2,1)S(1)} %collective-permute-done.refs_2_), channel_id=1, source_target_pairs={{0,4},{4,0},{8,12},{12,8},{16,20},{20,16},{24,28},{28,24},{1,5},{5... | collective-permute-start | bytes 3145736 | tf_op jit(solution)/shard_map/ppermute | solution.py:485
  58.9 1.0 copy-start.10
  59.8 79.1 %all-to-all-start = ((bf16[8,3,4,2,64,128]{5,4,3,2,1,0:T(8,128)(2,1)}), bf16[8,3,4,2,64,128]{5,4,3,2,1,0:T(8,128)(2,1)S(1)}, u32[]{:S(2)}, u32[]{:S(2)}) async-start(bf16[8,3,4,2,64,128]{5,4,3,2,1,0:T(8,128)(2,1)} %get-tuple-element.63), calls=%async_computation | async-start | bytes 6291456 | tf_op jit(solution)/shard_map/all_to_all | solution.py:497
  64.3 70.8 %collective-permute-start.7 = (bf16[1024,512]{1,0:T(8,128)(2,1)}, bf16[1024,512]{1,0:T(8,128)(2,1)}, u32[]{:S(2)}, u32[]{:S(2)}) collective-permute-start(bf16[1024,512]{1,0:T(8,128)(2,1)} %collective-permute-done.3), channel_id=1, source_target_pairs={{8,0},{12,4},{16,24},{20,28},{9,1},{13,5},{17,25},{21,29},{10,2},{... | collective-permute-start | bytes 3145736 | tf_op jit(solution)/shard_map/ppermute | solution.py:485
  68.5 70.3 %copy-start.7 = (bf16[1024,512]{1,0:T(8,128)(2,1)}, bf16[1024,512]{1,0:T(8,128)(2,1)S(1)}, u32[]{:S(2)}) copy-start(bf16[1024,512]{1,0:T(8,128)(2,1)S(1)} %broadcast_select_fusion.1.refs_4_) | copy-start | bytes 3145732
  68.5 70.3 %collective-permute-start.6 = (bf16[1024,512]{1,0:T(8,128)(2,1)S(1)}, bf16[1024,512]{1,0:T(8,128)(2,1)}, u32[]{:S(2)}, u32[]{:S(2)}) collective-permute-start(bf16[1024,512]{1,0:T(8,128)(2,1)S(1)} %broadcast_select_fusion.1.refs_4_), channel_id=1, source_target_pairs={{0,4},{4,0},{8,12},{12,8},{16,20},{20,16},{24,28},{28,24},{1,5},{5... | collective-permute-start | bytes 3145736 | tf_op jit(solution)/shard_map/ppermute | solution.py:485
  137.5 34.6 %collective-permute-start.8 = (bf16[1024,512]{1,0:T(8,128)(2,1)}, bf16[1024,512]{1,0:T(8,128)(2,1)}, u32[]{:S(2)}, u32[]{:S(2)}) collective-permute-start(bf16[1024,512]{1,0:T(8,128)(2,1)} %broadcast_select_fusion.refs_0_.refs_6_), channel_id=1, source_target_pairs={{0,4},{4,0},{8,12},{12,8},{16,20},{20,16},{24,28},{28,24},{1,5},{5... | collective-permute-start | bytes 3145736 | tf_op jit(solution)/shard_map/ppermute | solution.py:485
  138.9 8.7 %copy-start.1 = (bf16[8,3,4,2,64,128]{5,4,3,2,1,0:T(8,128)(2,1)}, bf16[8,3,4,2,64,128]{5,4,3,2,1,0:T(8,128)(2,1)S(1)}, u32[]{:S(2)}) copy-start(bf16[8,3,4,2,64,128]{5,4,3,2,1,0:T(8,128)(2,1)S(1)} %all-to-all-done.chunk_ref) | copy-start | bytes 9437188
  147.6 1.0 copy-start.5
  148.6 36.0 %all-to-all-start.1 = ((bf16[8,4,2,64,128]{4,3,2,1,0:T(8,128)(2,1)}), bf16[8,4,2,64,128]{4,3,2,1,0:T(8,128)(2,1)S(1)}, u32[]{:S(2)}, u32[]{:S(2)}) async-start(bf16[8,4,2,64,128]{4,3,2,1,0:T(8,128)(2,1)} %copy-done.5), calls=%async_computation.1 | async-start | bytes 2097152 | tf_op jit(solution)/shard_map/all_to_all | solution.py:497
  172.1 26.0 %collective-permute-start.9 = (bf16[2,512,512]{2,1,0:T(8,128)(2,1)}, bf16[2,512,512]{2,1,0:T(8,128)(2,1)S(1)}, u32[]{:S(2)}, u32[]{:S(2)}) collective-permute-start(bf16[2,512,512]{2,1,0:T(8,128)(2,1)} %proj_part.8), channel_id=1, source_target_pairs={{0,4},{4,0},{8,12},{12,8},{16,20},{20,16},{24,28},{28,24},{1,5},{5... | collective-permute-start | bytes 3145736 | tf_op jit(solution)/shard_map/ppermute | solution.py:485
  174.3 10.3 %copy-start = (bf16[1024,512]{1,0:T(8,128)(2,1)S(1)}, bf16[1024,512]{1,0:T(8,128)(2,1)}, u32[]{:S(2)}) copy-start(bf16[1024,512]{1,0:T(8,128)(2,1)} %row_forward.1.flat_ref.row_ref) | copy-start | bytes 3145732
  185.2 1.0 copy-start.3
  186.2 1.3 copy-start.4
  198.1 6.4 %copy-start.15 = (bf16[2,512,512]{2,1,0:T(8,128)(2,1)}, bf16[2,512,512]{2,1,0:T(8,128)(2,1)S(1)}, u32[]{:S(2)}) copy-start(bf16[2,512,512]{2,1,0:T(8,128)(2,1)S(1)} %collective-permute-done.9.refs_0_) | copy-start | bytes 3145732
  198.1 28.0 %all-to-all-start.2 = ((bf16[8,4,2,64,128]{4,3,2,1,0:T(8,128)(2,1)}), bf16[8,4,2,64,128]{4,3,2,1,0:T(8,128)(2,1)}, u32[]{:S(2)}, u32[]{:S(2)}) async-start(bf16[8,4,2,64,128]{4,3,2,1,0:T(8,128)(2,1)} %get-tuple-element.75), calls=%async_computation.2 | async-start | bytes 2097152 | tf_op jit(solution)/shard_map/all_to_all | solution.py:497
  205.1 21.1 %copy-start.2 = (bf16[8,3,4,2,64,128]{5,4,3,2,1,0:T(8,128)(2,1)S(1)}, bf16[8,3,4,2,64,128]{5,4,3,2,1,0:T(8,128)(2,1)}, u32[]{:S(2)}) copy-start(bf16[8,3,4,2,64,128]{5,4,3,2,1,0:T(8,128)(2,1)} %copy-done.1) | copy-start | bytes 9437188
  240.6 12.4 %copy-start.11 = (bf16[2,512,512]{2,1,0:T(8,128)(2,1)S(1)}, bf16[2,512,512]{2,1,0:T(8,128)(2,1)}, u32[]{:S(2)}) copy-start(bf16[2,512,512]{2,1,0:T(8,128)(2,1)} %proj_part.12) | copy-start | bytes 3145732
  252.5 78.8 %collective-permute-start.10 = (bf16[1024,2048]{1,0:T(8,128)(2,1)}, bf16[1024,2048]{1,0:T(8,128)(2,1)}, u32[]{:S(2)}, u32[]{:S(2)}) collective-permute-start(bf16[1024,2048]{1,0:T(8,128)(2,1)} %layer_part.3), channel_id=1, source_target_pairs={{0,1},{1,0},{2,3},{3,2},{4,5},{5,4},{6,7},{7,6},{8,9},{9,8},{10,11... | collective-permute-start | bytes 12582920 | tf_op jit(solution)/shard_map/ppermute | solution.py:513
  252.5 25.8 %collective-permute-start.12 = (bf16[2,512,512]{2,1,0:T(8,128)(2,1)}, bf16[2,512,512]{2,1,0:T(8,128)(2,1)S(1)}, u32[]{:S(2)}, u32[]{:S(2)}) collective-permute-start(bf16[2,512,512]{2,1,0:T(8,128)(2,1)} %proj_part.10), channel_id=1, source_target_pairs={{0,4},{4,0},{8,12},{12,8},{16,20},{20,16},{24,28},{28,24},{1,5},{5... | collective-permute-start | bytes 3145736 | tf_op jit(solution)/shard_map/ppermute | solution.py:485
  253.0 33.2 %collective-permute-start.14 = (bf16[2,512,512]{2,1,0:T(8,128)(2,1)S(1)}, bf16[2,512,512]{2,1,0:T(8,128)(2,1)S(1)}, u32[]{:S(2)}, u32[]{:S(2)}) collective-permute-start(bf16[2,512,512]{2,1,0:T(8,128)(2,1)S(1)} %copy-done.11), channel_id=1, source_target_pairs={{0,8},{4,12},{24,16},{28,20},{1,9},{5,13},{25,17},{29,21},{2,10},{... | collective-permute-start | bytes 3145736 | tf_op jit(solution)/shard_map/ppermute | solution.py:485
  278.3 1.0 copy-start.16
  284.3 27.8 %copy-start.12 = (bf16[2,512,512]{2,1,0:T(8,128)(2,1)S(1)}, bf16[2,512,512]{2,1,0:T(8,128)(2,1)}, u32[]{:S(2)}) copy-start(bf16[2,512,512]{2,1,0:T(8,128)(2,1)} %proj_part.13) | copy-start | bytes 3145732
  284.3 27.8 %collective-permute-start.13 = (bf16[2,512,512]{2,1,0:T(8,128)(2,1)}, bf16[2,512,512]{2,1,0:T(8,128)(2,1)S(1)}, u32[]{:S(2)}, u32[]{:S(2)}) collective-permute-start(bf16[2,512,512]{2,1,0:T(8,128)(2,1)} %proj_part.13), channel_id=1, source_target_pairs={{0,8},{4,12},{24,16},{28,20},{1,9},{5,13},{25,17},{29,21},{2,10},{... | collective-permute-start | bytes 3145736 | tf_op jit(solution)/shard_map/ppermute | solution.py:485
  285.8 29.9 %collective-permute-start.17 = (bf16[2,512,512]{2,1,0:T(8,128)(2,1)}, bf16[2,512,512]{2,1,0:T(8,128)(2,1)}, u32[]{:S(2)}, u32[]{:S(2)}) collective-permute-start(bf16[2,512,512]{2,1,0:T(8,128)(2,1)} %proj_part.9), channel_id=1, source_target_pairs={{0,4},{4,0},{8,12},{12,8},{16,20},{20,16},{24,28},{28,24},{1,5},{5... | collective-permute-start | bytes 3145736 | tf_op jit(solution)/shard_map/ppermute | solution.py:485
  287.5 34.6 %collective-permute-start.19 = (bf16[2,512,512]{2,1,0:T(8,128)(2,1)}, bf16[2,512,512]{2,1,0:T(8,128)(2,1)S(1)}, u32[]{:S(2)}, u32[]{:S(2)}) collective-permute-start(bf16[2,512,512]{2,1,0:T(8,128)(2,1)} %add_convert_fusion), channel_id=1, source_target_pairs={{8,16},{12,20},{16,8},{20,12},{9,17},{13,21},{17,9},{21,13},{10,18... | collective-permute-start | bytes 3145736 | tf_op jit(solution)/shard_map/ppermute | solution.py:485
  290.9 48.9 %collective-permute-start.16 = (bf16[2,512,512]{2,1,0:T(8,128)(2,1)}, bf16[2,512,512]{2,1,0:T(8,128)(2,1)}, u32[]{:S(2)}, u32[]{:S(2)}) collective-permute-start(bf16[2,512,512]{2,1,0:T(8,128)(2,1)} %proj_part.11), channel_id=1, source_target_pairs={{0,4},{4,0},{8,12},{12,8},{16,20},{20,16},{24,28},{28,24},{1,5},{5... | collective-permute-start | bytes 3145736 | tf_op jit(solution)/shard_map/ppermute | solution.py:485
  312.4 27.6 %collective-permute-start.15 = (bf16[2,512,512]{2,1,0:T(8,128)(2,1)S(1)}, bf16[2,512,512]{2,1,0:T(8,128)(2,1)S(1)}, u32[]{:S(2)}, u32[]{:S(2)}) collective-permute-start(bf16[2,512,512]{2,1,0:T(8,128)(2,1)S(1)} %add_convert_fusion.1), channel_id=1, source_target_pairs={{8,16},{12,20},{16,8},{20,12},{9,17},{13,21},{17,9},{21,13},{10,18... | collective-permute-start | bytes 3145736 | tf_op jit(solution)/shard_map/ppermute | solution.py:485
  320.9 18.9 %collective-permute-start.18 = (bf16[512,512]{1,0:T(8,128)(2,1)}, bf16[512,512]{1,0:T(8,128)(2,1)}, u32[]{:S(2)}, u32[]{:S(2)}) collective-permute-start(bf16[512,512]{1,0:T(8,128)(2,1)} %bitcast.53), channel_id=1, source_target_pairs={{0,8},{4,12},{24,16},{28,20},{1,9},{5,13},{25,17},{29,21},{2,10},{... | collective-permute-start | bytes 1572872 | tf_op jit(solution)/shard_map/ppermute | solution.py:485
  322.2 17.6 %copy-start.14 = (bf16[2,512,512]{2,1,0:T(8,128)(2,1)}, bf16[2,512,512]{2,1,0:T(8,128)(2,1)S(1)}, u32[]{:S(2)}) copy-start(bf16[2,512,512]{2,1,0:T(8,128)(2,1)S(1)} %collective-permute-done.19) | copy-start | bytes 3145732
  324.6 15.4 %collective-permute-start.20 = (bf16[512,512]{1,0:T(8,128)(2,1)}, bf16[512,512]{1,0:T(8,128)(2,1)}, u32[]{:S(2)}, u32[]{:S(2)}) collective-permute-start(bf16[512,512]{1,0:T(8,128)(2,1)} %fusion.5), channel_id=1, source_target_pairs={{8,0},{12,4},{16,24},{20,28},{9,1},{13,5},{17,25},{21,29},{10,2},{... | collective-permute-start | bytes 1572872 | tf_op jit(solution)/shard_map/ppermute | solution.py:485
  340.0 1.0 copy-start.13
  341.0 72.1 %all-to-all-start.3 = ((bf16[8,3,4,2,64,128]{5,4,3,2,1,0:T(8,128)(2,1)}), bf16[8,3,4,2,64,128]{5,4,3,2,1,0:T(8,128)(2,1)S(1)}, u32[]{:S(2)}, u32[]{:S(2)}) async-start(bf16[8,3,4,2,64,128]{5,4,3,2,1,0:T(8,128)(2,1)} %column_backward.1), calls=%async_computation.3 | async-start | bytes 6291456 | tf_op jit(solution)/shard_map/all_to_all | solution.py:497
  347.4 45.0 %collective-permute-start.11 = (bf16[1024,1024]{1,0:T(8,128)(2,1)}, bf16[1024,1024]{1,0:T(8,128)(2,1)}, u32[]{:S(2)}, u32[]{:S(2)}) collective-permute-start(bf16[1024,1024]{1,0:T(8,128)(2,1)} %layer_part.4), channel_id=1, source_target_pairs={{0,2},{1,3},{2,0},{3,1},{4,6},{5,7},{6,4},{7,5},{8,10},{9,11},{10,... | collective-permute-start | bytes 6291464 | tf_op jit(solution)/shard_map/ppermute | solution.py:513
  354.8 53.3 %collective-permute-start.21 = (bf16[512,512]{1,0:T(8,128)(2,1)}, bf16[512,512]{1,0:T(8,128)(2,1)}, u32[]{:S(2)}, u32[]{:S(2)}) collective-permute-start(bf16[512,512]{1,0:T(8,128)(2,1)} %bitcast.52), channel_id=1, source_target_pairs={{0,8},{4,12},{24,16},{28,20},{1,9},{5,13},{25,17},{29,21},{2,10},{... | collective-permute-start | bytes 1572872 | tf_op jit(solution)/shard_map/ppermute | solution.py:485
  358.2 49.9 %collective-permute-start.22 = (bf16[512,512]{1,0:T(8,128)(2,1)}, bf16[512,512]{1,0:T(8,128)(2,1)}, u32[]{:S(2)}, u32[]{:S(2)}) collective-permute-start(bf16[512,512]{1,0:T(8,128)(2,1)} %fusion), channel_id=1, source_target_pairs={{8,0},{12,4},{16,24},{20,28},{9,1},{13,5},{17,25},{21,29},{10,2},{... | collective-permute-start | bytes 1572872 | tf_op jit(solution)/shard_map/ppermute | solution.py:485
  413.0 1.6 copy-start.6
